TPU v7x, 32 devices: a whole 2x2x4 slice. The times are simulated.
32 devices in a mesh: ctx: 8 (over z, y), wa: 4 (over x, core).
Axes of the slice: x: 2, y: 2, z: 4, core: 2. Of those that a mesh axis runs over, the one named last changes fastest.
Arguments:
- tokens: bfloat16 [4, 1024, 2048], P('wa', 'ctx'), may hold values from -6 to 6
- cotangent: bfloat16 [4, 1024, 2048], P('wa', 'ctx'), may hold values from -6 to 6
- deal: int32 [16], replicated, may hold values from 0 to 15, each once
- doc_lengths: int32 [4, 16], P('wa'), may hold values from 1 to 512, 1024 in all within a row
- doc_adapter: int32 [4, 16], P('wa'), may hold values from 0 to 7
- ln1_gain: float32 [2048], replicated, may hold values from 0.5 to 1.5
- ln1_bias: float32 [2048], replicated, may hold values from -1 to 1
- ln2_gain: float32 [2048], replicated, may hold values from 0.5 to 1.5
- ln2_bias: float32 [2048], replicated, may hold values from -1 to 1
- qkv_weight: bfloat16 [2048, 6144], P('wa'), may hold values from -0.125 to 0.125
- qkv_bias: float32 [6144], replicated, may hold values from -1 to 1
- dense_weight: bfloat16 [2048, 2048], P('wa'), may hold values from -0.5 to 0.5
- dense_bias: float32 [2048], replicated, may hold values from -1 to 1
- in_weight: bfloat16 [2048, 8192], P('wa'), may hold values from -0.125 to 0.125
- in_bias: float32 [8192], replicated, may hold values from -1 to 1
- out_weight: bfloat16 [8192, 2048], P('wa'), may hold values from -0.0625 to 0.0625
- out_bias: float32 [2048], replicated, may hold values from -1 to 1
- qkv_down: bfloat16 [2048, 128], P('wa'), may hold values from -0.125 to 0.125
- qkv_up: bfloat16 [128, 6144], P('wa'), may hold values from -1.5 to 1.5
- dense_down: bfloat16 [2048, 128], P('wa'), may hold values from -0.125 to 0.125
- dense_up: bfloat16 [128, 2048], P('wa'), may hold values from -1.5 to 1.5
- in_down: bfloat16 [2048, 128], P('wa'), may hold values from -0.125 to 0.125
- in_up: bfloat16 [128, 8192], P('wa'), may hold values from -1.5 to 1.5
- out_down: bfloat16 [8192, 128], P('wa'), may hold values from -0.0625 to 0.0625
- out_up: bfloat16 [128, 2048], P('wa'), may hold values from -1.5 to 1.5
Outputs:
- output: bfloat16 [4, 1024, 2048], P('wa', 'ctx')
- tokens_grad: float32 [4, 1024, 2048], P('wa', 'ctx')
- qkv_down_grad: float32 [2048, 128], P('wa')
- qkv_up_grad: float32 [128, 6144], P('wa')
- dense_down_grad: float32 [2048, 128], P('wa')
- dense_up_grad: float32 [128, 2048], P('wa')
- in_down_grad: float32 [2048, 128], P('wa')
- in_up_grad: float32 [128, 8192], P('wa')
- out_down_grad: float32 [8192, 128], P('wa')
- out_up_grad: float32 [128, 2048], P('wa')
Inputs may be any that keep to these rules, and one draw needn't show every extreme that they name: `deal`: every block number appears once. `doc_lengths`: the lengths of each pack sum to 1024; the largest of each pack is exactly 512.
All inputs are finite; a program needn't handle non-finite values.
Results may differ from a plain program's by a relative error of at most 0.017.
Values may be sent and summed in bfloat16 or wider, within the bound.
No kernel may reach another device: no remote copies, remote signals or barrier semaphores. Data moves between devices by JAX's collectives and lax.ppermute only.
A program may use at most 448 MiB of HBM per device.

v0:
```python
import math

import jax
import jax.numpy as jnp
from jax import lax
from jax.sharding import PartitionSpec as P

HEADS = 8
HEAD = 256
ROT = 64
RANK = 16
BLOCK = 64
ADAPT_COLS = 128


epsilon = 1e-05
masked_score = -1e30


def product(left, right):
    return jnp.dot(left, right, preferred_element_type=jnp.float32)


def times_t(left, right):
    return lax.dot_general(
        left, right, (((1,), (1,)), ((), ())), preferred_element_type=jnp.float32
    )


def t_times(left, right):
    return lax.dot_general(
        left, right, (((0,), (0,)), ((), ())), preferred_element_type=jnp.float32
    )


def layer_norm(values, gain, shift):
    centered = values - jnp.mean(values, axis=-1, keepdims=True)
    spread = jnp.mean(centered * centered, axis=-1, keepdims=True)
    return centered * lax.rsqrt(spread + epsilon) * gain + shift


def gelu_exact(values):
    return jax.nn.gelu(values, approximate=False)


def rotate(values, offset, turn):
    half = ROT // 2
    freq = 10000.0 ** (-2.0 * jnp.arange(half, dtype=jnp.float32) / ROT)
    angle = offset.astype(jnp.float32)[:, None] * freq[None, :]
    cosine = jnp.cos(angle)[:, None, :]
    sine = turn * jnp.sin(angle)[:, None, :]
    first = values[..., :half]
    second = values[..., half:ROT]
    return jnp.concatenate(
        [first * cosine - second * sine, second * cosine + first * sine, values[..., ROT:]], axis=-1
    )


def pack_places(global_rows, deal):
    blocks = global_rows // BLOCK
    table = jnp.arange(deal.shape[0], dtype=jnp.int32)
    picked = jnp.sum(jnp.where(table[None, :] == blocks[:, None], deal[None, :], 0), axis=1)
    return picked * BLOCK + global_rows % BLOCK


def doc_tables(place, starts):
    inside = starts[None, :] <= place[:, None]
    docs = jnp.sum(inside.astype(jnp.int32), axis=1) - 1
    begin = jnp.max(jnp.where(inside, starts[None, :], 0), axis=1)
    return (docs, place - begin)


def block_size():
    return 1024


def add_columns(total, term):
    return total + term


def body(
    tokens,
    cotangent,
    deal,
    doc_lengths,
    doc_adapter,
    ln1_gain,
    ln1_bias,
    ln2_gain,
    ln2_bias,
    qkv_weight,
    qkv_bias,
    dense_weight,
    dense_bias,
    in_weight,
    in_bias,
    out_weight,
    out_bias,
    qkv_down,
    qkv_up,
    dense_down,
    dense_up,
    in_down,
    in_up,
    out_down,
    out_up,
):
    local_rows = tokens.shape[1]
    width = tokens.shape[2]
    scale = 1.0 / math.sqrt(HEAD)
    head_shape = (local_rows, HEADS, HEAD)
    values = tokens[0].astype(jnp.float32)
    lengths = doc_lengths[0]
    starts = jnp.cumsum(lengths) - lengths
    own_rows = lax.axis_index("ctx") * local_rows + jnp.arange(local_rows, dtype=jnp.int32)
    place = pack_places(own_rows, deal)
    docs, offset = doc_tables(place, starts)
    doc_table = jnp.arange(lengths.shape[0], dtype=jnp.int32)
    chosen = jnp.sum(
        jnp.where(docs[:, None] == doc_table[None, :], doc_adapter[0][None, :], 0), axis=1
    )
    columns = jnp.arange(ADAPT_COLS, dtype=jnp.int32) // RANK
    mask = (columns[None, :] == chosen[:, None]).astype(jnp.float32)
    (
        qkv_down_all,
        qkv_up_all,
        dense_down_all,
        dense_up_all,
        in_down_all,
        in_up_all,
        out_down_all,
        out_up_all,
    ) = (
        lax.all_gather(qkv_down, "wa", axis=0, tiled=True),
        lax.all_gather(qkv_up, "wa", axis=0, tiled=True),
        lax.all_gather(dense_down, "wa", axis=0, tiled=True),
        lax.all_gather(dense_up, "wa", axis=0, tiled=True),
        lax.all_gather(in_down, "wa", axis=0, tiled=True),
        lax.all_gather(in_up, "wa", axis=0, tiled=True),
        lax.all_gather(out_down, "wa", axis=0, tiled=True),
        lax.all_gather(out_up, "wa", axis=0, tiled=True),
    )
    first_norm = layer_norm(values, ln1_gain, ln1_bias).astype(jnp.bfloat16)
    second_norm = layer_norm(values, ln2_gain, ln2_bias).astype(jnp.bfloat16)
    first_inner = (product(first_norm, qkv_down_all) * mask).astype(jnp.bfloat16)
    second_inner = (product(second_norm, in_down_all) * mask).astype(jnp.bfloat16)
    pieces = (
        lax.all_gather(qkv_weight, "wa", axis=0, tiled=True),
        lax.all_gather(in_weight, "wa", axis=0, tiled=True),
    )
    first_part = first_norm
    second_part = second_norm
    mixed_sum = product(first_part, pieces[0])
    hidden_sum = product(second_part, pieces[1])
    mixed = mixed_sum + qkv_bias + product(first_inner, qkv_up_all)
    hidden_pre = hidden_sum + in_bias + product(second_inner, in_up_all)
    query = rotate(mixed[:, :width].reshape(head_shape), offset, 1.0).astype(jnp.bfloat16)
    key = rotate(mixed[:, width : 2 * width].reshape(head_shape), offset, 1.0).astype(jnp.bfloat16)
    key = key.reshape(local_rows, width)
    value = mixed[:, 2 * width :].astype(jnp.bfloat16)

    def key_masks(first, size):
        key_rows = first + jnp.arange(size, dtype=jnp.int32)
        key_place = pack_places(key_rows, deal)
        key_docs, unused = doc_tables(key_place, starts)
        return (docs[:, None] == key_docs[None, :]) & (key_place[None, :] <= place[:, None])

    initial = (
        jnp.full((HEADS, local_rows), masked_score, jnp.float32),
        jnp.zeros((HEADS, local_rows), jnp.float32),
        jnp.zeros(head_shape, jnp.float32),
    )
    carry = initial
    pieces = (
        lax.all_gather(key, "ctx", axis=0, tiled=True),
        lax.all_gather(value, "ctx", axis=0, tiled=True),
    )
    count = pieces[0].shape[0]
    attend_size = block_size()
    blocks = count // attend_size

    def step(state, item):
        key_block, value_block, first = item
        allowed = key_masks(first, attend_size)
        scores = (
            jnp.einsum(
                "qhd,khd->hqk",
                query,
                key_block.reshape(attend_size, HEADS, HEAD),
                preferred_element_type=jnp.float32,
            )
            * scale
        )
        scores = jnp.where(allowed[None], scores, masked_score)
        top, total, gathered = state
        new_top = jnp.maximum(top, jnp.max(scores, axis=2))
        weights = jnp.where(allowed[None], jnp.exp(scores - new_top[:, :, None]), 0.0)
        factor = jnp.exp(top - new_top)
        total = total * factor + jnp.sum(weights, axis=2)
        gathered = gathered * jnp.transpose(factor)[:, :, None] + jnp.einsum(
            "hqk,khd->qhd",
            weights.astype(jnp.bfloat16),
            value_block.reshape(attend_size, HEADS, HEAD),
            preferred_element_type=jnp.float32,
        )
        return ((new_top, total, gathered), None)

    firsts = jnp.arange(blocks, dtype=jnp.int32) * attend_size
    carry, unused = lax.scan(
        step,
        carry,
        (
            pieces[0].reshape(blocks, attend_size, width),
            pieces[1].reshape(blocks, attend_size, width),
            firsts,
        ),
    )
    top, total, gathered = carry
    attended_full = gathered / jnp.transpose(total)[:, :, None]
    log_total = top + jnp.log(total)
    attended = attended_full.reshape(local_rows, width).astype(jnp.bfloat16)
    dense_inner = (product(attended, dense_down_all) * mask).astype(jnp.bfloat16)
    hidden = gelu_exact(hidden_pre).astype(jnp.bfloat16)
    out_inner = (product(hidden, out_down_all) * mask).astype(jnp.bfloat16)
    pieces = (
        lax.all_gather(dense_weight, "wa", axis=0, tiled=True),
        lax.all_gather(out_weight, "wa", axis=0, tiled=True),
    )
    first_part = attended
    second_part = hidden
    branches = product(first_part, pieces[0]) + product(second_part, pieces[1])
    result = (
        values
        + branches
        + dense_bias
        + out_bias
        + product(dense_inner, dense_up_all)
        + product(out_inner, out_up_all)
    )
    output = result.astype(jnp.bfloat16)[None]
    grad = cotangent[0]
    dense_up_grad = t_times(dense_inner, grad)
    out_up_grad = t_times(out_inner, grad)
    dense_inner_grad = (times_t(grad, dense_up_all) * mask).astype(jnp.bfloat16)
    out_inner_grad = (times_t(grad, out_up_all) * mask).astype(jnp.bfloat16)
    dense_down_grad = t_times(attended, dense_inner_grad)
    out_down_grad = t_times(hidden, out_inner_grad)
    totals = (times_t(dense_inner_grad, dense_down_all), times_t(out_inner_grad, out_down_all))
    pieces = (
        lax.all_gather(dense_weight, "wa", axis=0, tiled=True),
        lax.all_gather(out_weight, "wa", axis=0, tiled=True),
    )
    attended_grad = add_columns(totals[0], times_t(grad, pieces[0]))
    hidden_grad = add_columns(totals[1], times_t(grad, pieces[1]))
    pre_grad = jax.vjp(gelu_exact, hidden_pre)[1](hidden_grad)[0].astype(jnp.bfloat16)
    out_grad = attended_grad.astype(jnp.bfloat16).reshape(head_shape)
    delta = jnp.einsum("qhd,qhd->hq", out_grad.astype(jnp.float32), attended_full)
    key_back, value_back = (
        lax.all_gather(key, "ctx", axis=0, tiled=True),
        lax.all_gather(value, "ctx", axis=0, tiled=True),
    )
    every = key_back.shape[0]
    size = block_size()
    blocks = every // size
    firsts = jnp.arange(blocks, dtype=jnp.int32) * size

    def back_step(query_grad, item):
        key_block, value_block, first = item
        allowed = key_masks(first, size)
        keys_split = key_block.reshape(size, HEADS, HEAD)
        values_split = value_block.reshape(size, HEADS, HEAD)
        scores = (
            jnp.einsum("qhd,khd->hqk", query, keys_split, preferred_element_type=jnp.float32)
            * scale
        )
        prob = jnp.where(allowed[None], jnp.exp(scores - log_total[:, :, None]), 0.0)
        value_grad = jnp.einsum(
            "hqk,qhd->khd", prob.astype(jnp.bfloat16), out_grad, preferred_element_type=jnp.float32
        )
        prob_grad = jnp.einsum(
            "qhd,khd->hqk", out_grad, values_split, preferred_element_type=jnp.float32
        )
        score_grad = (prob * (prob_grad - delta[:, :, None])).astype(jnp.bfloat16)
        query_grad = query_grad + scale * jnp.einsum(
            "hqk,khd->qhd", score_grad, keys_split, preferred_element_type=jnp.float32
        )
        key_grad = scale * jnp.einsum(
            "hqk,qhd->khd", score_grad, query, preferred_element_type=jnp.float32
        )
        return (
            query_grad,
            jnp.concatenate(
                [key_grad.reshape(size, width), value_grad.reshape(size, width)], axis=1
            ),
        )

    query_grad, pairs = lax.scan(
        back_step,
        jnp.zeros(head_shape, jnp.float32),
        (key_back.reshape(blocks, size, width), value_back.reshape(blocks, size, width), firsts),
    )
    own_pairs = lax.psum_scatter(
        pairs.reshape(every, 2 * width).astype(jnp.bfloat16), "ctx", scatter_dimension=0, tiled=True
    ).astype(jnp.float32)
    key_grad_own = rotate(own_pairs[:, :width].reshape(head_shape), offset, -1.0).reshape(
        local_rows, width
    )
    query_grad_own = rotate(query_grad, offset, -1.0).reshape(local_rows, width)
    mixed_grad = jnp.concatenate(
        [query_grad_own, key_grad_own, own_pairs[:, width:]], axis=1
    ).astype(jnp.bfloat16)
    qkv_up_grad = t_times(first_inner, mixed_grad)
    in_up_grad = t_times(second_inner, pre_grad)
    first_inner_grad = (times_t(mixed_grad, qkv_up_all) * mask).astype(jnp.bfloat16)
    second_inner_grad = (times_t(pre_grad, in_up_all) * mask).astype(jnp.bfloat16)
    qkv_down_grad = t_times(first_norm, first_inner_grad)
    in_down_grad = t_times(second_norm, second_inner_grad)
    totals = (times_t(first_inner_grad, qkv_down_all), times_t(second_inner_grad, in_down_all))
    pieces = (
        lax.all_gather(qkv_weight, "wa", axis=0, tiled=True),
        lax.all_gather(in_weight, "wa", axis=0, tiled=True),
    )
    first_grad = add_columns(totals[0], times_t(mixed_grad, pieces[0]))
    second_grad = add_columns(totals[1], times_t(pre_grad, pieces[1]))

    def first_layer(inputs):
        return layer_norm(inputs, ln1_gain, ln1_bias)

    def second_layer(inputs):
        return layer_norm(inputs, ln2_gain, ln2_bias)

    first_back = jax.vjp(first_layer, values)[1](first_grad)[0]
    second_back = jax.vjp(second_layer, values)[1](second_grad)[0]
    tokens_grad = (grad.astype(jnp.float32) + first_back + second_back)[None]
    totals = (
        lax.psum(qkv_down_grad.astype(jnp.bfloat16), "ctx").astype(jnp.float32),
        lax.psum(qkv_up_grad.astype(jnp.bfloat16), "ctx").astype(jnp.float32),
        lax.psum(dense_down_grad.astype(jnp.bfloat16), "ctx").astype(jnp.float32),
        lax.psum(dense_up_grad.astype(jnp.bfloat16), "ctx").astype(jnp.float32),
        lax.psum(in_down_grad.astype(jnp.bfloat16), "ctx").astype(jnp.float32),
        lax.psum(in_up_grad.astype(jnp.bfloat16), "ctx").astype(jnp.float32),
        lax.psum(out_down_grad.astype(jnp.bfloat16), "ctx").astype(jnp.float32),
        lax.psum(out_up_grad.astype(jnp.bfloat16), "ctx").astype(jnp.float32),
    )
    shares = (
        lax.psum_scatter(
            totals[0].astype(jnp.bfloat16), "wa", scatter_dimension=0, tiled=True
        ).astype(jnp.float32),
        lax.psum_scatter(
            totals[1].astype(jnp.bfloat16), "wa", scatter_dimension=0, tiled=True
        ).astype(jnp.float32),
        lax.psum_scatter(
            totals[2].astype(jnp.bfloat16), "wa", scatter_dimension=0, tiled=True
        ).astype(jnp.float32),
        lax.psum_scatter(
            totals[3].astype(jnp.bfloat16), "wa", scatter_dimension=0, tiled=True
        ).astype(jnp.float32),
        lax.psum_scatter(
            totals[4].astype(jnp.bfloat16), "wa", scatter_dimension=0, tiled=True
        ).astype(jnp.float32),
        lax.psum_scatter(
            totals[5].astype(jnp.bfloat16), "wa", scatter_dimension=0, tiled=True
        ).astype(jnp.float32),
        lax.psum_scatter(
            totals[6].astype(jnp.bfloat16), "wa", scatter_dimension=0, tiled=True
        ).astype(jnp.float32),
        lax.psum_scatter(
            totals[7].astype(jnp.bfloat16), "wa", scatter_dimension=0, tiled=True
        ).astype(jnp.float32),
    )
    return (
        output,
        tokens_grad,
        shares[0],
        shares[1],
        shares[2],
        shares[3],
        shares[4],
        shares[5],
        shares[6],
        shares[7],
    )


def solution(mesh):
    in_specs = (
        P("wa", "ctx", None),
        P("wa", "ctx", None),
        P(),
        P("wa", None),
        P("wa", None),
        P(),
        P(),
        P(),
        P(),
        P("wa", None),
        P(),
        P("wa", None),
        P(),
        P("wa", None),
        P(),
        P("wa", None),
        P(),
        P("wa", None),
        P("wa", None),
        P("wa", None),
        P("wa", None),
        P("wa", None),
        P("wa", None),
        P("wa", None),
        P("wa", None),
    )
    out_specs = (
        P("wa", "ctx", None),
        P("wa", "ctx", None),
        P("wa", None),
        P("wa", None),
        P("wa", None),
        P("wa", None),
        P("wa", None),
        P("wa", None),
        P("wa", None),
        P("wa", None),
    )
    return jax.shard_map(body, mesh=mesh, in_specs=in_specs, out_specs=out_specs, check_vma=False)
```

profile of v0, /device:TPU:0, one launch (start us, length us, event | category | flops | bytes accessed | tf_op | source)
XLA Modules:
  0.0 1362.4 jit_solution(15305505163798155657)
XLA Ops:
  11.2 8.6 all_gather.49
  21.2 146.0 %all-gather.10.cloned.1.call-done = bf16[2048,6144]{1,0:T(8,128)(2,1)} async-done(((bf16[512,6144]{1,0:T(8,128)(2,1)}), bf16[2048,6144]{1,0:T(8,128)(2,1)}) %all-gather.10.cloned.1.call-update) | async-done | bytes 25165840 | tf_op jit(solution)/shard_map/all_gather | solution.py:148
  167.2 13.5 convolution_add_fusion.4
  180.7 7.8 all-gather.12.cloned.1.call-done
  188.5 2.9 convolution_add_fusion.3
  196.9 2.2 slice.104
  202.5 10.4 all_gather.59
  212.9 10.9 all_gather.58
  223.8 1.6 fusion.60
  225.4 28.6 %all-gather.18.cloned.1.call-done = bf16[2048,2048]{1,0:T(8,128)(2,1)} async-done(((bf16[512,2048]{1,0:T(8,128)(2,1)}), bf16[2048,2048]{1,0:T(8,128)(2,1)}) %all-gather.18.cloned.1.call-update) | async-done | bytes 8388624 | tf_op jit(solution)/shard_map/all_gather | solution.py:226
  254.0 6.3 fusion.81
  261.8 2.5 copy.112
  265.9 65.6 %all-gather.14.cloned.1.call-done = bf16[1024,2048]{0,1:T(8,128)(2,1)} async-done(((bf16[128,2048]{0,1:T(8,128)(2,1)}), bf16[1024,2048]{0,1:T(8,128)(2,1)}) %all-gather.14.cloned.1.call-update) | async-done | bytes 4194320 | tf_op jit(solution)/shard_map/all_gather | solution.py:175
  331.5 3.7 select_reduce_fusion
  335.2 2.0 copy-done
  337.2 1.3 fusion.13
  339.7 65.9 %all-gather.16.cloned.1.call-done = bf16[1024,2048]{1,0:T(8,128)(2,1)} async-done(((bf16[128,2048]{1,0:T(8,128)(2,1)}), bf16[1024,2048]{1,0:T(8,128)(2,1)}) %all-gather.16.cloned.1.call-update) | async-done | bytes 4194320 | tf_op jit(solution)/shard_map/all_gather | solution.py:176
  405.7 6.6 fusion.117
  412.9 2.8 multiply_convert_fusion.1
  415.8 3.8 multiply_convert_fusion
  419.6 3.9 convolution_convert_fusion.3
  423.4 10.2 pad_maximum_fusion
  433.7 11.5 copy.115
  446.0 10.4 all_gather.55
  457.6 10.5 all_gather.61
  471.1 141.4 %all-gather.24.cloned.1.call-done = bf16[8192,2048]{1,0:T(8,128)(2,1)} async-done(((bf16[2048,2048]{1,0:T(8,128)(2,1)}), bf16[8192,2048]{1,0:T(8,128)(2,1)}) %all-gather.24.cloned.1.call-update) | async-done | bytes 33554448 | tf_op jit(solution)/shard_map/all_gather | solution.py:227
  612.5 22.1 %fusion.78 = f32[128,8192]{1,0:T(8,128)} fusion(bf16[8192,2048]{1,0:T(8,128)(2,1)} %all-gather.24.cloned.1.call-done, bf16[1,128,2048]{2,1,0:T(8,128)(2,1)S(1)} %copy-done.3), kind=kOutput, calls=%fused_computation.123 | convolution fusion | flops 4294967296 | bytes 38273024 | tf_op jit(solution)/shard_map/dot_general | solution.py:25
  634.6 181.1 %all-gather.20.cloned.1.call-done = bf16[2048,8192]{1,0:T(8,128)(2,1)} async-done(((bf16[512,8192]{1,0:T(8,128)(2,1)}), bf16[2048,8192]{1,0:T(8,128)(2,1)}) %all-gather.20.cloned.1.call-update) | async-done | bytes 33554448 | tf_op jit(solution)/shard_map/all_gather | solution.py:149
  815.7 17.9 %convolution_add_fusion.2 = f32[128,8192]{1,0:T(8,128)} fusion(bf16[2048,8192]{1,0:T(8,128)(2,1)} %all-gather.20.cloned.1.call-done, f32[8192]{0:T(1024)S(1)} %copy-done.56, bf16[1,128,2048]{2,1,0:T(8,128)(2,1)S(1)} %copy-done.2, f32[2048]{0:T(1024)S(1)} %copy-done.68, f32[2048]{0:T(1024)S(1)} %copy-done.57, f32[128]{0:T(128)S(1)} %fusion.96, ...), kind=kOutput, calls=%fused_computation.2 | convolution fusion | flops 4297588736 | bytes 38323200 | tf_op jit(solution)/shard_map/dot_general | solution.py:21
  833.5 6.3 all-gather.22.cloned.1.call-done
  839.8 13.2 multiply_convert_fusion.2
  853.1 10.9 all-gather.26.cloned.1.call-done
  864.0 6.7 add_convert_fusion
  874.7 2.4 fusion.59
  879.1 3.7 convolution_convert_fusion.1
  882.8 2.1 convolution_convert_fusion
  885.0 4.4 fusion.36
  891.4 125.1 %reduce-scatter.28.cloned.1.call-done = bf16[128,4096]{1,0:T(8,128)(2,1)} async-done(((bf16[1024,4096]{1,0:T(8,128)(2,1)}), bf16[128,4096]{1,0:T(8,128)(2,1)}) %reduce-scatter.28.cloned.1.call-update) | async-done | bytes 1048592
  1016.5 2.3 fusion.114
  1018.8 2.0 copy.119
  1020.9 2.0 copy.103
  1025.2 2.5 subtract_convert_fusion.1
  1028.9 2.1 copy.100
  1031.0 1.7 copy.104
  1032.7 1.7 copy.105
  1034.4 2.0 copy.120
  1038.1 2.4 fusion.61
  1041.9 5.9 fusion.118
  1047.9 1.7 convolution_convert_fusion.2
  1050.0 13.7 %fusion.19 = f32[128,2048]{1,0:T(8,128)S(1)} fusion(f32[128,2048]{1,0:T(8,128)} %fusion.118, bf16[128,8192]{1,0:T(8,128)(2,1)S(1)} %get-tuple-element.98, bf16[8192,2048]{1,0:T(8,128)(2,1)} %all-gather.24.cloned.1.call-done, bf16[1,128,2048]{2,1,0:T(8,128)(2,1)S(1)} %copy-done.2, f32[2048]{0:T(1024)S(1)} %copy-done.66, f32[2048]{0:T(1024)S(1)} %copy-done.67), kind=kOutput, calls=%fused_computation.51 | convolution fusion | flops 4296278016 | bytes 38289408 | tf_op jit(solution)/shard_map/dot_general | solution.py:21
  1065.4 16.0 %fusion.119 = f32[128,2048]{1,0:T(8,128)S(1)} fusion(bf16[128,8192]{1,0:T(8,128)(2,1)S(1)} %copy-done.5, bf16[2048,8192]{1,0:T(8,128)(2,1)} %all-gather.20.cloned.1.call-done), kind=kOutput, calls=%fused_computation.209 | convolution fusion | flops 4294967296 | bytes 36700160 | tf_op jit(solution)/shard_map/dot_general | solution.py:25
  1081.8 6.4 reduce-scatter.20.cloned.1.call-done
  1088.3 24.0 %reduce-scatter.26.cloned.1.call-done = bf16[32,2048]{1,0:T(8,128)(2,1)} async-done(((bf16[128,2048]{1,0:T(8,128)(2,1)}), bf16[32,2048]{1,0:T(8,128)(2,1)}) %reduce-scatter.26.cloned.1.call-update) | async-done | bytes 131088 | tf_op jit(solution)/shard_map/reduce_scatter | solution.py:367
  1112.3 34.0 %reduce-scatter.22.cloned.1.call-done = bf16[32,8192]{1,0:T(8,128)(2,1)} async-done(((bf16[128,8192]{1,0:T(8,128)(2,1)}), bf16[32,8192]{1,0:T(8,128)(2,1)}) %reduce-scatter.22.cloned.1.call-update) | async-done | bytes 524304 | tf_op jit(solution)/shard_map/reduce_scatter | solution.py:361
  1146.3 33.8 %reduce-scatter.24.cloned.1.call-done = bf16[2048,128]{1,0:T(8,128)(2,1)} async-done(((bf16[8192,128]{1,0:T(8,128)(2,1)}), bf16[2048,128]{1,0:T(8,128)(2,1)}) %reduce-scatter.24.cloned.1.call-update) | async-done | bytes 524304 | tf_op jit(solution)/shard_map/reduce_scatter | solution.py:364
  1180.1 24.2 %reduce-scatter.12.cloned.1.call-done = bf16[512,128]{1,0:T(8,128)(2,1)} async-done(((bf16[2048,128]{1,0:T(8,128)(2,1)}), bf16[512,128]{1,0:T(8,128)(2,1)}) %reduce-scatter.12.cloned.1.call-update) | async-done | bytes 131088 | tf_op jit(solution)/shard_map/reduce_scatter | solution.py:346
  1204.3 30.6 %reduce-scatter.14.cloned.1.call-done = bf16[32,6144]{1,0:T(8,128)(2,1)} async-done(((bf16[128,6144]{1,0:T(8,128)(2,1)}), bf16[32,6144]{1,0:T(8,128)(2,1)}) %reduce-scatter.14.cloned.1.call-update) | async-done | bytes 393232 | tf_op jit(solution)/shard_map/reduce_scatter | solution.py:349
  1235.0 14.0 %fusion.105 = f32[128,2048]{1,0:T(8,128)} fusion(bf16[2048,6144]{1,0:T(8,128)(2,1)} %all-gather.10.cloned.1.call-done, bf16[128,2048]{0,1:T(8,128)(2,1)S(1)} %copy-done.31, bf16[128,2048]{0,1:T(8,128)(2,1)} %bitcast.208, bf16[128,2048]{0,1:T(8,128)(2,1)S(1)} %bitcast.206), kind=kOutput, calls=%fused_computation.202 | convolution fusion | flops 3225944064 | bytes 27787264 | tf_op jit(solution)/shard_map/dot_general | solution.py:25
  1249.0 1.9 fusion.69
  1251.5 1.6 add_bitcast_fusion
  1253.0 92.5 %all-reduce.3.cloned.1.call-done = (bf16[512,128]{1,0:T(8,128)(2,1)}, bf16[32,6144]{1,0:T(8,128)(2,1)}, bf16[512,128]{1,0:T(8,128)(2,1)}, bf16[32,2048]{1,0:T(8,...) async-done(((bf16[512,128]{1,0:T(8,128)(2,1)}, bf16[32,6144]{1,0:T(8,128)(2,1)}, ...) | async-done | bytes 2097168 | tf_op jit(solution)/shard_map/psum | solution.py:336
  1345.6 2.1 convert_element_type.201
  1347.8 2.1 convert_element_type.203
  1349.8 1.9 convert_element_type.193
  (273 shorter events, 44.7 us)
Async XLA Ops:
  7.2 13.6 copy-start.51
  7.2 13.6 copy-start.52
  7.3 159.9 %all-gather.10.cloned.1.call-start = ((), (), s32[]{:S(2)}) async-start(), calls=%async_computation.9 | async-start | bytes 31457280 | tf_op jit(solution)/shard_map/all_gather | solution.py:148
  8.0 159.2 %copy-start.59 = (f32[6144]{0:T(1024)S(1)}, f32[6144]{0:T(1024)}, u32[]{:S(2)}) copy-start(f32[6144]{0:T(1024)} %param.35) | copy-start | bytes 73732
  8.0 180.5 %all-gather.12.cloned.1.call-start = ((), (), s32[]{:S(2)}) async-start(), calls=%async_computation.10 | async-start | bytes 1966080 | tf_op jit(solution)/shard_map/all_gather | solution.py:135
  8.7 245.2 %all-gather.18.cloned.1.call-start = ((), (), s32[]{:S(2)}) async-start(), calls=%async_computation.13 | async-start | bytes 10485760 | tf_op jit(solution)/shard_map/all_gather | solution.py:226
  9.5 322.0 %all-gather.14.cloned.1.call-start = ((), (), s32[]{:S(2)}) async-start(), calls=%async_computation.11 | async-start | bytes 4718592 | tf_op jit(solution)/shard_map/all_gather | solution.py:175
  9.7 170.9 %copy-start.62 = (s32[128]{0:T(128)}, s32[128]{0:T(128)S(1)}, u32[]{:S(2)}) copy-start(s32[128]{0:T(128)S(1)} %and_select_fusion) | copy-start | bytes 1540
  9.9 170.8 %copy-start.71 = (s32[16]{0:T(128)}, s32[16]{0:T(128)S(1)}, u32[]{:S(2)}) copy-start(s32[16]{0:T(128)S(1)} %subtract_bitcast_fusion) | copy-start | bytes 196
  10.5 170.2 %copy-start.64 = (s32[128]{0:T(128)}, s32[128]{0:T(128)S(1)}, u32[]{:S(2)}) copy-start(s32[128]{0:T(128)S(1)} %select_reduce_fusion.2) | copy-start | bytes 1540
  11.2 169.5 %copy-start.73 = (f32[128]{0:T(128)}, f32[128]{0:T(128)S(1)}, u32[]{:S(2)}) copy-start(f32[128]{0:T(128)S(1)} %fusion.68) | copy-start | bytes 1540
  20.8 172.8 %copy-start.27 = (f32[128,32]{1,0:T(8,128)}, f32[128,32]{1,0:T(8,128)S(1)}, u32[]{:S(2)}) copy-start(f32[128,32]{1,0:T(8,128)S(1)} %get-tuple-element.124) | copy-start | bytes 49156
  21.2 167.2 %copy-start.54 = (bf16[128,128]{1,0:T(8,128)(2,1)}, bf16[128,128]{1,0:T(8,128)(2,1)S(1)}, u32[]{:S(2)}) copy-start(bf16[128,128]{1,0:T(8,128)(2,1)S(1)} %fusion.56) | copy-start | bytes 98308
  196.8 208.9 %all-gather.16.cloned.1.call-start = ((), (), s32[]{:S(2)}) async-start(), calls=%async_computation.12 | async-start | bytes 4718592 | tf_op jit(solution)/shard_map/all_gather | solution.py:176
  199.1 413.4 %all-gather.24.cloned.1.call-start = ((), (), s32[]{:S(2)}) async-start(), calls=%async_computation.16 | async-start | bytes 41943040 | tf_op jit(solution)/shard_map/all_gather | solution.py:227
  199.8 24.1 %copy-start.3 = (bf16[1,128,2048]{2,1,0:T(8,128)(2,1)S(1)}, bf16[1,128,2048]{2,1,0:T(8,128)(2,1)}, u32[]{:S(2)}) copy-start(bf16[1,128,2048]{2,1,0:T(8,128)(2,1)} %param.26) | copy-start | bytes 1572868
  199.8 615.9 %all-gather.20.cloned.1.call-start = ((), (), s32[]{:S(2)}) async-start(), calls=%async_computation.14 | async-start | bytes 41943040 | tf_op jit(solution)/shard_map/all_gather | solution.py:149
  200.5 639.3 %all-gather.22.cloned.1.call-start = ((), (), s32[]{:S(2)}) async-start(), calls=%async_computation.15 | async-start | bytes 2621440 | tf_op jit(solution)/shard_map/all_gather | solution.py:139
  201.3 662.8 %all-gather.26.cloned.1.call-start = ((), (), s32[]{:S(2)}) async-start(), calls=%async_computation.17 | async-start | bytes 2621440 | tf_op jit(solution)/shard_map/all_gather | solution.py:140
  202.0 814.5 %reduce-scatter.28.cloned.1.call-start = ((), (), s32[]{:S(2)}) async-start(), calls=%async_computation.26 | async-start | bytes 9437184
  212.9 47.3 %copy-start.12 = (bf16[128,2048]{1,0:T(8,128)(2,1)}, bf16[128,2048]{1,0:T(8,128)(2,1)S(1)}, u32[]{:S(2)}) copy-start(bf16[128,2048]{1,0:T(8,128)(2,1)S(1)} %all_gather.59) | copy-start | bytes 1572868
  223.8 36.4 %copy-start.16 = (bf16[2048,128]{1,0:T(8,128)(2,1)}, bf16[2048,128]{1,0:T(8,128)(2,1)S(1)}, u32[]{:S(2)}) copy-start(bf16[2048,128]{1,0:T(8,128)(2,1)S(1)} %all_gather.58) | copy-start | bytes 1572868
  260.6 70.9 %copy-start.19 = (bf16[128,8,32]{2,0,1:T(8,128)(2,1)S(1)}, bf16[128,8,32]{2,0,1:T(8,128)(2,1)}, u32[]{:S(2)}) copy-start(bf16[128,8,32]{2,0,1:T(8,128)(2,1)} %get-tuple-element.107) | copy-start | bytes 196612
  265.8 69.3 %copy-start.10 = (bf16[128,8,192]{2,0,1:T(8,128)(2,1)}, bf16[128,8,192]{2,0,1:T(8,128)(2,1)S(1)}, u32[]{:S(2)}) copy-start(bf16[128,8,192]{2,0,1:T(8,128)(2,1)S(1)} %copy.154) | copy-start | bytes 1179652
  335.2 70.4 %copy-start.61 = (f32[8,128]{1,0:T(8,128)}, f32[8,128]{1,0:T(8,128)S(1)}, u32[]{:S(2)}) copy-start(f32[8,128]{1,0:T(8,128)S(1)} %broadcast_maximum_fusion) | copy-start | bytes 12292
  405.7 6.7 copy-start.1
  405.7 6.7 copy-start.23
  405.7 6.7 copy-start.60
  405.7 7.2 copy-start.79
  415.8 7.7 copy-start.7
  445.1 11.3 copy-start.8
  445.1 11.3 copy-start.37
  445.1 12.5 copy-start.43
  445.2 23.0 %copy-start.63 = (s32[128]{0:T(128)S(1)}, s32[128]{0:T(128)}, u32[]{:S(2)}) copy-start(s32[128]{0:T(128)} %copy-done.62) | copy-start | bytes 1540
  445.2 23.0 %copy-start.65 = (s32[128]{0:T(128)S(1)}, s32[128]{0:T(128)}, u32[]{:S(2)}) copy-start(s32[128]{0:T(128)} %copy-done.64) | copy-start | bytes 1540
  445.2 23.3 %copy-start.57 = (f32[2048]{0:T(1024)S(1)}, f32[2048]{0:T(1024)}, u32[]{:S(2)}) copy-start(f32[2048]{0:T(1024)} %param.32) | copy-start | bytes 24580
  445.2 23.3 %copy-start.68 = (f32[2048]{0:T(1024)S(1)}, f32[2048]{0:T(1024)}, u32[]{:S(2)}) copy-start(f32[2048]{0:T(1024)} %param.33) | copy-start | bytes 24580
  445.2 23.6 %copy-start.17 = (bf16[2048,128]{1,0:T(8,128)(2,1)S(1)}, bf16[2048,128]{1,0:T(8,128)(2,1)}, u32[]{:S(2)}) copy-start(bf16[2048,128]{1,0:T(8,128)(2,1)} %copy-done.16) | copy-start | bytes 1572868
  445.2 636.6 %reduce-scatter.16.cloned.1.call-start = ((), (), s32[]{:S(2)}) async-start(), calls=%async_computation.20 | async-start | bytes 655360 | tf_op jit(solution)/shard_map/reduce_scatter | solution.py:352
  456.5 178.1 %copy-start.25 = (bf16[2048,128]{1,0:T(8,128)(2,1)}, bf16[2048,128]{1,0:T(8,128)(2,1)S(1)}, u32[]{:S(2)}) copy-start(bf16[2048,128]{1,0:T(8,128)(2,1)S(1)} %all_gather.55) | copy-start | bytes 1572868
  457.6 624.2 %reduce-scatter.18.cloned.1.call-start = ((), (), s32[]{:S(2)}) async-start(), calls=%async_computation.21 | async-start | bytes 655360 | tf_op jit(solution)/shard_map/reduce_scatter | solution.py:355
  468.1 166.5 %copy-start.14 = (bf16[128,2048]{1,0:T(8,128)(2,1)}, bf16[128,2048]{1,0:T(8,128)(2,1)S(1)}, u32[]{:S(2)}) copy-start(bf16[128,2048]{1,0:T(8,128)(2,1)S(1)} %all_gather.61) | copy-start | bytes 1572868
  471.0 344.7 %copy-start.56 = (f32[8192]{0:T(1024)S(1)}, f32[8192]{0:T(1024)}, u32[]{:S(2)}) copy-start(f32[8192]{0:T(1024)} %param.39) | copy-start | bytes 98308
  471.0 617.3 %reduce-scatter.20.cloned.1.call-start = ((), (), s32[]{:S(2)}) async-start(), calls=%async_computation.22 | async-start | bytes 655360 | tf_op jit(solution)/shard_map/reduce_scatter | solution.py:358
  864.0 8.0 copy-start.22
  874.6 237.7 %reduce-scatter.26.cloned.1.call-start = ((), (), s32[]{:S(2)}) async-start(), calls=%async_computation.25 | async-start | bytes 655360 | tf_op jit(solution)/shard_map/reduce_scatter | solution.py:367
  878.8 267.4 %reduce-scatter.22.cloned.1.call-start = ((), (), s32[]{:S(2)}) async-start(), calls=%async_computation.23 | async-start | bytes 2621440 | tf_op jit(solution)/shard_map/reduce_scatter | solution.py:361
  882.8 297.3 %reduce-scatter.24.cloned.1.call-start = ((), (), s32[]{:S(2)}) async-start(), calls=%async_computation.24 | async-start | bytes 2621440 | tf_op jit(solution)/shard_map/reduce_scatter | solution.py:364
  884.9 319.4 %reduce-scatter.12.cloned.1.call-start = ((), (), s32[]{:S(2)}) async-start(), calls=%async_computation.18 | async-start | bytes 655360 | tf_op jit(solution)/shard_map/reduce_scatter | solution.py:346
  1041.9 193.0 %reduce-scatter.14.cloned.1.call-start = ((), (), s32[]{:S(2)}) async-start(), calls=%async_computation.19 | async-start | bytes 1966080 | tf_op jit(solution)/shard_map/reduce_scatter | solution.py:349
  1049.7 14.1 %copy-start.39 = (bf16[128,128]{1,0:T(8,128)(2,1)S(1)}, bf16[128,128]{1,0:T(8,128)(2,1)}, u32[]{:S(2)}) copy-start(bf16[128,128]{1,0:T(8,128)(2,1)} %copy-done.38) | copy-start | bytes 98308
  1049.7 14.4 %copy-start.35 = (bf16[128,128]{1,0:T(8,128)(2,1)S(1)}, bf16[128,128]{1,0:T(8,128)(2,1)}, u32[]{:S(2)}) copy-start(bf16[128,128]{1,0:T(8,128)(2,1)} %copy-done.34) | copy-start | bytes 98308
  1049.7 295.9 %all-reduce.3.cloned.1.call-start = ((), (), s32[]{:S(2)}) async-start(), calls=%async_computation.27 | async-start | bytes 4194304 | tf_op jit(solution)/shard_map/psum | solution.py:336
  1050.0 13.8 %copy-start.13 = (bf16[128,2048]{1,0:T(8,128)(2,1)S(1)}, bf16[128,2048]{1,0:T(8,128)(2,1)}, u32[]{:S(2)}) copy-start(bf16[128,2048]{1,0:T(8,128)(2,1)} %copy-done.12) | copy-start | bytes 1572868
  1050.0 14.1 %copy-start.15 = (bf16[128,2048]{1,0:T(8,128)(2,1)S(1)}, bf16[128,2048]{1,0:T(8,128)(2,1)}, u32[]{:S(2)}) copy-start(bf16[128,2048]{1,0:T(8,128)(2,1)} %copy-done.14) | copy-start | bytes 1572868
  1065.4 16.1 %copy-start.26 = (bf16[2048,128]{1,0:T(8,128)(2,1)S(1)}, bf16[2048,128]{1,0:T(8,128)(2,1)}, u32[]{:S(2)}) copy-start(bf16[2048,128]{1,0:T(8,128)(2,1)} %copy-done.25) | copy-start | bytes 1572868
  1065.4 16.1 %copy-start.50 = (bf16[128,128]{1,0:T(8,128)(2,1)S(1)}, bf16[128,128]{1,0:T(8,128)(2,1)}, u32[]{:S(2)}) copy-start(bf16[128,128]{1,0:T(8,128)(2,1)} %copy-done.49) | copy-start | bytes 98308
  1065.4 16.1 %copy-start.58 = (f32[2048]{0:T(1024)S(1)}, f32[2048]{0:T(1024)}, u32[]{:S(2)}) copy-start(f32[2048]{0:T(1024)} %param.32) | copy-start | bytes 24580
  1081.4 153.5 %copy-start.29 = (bf16[128,8,256]{0,2,1:T(8,128)(2,1)S(1)}, bf16[128,8,256]{0,2,1:T(8,128)(2,1)}, u32[]{:S(2)}) copy-start(bf16[128,8,256]{0,2,1:T(8,128)(2,1)} %copy.100) | copy-start | bytes 1572868
  1081.5 153.5 %copy-start.31 = (bf16[128,2048]{0,1:T(8,128)(2,1)S(1)}, bf16[128,2048]{0,1:T(8,128)(2,1)}, u32[]{:S(2)}) copy-start(bf16[128,2048]{0,1:T(8,128)(2,1)} %copy.120) | copy-start | bytes 1572868
  1345.6 6.9 copy-start.47
  1345.6 7.6 copy-start.46
  1345.6 8.3 copy-start.45
  1345.6 9.1 copy-start.44
  (37 other events, 104.7 us)
Sparse Core Ops, SparseCore 0:
  9.7 157.4 all-gather.9
  168.8 19.6 all-gather.11
  190.0 63.8 all-gather.17
  256.4 75.0 all-gather.13
  334.0 71.5 all-gather.15
  407.1 205.3 all-gather.23
  614.1 201.5 all-gather.19
  817.2 22.5 all-gather.21
  841.4 22.5 all-gather.25
  867.5 148.9 reduce-scatter.27
  1019.2 20.6 reduce-scatter.15
  1042.2 21.6 reduce-scatter.17
  1066.5 21.6 reduce-scatter.19
  1090.6 21.6 reduce-scatter.25
  1114.8 31.3 reduce-scatter.21
  1148.7 31.4 reduce-scatter.23
  1182.6 21.6 reduce-scatter.11
  1206.7 28.1 reduce-scatter.13
  1240.1 105.4 all-reduce.2
where the time goes:
time: 1370 us; the launch traced here: 1360 us
  waiting for transfers between devices  1030 us (75%)
  matrix products  183 us (13%)
  blocking collectives  50.8 us (4%)
  local copies, waits for them, and re-layouts  46.8 us (3%)
  other arithmetic  35.6 us (3%)
  between operations  15.5 us (1%)
    all_gather x1, waiting for transfers between devices, body(): lax.all_gather(in_weight, 'wa', axis=0, tiled=True)  181 us
    all_gather x1, waiting for transfers between devices, body(): lax.all_gather(qkv_weight, 'wa', axis=0, tiled=True)  146 us
    all_gather x1, waiting for transfers between devices, body(): lax.all_gather(out_weight, 'wa', axis=0, tiled=True)  141 us
    unnamed x20, waiting for transfers between devices  130 us
    psum x1, waiting for transfers between devices, body(): lax.psum(qkv_down_grad.astype(jnp.bfloat16), 'ctx').astype(jnp.float32)  92.5 us
    dot_general x12, matrix products, times_t(): lax.dot_general(left, right, (((1,), (1,)), ((), ())), preferred_element_...  72.5 us
    dot_general x12, matrix products, product(): return jnp.dot(left, right, preferred_element_type=jnp.float32)  72 us
    all_gather x1, waiting for transfers between devices, body(): lax.all_gather(value, 'ctx', axis=0, tiled=True)  65.9 us
  transfers between devices with their start and end apart: 19, of which 17 were waited for; matrix products, arithmetic and copies ran while one was open for 18% of the time, Pallas kernels for 0%

commit v1 on v0

v1 whole, which is shorter than its diff:
```python
import functools
import math

import jax
import jax.numpy as jnp
from jax import lax
from jax.experimental import pallas as pl
from jax.experimental.pallas import tpu as pltpu
from jax.sharding import PartitionSpec as P

HEADS = 8
HEAD = 256
ROT = 64
RANK = 16
BLOCK = 64
ADAPT_COLS = 128
WA = 4
PAIRS = 8

epsilon = 1e-05
masked_score = -1e30
f32 = jnp.float32
bf16 = jnp.bfloat16


def product(left, right):
    return jnp.dot(left, right, preferred_element_type=f32)


def times_t(left, right):
    return lax.dot_general(left, right, (((1,), (1,)), ((), ())), preferred_element_type=f32)


def t_times(left, right):
    return lax.dot_general(left, right, (((0,), (0,)), ((), ())), preferred_element_type=f32)


def swap(value, bits):
    return lax.ppermute(value, "wa", [(i, i ^ bits) for i in range(WA)])


def gather_relative(value):
    mate = swap(value, 1)
    peer = swap(value, 2)
    return [value, mate, peer, swap(peer, 1)]


def absolute(pieces, wa):
    low = wa % 2 == 1
    high = wa >= 2
    p = [
        jnp.where(low, pieces[1], pieces[0]),
        jnp.where(low, pieces[0], pieces[1]),
        jnp.where(low, pieces[3], pieces[2]),
        jnp.where(low, pieces[2], pieces[3]),
    ]
    return [
        jnp.where(high, p[2], p[0]),
        jnp.where(high, p[3], p[1]),
        jnp.where(high, p[0], p[2]),
        jnp.where(high, p[1], p[3]),
    ]


def rotary_tables(offset):
    half = ROT // 2
    freq = 10000.0 ** (-2.0 * jnp.arange(half, dtype=f32) / ROT)
    angle = offset.astype(f32)[:, None] * freq[None, :]
    cosine = jnp.cos(angle)
    sine = jnp.sin(angle)
    rest = jnp.zeros((offset.shape[0], 128 - ROT), f32)
    return (
        jnp.concatenate([cosine, cosine, rest + 1.0], axis=1),
        jnp.concatenate([-sine, sine, rest], axis=1),
    )


def turn_first(values, cosine, sine):
    lane = lax.broadcasted_iota(jnp.int32, values.shape, 1)
    partner = jnp.where(
        lane < ROT // 2, pltpu.roll(values, 128 - ROT // 2, 1), pltpu.roll(values, ROT // 2, 1)
    )
    return values * cosine + partner * sine


def rotate_kernel(value_ref, cos_ref, sin_ref, out_ref):
    for head in range(2):
        first = head * HEAD
        turned = turn_first(value_ref[:, first : first + 128], cos_ref[...], sin_ref[...])
        out_ref[head, :, :128] = turned.astype(bf16)
        out_ref[head, :, 128:] = value_ref[:, first + 128 : first + HEAD].astype(bf16)


def rotate_heads(values, cosine, sine):
    total = values.shape[0]
    rows = total // WA
    return pl.pallas_call(
        rotate_kernel,
        grid=(WA,),
        in_specs=[
            pl.BlockSpec((rows, 2 * HEAD), lambda i: (i, 0)),
            pl.BlockSpec((rows, 128), lambda i: (i, 0)),
            pl.BlockSpec((rows, 128), lambda i: (i, 0)),
        ],
        out_specs=pl.BlockSpec((None, 2, rows, HEAD), lambda i: (i, 0, 0, 0)),
        out_shape=jax.ShapeDtypeStruct((WA, 2, rows, HEAD), bf16),
        cost_estimate=pl.CostEstimate(
            flops=4 * total * 512, bytes_accessed=total * 512 * 6, transcendentals=0
        ),
    )(values, cosine, sine)


def attention_kernel(
    query_ref,
    key_ref,
    value_ref,
    grad_ref,
    begin_ref,
    place_ref,
    key_place_ref,
    q_cos_ref,
    q_sin_ref,
    k_cos_ref,
    k_sin_ref,
    out_ref,
    dq_ref,
    dk_ref,
    dv_ref,
    dk_sum,
    dv_sum,
):
    step = pl.program_id(0)
    scale = 1.0 / math.sqrt(HEAD)

    @pl.when(step == 0)
    def _():
        dk_sum[...] = jnp.zeros_like(dk_sum)
        dv_sum[...] = jnp.zeros_like(dv_sum)

    query = query_ref[...]
    key = key_ref[...]
    value = value_ref[...]
    grad = grad_ref[...]
    key_place = key_place_ref[...]
    allowed = (key_place >= begin_ref[...]) & (key_place <= place_ref[...])
    scores = jnp.where(allowed, times_t(query, key) * scale, masked_score)
    top = jnp.max(scores, axis=1, keepdims=True)
    weights = jnp.exp(scores - top)
    prob = weights * (1.0 / jnp.sum(weights, axis=1, keepdims=True))
    prob_low = prob.astype(bf16)
    out_ref[...] = product(prob_low, value).astype(bf16)
    prob_grad = times_t(grad, value)
    delta = jnp.sum(prob * prob_grad, axis=1, keepdims=True)
    score_grad = (prob * (prob_grad - delta)).astype(bf16)
    dq = product(score_grad, key) * scale
    dq_ref[:, :128] = turn_first(dq[:, :128], q_cos_ref[...], -q_sin_ref[...]).astype(bf16)
    dq_ref[:, 128:] = dq[:, 128:].astype(bf16)
    dk_sum[...] += t_times(score_grad, query)
    dv_sum[...] += t_times(prob_low, grad)

    @pl.when(step == pl.num_programs(0) - 1)
    def _():
        dk = dk_sum[...] * scale
        dk_ref[:, :128] = turn_first(dk[:, :128], k_cos_ref[...], -k_sin_ref[...]).astype(bf16)
        dk_ref[:, 128:] = dk[:, 128:].astype(bf16)
        dv_ref[...] = dv_sum[...].astype(bf16)


def attend(query, key, value, grad, begin, place, key_place, q_tables, k_tables):
    rows = query.shape[0]
    keys = key.shape[0]
    part = min(256, rows)
    by_rows = lambda i: (i, 0)
    whole = lambda i: (0, 0)
    return pl.pallas_call(
        attention_kernel,
        grid=(rows // part,),
        in_specs=[
            pl.BlockSpec((part, HEAD), by_rows),
            pl.BlockSpec((keys, HEAD), whole),
            pl.BlockSpec((keys, HEAD), whole),
            pl.BlockSpec((part, HEAD), by_rows),
            pl.BlockSpec((part, 1), by_rows),
            pl.BlockSpec((part, 1), by_rows),
            pl.BlockSpec((1, keys), whole),
            pl.BlockSpec((part, 128), by_rows),
            pl.BlockSpec((part, 128), by_rows),
            pl.BlockSpec((keys, 128), whole),
            pl.BlockSpec((keys, 128), whole),
        ],
        out_specs=[
            pl.BlockSpec((part, HEAD), by_rows),
            pl.BlockSpec((part, HEAD), by_rows),
            pl.BlockSpec((keys, HEAD), whole),
            pl.BlockSpec((keys, HEAD), whole),
        ],
        out_shape=[
            jax.ShapeDtypeStruct((rows, HEAD), bf16),
            jax.ShapeDtypeStruct((rows, HEAD), bf16),
            jax.ShapeDtypeStruct((keys, HEAD), bf16),
            jax.ShapeDtypeStruct((keys, HEAD), bf16),
        ],
        scratch_shapes=[pltpu.VMEM((keys, HEAD), f32), pltpu.VMEM((keys, HEAD), f32)],
        compiler_params=pltpu.CompilerParams(vmem_limit_bytes=56 * 1024 * 1024),
        cost_estimate=pl.CostEstimate(
            flops=14 * rows * keys * HEAD,
            bytes_accessed=16 * keys * HEAD,
            transcendentals=rows * keys,
        ),
    )(query, key, value, grad, begin, place, key_place, *q_tables, *k_tables)


def body(
    contexts,
    tokens,
    cotangent,
    deal,
    doc_lengths,
    doc_adapter,
    ln1_gain,
    ln1_bias,
    ln2_gain,
    ln2_bias,
    qkv_weight,
    qkv_bias,
    dense_weight,
    dense_bias,
    in_weight,
    in_bias,
    out_weight,
    out_bias,
    qkv_down,
    qkv_up,
    dense_down,
    dense_up,
    in_down,
    in_up,
    out_down,
    out_up,
):
    rows = tokens.shape[1]
    width = tokens.shape[2]
    wa = lax.axis_index("wa")
    ctx = lax.axis_index("ctx")
    mate, peer, far = wa ^ 1, wa ^ 2, wa ^ 3
    total = WA * rows
    own_width = width // WA
    hidden_width = in_weight.shape[1] // WA
    part_cols = ADAPT_COLS // WA
    groups = contexts // PAIRS

    def columns(value, index, size):
        return lax.dynamic_slice_in_dim(value, index * size, size, axis=1)

    def part_rows(value, index, size):
        return lax.dynamic_slice_in_dim(value, index * size, size, axis=0)

    tables = lax.all_gather(
        jnp.concatenate([doc_lengths, doc_adapter], axis=1), "wa", axis=0, tiled=True
    )
    docs_per_pack = doc_lengths.shape[1]
    lengths = tables[:, :docs_per_pack]
    adapters = tables[:, docs_per_pack:]
    starts = jnp.cumsum(lengths, axis=1) - lengths

    def places(first, size):
        slots = first + jnp.arange(size, dtype=jnp.int32)
        blocks = slots // BLOCK
        table = jnp.arange(deal.shape[0], dtype=jnp.int32)
        block = jnp.sum(jnp.where(table[None, :] == blocks[:, None], deal[None, :], 0), axis=1)
        return block * BLOCK + slots % BLOCK

    place = places(ctx * rows, rows)
    inside = starts[:, None, :] <= place[None, :, None]
    docs = jnp.sum(inside.astype(jnp.int32), axis=2) - 1
    begin = jnp.max(jnp.where(inside, starts[:, None, :], 0), axis=2)
    offset = (place[None, :] - begin).reshape(total)
    doc_table = jnp.arange(docs_per_pack, dtype=jnp.int32)
    chosen = jnp.sum(
        jnp.where(docs[:, :, None] == doc_table, adapters[:, None, :], 0), axis=2
    ).reshape(total)
    adapter_of = jnp.arange(ADAPT_COLS, dtype=jnp.int32) // RANK
    mask = (adapter_of[None, :] == chosen[:, None]).astype(f32)
    mask_t = (adapter_of[:, None] == chosen[None, :]).astype(f32)
    own_mask_t = part_rows(mask_t, wa, part_cols)
    cosine, sine = rotary_tables(offset)

    def gather_rows(value):
        full = jnp.zeros((WA, rows, width), bf16)
        for r, part in enumerate(gather_relative(value)):
            full = lax.dynamic_update_index_in_dim(full, part, wa ^ r, 0)
        return full.reshape(total, width)

    token_rows = gather_rows(tokens[0])
    downs = gather_relative(jnp.concatenate([qkv_down, in_down], axis=1))
    downs = jnp.concatenate(absolute(downs, wa), axis=0)
    qkv_down_all = downs[:, :ADAPT_COLS]
    in_down_all = downs[:, ADAPT_COLS:]
    grad = gather_rows(cotangent[0])

    qkv_split = qkv_weight.reshape(own_width, 3, WA, own_width)

    def qkv_columns(index):
        return lax.dynamic_index_in_dim(qkv_split, index, axis=2, keepdims=False).reshape(
            own_width, 3 * own_width
        )

    qkv_own = [qkv_columns(wa), swap(qkv_columns(mate), 1)]
    qkv_peer = [qkv_columns(peer), swap(qkv_columns(far), 1)]
    in_own = [columns(in_weight, wa, hidden_width), swap(columns(in_weight, mate, hidden_width), 1)]
    in_peer = [
        columns(in_weight, peer, hidden_width),
        swap(columns(in_weight, far, hidden_width), 1),
    ]

    def up_columns(index):
        qkv_part = lax.dynamic_index_in_dim(
            qkv_up.reshape(part_cols, 3, WA, own_width), index, axis=2, keepdims=False
        ).reshape(part_cols, 3 * own_width)
        return jnp.concatenate([qkv_part, columns(in_up, index, hidden_width)], axis=1)

    ups = [up_columns(wa), swap(up_columns(mate), 1), swap(up_columns(peer), 2), swap(up_columns(far), 3)]
    ups = jnp.concatenate(absolute(ups, wa), axis=0)
    qkv_up_own = ups[:, : 3 * own_width]
    in_up_own = ups[:, 3 * own_width :]

    values = token_rows.astype(f32)
    centered = values - jnp.mean(values, axis=1, keepdims=True)
    normal = centered * lax.rsqrt(jnp.mean(centered * centered, axis=1, keepdims=True) + epsilon)
    first_norm = (normal * ln1_gain + ln1_bias).astype(bf16)
    second_norm = (normal * ln2_gain + ln2_bias).astype(bf16)
    first_inner = (product(first_norm, qkv_down_all) * mask).astype(bf16)
    second_inner = (product(second_norm, in_down_all) * mask).astype(bf16)
    first_pair = [columns(first_norm, wa, own_width), columns(first_norm, mate, own_width)]
    second_pair = [columns(second_norm, wa, own_width), columns(second_norm, mate, own_width)]

    def both(left, right):
        return product(left[0], right[0]) + product(left[1], right[1])

    mixed = []
    for kind in (2, 1, 0):
        cut = slice(kind * own_width, (kind + 1) * own_width)
        sent = both(first_pair, [item[:, cut] for item in qkv_peer]).astype(bf16)
        arrived = swap(sent, 2)
        bias = lax.dynamic_slice_in_dim(
            qkv_bias, kind * width + wa * own_width, own_width, axis=0
        )
        mixed.append(
            both(first_pair, [item[:, cut] for item in qkv_own])
            + product(first_inner, qkv_up_own[:, cut])
            + bias
            + arrived.astype(f32)
        )
    value, key, query = mixed

    def to_pairs(item):
        item = item.reshape(PAIRS, rows, HEAD)
        if groups == 1:
            return lax.all_to_all(item, "ctx", 0, 0, tiled=True)
        names = [[g * PAIRS + j for j in range(PAIRS)] for g in range(groups)]
        return lax.all_to_all(item, "ctx", 0, 0, axis_index_groups=names, tiled=True)

    def split_heads(item):
        return jnp.transpose(item.reshape(WA, rows, 2, HEAD), (0, 2, 1, 3))

    def join_heads(item):
        return jnp.transpose(item.reshape(WA, 2, rows, HEAD), (0, 2, 1, 3)).reshape(
            total, own_width
        )

    query = to_pairs(rotate_heads(query, cosine, sine))
    key = to_pairs(rotate_heads(key, cosine, sine))
    value = to_pairs(split_heads(value.astype(bf16)))

    inner_grads_t = times_t(jnp.concatenate([dense_up, out_up], axis=0), grad)
    inner_grads_t = (inner_grads_t.reshape(2, part_cols, total) * own_mask_t).astype(bf16)
    inner_grads_t = jnp.concatenate(
        absolute(gather_relative(inner_grads_t), wa), axis=1
    )
    dense_inner_grad = inner_grads_t[0]
    out_inner_grad = inner_grads_t[1]
    attended_grad = times_t(grad, dense_weight) + lax.dot_general(
        dense_inner_grad, dense_down, (((0,), (1,)), ((), ())), preferred_element_type=f32
    )
    attended_grad = to_pairs(split_heads(attended_grad.astype(bf16)))

    pair_rows = PAIRS * rows
    group = ctx // PAIRS
    own_pack = (ctx % PAIRS) // 2
    own_starts = jnp.sum(
        jnp.where(jnp.arange(WA)[:, None] == own_pack, starts, 0), axis=0
    )
    all_places = places(0, groups * pair_rows)
    all_inside = own_starts[None, :] <= all_places[:, None]
    all_begins = jnp.max(jnp.where(all_inside, own_starts[None, :], 0), axis=1)
    k_tables = rotary_tables(all_places - all_begins)
    if groups == 1:
        q_place, q_begin, q_tables = all_places, all_begins, k_tables
    else:
        q_place = part_rows(all_places, group, pair_rows)
        q_begin = part_rows(all_begins, group, pair_rows)
        q_tables = [part_rows(item, group, pair_rows) for item in k_tables]
    query, key, value, attended_grad = [
        item.reshape(pair_rows, HEAD) for item in (query, key, value, attended_grad)
    ]
    sets = [[g * PAIRS + j for g in range(groups)] for j in range(PAIRS)]
    if groups > 1:
        key, value = [
            lax.all_gather(item, "ctx", axis=0, axis_index_groups=sets, tiled=True)
            for item in (key, value)
        ]
    attended, dq, dk, dv = attend(
        query,
        key,
        value,
        attended_grad,
        q_begin[:, None],
        q_place[:, None],
        all_places[None, :],
        q_tables,
        k_tables,
    )
    if groups > 1:
        dk, dv = [
            lax.psum_scatter(
                item, "ctx", scatter_dimension=0, axis_index_groups=sets, tiled=True
            )
            for item in (dk, dv)
        ]
    dv, dk, dq, attended = [join_heads(to_pairs(item)) for item in (dv, dk, dq, attended)]

    hidden_sent = both(second_pair, in_peer).astype(bf16)
    hidden_arrived = swap(hidden_sent, 2)
    hidden_pre = (
        both(second_pair, in_own)
        + product(second_inner, in_up_own)
        + lax.dynamic_slice_in_dim(in_bias, wa * hidden_width, hidden_width, axis=0)
        + hidden_arrived.astype(f32)
    )
    hidden, gelu_pull = jax.vjp(lambda v: jax.nn.gelu(v, approximate=False), hidden_pre)
    hidden = hidden.astype(bf16)
    hidden_grad = times_t(grad, out_weight) + lax.dot_general(
        out_inner_grad, out_down, (((0,), (1,)), ((), ())), preferred_element_type=f32
    )
    pre_grad = gelu_pull(hidden_grad)[0].astype(bf16)
    pre_peer = swap(pre_grad, 2)

    def scatter_inner(partial):
        own = [part_rows(partial, wa, part_cols), part_rows(partial, peer, part_cols)]
        sent = [part_rows(partial, mate, part_cols), part_rows(partial, far, part_cols)]
        arrived = swap(jnp.concatenate(sent, axis=0), 1)
        crossing = swap(own[1] + arrived[part_cols:], 2)
        return ((own[0] + arrived[:part_cols] + crossing) * own_mask_t).astype(bf16)

    out_inner_t = scatter_inner(
        lax.dot_general(out_down, hidden, (((0,), (1,)), ((), ())), preferred_element_type=f32)
    )
    dense_inner_t = scatter_inner(
        lax.dot_general(
            dense_down, attended, (((0,), (1,)), ((), ())), preferred_element_type=f32
        )
    )
    branches = (
        product(hidden, out_weight)
        + product(attended, dense_weight)
        + t_times(out_inner_t, out_up)
        + t_times(dense_inner_t, dense_up)
    ).reshape(WA, rows, width)

    def pack_of(value, index):
        return lax.dynamic_index_in_dim(value, index, axis=0, keepdims=False)

    arrived = swap(jnp.stack([pack_of(branches, mate), pack_of(branches, far)]).astype(bf16), 1)
    crossing = swap((pack_of(branches, peer) + arrived[1].astype(f32)).astype(bf16), 2)
    output = (
        pack_of(branches, wa)
        + arrived[0].astype(f32)
        + crossing.astype(f32)
        + dense_bias
        + out_bias
        + tokens[0].astype(f32)
    ).astype(bf16)[None]

    def sum_inner(partial):
        partial = partial + swap(partial, 1)
        partial = partial + swap(partial, 2)
        return (partial * mask_t).astype(bf16)

    mixed_grad = jnp.concatenate([dq, dk, dv], axis=1)
    mixed_peer = jnp.concatenate([swap(item, 2) for item in (dq, dk, dv)], axis=1)
    first_inner_grad = sum_inner(times_t(qkv_up_own, mixed_grad))
    second_inner_grad = sum_inner(times_t(in_up_own, pre_grad))

    def norm_grad(own, other, own_weight, other_weight):
        return times_t(own, own_weight) + times_t(other, other_weight)

    combined = []
    for row, index in ((0, wa), (1, mate)):
        gain1 = lax.dynamic_slice_in_dim(ln1_gain, index * own_width, own_width, axis=0)
        gain2 = lax.dynamic_slice_in_dim(ln2_gain, index * own_width, own_width, axis=0)
        combined.append(
            norm_grad(mixed_grad, mixed_peer, qkv_own[row], qkv_peer[row]) * gain1
            + norm_grad(pre_grad, pre_peer, in_own[row], in_peer[row]) * gain2
        )
    combined = [item.reshape(WA, rows, own_width) for item in combined]

    def both_columns(first, index):
        return jnp.concatenate(
            [pack_of(combined[first], index), pack_of(combined[1 - first], index)], axis=1
        )

    sent = jnp.stack([both_columns(1, mate), both_columns(1, far)]).astype(bf16)
    arrived = swap(sent, 1).astype(f32)
    near = both_columns(0, wa) + arrived[0]
    away = both_columns(0, peer) + arrived[1]
    away = swap(away.astype(bf16), 2).astype(f32)
    combined = jnp.concatenate(
        absolute(
            [near[:, :own_width], near[:, own_width:], away[:, :own_width], away[:, own_width:]],
            wa,
        ),
        axis=1,
    )
    combined = (
        combined
        + lax.dot_general(
            columns(first_inner_grad, wa, rows),
            qkv_down_all,
            (((0,), (1,)), ((), ())),
            preferred_element_type=f32,
        )
        * ln1_gain
        + lax.dot_general(
            columns(second_inner_grad, wa, rows),
            in_down_all,
            (((0,), (1,)), ((), ())),
            preferred_element_type=f32,
        )
        * ln2_gain
    )
    own_values = tokens[0].astype(f32)
    own_centered = own_values - jnp.mean(own_values, axis=1, keepdims=True)
    own_rstd = lax.rsqrt(jnp.mean(own_centered * own_centered, axis=1, keepdims=True) + epsilon)
    own_normal = own_centered * own_rstd
    tokens_grad = (
        cotangent[0].astype(f32)
        + own_rstd
        * (
            combined
            - jnp.mean(combined, axis=1, keepdims=True)
            - own_normal * jnp.mean(combined * own_normal, axis=1, keepdims=True)
        )
    )[None]

    def up_grad(inner, own, other):
        def block(index):
            part = columns(inner, index, part_cols)
            return [t_times(part, own).astype(bf16), t_times(part, other).astype(bf16)]

        mine = block(wa)
        arrived = swap(jnp.stack(block(mate)), 1)
        return [mine[0], arrived[0], mine[1], arrived[1]]

    out_down_grad = t_times(hidden, out_inner_grad.T).astype(bf16)
    out_up_grad = product(out_inner_t, grad).astype(bf16)
    in_down_grad = lax.dot_general(
        second_pair[0], second_inner_grad, (((0,), (1,)), ((), ())), preferred_element_type=f32
    ).astype(bf16)
    in_up_grad = jnp.concatenate(up_grad(second_inner, pre_grad, pre_peer), axis=1)
    out_down_grad, out_up_grad, in_down_grad, in_up_grad = lax.psum(
        (out_down_grad, out_up_grad, in_down_grad, in_up_grad), "ctx"
    )
    dense_down_grad = t_times(attended, dense_inner_grad.T).astype(bf16)
    dense_up_grad = product(dense_inner_t, grad).astype(bf16)
    qkv_down_grad = lax.dot_general(
        first_pair[0], first_inner_grad, (((0,), (1,)), ((), ())), preferred_element_type=f32
    ).astype(bf16)
    qkv_up_grad = jnp.concatenate(up_grad(first_inner, mixed_grad, mixed_peer), axis=1)
    dense_down_grad, dense_up_grad, qkv_down_grad, qkv_up_grad = lax.psum(
        (dense_down_grad, dense_up_grad, qkv_down_grad, qkv_up_grad), "ctx"
    )
    in_up_grad = jnp.concatenate(absolute(jnp.split(in_up_grad, WA, axis=1), wa), axis=1)
    qkv_parts = absolute(jnp.split(qkv_up_grad, WA, axis=1), wa)
    qkv_up_grad = jnp.stack(
        [item.reshape(part_cols, 3, own_width) for item in qkv_parts], axis=2
    ).reshape(part_cols, 3 * width)
    return (
        output,
        tokens_grad,
        qkv_down_grad.astype(f32),
        qkv_up_grad.astype(f32),
        dense_down_grad.astype(f32),
        dense_up_grad.astype(f32),
        in_down_grad.astype(f32),
        in_up_grad.astype(f32),
        out_down_grad.astype(f32),
        out_up_grad.astype(f32),
    )


def solution(mesh):
    rows = P("wa", "ctx", None)
    shard = P("wa", None)
    in_specs = (
        (rows, rows, P(), shard, shard)
        + (P(),) * 4
        + (shard, P()) * 4
        + (shard,) * 8
    )
    out_specs = (rows, rows) + (shard,) * 8
    return jax.shard_map(
        functools.partial(body, mesh.shape["ctx"]),
        mesh=mesh,
        in_specs=in_specs,
        out_specs=out_specs,
        check_vma=False,
    )
```

time: 1370 us -> 599 us (0.44)
  waiting for transfers between devices: 1030 us -> 227 us
  starting transfers between devices: 1.23 us -> 65.5 us
  matrix products: 183 us -> 135 us
  blocking collectives: 50.8 us -> 10.7 us
  local copies, waits for them, and re-layouts: 46.8 us -> 74.5 us
  Pallas kernels: 0 us -> 16.9 us
    all_gather x9 -> x0, waiting for transfers between devices: 654 us -> none  [the longest x1 181 us: body(): lax.all_gather(in_weight, 'wa', axis=0, tiled=True)]
    reduce_scatter x8 -> x0, waiting for transfers between devices: 153 us -> none  [the longest x1 34 us: body(): lax.psum_scatter(totals[5].astype(jnp.bfloat16), 'wa', scatter_dimension=...]
    unnamed x20 -> x1, waiting for transfers between devices: 130 us -> 0.02 us
    ppermute x0 -> x41, waiting for transfers between devices: none -> 126 us  [swap(): return lax.ppermute(value, 'wa', [(i, i ^ bits) for i in range(WA)])]
    all_to_all x0 -> x8, starting transfers between devices: none -> 40.5 us  [to_pairs(): return lax.all_to_all(item, 'ctx', 0, 0, tiled=True)]
    all_gather x5 -> x1, blocking collectives: 50.8 us -> 10.7 us  [body(): lax.all_gather(jnp.concatenate([doc_lengths, doc_adapter], axis=1), 'wa',...]
    dot_general x12 -> x13, matrix products: 72.5 us -> 43.7 us  [times_t(): lax.dot_general(left, right, (((1,), (1,)), ((), ())), preferred_element_...]
    ppermute x0 -> x41, starting transfers between devices: none -> 25 us  [swap(): return lax.ppermute(value, 'wa', [(i, i ^ bits) for i in range(WA)])]
  transfers between devices with their start and end apart: 19 -> 50, of which waited for: 17 -> 18; matrix products, arithmetic and copies ran while one was open for 18% -> 41% of each run, Pallas kernels for 0% -> 3%
where the time goes in v1:
time: 599 us; the launch traced here: 593 us
  waiting for transfers between devices  227 us (38%)
  matrix products  135 us (23%)
  local copies, waits for them, and re-layouts  74.5 us (12%)
  starting transfers between devices  65.5 us (11%)
  other arithmetic  47.1 us (8%)
  Pallas kernels  16.9 us (3%)
  between operations  15.9 us (3%)
  blocking collectives  10.7 us (2%)
    ppermute x41, waiting for transfers between devices, swap(): return lax.ppermute(value, 'wa', [(i, i ^ bits) for i in range(WA)])  126 us
    psum x1, waiting for transfers between devices, body(): lax.psum((dense_down_grad, dense_up_grad, qkv_down_grad, qkv_up_grad), 'c...  83.3 us
    dot_general x26, matrix products, product(): return jnp.dot(left, right, preferred_element_type=f32)  73.9 us
    dot_general x13, matrix products, times_t(): lax.dot_general(left, right, (((1,), (1,)), ((), ())), preferred_element_...  43.7 us
    all_to_all x8, starting transfers between devices, to_pairs(): return lax.all_to_all(item, 'ctx', 0, 0, tiled=True)  40.5 us
    ppermute x41, starting transfers between devices, swap(): return lax.ppermute(value, 'wa', [(i, i ^ bits) for i in range(WA)])  25 us
    unnamed x178, local copies, waits for them, and re-layouts  23.1 us
    all_to_all x8, waiting for transfers between devices, to_pairs(): return lax.all_to_all(item, 'ctx', 0, 0, tiled=True)  18.6 us
  transfers between devices with their start and end apart: 50, of which 18 were waited for; matrix products, arithmetic and copies ran while one was open for 41% of the time, Pallas kernels for 3%

profile of v1, /device:TPU:0, one launch (start us, length us, event | category | flops | bytes accessed | tf_op | source)
XLA Modules:
  0.0 592.7 jit_solution(4247701305744979458)
XLA Ops:
  7.7 2.6 collective-permute-start.18
  11.6 2.6 dynamic-slice_reduce_fusion
  23.1 10.7 %all-gather = s32[4,1,32]{2,1,0:T(1,128)S(1)} all-gather(s32[1,1,32]{2,1,0:T(1,128)S(1)} %add_bitcast_fusion), channel_id=1, replica_groups=mesh['ctx'=8,'wa'=4] {'wa'}, dimensions={0}, use_global_device_ids=true | all-gather | bytes 640 | tf_op jit(solution)/shard_map/all_gather | solution.py:258
  34.3 4.9 constant_dynamic-slice_fusion.9
  40.6 8.7 %copy.96 = bf16[512,6144]{0,1:T(8,128)(2,1)} copy(bf16[512,6144]{1,0:T(8,128)(2,1)} %param.34) | data formatting | bytes 12582912 | tf_op args[9]
  49.2 5.6 constant_dynamic-slice_fusion.2
  58.3 3.2 fusion.128
  74.8 16.1 %collective-permute-done.4 = bf16[512,256]{1,0:T(8,128)(2,1)S(1)} collective-permute-done((bf16[512,256]{1,0:T(8,128)(2,1)}, bf16[512,256]{1,0:T(8,128)(2,1)S(1)}, u32[]{:S(2)}, u32[]{:S(2)}) %collective-permute-start.4) | collective-permute-done | bytes 262176 | tf_op jit(solution)/shard_map/ppermute | solution.py:39
  94.2 2.1 bitcast_dynamic-update-slice_fusion.1
  98.5 4.2 collective-permute-done.19
  103.5 2.3 fusion.50
  105.9 2.1 collective-permute-start.20
  108.8 2.0 convert_reduce_fusion
  110.8 2.3 multiply_reduce_fusion
  113.2 4.3 add_convert_fusion.3
  124.4 3.7 fusion.43
  128.0 2.0 reshape.444
  131.9 6.1 %all-to-all-start.3 = ((bf16[8,128,256]{2,1,0:T(8,128)(2,1)}), bf16[8,128,256]{2,1,0:T(8,128)(2,1)}, u32[]{:S(2)}, u32[]{:S(2)}) async-start(bf16[8,128,256]{2,1,0:T(8,128)(2,1)} %bitcast.267), calls=%async_computation.3 | async-start | bytes 1048576 | tf_op jit(solution)/shard_map/all_to_all | solution.py:359
  141.8 2.5 fusion.76
  145.8 9.7 %collective-permute-done.14 = bf16[512,512]{1,0:T(8,128)(2,1)S(1)} collective-permute-done((bf16[512,512]{1,0:T(8,128)(2,1)S(1)}, bf16[512,512]{1,0:T(8,128)(2,1)S(1)}, u32[]{:S(2)}, u32[]{:S(2)}) %collective-permute-start.14) | collective-permute-done | bytes 524320 | tf_op jit(solution)/shard_map/ppermute | solution.py:39
  156.9 3.6 shard_map.312
  160.5 5.7 all-to-all-start
  166.2 2.2 add_convert_fusion.6
  170.3 2.5 fusion.66
  172.8 8.3 %collective-permute-done.15 = bf16[512,512]{1,0:T(8,128)(2,1)S(1)} collective-permute-done((bf16[512,512]{1,0:T(8,128)(2,1)S(1)}, bf16[512,512]{1,0:T(8,128)(2,1)S(1)}, u32[]{:S(2)}, u32[]{:S(2)}) %collective-permute-start.15) | collective-permute-done | bytes 524320 | tf_op jit(solution)/shard_map/ppermute | solution.py:39
  182.4 3.6 shard_map.313
  186.0 5.7 all-to-all-start.1
  191.8 2.2 add_convert_fusion.5
  197.4 7.8 %collective-permute-done.16 = bf16[512,512]{1,0:T(8,128)(2,1)S(1)} collective-permute-done((bf16[512,512]{1,0:T(8,128)(2,1)S(1)}, bf16[512,512]{1,0:T(8,128)(2,1)S(1)}, u32[]{:S(2)}, u32[]{:S(2)}) %collective-permute-start.16) | collective-permute-done | bytes 524320 | tf_op jit(solution)/shard_map/ppermute | solution.py:39
  210.2 5.7 all-to-all-start.2
  216.5 2.2 maximum_maximum_fusion.q_cos_ref.k_cos_ref
  218.7 2.2 maximum_maximum_fusion.1.q_sin_ref.k_sin_ref
  221.8 5.0 all-to-all-done.2
  226.8 9.7 %shard_map.314 = (bf16[1024,256]{1,0:T(8,128)(2,1)}, bf16[1024,256]{1,0:T(8,128)(2,1)}, bf16[1024,256]{1,0:T(8,128)(2,1)}, bf16[1024,256]{1,0:T(8,128)(2,1)}) custom-call(bf16[1024,256]{1,0:T(8,128)(2,1)} %bitcast.17.query_ref, bf16[1024,256]{1,0:T(8,128)(2,1)} %bitcast.19.key_ref, bf16[1024,256]{1,0:T(8,128)(2,1)} %bitcast.22.value_ref, ...), custom_call_target="tpu_custom_call" | custom-call | flops 3758096384 | bytes 4194304 | tf_op jit(solution)/shard_map/pallas_call | solution.py:175
  236.5 4.2 all-to-all-start.5
  245.5 6.4 %all-to-all-done.5 = bf16[8,128,256]{2,1,0:T(8,128)(2,1)} async-done(((bf16[8,128,256]{2,1,0:T(8,128)(2,1)}), bf16[8,128,256]{2,1,0:T(8,128)(2,1)}, u32[]{:S(2)}, u32[]{:S(2)}) %all-to-all-start.5) | async-done | bytes 524320 | tf_op jit(solution)/shard_map/all_to_all | solution.py:359
  251.8 4.1 all-to-all-start.6
  256.1 2.8 fusion.48
  259.6 2.8 fusion.103
  262.3 5.8 all-to-all-done.6
  268.2 4.4 all-to-all-start.7
  272.5 4.0 fusion.162
  276.6 2.9 fusion.107
  279.4 4.3 add_convert_fusion.2
  285.4 4.6 all-to-all-start.4
  290.1 5.1 fusion.109
  317.5 15.2 %collective-permute-done.11 = bf16[512,2048]{1,0:T(8,128)(2,1)} collective-permute-done((bf16[512,2048]{1,0:T(8,128)(2,1)}, bf16[512,2048]{1,0:T(8,128)(2,1)}, u32[]{:S(2)}, u32[]{:S(2)}) %collective-permute-start.11) | collective-permute-done | bytes 2097184 | tf_op jit(solution)/shard_map/ppermute | solution.py:39
  332.7 13.6 %multiply_convert_fusion = (bf16[512,2048]{1,0:T(8,128)(2,1)S(1)}, f32[512,2048]{1,0:T(8,128)}) fusion(bf16[512,2048]{1,0:T(8,128)(2,1)} %collective-permute-done.11, f32[2048]{0:T(1024)S(1)} %dynamic-slice-done, f32[512,2048]{1,0:T(8,128)S(1)} %copy-done.20, f32[512,2048]{1,0:T(8,128)S(1)} %copy-done.21, bf16[512,8192]{1,0:T(8,128)(2,1)} %param.38, ...), kind=kOutput, calls=%fused_computation.7 | convolution fusion | flops 1147142144 | bytes 19407364 | tf_op jit(solution)/shard_map/dot_general | solution.py:27
  346.2 19.3 %add_convert_fusion = bf16[512,2048]{1,0:T(8,128)(2,1)S(1)} fusion(f32[512,2048]{1,0:T(8,128)} %fusion.162, f32[512,2048]{1,0:T(8,128)} %get-tuple-element.118, bf16[512,2048]{1,0:T(8,128)(2,1)} %bitcast.27, bf16[2048,2048]{1,0:T(8,128)(2,1)} %param.40), kind=kOutput, calls=%fused_computation.4 | convolution fusion | flops 4371513344 | bytes 20971520 | tf_op jit(solution)/shard_map/dot_general | solution.py:31
  365.6 2.4 fusion.19
  369.8 7.1 %fusion.231 = f32[512,2048]{1,0:T(8,128)S(1)} fusion(bf16[512,2048]{1,0:T(8,128)(2,1)S(1)} %get-tuple-element.117, bf16[2048,2048]{1,0:T(8,128)(2,1)} %param.40), kind=kOutput, calls=%fused_computation.447 | convolution fusion | flops 4294967296 | bytes 14680064 | tf_op jit(solution)/shard_map/dot_general | solution.py:27
  386.5 2.8 convolution_convert_fusion.6
  390.3 4.2 convolution_convert_fusion.1
  400.9 2.4 fusion.237
  404.5 42.4 %collective-permute-done.36 = f32[128,512]{1,0:T(8,128)S(1)} collective-permute-done((f32[128,512]{1,0:T(8,128)S(1)}, f32[128,512]{1,0:T(8,128)S(1)}, u32[]{:S(2)}, u32[]{:S(2)}) %collective-permute-start.36) | collective-permute-done | bytes 262176 | tf_op jit(solution)/shard_map/ppermute | solution.py:39
  446.8 4.8 collective-permute-done.38
  451.8 2.1 convolution_convert_fusion.13
  457.3 2.9 fusion.238
  460.2 2.9 fusion.41
  463.1 2.4 fusion.34
  473.3 5.2 collective-permute-done.34
  479.9 9.3 %collective-permute-done.28 = bf16[128,2048]{1,0:T(8,128)(2,1)S(1)} collective-permute-done((bf16[128,2048]{1,0:T(8,128)(2,1)S(1)}, bf16[128,2048]{1,0:T(8,128)(2,1)S(1)}, u32[]{:S(2)}, u32[]{:S(2)}) %collective-permute-start.28) | collective-permute-done | bytes 524320 | tf_op jit(solution)/shard_map/ppermute | solution.py:39
  489.2 3.0 fusion.55
  492.1 83.3 %all-reduce.3.cloned.1.call-done = (bf16[512,128]{1,0:T(8,128)(2,1)}, bf16[32,6144]{1,0:T(8,128)(2,1)}, bf16[512,128]{1,0:T(8,128)(2,1)}, bf16[32,2048]{1,0:T(8,...) async-done(((bf16[512,128]{1,0:T(8,128)(2,1)}, bf16[32,6144]{1,0:T(8,128)(2,1)}, ...) | async-done | bytes 2097168 | tf_op jit(solution)/shard_map/psum | solution.py:579
  (414 shorter events, 136.7 us)
Async XLA Ops:
  7.2 117.2 %copy-start = (bf16[512,2048]{1,0:T(8,128)(2,1)S(1)}, bf16[512,2048]{1,0:T(8,128)(2,1)}, u32[]{:S(2)}) copy-start(bf16[512,2048]{1,0:T(8,128)(2,1)} %param.36) | copy-start | bytes 6291460
  7.2 83.7 %collective-permute-start.17 = (bf16[128,2048]{1,0:T(8,128)(2,1)}, bf16[128,2048]{1,0:T(8,128)(2,1)}, u32[]{:S(2)}, u32[]{:S(2)}) collective-permute-start(bf16[128,2048]{1,0:T(8,128)(2,1)} %bitcast.277), channel_id=1, source_target_pairs={{0,1},{1,0},{2,3},{3,2},{4,5},{5,4},{6,7},{7,6},{8,9},{9,8},{10,11... | collective-permute-start | bytes 1572872 | tf_op jit(solution)/shard_map/ppermute | solution.py:39
  7.7 86.3 %collective-permute-start.18 = (bf16[128,2048]{1,0:T(8,128)(2,1)}, bf16[128,2048]{1,0:T(8,128)(2,1)}, u32[]{:S(2)}, u32[]{:S(2)}) collective-permute-start(bf16[128,2048]{1,0:T(8,128)(2,1)} %bitcast.278), channel_id=1, source_target_pairs={{0,2},{1,3},{2,0},{3,1},{4,6},{5,7},{6,4},{7,5},{8,10},{9,11},{10,... | collective-permute-start | bytes 1572872 | tf_op jit(solution)/shard_map/ppermute | solution.py:39
  17.2 53.7 %collective-permute-start.7 = (bf16[32,3584]{1,0:T(8,128)(2,1)}, bf16[32,3584]{1,0:T(8,128)(2,1)}, u32[]{:S(2)}, u32[]{:S(2)}) collective-permute-start(bf16[32,3584]{1,0:T(8,128)(2,1)} %pad_maximum_fusion.9), channel_id=1, source_target_pairs={{0,3},{1,2},{2,1},{3,0},{4,7},{5,6},{6,5},{7,4},{8,11},{9,10},{10,... | collective-permute-start | bytes 688136 | tf_op jit(solution)/shard_map/ppermute | solution.py:39
  17.3 16.7 %copy-start.76 = (s32[16]{0:T(128)S(1)}, s32[16]{0:T(128)}, u32[]{:S(2)}) copy-start(s32[16]{0:T(128)} %param.27) | copy-start | bytes 196
  18.0 53.3 %collective-permute-start.8 = (bf16[32,3584]{1,0:T(8,128)(2,1)}, bf16[32,3584]{1,0:T(8,128)(2,1)}, u32[]{:S(2)}, u32[]{:S(2)}) collective-permute-start(bf16[32,3584]{1,0:T(8,128)(2,1)} %pad_maximum_fusion.10), channel_id=1, source_target_pairs={{0,2},{1,3},{2,0},{3,1},{4,6},{5,7},{6,4},{7,5},{8,10},{9,11},{10,... | collective-permute-start | bytes 688136 | tf_op jit(solution)/shard_map/ppermute | solution.py:39
  20.5 52.5 %collective-permute-start.9 = (bf16[32,3584]{1,0:T(8,128)(2,1)}, bf16[32,3584]{1,0:T(8,128)(2,1)}, u32[]{:S(2)}, u32[]{:S(2)}) collective-permute-start(bf16[32,3584]{1,0:T(8,128)(2,1)} %pad_maximum_fusion.11), channel_id=1, source_target_pairs={{0,1},{1,0},{2,3},{3,2},{4,5},{5,4},{6,7},{7,6},{8,9},{9,8},{10,11... | collective-permute-start | bytes 688136 | tf_op jit(solution)/shard_map/ppermute | solution.py:39
  20.6 41.0 %copy-start.64 = (s32[128]{0:T(128)}, s32[128]{0:T(128)S(1)}, u32[]{:S(2)}) copy-start(s32[128]{0:T(128)S(1)} %and_select_fusion.3) | copy-start | bytes 1540
  66.9 24.1 %copy-start.38 = (bf16[512,256]{1,0:T(8,128)(2,1)S(1)}, bf16[512,256]{1,0:T(8,128)(2,1)}, u32[]{:S(2)}) copy-start(bf16[512,256]{1,0:T(8,128)(2,1)} %constant_dynamic-update-slice_fusion) | copy-start | bytes 786436
  70.9 25.5 %collective-permute-start = (bf16[128,2048]{1,0:T(8,128)(2,1)S(1)}, bf16[128,2048]{1,0:T(8,128)(2,1)S(1)}, u32[]{:S(2)}, u32[]{:S(2)}) collective-permute-start(bf16[128,2048]{1,0:T(8,128)(2,1)S(1)} %bitcast.247), channel_id=1, source_target_pairs={{0,1},{1,0},{2,3},{3,2},{4,5},{5,4},{6,7},{7,6},{8,9},{9,8},{10,11... | collective-permute-start | bytes 1572872 | tf_op jit(solution)/shard_map/ppermute | solution.py:39
  71.3 25.3 %collective-permute-start.1 = (bf16[128,2048]{1,0:T(8,128)(2,1)S(1)}, bf16[128,2048]{1,0:T(8,128)(2,1)S(1)}, u32[]{:S(2)}, u32[]{:S(2)}) collective-permute-start(bf16[128,2048]{1,0:T(8,128)(2,1)S(1)} %bitcast.248), channel_id=1, source_target_pairs={{0,2},{1,3},{2,0},{3,1},{4,6},{5,7},{6,4},{7,5},{8,10},{9,11},{10,... | collective-permute-start | bytes 1572872 | tf_op jit(solution)/shard_map/ppermute | solution.py:39
  73.0 17.9 %collective-permute-start.4 = (bf16[512,256]{1,0:T(8,128)(2,1)}, bf16[512,256]{1,0:T(8,128)(2,1)S(1)}, u32[]{:S(2)}, u32[]{:S(2)}) collective-permute-start(bf16[512,256]{1,0:T(8,128)(2,1)} %constant_dynamic-update-slice_fusion), channel_id=1, source_target_pairs={{0,2},{1,3},{2,0},{3,1},{4,6},{5,7},{6,4},{7,5},{8,10},{9,11},{10,... | collective-permute-start | bytes 786440 | tf_op jit(solution)/shard_map/ppermute | solution.py:39
  90.9 2.4 collective-permute-start.6
  90.9 2.5 collective-permute-start.5
  93.4 183.2 %collective-permute-start.10 = (bf16[512,2048]{1,0:T(8,128)(2,1)}, bf16[512,2048]{1,0:T(8,128)(2,1)}, u32[]{:S(2)}, u32[]{:S(2)}) collective-permute-start(bf16[512,2048]{1,0:T(8,128)(2,1)} %get-tuple-element.37), channel_id=1, source_target_pairs={{0,1},{1,0},{2,3},{3,2},{4,5},{5,4},{6,7},{7,6},{8,9},{9,8},{10,11... | collective-permute-start | bytes 6291464 | tf_op jit(solution)/shard_map/ppermute | solution.py:39
  93.4 196.6 %collective-permute-start.3 = (bf16[512,2048]{1,0:T(8,128)(2,1)}, bf16[512,2048]{1,0:T(8,128)(2,1)}, u32[]{:S(2)}, u32[]{:S(2)}) collective-permute-start(bf16[512,2048]{1,0:T(8,128)(2,1)} %get-tuple-element.36), channel_id=1, source_target_pairs={{0,1},{1,0},{2,3},{3,2},{4,5},{5,4},{6,7},{7,6},{8,9},{9,8},{10,11... | collective-permute-start | bytes 6291464 | tf_op jit(solution)/shard_map/ppermute | solution.py:39
  94.0 23.5 %copy-start.13 = (bf16[2048,256]{1,0:T(8,128)(2,1)}, bf16[2048,256]{1,0:T(8,128)(2,1)S(1)}, u32[]{:S(2)}) copy-start(bf16[2048,256]{1,0:T(8,128)(2,1)S(1)} %pad_maximum_fusion) | copy-start | bytes 3145732
  94.1 43.9 %collective-permute-start.13 = (bf16[512,1536]{0,1:T(8,128)(2,1)}, bf16[512,1536]{0,1:T(8,128)(2,1)}, u32[]{:S(2)}, u32[]{:S(2)}) collective-permute-start(bf16[512,1536]{0,1:T(8,128)(2,1)} %bitcast.14), channel_id=1, source_target_pairs={{0,1},{1,0},{2,3},{3,2},{4,5},{5,4},{6,7},{7,6},{8,9},{9,8},{10,11... | collective-permute-start | bytes 4718600 | tf_op jit(solution)/shard_map/ppermute | solution.py:39
  96.4 6.3 %collective-permute-start.19 = (bf16[128,2048]{1,0:T(8,128)(2,1)}, bf16[128,2048]{1,0:T(8,128)(2,1)S(1)}, u32[]{:S(2)}, u32[]{:S(2)}) collective-permute-start(bf16[128,2048]{1,0:T(8,128)(2,1)} %collective-permute-done.18), channel_id=1, source_target_pairs={{0,1},{1,0},{2,3},{3,2},{4,5},{5,4},{6,7},{7,6},{8,9},{9,8},{10,11... | collective-permute-start | bytes 1572872 | tf_op jit(solution)/shard_map/ppermute | solution.py:39
  96.5 11.4 %collective-permute-start.2 = (bf16[128,2048]{1,0:T(8,128)(2,1)S(1)}, bf16[128,2048]{1,0:T(8,128)(2,1)S(1)}, u32[]{:S(2)}, u32[]{:S(2)}) collective-permute-start(bf16[128,2048]{1,0:T(8,128)(2,1)S(1)} %collective-permute-done.1), channel_id=1, source_target_pairs={{0,1},{1,0},{2,3},{3,2},{4,5},{5,4},{6,7},{7,6},{8,9},{9,8},{10,11... | collective-permute-start | bytes 1572872 | tf_op jit(solution)/shard_map/ppermute | solution.py:39
  105.9 15.3 %collective-permute-start.20 = (bf16[2,32,512]{2,1,0:T(8,128)(2,1)S(1)}, bf16[2,32,512]{2,1,0:T(8,128)(2,1)S(1)}, u32[]{:S(2)}, u32[]{:S(2)}) collective-permute-start(bf16[2,32,512]{2,1,0:T(8,128)(2,1)S(1)} %fusion.50), channel_id=1, source_target_pairs={{0,2},{1,3},{2,0},{3,1},{4,6},{5,7},{6,4},{7,5},{8,10},{9,11},{10,... | collective-permute-start | bytes 196616 | tf_op jit(solution)/shard_map/ppermute | solution.py:39
  108.0 15.3 %collective-permute-start.22 = (bf16[2,32,512]{2,1,0:T(8,128)(2,1)S(1)}, bf16[2,32,512]{2,1,0:T(8,128)(2,1)S(1)}, u32[]{:S(2)}, u32[]{:S(2)}) collective-permute-start(bf16[2,32,512]{2,1,0:T(8,128)(2,1)S(1)} %fusion.50), channel_id=1, source_target_pairs={{0,1},{1,0},{2,3},{3,2},{4,5},{5,4},{6,7},{7,6},{8,9},{9,8},{10,11... | collective-permute-start | bytes 196616 | tf_op jit(solution)/shard_map/ppermute | solution.py:39
  121.2 2.1 collective-permute-start.21
  123.2 21.1 %collective-permute-start.12 = (bf16[512,1536]{0,1:T(8,128)(2,1)}, bf16[512,1536]{0,1:T(8,128)(2,1)}, u32[]{:S(2)}, u32[]{:S(2)}) collective-permute-start(bf16[512,1536]{0,1:T(8,128)(2,1)} %bitcast.12), channel_id=1, source_target_pairs={{0,1},{1,0},{2,3},{3,2},{4,5},{5,4},{6,7},{7,6},{8,9},{9,8},{10,11... | collective-permute-start | bytes 4718600 | tf_op jit(solution)/shard_map/ppermute | solution.py:39
  131.9 28.6 %all-to-all-start.3 = ((bf16[8,128,256]{2,1,0:T(8,128)(2,1)}), bf16[8,128,256]{2,1,0:T(8,128)(2,1)}, u32[]{:S(2)}, u32[]{:S(2)}) async-start(bf16[8,128,256]{2,1,0:T(8,128)(2,1)} %bitcast.267), calls=%async_computation.3 | async-start | bytes 1048576 | tf_op jit(solution)/shard_map/all_to_all | solution.py:359
  141.4 14.1 %collective-permute-start.14 = (bf16[512,512]{1,0:T(8,128)(2,1)S(1)}, bf16[512,512]{1,0:T(8,128)(2,1)S(1)}, u32[]{:S(2)}, u32[]{:S(2)}) collective-permute-start(bf16[512,512]{1,0:T(8,128)(2,1)S(1)} %add_convert_fusion.7), channel_id=1, source_target_pairs={{0,2},{1,3},{2,0},{3,1},{4,6},{5,7},{6,4},{7,5},{8,10},{9,11},{10,... | collective-permute-start | bytes 1572872 | tf_op jit(solution)/shard_map/ppermute | solution.py:39
  160.5 25.6 %all-to-all-start = ((bf16[8,128,256]{2,1,0:T(8,128)(2,1)}), bf16[8,128,256]{2,1,0:T(8,128)(2,1)}, u32[]{:S(2)}, u32[]{:S(2)}) async-start(bf16[8,128,256]{2,1,0:T(8,128)(2,1)} %bitcast.276), calls=%async_computation | async-start | bytes 1048576 | tf_op jit(solution)/shard_map/all_to_all | solution.py:359
  168.4 12.7 %collective-permute-start.15 = (bf16[512,512]{1,0:T(8,128)(2,1)S(1)}, bf16[512,512]{1,0:T(8,128)(2,1)S(1)}, u32[]{:S(2)}, u32[]{:S(2)}) collective-permute-start(bf16[512,512]{1,0:T(8,128)(2,1)S(1)} %add_convert_fusion.6), channel_id=1, source_target_pairs={{0,2},{1,3},{2,0},{3,1},{4,6},{5,7},{6,4},{7,5},{8,10},{9,11},{10,... | collective-permute-start | bytes 1572872 | tf_op jit(solution)/shard_map/ppermute | solution.py:39
  186.0 24.2 %all-to-all-start.1 = ((bf16[8,128,256]{2,1,0:T(8,128)(2,1)}), bf16[8,128,256]{2,1,0:T(8,128)(2,1)}, u32[]{:S(2)}, u32[]{:S(2)}) async-start(bf16[8,128,256]{2,1,0:T(8,128)(2,1)} %bitcast.275), calls=%async_computation.1 | async-start | bytes 1048576 | tf_op jit(solution)/shard_map/all_to_all | solution.py:359
  194.0 11.2 %collective-permute-start.16 = (bf16[512,512]{1,0:T(8,128)(2,1)S(1)}, bf16[512,512]{1,0:T(8,128)(2,1)S(1)}, u32[]{:S(2)}, u32[]{:S(2)}) collective-permute-start(bf16[512,512]{1,0:T(8,128)(2,1)S(1)} %add_convert_fusion.5), channel_id=1, source_target_pairs={{0,2},{1,3},{2,0},{3,1},{4,6},{5,7},{6,4},{7,5},{8,10},{9,11},{10,... | collective-permute-start | bytes 1572872 | tf_op jit(solution)/shard_map/ppermute | solution.py:39
  210.2 16.6 %all-to-all-start.2 = ((bf16[8,128,256]{2,1,0:T(8,128)(2,1)}), bf16[8,128,256]{2,1,0:T(8,128)(2,1)}, u32[]{:S(2)}, u32[]{:S(2)}) async-start(bf16[8,128,256]{2,1,0:T(8,128)(2,1)} %bitcast.268), calls=%async_computation.2 | async-start | bytes 1048576 | tf_op jit(solution)/shard_map/all_to_all | solution.py:359
  236.5 15.3 %all-to-all-start.5 = ((bf16[8,128,256]{2,1,0:T(8,128)(2,1)}), bf16[8,128,256]{2,1,0:T(8,128)(2,1)}, u32[]{:S(2)}, u32[]{:S(2)}) async-start(bf16[8,128,256]{2,1,0:T(8,128)(2,1)} %bitcast.291), calls=%async_computation.5 | async-start | bytes 1048576 | tf_op jit(solution)/shard_map/all_to_all | solution.py:359
  240.7 15.4 %copy-start.66 = (s32[128]{0:T(128)S(1)}, s32[128]{0:T(128)}, u32[]{:S(2)}) copy-start(s32[128]{0:T(128)} %copy-done.64) | copy-start | bytes 1540
  251.8 16.3 %all-to-all-start.6 = ((bf16[8,128,256]{2,1,0:T(8,128)(2,1)}), bf16[8,128,256]{2,1,0:T(8,128)(2,1)}, u32[]{:S(2)}, u32[]{:S(2)}) async-start(bf16[8,128,256]{2,1,0:T(8,128)(2,1)} %bitcast.290), calls=%async_computation.6 | async-start | bytes 1048576 | tf_op jit(solution)/shard_map/all_to_all | solution.py:359
  268.2 17.3 %all-to-all-start.7 = ((bf16[8,128,256]{2,1,0:T(8,128)(2,1)}), bf16[8,128,256]{2,1,0:T(8,128)(2,1)}, u32[]{:S(2)}, u32[]{:S(2)}) async-start(bf16[8,128,256]{2,1,0:T(8,128)(2,1)} %bitcast.289), calls=%async_computation.7 | async-start | bytes 1048576 | tf_op jit(solution)/shard_map/all_to_all | solution.py:359
  283.8 48.9 %collective-permute-start.11 = (bf16[512,2048]{1,0:T(8,128)(2,1)}, bf16[512,2048]{1,0:T(8,128)(2,1)}, u32[]{:S(2)}, u32[]{:S(2)}) collective-permute-start(bf16[512,2048]{1,0:T(8,128)(2,1)} %add_convert_fusion.2), channel_id=1, source_target_pairs={{0,2},{1,3},{2,0},{3,1},{4,6},{5,7},{6,4},{7,5},{8,10},{9,11},{10,... | collective-permute-start | bytes 6291464 | tf_op jit(solution)/shard_map/ppermute | solution.py:39
  285.4 23.3 %all-to-all-start.4 = ((bf16[8,128,256]{2,1,0:T(8,128)(2,1)}), bf16[8,128,256]{2,1,0:T(8,128)(2,1)}, u32[]{:S(2)}, u32[]{:S(2)}) async-start(bf16[8,128,256]{2,1,0:T(8,128)(2,1)} %bitcast.288), calls=%async_computation.4 | async-start | bytes 1048576 | tf_op jit(solution)/shard_map/all_to_all | solution.py:359
  290.0 285.4 %all-reduce.3.cloned.1.call-start = ((), (), s32[]{:S(2)}) async-start(), calls=%async_computation.8 | async-start | bytes 4194304 | tf_op jit(solution)/shard_map/psum | solution.py:579
  297.6 98.9 %collective-permute-start.29 = (bf16[512,512]{1,0:T(8,128)(2,1)}, bf16[512,512]{1,0:T(8,128)(2,1)}, u32[]{:S(2)}, u32[]{:S(2)}) collective-permute-start(bf16[512,512]{1,0:T(8,128)(2,1)} %bitcast.103), channel_id=1, source_target_pairs={{0,2},{1,3},{2,0},{3,1},{4,6},{5,7},{6,4},{7,5},{8,10},{9,11},{10,... | collective-permute-start | bytes 1572872 | tf_op jit(solution)/shard_map/ppermute | solution.py:39
  301.9 96.0 %collective-permute-start.30 = (bf16[512,512]{1,0:T(8,128)(2,1)}, bf16[512,512]{1,0:T(8,128)(2,1)}, u32[]{:S(2)}, u32[]{:S(2)}) collective-permute-start(bf16[512,512]{1,0:T(8,128)(2,1)} %bitcast.106), channel_id=1, source_target_pairs={{0,2},{1,3},{2,0},{3,1},{4,6},{5,7},{6,4},{7,5},{8,10},{9,11},{10,... | collective-permute-start | bytes 1572872 | tf_op jit(solution)/shard_map/ppermute | solution.py:39
  308.8 72.1 %collective-permute-start.35 = (f32[128,512]{1,0:T(8,128)}, f32[128,512]{1,0:T(8,128)S(1)}, u32[]{:S(2)}, u32[]{:S(2)}) collective-permute-start(f32[128,512]{1,0:T(8,128)} %fusion.114), channel_id=1, source_target_pairs={{0,1},{1,0},{2,3},{3,2},{4,5},{5,4},{6,7},{7,6},{8,9},{9,8},{10,11... | collective-permute-start | bytes 786440 | tf_op jit(solution)/shard_map/ppermute | solution.py:39
  311.0 4.6 collective-permute-start.25
  312.9 19.7 %copy-start.21 = (f32[512,2048]{1,0:T(8,128)S(1)}, f32[512,2048]{1,0:T(8,128)}, u32[]{:S(2)}) copy-start(f32[512,2048]{1,0:T(8,128)} %fusion.109) | copy-start | bytes 12582916
  313.9 18.7 %copy-start.7 = (bf16[512,2048]{1,0:T(8,128)(2,1)S(1)}, bf16[512,2048]{1,0:T(8,128)(2,1)}, u32[]{:S(2)}) copy-start(bf16[512,2048]{1,0:T(8,128)(2,1)} %get-tuple-element.44) | copy-start | bytes 6291460
  313.9 18.7 %copy-start.20 = (f32[512,2048]{1,0:T(8,128)S(1)}, f32[512,2048]{1,0:T(8,128)}, u32[]{:S(2)}) copy-start(f32[512,2048]{1,0:T(8,128)} %fusion.103) | copy-start | bytes 12582916
  313.9 18.7 %dynamic-slice-start = ((f32[8192]{0:T(1024)}, s32[]{:T(128)}), f32[2048]{0:T(1024)S(1)}, s32[]{:S(2)}) async-start(f32[8192]{0:T(1024)} %param.39, s32[]{:T(128)} %select_n.457), calls=%async_computation.11 | async-start | bytes 16896 | tf_op jit(solution)/shard_map/dynamic_slice | solution.py:437
  315.7 68.0 %collective-permute-start.26 = (f32[32,512]{1,0:T(8,128)S(1)}, f32[32,512]{1,0:T(8,128)S(1)}, u32[]{:S(2)}, u32[]{:S(2)}) collective-permute-start(f32[32,512]{1,0:T(8,128)S(1)} %slice_add_fusion), channel_id=1, source_target_pairs={{0,2},{1,3},{2,0},{3,1},{4,6},{5,7},{6,4},{7,5},{8,10},{9,11},{10,... | collective-permute-start | bytes 196616 | tf_op jit(solution)/shard_map/ppermute | solution.py:39
  332.7 32.9 %slice-start = ((s8[8388608]{0:T(1024)(128)(4,1)}), s8[4194304]{0:T(1024)(128)(4,1)S(1)}, s32[]{:S(2)}) async-start(s8[8388608]{0:T(1024)(128)(4,1)} %bitcast.263), calls=%async_computation.9 | async-start | bytes 8388608
  346.2 19.3 %slice-start.1 = ((s8[8388608]{0:T(1024)(128)(4,1)}), s8[4194304]{0:T(1024)(128)(4,1)S(1)}, s32[]{:S(2)}) async-start(s8[8388608]{0:T(1024)(128)(4,1)} %bitcast.263), calls=%async_computation.10 | async-start | bytes 8388608
  378.6 1.4 collective-permute-start.23
  380.0 5.0 collective-permute-start.24
  380.8 19.5 %collective-permute-start.31 = (bf16[512,512]{1,0:T(8,128)(2,1)S(1)}, bf16[512,512]{1,0:T(8,128)(2,1)S(1)}, u32[]{:S(2)}, u32[]{:S(2)}) collective-permute-start(bf16[512,512]{1,0:T(8,128)(2,1)S(1)} %bitcast.266), channel_id=1, source_target_pairs={{0,2},{1,3},{2,0},{3,1},{4,6},{5,7},{6,4},{7,5},{8,10},{9,11},{10,... | collective-permute-start | bytes 1572872 | tf_op jit(solution)/shard_map/ppermute | solution.py:39
  383.7 71.2 %collective-permute-start.32 = (bf16[512,2048]{1,0:T(8,128)(2,1)S(1)}, bf16[512,2048]{1,0:T(8,128)(2,1)S(1)}, u32[]{:S(2)}, u32[]{:S(2)}) collective-permute-start(bf16[512,2048]{1,0:T(8,128)(2,1)S(1)} %add_convert_fusion), channel_id=1, source_target_pairs={{0,2},{1,3},{2,0},{3,1},{4,6},{5,7},{6,4},{7,5},{8,10},{9,11},{10,... | collective-permute-start | bytes 6291464 | tf_op jit(solution)/shard_map/ppermute | solution.py:39
  385.0 10.7 %collective-permute-start.37 = (f32[128,512]{1,0:T(8,128)S(1)}, f32[128,512]{1,0:T(8,128)S(1)}, u32[]{:S(2)}, u32[]{:S(2)}) collective-permute-start(f32[128,512]{1,0:T(8,128)S(1)} %fusion.101), channel_id=1, source_target_pairs={{0,1},{1,0},{2,3},{3,2},{4,5},{5,4},{6,7},{7,6},{8,9},{9,8},{10,11... | collective-permute-start | bytes 786440 | tf_op jit(solution)/shard_map/ppermute | solution.py:39
  395.7 51.1 %collective-permute-start.36 = (f32[128,512]{1,0:T(8,128)S(1)}, f32[128,512]{1,0:T(8,128)S(1)}, u32[]{:S(2)}, u32[]{:S(2)}) collective-permute-start(f32[128,512]{1,0:T(8,128)S(1)} %add.584), channel_id=1, source_target_pairs={{0,2},{1,3},{2,0},{3,1},{4,6},{5,7},{6,4},{7,5},{8,10},{9,11},{10,... | collective-permute-start | bytes 786440 | tf_op jit(solution)/shard_map/ppermute | solution.py:39
  396.5 73.8 %collective-permute-start.27 = (bf16[2,128,2048]{2,1,0:T(8,128)(2,1)}, bf16[2,128,2048]{2,1,0:T(8,128)(2,1)}, u32[]{:S(2)}, u32[]{:S(2)}) collective-permute-start(bf16[2,128,2048]{2,1,0:T(8,128)(2,1)} %pad_maximum_fusion.1), channel_id=1, source_target_pairs={{0,1},{1,0},{2,3},{3,2},{4,5},{5,4},{6,7},{7,6},{8,9},{9,8},{10,11... | collective-permute-start | bytes 3145736 | tf_op jit(solution)/shard_map/ppermute | solution.py:39
  397.9 53.7 %collective-permute-start.38 = (f32[128,512]{1,0:T(8,128)S(1)}, f32[128,512]{1,0:T(8,128)S(1)}, u32[]{:S(2)}, u32[]{:S(2)}) collective-permute-start(f32[128,512]{1,0:T(8,128)S(1)} %add.588), channel_id=1, source_target_pairs={{0,2},{1,3},{2,0},{3,1},{4,6},{5,7},{6,4},{7,5},{8,10},{9,11},{10,... | collective-permute-start | bytes 786440 | tf_op jit(solution)/shard_map/ppermute | solution.py:39
  400.8 2.9 collective-permute-start.39
  403.6 51.2 %copy-start.73 = (f32[512]{0:T(512)S(1)}, f32[512]{0:T(512)}, u32[]{:S(2)}) copy-start(f32[512]{0:T(512)} %get-tuple-element.102) | copy-start | bytes 6148
  403.6 51.2 %copy-start.79 = (f32[512,512]{1,0:T(8,128)S(1)}, f32[512,512]{1,0:T(8,128)}, u32[]{:S(2)}) copy-start(f32[512,512]{1,0:T(8,128)} %fusion.19) | copy-start | bytes 3145732
  465.8 3.2 collective-permute-start.33
  466.4 1.8 collective-permute-start.40
  469.3 9.2 %collective-permute-start.34 = (bf16[128,1024]{1,0:T(8,128)(2,1)S(1)}, bf16[128,1024]{1,0:T(8,128)(2,1)S(1)}, u32[]{:S(2)}, u32[]{:S(2)}) collective-permute-start(bf16[128,1024]{1,0:T(8,128)(2,1)S(1)} %get-tuple-element.51), channel_id=1, source_target_pairs={{0,2},{1,3},{2,0},{3,1},{4,6},{5,7},{6,4},{7,5},{8,10},{9,11},{10,... | collective-permute-start | bytes 786440 | tf_op jit(solution)/shard_map/ppermute | solution.py:39
  472.4 16.8 %collective-permute-start.28 = (bf16[128,2048]{1,0:T(8,128)(2,1)S(1)}, bf16[128,2048]{1,0:T(8,128)(2,1)S(1)}, u32[]{:S(2)}, u32[]{:S(2)}) collective-permute-start(bf16[128,2048]{1,0:T(8,128)(2,1)S(1)} %fusion.61), channel_id=1, source_target_pairs={{0,2},{1,3},{2,0},{3,1},{4,6},{5,7},{6,4},{7,5},{8,10},{9,11},{10,... | collective-permute-start | bytes 1572872 | tf_op jit(solution)/shard_map/ppermute | solution.py:39
  (69 other events, 355.8 us)
Sparse Core Ops, SparseCore 0:
  469.1 106.2 all-reduce.2

commit v2 on v1

v2 whole, which is shorter than its diff:
```python
import functools
import math

import jax
import jax.numpy as jnp
from jax import lax
from jax.experimental import pallas as pl
from jax.experimental.pallas import tpu as pltpu
from jax.sharding import PartitionSpec as P

HEADS = 8
HEAD = 256
ROT = 64
RANK = 16
BLOCK = 64
ADAPT_COLS = 128
WA = 4
PAIRS = 8
VMEM_BYTES = 58 * 1024 * 1024

epsilon = 1e-05
masked_score = -1e30
f32 = jnp.float32
bf16 = jnp.bfloat16


def product(left, right):
    return jnp.dot(left, right, preferred_element_type=f32)


def times_t(left, right):
    return lax.dot_general(left, right, (((1,), (1,)), ((), ())), preferred_element_type=f32)


def t_times(left, right):
    return lax.dot_general(left, right, (((0,), (0,)), ((), ())), preferred_element_type=f32)


def swap(value, bits):
    return lax.ppermute(value, "wa", [(i, i ^ bits) for i in range(WA)])


def after(value, *earlier):
    return lax.optimization_barrier((value, *earlier))[0]


def absolute(pieces, wa):
    low = wa % 2 == 1
    high = wa >= 2
    p = [
        jnp.where(low, pieces[1], pieces[0]),
        jnp.where(low, pieces[0], pieces[1]),
        jnp.where(low, pieces[3], pieces[2]),
        jnp.where(low, pieces[2], pieces[3]),
    ]
    return [
        jnp.where(high, p[2], p[0]),
        jnp.where(high, p[3], p[1]),
        jnp.where(high, p[0], p[2]),
        jnp.where(high, p[1], p[3]),
    ]


def rotary_tables(offset):
    half = ROT // 2
    lane = jnp.arange(128, dtype=jnp.int32)
    freq = 10000.0 ** (-2.0 * (lane % half).astype(f32) / ROT)
    freq = jnp.where(lane < ROT, freq, 0.0)
    angle = offset.astype(f32)[:, None] * freq[None, :]
    sign = jnp.where(lane < half, -1.0, 1.0)
    return jnp.cos(angle), jnp.sin(angle) * sign[None, :]


def turn_first(values, cosine, sine):
    lane = lax.broadcasted_iota(jnp.int32, values.shape, 1)
    partner = jnp.where(
        lane < ROT // 2, pltpu.roll(values, 128 - ROT // 2, 1), pltpu.roll(values, ROT // 2, 1)
    )
    return values * cosine + partner * sine


def call(kernel, index, inputs, outputs, grid=(1,), scratch=(), flops=0, name=None):
    def spec(shape, block, where):
        if where is None:
            zeros = (0,) * len(shape)
            return pl.BlockSpec(shape, lambda *_: zeros)
        return pl.BlockSpec(block, where)

    size = sum(a.size * a.dtype.itemsize if w is None else math.prod(i or 1 for i in b) * 2 * math.prod(grid)
               for a, b, w in inputs)
    return pl.pallas_call(
        kernel,
        grid_spec=pltpu.PrefetchScalarGridSpec(
            num_scalar_prefetch=1,
            grid=grid,
            in_specs=[spec(a.shape, b, w) for a, b, w in inputs],
            out_specs=[spec(s, b, w) for s, _, b, w in outputs],
            scratch_shapes=list(scratch),
        ),
        out_shape=[jax.ShapeDtypeStruct(s, d) for s, d, _, _ in outputs],
        compiler_params=pltpu.CompilerParams(vmem_limit_bytes=VMEM_BYTES),
        cost_estimate=pl.CostEstimate(flops=flops, bytes_accessed=size, transcendentals=0),
    )(index, *[a for a, _, _ in inputs])


def whole(array):
    return (array, None, None)


def copy_kernel(index_ref, *refs):
    count = len(refs) // 2
    for source, target in zip(refs[:count], refs[count:]):
        target[...] = source[...].reshape(target.shape)


def cut_columns(index, weight, size, kinds, cuts, parts=1):
    rows = weight.shape[0]
    part = size // parts
    inputs, outputs = [], []
    for r, halved in cuts:
        height = rows // 2 if halved else rows

        def where(slot, t, ref, r=r, halved=halved):
            kind = sum(kind * (slot == i) for i, kind in enumerate(kinds))
            return (ref[4] if halved else 0, (kind * WA + ref[r]) * parts + t)

        inputs.append((weight, (height, part), where))
        outputs.append(
            (
                (len(kinds), height, size),
                weight.dtype,
                (1, height, part),
                lambda slot, t, ref: (slot, 0, t),
            )
        )
    return call(copy_kernel, index, inputs, outputs, grid=(len(kinds), parts))


def strips(value):
    return [value[:, i : i + 128] for i in range(0, value.shape[1], 128)]


def store_strips(target, first, value):
    for item in strips(value):
        target[first : first + item.shape[0], :] = item
        first += item.shape[0]
    return first


def pack_kernel(index_ref, *refs):
    plain, last_ref = refs[:-6], refs[-6]
    (ups_mate, ups_peer, ups_far), (away_ref, near_ref) = refs[-5:-2], refs[-2:]
    first = 0
    for ref in plain:
        store_strips(away_ref, first, ref)
        first = store_strips(near_ref, first, ref)
    blank = ups_peer.shape[0] * ups_peer.shape[1] // 128
    store_strips(near_ref, first, ups_mate)
    store_strips(near_ref, first + blank, ups_mate)
    store_strips(away_ref, first, ups_peer)
    store_strips(away_ref, first + blank, ups_far)
    store_strips(near_ref, first + 2 * blank, last_ref)
    store_strips(away_ref, first + 2 * blank, last_ref)


def pack_small(index, plain, up, kinds, last):
    block = up.shape[1] // len(kinds) // WA
    items = [whole(item) for item in plain + [last]]
    size = sum(item.size for item in plain) // 128
    ups = up.shape[0] * block * len(kinds) // 128
    cut = jnp.concatenate if len(kinds) > 1 else (lambda v, axis: v[0])
    for r in (1, 2, 3):
        items.append(
            whole(
                cut(
                    [
                        lax.dynamic_slice_in_dim(up, (kind * WA + index[r]) * block, block, axis=1)
                        for kind in kinds
                    ],
                    axis=1,
                )
            )
        )
    shape = (size + 2 * ups + last.shape[0], 128)
    return call(pack_kernel, index, items, [(shape, bf16, None, None)] * 2)


def front_kernel(index_ref, *refs):
    token_ref, down_ref = refs[:2]
    packs = refs[2:5]
    mask_ref, g1, b1, g2, b2, first_ref, second_ref, inner_ref = refs[5:]
    rows, width = token_ref.shape
    wide = down_ref.shape[0]
    step = 32
    for r in range(WA):
        base = pl.multiple_of(index_ref[r] * rows, rows)
        for start in range(0, rows, step):
            if r == 0:
                values = token_ref[start : start + step, :]
            else:
                values = jnp.concatenate(
                    [
                        packs[r - 1][i * rows + start : i * rows + start + step, :]
                        for i in range(width // 128)
                    ],
                    axis=1,
                )
            values = values.astype(f32)
            centered = values - jnp.mean(values, axis=1, keepdims=True)
            spread = jnp.mean(centered * centered, axis=1, keepdims=True)
            normal = centered * lax.rsqrt(spread + epsilon)
            first_ref[pl.ds(base + start, step), :] = (normal * g1[...] + b1[...]).astype(bf16)
            second_ref[pl.ds(base + start, step), :] = (normal * g2[...] + b2[...]).astype(bf16)
    total = 0.0
    first = rows * width // 128
    for r in range(WA):
        columns = pl.ds(pl.multiple_of(index_ref[r] * wide, wide), wide)
        down = down_ref[...] if r == 0 else packs[r - 1][first : first + wide, :]
        total += product(first_ref[:, columns], down)
    inner_ref[...] = (total * mask_ref[...]).astype(bf16)


def pieces_of(index_ref, refs):
    wide = refs[0].shape[-2]
    half = wide // 2
    y = index_ref[4]
    firsts = [
        index_ref[0] * wide,
        index_ref[1] * wide,
        index_ref[2] * wide + y * half,
        index_ref[2] * wide + (1 - y) * half,
        index_ref[3] * wide + y * half,
        index_ref[3] * wide + (1 - y) * half,
    ]
    return [
        (pl.ds(pl.multiple_of(first, half), ref.shape[-2]), ref) for first, ref in zip(firsts, refs)
    ]


def read(ref):
    return ref[...].reshape(ref.shape[-2:])


def join_ups(index_ref, ups, joined):
    size = ADAPT_COLS // WA
    for r, ref in enumerate(ups):
        first = pl.multiple_of(index_ref[r] * size, size)
        if ref.shape[-1] == joined.shape[-1]:
            joined[pl.ds(first, size), :] = read(ref)
        else:
            for i in range(joined.shape[-1] // 128):
                joined[pl.ds(first, size), i * 128 : (i + 1) * 128] = ref[
                    i * size : (i + 1) * size, :
                ]


def qkv_kernel(turned, index_ref, hidden_ref, *refs):
    weights, ups = refs[:6], refs[6:10]
    inner_ref, bias_ref, cos_ref, sin_ref, out_ref, joined = refs[10:]
    join_ups(index_ref, ups, joined)
    total = product(inner_ref[...], joined[...]) + bias_ref[...]
    for columns, ref in pieces_of(index_ref, weights):
        total += product(hidden_ref[:, columns], read(ref))
    shape = out_ref.shape
    if turned:
        first = turn_first(total[:, :128], cos_ref[...], sin_ref[...])
        out_ref[..., :128] = first.astype(bf16).reshape(shape[:-1] + (128,))
        out_ref[..., 128:] = total[:, 128:].astype(bf16).reshape(shape[:-1] + (HEAD - 128,))
    else:
        out_ref[...] = total.astype(bf16).reshape(shape)


def grad_kernel(index_ref, *refs):
    parts = refs[:WA]
    mask_ref, weight_ref, down_ref = refs[WA : WA + 3]
    grad_ref, dense_ref, out_ref, heads_ref, ups_ref, dense_joined, out_joined = refs[WA + 3 :]
    size = ADAPT_COLS // WA
    rows = parts[0].shape[0] - 2 * size
    for r in range(WA):
        first = pl.ds(pl.multiple_of(index_ref[r] * size, size), size)
        dense_joined[first, :] = parts[r][rows : rows + size, :]
        out_joined[first, :] = parts[r][rows + size :, :]
        grad_ref[pl.ds(pl.multiple_of(index_ref[r] * rows, rows), rows), :] = parts[r][:rows, :]
    ups_ref[0] = dense_joined[...]
    ups_ref[1] = out_joined[...]
    grad = grad_ref[...]
    dense = (times_t(grad, dense_joined[...]) * mask_ref[...]).astype(bf16)
    dense_ref[...] = dense
    out_ref[...] = (times_t(grad, out_joined[...]) * mask_ref[...]).astype(bf16)
    for head in range(2):
        span = slice(head * HEAD, (head + 1) * HEAD)
        total = times_t(grad, weight_ref[span, :]) + times_t(dense, down_ref[span, :])
        heads_ref[:, head] = total.astype(bf16).reshape(WA, rows, HEAD)


def gelu_parts(values):
    bell = jnp.exp(-0.5 * values * values)
    t = 1.0 / (1.0 + (0.3275911 * math.sqrt(0.5)) * jnp.abs(values))
    series = 1.061405429 * 0.5
    for factor in (-1.453152027, 1.421413741, -0.284496736, 0.254829592):
        series = series * t + 0.5 * factor
    tail = series * t * bell
    below = jnp.where(values > 0, 1.0 - tail, tail)
    return values * below, below + values * bell * (1.0 / math.sqrt(2.0 * math.pi))


def feed_kernel(index_ref, hidden_ref, grad_ref, *refs):
    weights, ups, downs = refs[:6], refs[6:10], refs[10:14]
    mask_ref, bias_ref, gain_ref, out_w_ref, out_down_ref, out_inner_grad_ref = refs[14:20]
    (
        out_ref,
        norm_grad_ref,
        out_inner_ref,
        inner_grad_ref,
        out_down_grad_ref,
        in_up_grad_ref,
        inner_ref,
        joined,
    ) = refs[20:]
    step = pl.program_id(0)

    @pl.when(step == 0)
    def _():
        wide = downs[0].shape[0]
        total = 0.0
        for r in range(WA):
            columns = pl.ds(pl.multiple_of(index_ref[r] * wide, wide), wide)
            total += product(hidden_ref[:, columns], downs[r][...])
        inner_ref[...] = (total * mask_ref[...]).astype(bf16)
        out_ref[...] = jnp.zeros_like(out_ref)
        norm_grad_ref[...] = jnp.zeros_like(norm_grad_ref)
        out_inner_ref[...] = jnp.zeros_like(out_inner_ref)
        inner_grad_ref[...] = jnp.zeros_like(inner_grad_ref)

    join_ups(index_ref, ups, joined)
    pre = product(inner_ref[...], joined[...]) + bias_ref[...]
    for columns, ref in pieces_of(index_ref, weights):
        pre += product(hidden_ref[:, columns], read(ref))
    units, slope = gelu_parts(pre)
    units = units.astype(bf16)
    pre_grad = times_t(grad_ref[...], out_w_ref[...]) + times_t(
        out_inner_grad_ref[...], out_down_ref[...]
    )
    pre_grad = (pre_grad * slope).astype(bf16)
    out_ref[...] += product(units, out_w_ref[...])
    for columns, ref in pieces_of(index_ref, weights):
        norm_grad_ref[:, columns] += times_t(pre_grad, read(ref))
    out_inner_ref[...] += product(units, out_down_ref[...])
    inner_grad_ref[...] += times_t(pre_grad, joined[...])
    out_down_grad_ref[...] = t_times(units, out_inner_grad_ref[...]).astype(bf16)
    in_up_grad_ref[...] = t_times(inner_ref[...], pre_grad).astype(bf16)

    @pl.when(step == pl.num_programs(0) - 1)
    def _():
        norm_grad_ref[...] = norm_grad_ref[...] * gain_ref[...]


def scatter_rows(index_ref, total_ref, keep_ref, send_ref):
    rows = keep_ref.shape[1]
    for r, (ref, slot) in enumerate(((keep_ref, 0), (send_ref, 0), (keep_ref, 1), (send_ref, 1))):
        part = total_ref[pl.ds(pl.multiple_of(index_ref[r] * rows, rows), rows), :]
        ref[slot] = part.astype(ref.dtype)


def head_rows(ref, head):
    return ref[:, head, 0].reshape(-1, HEAD)


def dense_kernel(
    index_ref,
    heads_ref,
    sum_ref,
    weight_ref,
    down_ref,
    inner_grad_ref,
    keep_ref,
    send_ref,
    inner_ref,
    down_grad_ref,
    total,
):
    result = sum_ref[...]
    inner = 0.0
    for head in range(2):
        span = slice(head * HEAD, (head + 1) * HEAD)
        heads = head_rows(heads_ref, head)
        result += product(heads, weight_ref[span, :])
        inner += product(heads, down_ref[span, :])
        down_grad_ref[span, :] = t_times(heads, inner_grad_ref[...]).astype(bf16)
    inner_ref[...] = inner
    total[...] = result
    scatter_rows(index_ref, total, keep_ref, send_ref)


def mixed_rows(query_grad_ref, key_grad_ref, kind, head):
    if kind == 0:
        return query_grad_ref[:, head, 1].reshape(-1, HEAD)
    return key_grad_ref[:, head, kind + 1].reshape(-1, HEAD)


def mix_kernel(index_ref, *refs):
    grads, ups = refs[:2], refs[2 : 2 + 3 * WA]
    inner_ref, inner_grad_ref, up_grad_ref, joined = refs[2 + 3 * WA :]
    width = 2 * HEAD
    for kind in range(3):
        for r in range(WA):
            size = ADAPT_COLS // WA
            first = pl.multiple_of(index_ref[r] * size, size)
            ref = ups[kind * WA + r]
            if r == 0:
                joined[kind, pl.ds(first, size), :] = ref[...]
            else:
                for i in range(width // 128):
                    joined[kind, pl.ds(first, size), i * 128 : (i + 1) * 128] = ref[
                        i * size : (i + 1) * size, :
                    ]
    total = 0.0
    for kind in range(3):
        for head in range(2):
            span = slice(head * HEAD, (head + 1) * HEAD)
            rows = mixed_rows(*grads, kind, head)
            total += times_t(rows, joined[kind, :, span])
            out = slice(kind * width + head * HEAD, kind * width + (head + 1) * HEAD)
            up_grad_ref[:, out] = t_times(inner_ref[...], rows).astype(bf16)
    inner_grad_ref[...] = total


def norm_grad_kernel(index_ref, *refs):
    grads, weights = refs[:2], refs[2:20]
    gain_ref, sum_ref, keep_ref, send_ref, total = refs[20:]
    sets = [pieces_of(index_ref, weights[6 * kind : 6 * kind + 6]) for kind in range(3)]
    rows = [[mixed_rows(*grads, kind, head) for head in range(2)] for kind in range(3)]
    for piece in range(6):
        columns = sets[0][piece][0]
        part = 0.0
        for kind in range(3):
            weight = read(sets[kind][piece][1])
            for head in range(2):
                part += times_t(rows[kind][head], weight[:, head * HEAD : (head + 1) * HEAD])
        total[:, columns] = part * gain_ref[:, columns] + sum_ref[:, columns]
    scatter_rows(index_ref, total, keep_ref, send_ref)


def finish_kernel(index_ref, *refs):
    keep_ref, near_ref, away_ref, first_ref, second_ref = refs[:5]
    first_downs, second_downs = refs[5:9], refs[9:13]
    g1, g2, token_ref, grad_ref, out_ref, total = refs[13:]
    total[...] = keep_ref[0] + near_ref[0].astype(f32) + away_ref[...].astype(f32)
    wide = first_downs[0].shape[0]
    for r in range(WA):
        columns = pl.ds(pl.multiple_of(index_ref[r] * wide, wide), wide)
        total[:, columns] += (
            times_t(first_ref[...], first_downs[r][...]) * g1[:, columns]
            + times_t(second_ref[...], second_downs[r][...]) * g2[:, columns]
        )
    step = 32
    for start in range(0, total.shape[0], step):
        span = slice(start, start + step)
        values = token_ref[span, :].astype(f32)
        centered = values - jnp.mean(values, axis=1, keepdims=True)
        rstd = lax.rsqrt(jnp.mean(centered * centered, axis=1, keepdims=True) + epsilon)
        normal = centered * rstd
        part = total[span, :]
        part = (
            part
            - jnp.mean(part, axis=1, keepdims=True)
            - normal * jnp.mean(part * normal, axis=1, keepdims=True)
        )
        out_ref[span, :] = grad_ref[span, :].astype(f32) + rstd * part


def attention_kernel(
    joint,
    query_ref,
    key_ref,
    value_ref,
    grad_ref,
    begin_ref,
    place_ref,
    key_place_ref,
    q_cos_ref,
    q_sin_ref,
    k_cos_ref,
    k_sin_ref,
    rows_ref,
    *refs,
):
    keys_ref, dk_sum, dv_sum = (rows_ref, *refs) if joint else refs
    step = pl.program_id(0)
    scale = 1.0 / math.sqrt(HEAD)

    @pl.when(step == 0)
    def _():
        dk_sum[...] = jnp.zeros_like(dk_sum)
        dv_sum[...] = jnp.zeros_like(dv_sum)

    query = query_ref[...]
    key = key_ref[...]
    value = value_ref[...]
    grad = grad_ref[...]
    key_place = key_place_ref[...]
    allowed = (key_place >= begin_ref[...]) & (key_place <= place_ref[...])
    scores = jnp.where(allowed, times_t(query, key) * scale, masked_score)
    top = jnp.max(scores, axis=1, keepdims=True)
    weights = jnp.exp(scores - top)
    prob = weights * (1.0 / jnp.sum(weights, axis=1, keepdims=True))
    prob_low = prob.astype(bf16)
    part, block = query.shape[0], rows_ref.shape[2]
    shape = (part // block, block)
    own = pl.ds(step * shape[0], shape[0]) if joint else slice(None)
    rows_ref[own, 0] = product(prob_low, value).astype(bf16).reshape(shape + (HEAD,))
    prob_grad = times_t(grad, value)
    delta = jnp.sum(prob * prob_grad, axis=1, keepdims=True)
    score_grad = (prob * (prob_grad - delta)).astype(bf16)
    dq = product(score_grad, key) * scale
    first = turn_first(dq[:, :128], q_cos_ref[...], -q_sin_ref[...])
    rows_ref[own, 1, :, :128] = first.astype(bf16).reshape(shape + (128,))
    rows_ref[own, 1, :, 128:] = dq[:, 128:].astype(bf16).reshape(shape + (HEAD - 128,))
    dk_sum[...] += t_times(score_grad, query)
    dv_sum[...] += t_times(prob_low, grad)

    @pl.when(step == pl.num_programs(0) - 1)
    def _():
        base = 2 if joint else 0
        shape = keys_ref.shape[:1] + keys_ref.shape[2:3]
        dk = dk_sum[...] * scale
        first = turn_first(dk[:, :128], k_cos_ref[...], -k_sin_ref[...])
        keys_ref[:, base, :, :128] = first.astype(bf16).reshape(shape + (128,))
        keys_ref[:, base, :, 128:] = dk[:, 128:].astype(bf16).reshape(shape + (HEAD - 128,))
        keys_ref[:, base + 1] = dv_sum[...].astype(bf16).reshape(shape + (HEAD,))


def attend(query, key, value, grad, begin, place, key_place, q_tables, k_tables, block):
    rows = query.shape[0]
    keys = key.shape[0]
    part = min(256, rows)
    joint = rows == keys
    by_rows = lambda i: (i, 0)
    all_rows = lambda i: (0, 0)
    fixed = lambda i: (0, 0, 0, 0)
    if joint:
        shapes = [(keys // block, 4, block, HEAD)]
        out_specs = [pl.BlockSpec(shapes[0], fixed)]
    else:
        shapes = [(rows // block, 2, block, HEAD), (keys // block, 2, block, HEAD)]
        out_specs = [
            pl.BlockSpec((part // block, 2, block, HEAD), lambda i: (i, 0, 0, 0)),
            pl.BlockSpec(shapes[1], fixed),
        ]
    return pl.pallas_call(
        functools.partial(attention_kernel, joint),
        grid=(rows // part,),
        in_specs=[
            pl.BlockSpec((part, HEAD), by_rows),
            pl.BlockSpec((keys, HEAD), all_rows),
            pl.BlockSpec((keys, HEAD), all_rows),
            pl.BlockSpec((part, HEAD), by_rows),
            pl.BlockSpec((part, 1), by_rows),
            pl.BlockSpec((part, 1), by_rows),
            pl.BlockSpec((1, keys), all_rows),
            pl.BlockSpec((part, 128), by_rows),
            pl.BlockSpec((part, 128), by_rows),
            pl.BlockSpec((keys, 128), all_rows),
            pl.BlockSpec((keys, 128), all_rows),
        ],
        out_specs=out_specs,
        out_shape=[jax.ShapeDtypeStruct(shape, bf16) for shape in shapes],
        scratch_shapes=[pltpu.VMEM((keys, HEAD), f32), pltpu.VMEM((keys, HEAD), f32)],
        compiler_params=pltpu.CompilerParams(vmem_limit_bytes=VMEM_BYTES),
        cost_estimate=pl.CostEstimate(
            flops=14 * rows * keys * HEAD,
            bytes_accessed=16 * keys * HEAD,
            transcendentals=rows * keys,
        ),
    )(query, key, value, grad, begin, place, key_place, *q_tables, *k_tables)


def body(
    contexts,
    tokens,
    cotangent,
    deal,
    doc_lengths,
    doc_adapter,
    ln1_gain,
    ln1_bias,
    ln2_gain,
    ln2_bias,
    qkv_weight,
    qkv_bias,
    dense_weight,
    dense_bias,
    in_weight,
    in_bias,
    out_weight,
    out_bias,
    qkv_down,
    qkv_up,
    dense_down,
    dense_up,
    in_down,
    in_up,
    out_down,
    out_up,
):
    rows = tokens.shape[1]
    width = tokens.shape[2]
    wa = lax.axis_index("wa")
    ctx = lax.axis_index("ctx")
    total = WA * rows
    own_width = width // WA
    hidden_width = in_weight.shape[1] // WA
    part_cols = ADAPT_COLS // WA
    groups = contexts // PAIRS
    half = own_width // 2
    relative = [wa, wa ^ 1, wa ^ 2, wa ^ 3]
    index = jnp.stack(relative + [ctx % 2]).astype(jnp.int32)

    def columns(value, which, size):
        return lax.dynamic_slice_in_dim(value, which * size, size, axis=1)

    def part_rows(value, which, size):
        return lax.dynamic_slice_in_dim(value, which * size, size, axis=0)

    def swap_y(value):
        return lax.ppermute(value, "ctx", [(i, i ^ 1) for i in range(contexts)])

    def gather(value, peer=None):
        peer = swap(value, 2) if peer is None else peer
        return [value, swap(value, 1), peer, swap(peer, 1)]

    value_cuts = cut_columns(index, qkv_weight, own_width, [2], [(2, True), (3, True)])
    limit = 64
    numbers = jnp.concatenate(
        [doc_lengths // limit, doc_lengths % limit, doc_adapter], axis=1
    ).astype(bf16)
    numbers = jnp.pad(numbers, ((0, 15), (0, 128 - numbers.shape[1])))
    first_pack = pack_small(index, [tokens[0], qkv_down], qkv_up, [0, 1, 2], numbers)

    def cross(value, *earlier):
        peer = swap(after(value[0], *earlier), 2)
        far = swap(after(value[1], *earlier), 3)
        return [peer, swap_y(peer), far, swap_y(far)]

    def hand_on(away, near, *earlier):
        peer = swap(after(away, *earlier), 2)
        return [swap(near, 1), peer, swap(peer, 1)]

    first_packs = hand_on(*first_pack)
    value_halves = cross(value_cuts)
    mate_cuts = cut_columns(index, qkv_weight, own_width, [0, 1, 2], [(1, False)])[0]
    key_cuts = cut_columns(index, qkv_weight, own_width, [1], [(2, True), (3, True)])
    query_cuts = cut_columns(index, qkv_weight, own_width, [0], [(2, True), (3, True)])
    in_cuts = cut_columns(
        index, in_weight, hidden_width, [0], [(2, True), (3, True), (1, False)], 4
    )
    feed_pack = pack_small(index, [in_down], in_up, [0], numbers)
    value_there = (value_halves[0], value_halves[2])
    mate_weights = swap(mate_cuts, 1)
    grad_pack = jnp.concatenate([cotangent[0], dense_up, out_up], axis=0)
    grad_packs = hand_on(grad_pack, grad_pack, *value_there)
    key_halves = cross(key_cuts, *value_there)
    key_there = (key_halves[0], key_halves[2])
    query_halves = cross(query_cuts, grad_packs[1])
    query_there = (query_halves[0], query_halves[2])
    in_mate = swap(after(in_cuts[2], mate_weights), 1)
    in_peer = swap(after(in_cuts[0], *key_there), 2)
    in_far = swap(after(in_cuts[1], *query_there), 3)
    in_halves = [in_peer, swap_y(in_peer), in_far, swap_y(in_far)]
    feed_packs = hand_on(*feed_pack, in_peer)

    docs_per_pack = doc_lengths.shape[1]
    tables = [numbers] + [item[-16:] for item in first_packs]
    tables = jnp.stack(absolute([item[0] for item in tables], wa)).astype(jnp.int32)
    lengths = tables[:, :docs_per_pack] * limit + tables[:, docs_per_pack : 2 * docs_per_pack]
    adapters = tables[:, 2 * docs_per_pack : 3 * docs_per_pack]
    starts = jnp.cumsum(lengths, axis=1) - lengths

    def places(first, size):
        slots = first + jnp.arange(size, dtype=jnp.int32)
        blocks = slots // BLOCK
        table = jnp.arange(deal.shape[0], dtype=jnp.int32)
        block = jnp.sum(jnp.where(table[None, :] == blocks[:, None], deal[None, :], 0), axis=1)
        return block * BLOCK + slots % BLOCK

    place = places(ctx * rows, rows)
    inside = starts[:, None, :] <= place[None, :, None]
    docs = jnp.sum(inside.astype(jnp.int32), axis=2) - 1
    begin = jnp.max(jnp.where(inside, starts[:, None, :], 0), axis=2)
    offset = (place[None, :] - begin).reshape(total)
    doc_table = jnp.arange(docs_per_pack, dtype=jnp.int32)
    chosen = jnp.sum(
        jnp.where(docs[:, :, None] == doc_table, adapters[:, None, :], 0), axis=2
    ).reshape(total)
    adapter_of = jnp.arange(ADAPT_COLS, dtype=jnp.int32) // RANK
    mask = (adapter_of[None, :] == chosen[:, None]).astype(f32)
    cosine, sine = rotary_tables(offset)

    gains = [item[None, :] for item in (ln1_gain, ln1_bias, ln2_gain, ln2_bias)]
    first_norm, second_norm, first_inner = call(
        front_kernel,
        index,
        [whole(after(tokens[0], *value_there, *key_cuts, *query_cuts, *in_cuts, *feed_pack))]
        + [whole(item) for item in [qkv_down] + first_packs + [mask] + gains],
        [
            ((total, width), bf16, None, None),
            ((total, width), bf16, None, None),
            ((total, ADAPT_COLS), bf16, None, None),
        ],
        flops=2 * total * width * ADAPT_COLS,
    )

    strip = strip_rows = part_cols * HEAD // 128
    ups_row = (tokens.size + qkv_down.size) // 128
    ups_size = 3 * own_width * part_cols // 128

    def project(kind, halves, turned):
        own_block = lambda head, ref: (0, (kind * WA + ref[0]) * 2 + head)
        items = [whole(first_norm), (qkv_weight, (own_width, HEAD), own_block)]
        items.append((mate_weights, (1, own_width, HEAD), lambda head, ref: (kind, 0, head)))
        items += [
            (item, (1, own_width // 2, HEAD), lambda head, ref: (0, 0, head)) for item in halves
        ]
        items.append((qkv_up, (part_cols, HEAD), own_block))
        for r, item in zip((1, 2, 3), first_packs):
            row = (ups_row + (r == 3) * ups_size) // strip + kind * 2
            items.append((item, (strip, 128), lambda head, ref, row=row: (row + head, 0)))
        items += [
            whole(first_inner),
            (qkv_bias[None, :], (1, HEAD), own_block),
            whole(cosine),
            whole(sine),
        ]
        out = call(
            functools.partial(qkv_kernel, turned),
            index,
            items,
            [
                (
                    (WA, 2, rows, HEAD),
                    bf16,
                    (WA, 1, rows, HEAD),
                    lambda head, ref: (0, head, 0, 0),
                )
            ],
            grid=(2,),
            scratch=[pltpu.VMEM((ADAPT_COLS, HEAD), bf16)],
            flops=2 * total * width * own_width,
        )[0]
        return out.reshape(PAIRS, rows, HEAD)

    def to_pairs(item):
        if groups == 1:
            return lax.all_to_all(item, "ctx", 0, 0, tiled=True)
        names = [[g * PAIRS + j for j in range(PAIRS)] for g in range(groups)]
        return lax.all_to_all(item, "ctx", 0, 0, axis_index_groups=names, tiled=True)

    value_halves[1] = after(value_halves[1], *grad_packs)
    value = to_pairs(project(2, value_halves, False))

    grad_own = after(grad_pack, *key_there, value_halves[1])
    grad, dense_inner_grad, out_inner_grad, attended_grad, all_ups = call(
        grad_kernel,
        index,
        [
            whole(item)
            for item in [grad_own] + grad_packs + [mask, dense_weight, dense_down]
        ],
        [
            ((total, width), bf16, None, None),
            ((total, ADAPT_COLS), bf16, None, None),
            ((total, ADAPT_COLS), bf16, None, None),
            ((WA, 2, rows, HEAD), bf16, None, None),
            ((2, ADAPT_COLS, width), bf16, None, None),
        ],
        scratch=[pltpu.VMEM((ADAPT_COLS, width), bf16), pltpu.VMEM((ADAPT_COLS, width), bf16)],
        flops=2 * total * width * (own_width + 2 * ADAPT_COLS),
    )
    attended_grad = to_pairs(after(attended_grad, value).reshape(PAIRS, rows, HEAD))
    key_halves[1] = after(key_halves[1], *query_there)
    key = to_pairs(after(project(1, key_halves, True), attended_grad))
    query_halves[1] = after(query_halves[1], in_peer)
    query = to_pairs(after(project(0, query_halves, True), key))

    pair_rows = PAIRS * rows
    group = ctx // PAIRS
    own_pack = (ctx % PAIRS) // 2
    own_starts = jnp.sum(
        jnp.where(jnp.arange(WA)[:, None] == own_pack, starts, 0), axis=0
    )
    all_places = places(0, groups * pair_rows)
    all_inside = own_starts[None, :] <= all_places[:, None]
    all_begins = jnp.max(jnp.where(all_inside, own_starts[None, :], 0), axis=1)
    k_tables = rotary_tables(all_places - all_begins)
    if groups == 1:
        q_place, q_begin, q_tables = all_places, all_begins, k_tables
    else:
        q_place = part_rows(all_places, group, pair_rows)
        q_begin = part_rows(all_begins, group, pair_rows)
        q_tables = [part_rows(item, group, pair_rows) for item in k_tables]
    query, key, value, attended_grad = [
        item.reshape(pair_rows, HEAD) for item in (query, key, value, attended_grad)
    ]
    sets = [[g * PAIRS + j for g in range(groups)] for j in range(PAIRS)]
    if groups > 1:
        key, value = [
            lax.all_gather(item, "ctx", axis=0, axis_index_groups=sets, tiled=True)
            for item in (key, value)
        ]
    both = attend(
        after(query, in_far, in_halves[1], feed_packs[2]),
        key,
        value,
        attended_grad,
        q_begin[:, None],
        q_place[:, None],
        all_places[None, :],
        q_tables,
        k_tables,
        rows,
    )
    if groups > 1:
        dkv = lax.psum_scatter(
            both[1], "ctx", scatter_dimension=0, axis_index_groups=sets, tiled=True
        )
        both = [jnp.concatenate([both[0], dkv], axis=1)]
    both = to_pairs(after(both[0], in_halves[3])).reshape(WA, 2, 4, rows, HEAD)
    odq, dkv = both, both

    tile = min(512, hidden_width)
    tiles = hidden_width // tile
    own_tile = lambda t, ref: (0, ref[0] * tiles + t)
    items = [whole(second_norm), whole(grad), (in_weight, (own_width, tile), own_tile)]
    items += [
        (item, (1, item.shape[1], tile), lambda t, ref: (0, 0, t)) for item in [in_mate] + in_halves
    ]
    items += [(in_up, (part_cols, tile), own_tile)]
    strip = part_cols * tile // 128
    for r, item in zip((1, 2, 3), feed_packs):
        row = (own_width + (r == 3) * part_cols * hidden_width // 128) // strip
        items.append((item, (strip, 128), lambda t, ref, row=row: (row + t, 0)))
    in_downs = [whole(in_down)] + [
        (item, (own_width, ADAPT_COLS), lambda *_: (0, 0)) for item in feed_packs
    ]
    items += in_downs + [whole(mask)]
    items += [
        (in_bias[None, :], (1, tile), own_tile),
        whole(gains[2]),
        (out_weight, (tile, width), lambda t, ref: (t, 0)),
        (out_down, (tile, ADAPT_COLS), lambda t, ref: (t, 0)),
        whole(out_inner_grad),
    ]
    (
        branch_sum,
        norm_grad,
        out_inner,
        second_inner_grad,
        out_down_grad,
        in_up_grad,
        second_inner,
    ) = call(
        feed_kernel,
        index,
        items,
        [
            ((total, width), f32, None, None),
            ((total, width), f32, None, None),
            ((total, ADAPT_COLS), f32, None, None),
            ((total, ADAPT_COLS), f32, None, None),
            ((hidden_width, ADAPT_COLS), bf16, (tile, ADAPT_COLS), lambda t, ref: (t, 0)),
            ((ADAPT_COLS, hidden_width), bf16, (ADAPT_COLS, tile), lambda t, ref: (0, t)),
            ((total, ADAPT_COLS), bf16, None, None),
        ],
        grid=(tiles,),
        scratch=[pltpu.VMEM((ADAPT_COLS, tile), bf16)],
        flops=8 * total * width * hidden_width,
    )

    def sum_inner(partial):
        partial = (partial + swap(partial, 1)).astype(bf16)
        partial = partial.astype(f32) + swap(partial, 2).astype(f32)
        return (partial * mask).astype(bf16)

    def spread_rows(value):
        return [part_rows(value, wa, part_cols)] + [
            swap(part_rows(value, wa ^ r, part_cols), r) for r in (1, 2, 3)
        ]

    def own_columns(left, right):
        return t_times(columns(left, wa, left.shape[1] // WA), right).astype(bf16)

    out_inner = sum_inner(out_inner)
    second_inner_grad = sum_inner(second_inner_grad)
    feed_grads = lax.psum([out_down_grad, in_up_grad], "ctx")

    dense_items = [odq, branch_sum, dense_weight, dense_down, dense_inner_grad]
    reduced = [
        ((2, rows, width), f32, None, None),
        ((2, rows, width), bf16, None, None),
    ]
    keep, send, dense_inner, dense_down_grad = call(
        dense_kernel,
        index,
        [whole(item) for item in dense_items],
        reduced
        + [
            ((total, ADAPT_COLS), f32, None, None),
            ((own_width, ADAPT_COLS), bf16, None, None),
        ],
        scratch=[pltpu.VMEM((total, width), f32)],
        flops=2 * total * width * own_width,
    )
    dense_inner = sum_inner(dense_inner)
    near = swap(send, 1)
    away = swap((keep[1] + near[1].astype(f32)).astype(bf16), 2)
    output = (
        keep[0]
        + near[0].astype(f32)
        + away.astype(f32)
        + product(part_rows(dense_inner, wa, rows), all_ups[0])
        + product(part_rows(out_inner, wa, rows), all_ups[1])
        + dense_bias
        + out_bias
        + tokens[0].astype(f32)
    ).astype(bf16)[None]

    mixed_grads = [odq, dkv]
    up_items = []
    for kind in range(3):
        up_items.append(
            (qkv_up, (part_cols, own_width), lambda _, ref, kind=kind: (0, kind * WA + ref[0]))
        )
        for r, item in zip((1, 2, 3), first_packs):
            row = (ups_row + (r == 3) * ups_size) // (2 * strip_rows) + kind
            up_items.append(
                (item, (2 * strip_rows, 128), lambda _, ref, row=row: (row, 0))
            )
    first_inner_grad, qkv_up_grad = call(
        mix_kernel,
        index,
        [whole(item) for item in mixed_grads] + up_items + [whole(first_inner)],
        [
            ((total, ADAPT_COLS), f32, None, None),
            ((ADAPT_COLS, 3 * own_width), bf16, None, None),
        ],
        scratch=[pltpu.VMEM((3, ADAPT_COLS, own_width), bf16)],
        flops=4 * total * ADAPT_COLS * 3 * own_width,
    )
    first_inner_grad = sum_inner(first_inner_grad)
    weight_items = []
    for kind, halves in ((0, query_halves), (1, key_halves), (2, value_halves)):
        weight_items.append(
            (
                qkv_weight,
                (own_width, own_width),
                lambda _, ref, kind=kind: (0, kind * WA + ref[0]),
            )
        )
        weight_items.append(
            (mate_weights, (1, own_width, own_width), lambda _, ref, kind=kind: (kind, 0, 0))
        )
        weight_items += [whole(item) for item in halves]
    keep, send = call(
        norm_grad_kernel,
        index,
        [whole(item) for item in mixed_grads]
        + weight_items
        + [whole(gains[0]), whole(norm_grad)],
        reduced,
        scratch=[pltpu.VMEM((total, width), f32)],
        flops=2 * total * width * 3 * own_width,
    )
    near = swap(send, 1)
    combined = (keep[1] + near[1].astype(f32)).astype(bf16)
    away = swap(combined, 2)
    down_at = rows * width // 128 // own_width
    down_block = lambda *_: (down_at, 0)
    tokens_grad = call(
        finish_kernel,
        index,
        [
            whole(item)
            for item in [
                keep,
                near,
                away,
                part_rows(first_inner_grad, wa, rows),
                part_rows(second_inner_grad, wa, rows),
            ]
        ]
        + [whole(qkv_down)]
        + [(item, (own_width, ADAPT_COLS), down_block) for item in first_packs]
        + in_downs
        + [whole(item) for item in [gains[0], gains[2], tokens[0], cotangent[0]]],
        [((rows, width), f32, None, None)],
        scratch=[pltpu.VMEM((rows, width), f32)],
    )[0][None]

    attention_grads = [
        dense_down_grad,
        own_columns(dense_inner, grad),
        own_columns(first_norm, first_inner_grad),
        own_columns(out_inner, grad),
        own_columns(second_norm, second_inner_grad),
    ] + spread_rows(qkv_up_grad)
    feed_grads = [after(item, *attention_grads, combined, output) for item in feed_grads]
    out_down_grad, in_up_grad = feed_grads
    in_up_parts = spread_rows(in_up_grad)
    attention_grads = [after(item, *feed_grads) for item in attention_grads]
    attention_grads = lax.psum(attention_grads, "ctx")
    out_down_grad = out_down_grad.astype(f32)
    dense_down_grad, dense_up_grad, qkv_down_grad, out_up_grad, in_down_grad = [
        item.astype(f32) for item in attention_grads[:5]
    ]
    in_up_grad = jnp.concatenate(absolute(in_up_parts, wa), axis=1).astype(f32)
    qkv_parts = absolute(attention_grads[5:], wa)
    qkv_up_grad = jnp.concatenate(
        [
            part[:, kind * own_width : (kind + 1) * own_width]
            for kind in range(3)
            for part in qkv_parts
        ],
        axis=1,
    ).astype(f32)
    return (
        output,
        tokens_grad,
        qkv_down_grad,
        qkv_up_grad,
        dense_down_grad,
        dense_up_grad,
        in_down_grad,
        in_up_grad,
        out_down_grad,
        out_up_grad,
    )


def solution(mesh):
    rows = P("wa", "ctx", None)
    shard = P("wa", None)
    in_specs = (
        (rows, rows, P(), shard, shard)
        + (P(),) * 4
        + (shard, P()) * 4
        + (shard,) * 8
    )
    out_specs = (rows, rows) + (shard,) * 8
    return jax.shard_map(
        functools.partial(body, mesh.shape["ctx"]),
        mesh=mesh,
        in_specs=in_specs,
        out_specs=out_specs,
        check_vma=False,
    )
```

time: 599 us -> 454 us (0.76)
  matrix products: 135 us -> 8.14 us
  Pallas kernels: 16.9 us -> 126 us
  local copies, waits for them, and re-layouts: 74.5 us -> 13.3 us
  other arithmetic: 47.1 us -> 25.3 us
  waiting for transfers between devices: 227 us -> 207 us
  blocking collectives: 10.7 us -> 0 us
  starting transfers between devices: 65.5 us -> 57.9 us
    pallas_call x3 -> x18, Pallas kernels: 16.9 us -> 126 us  [the longest x17 116 us: call(): pl.pallas_call(kernel, grid_spec=pltpu.PrefetchScalarGridSpec(num_scalar_...]
    dot_general x26 -> x2, matrix products: 73.9 us -> 1.44 us  [product(): return jnp.dot(left, right, preferred_element_type=f32)]
    dot_general x21 -> x0, matrix products: 53.2 us -> none  [the longest x13 43.7 us: times_t(): lax.dot_general(left, right, (((1,), (1,)), ((), ())), preferred_element_...]
    ppermute x41 -> x37, waiting for transfers between devices: 126 us -> 74.3 us  [swap(): return lax.ppermute(value, 'wa', [(i, i ^ bits) for i in range(WA)])]
    ppermute x0 -> x8, waiting for transfers between devices: none -> 39 us  [swap_y(): return lax.ppermute(value, 'ctx', [(i, i ^ 1) for i in range(contexts)])]
    unnamed x178 -> x115, local copies, waits for them, and re-layouts: 23.1 us -> 6.55 us
    all_to_all x8 -> x5, starting transfers between devices: 40.5 us -> 24 us  [to_pairs(): return lax.all_to_all(item, 'ctx', 0, 0, tiled=True)]
    dynamic_slice x11 -> x6, local copies, waits for them, and re-layouts: 17.3 us -> 4.79 us  [the longest x4 3.04 us: part_rows(): return lax.dynamic_slice_in_dim(value, which * size, size, axis=0)]
  transfers between devices with their start and end apart: 50 -> 52, of which waited for: 18 -> 22; matrix products, arithmetic and copies ran while one was open for 41% -> 7% of each run, Pallas kernels for 3% -> 26%
where the time goes in v2:
time: 454 us; the launch traced here: 452 us
  waiting for transfers between devices  207 us (46%)
  Pallas kernels  126 us (28%)
  starting transfers between devices  57.9 us (13%)
  other arithmetic  25.3 us (6%)
  between operations  14.8 us (3%)
  local copies, waits for them, and re-layouts  13.3 us (3%)
  matrix products  8.14 us (2%)
    pallas_call x17, Pallas kernels, call(): pl.pallas_call(kernel, grid_spec=pltpu.PrefetchScalarGridSpec(num_scalar_...  116 us
    ppermute x37, waiting for transfers between devices, swap(): return lax.ppermute(value, 'wa', [(i, i ^ bits) for i in range(WA)])  74.3 us
    psum x1, waiting for transfers between devices, body(): attention_grads = lax.psum(attention_grads, 'ctx')  72.4 us
    ppermute x8, waiting for transfers between devices, swap_y(): return lax.ppermute(value, 'ctx', [(i, i ^ 1) for i in range(contexts)])  39 us
    all_to_all x5, starting transfers between devices, to_pairs(): return lax.all_to_all(item, 'ctx', 0, 0, tiled=True)  24 us
    ppermute x37, starting transfers between devices, swap(): return lax.ppermute(value, 'wa', [(i, i ^ bits) for i in range(WA)])  23.3 us
    all_to_all x5, waiting for transfers between devices, to_pairs(): return lax.all_to_all(item, 'ctx', 0, 0, tiled=True)  12.9 us
    ppermute x8, starting transfers between devices, swap_y(): return lax.ppermute(value, 'ctx', [(i, i ^ 1) for i in range(contexts)])  10.3 us
  transfers between devices with their start and end apart: 52, of which 22 were waited for; matrix products, arithmetic and copies ran while one was open for 7% of the time, Pallas kernels for 26%

profile of v2, /device:TPU:0, one launch (start us, length us, event | category | flops | bytes accessed | tf_op | source)
XLA Modules:
  0.0 452.2 jit_solution(10817523598945594362)
XLA Ops:
  12.1 3.3 shard_map.317
  15.5 3.0 collective-permute-start.3
  18.5 2.5 shard_map.312
  22.8 1.2 collective-permute-start.17
  24.1 14.5 %collective-permute-done.3.refs_3_.refs_8_.refs_4_.refs_12_.refs_7_ = bf16[3344,128]{1,0:T(8,128)(2,1)S(1)} collective-permute-done((bf16[3344,128]{1,0:T(8,128)(2,1)}, bf16[3344,128]{1,0:T(8,128)(2,1)S(1)}, u32[]{:S(2)}, u32[]{:S(2)}) %collective-permute-start.3) | collective-permute-done | bytes 856096 | tf_op jit(solution)/shard_map/ppermute | solution.py:40
  39.4 2.5 shard_map.313
  41.9 2.5 shard_map.314
  44.4 4.1 shard_map.319
  48.5 5.6 %shard_map.315 = (bf16[1,256,2048]{2,1,0:T(8,128)(2,1)}, bf16[1,256,2048]{2,1,0:T(8,128)(2,1)}, bf16[1,512,2048]{2,1,0:T(8,128)(2,1)}) custom-call(s32[5]{0:T(128)} %stack.30.index_ref, bf16[512,8192]{1,0:T(8,128)(2,1)} %refs_0_.19, bf16[512,8192]{1,0:T(8,128)(2,1)} %refs_0_.19, bf16[512,8192]{1,0:T(8,128)(2,1)} %refs_0_.19), custom_call_target="tpu_custom_call" | custom-call | bytes 4194304 | tf_op jit(solution)/shard_map/pallas_call | solution.py:91
  54.0 2.8 shard_map.316
  57.3 2.1 collective-permute-start.6
  59.5 1.6 collective-permute-start.16
  61.1 16.4 %collective-permute-done.6.refs_2_ = bf16[192,2048]{1,0:T(8,128)(2,1)} collective-permute-done((bf16[192,2048]{1,0:T(8,128)(2,1)}, bf16[192,2048]{1,0:T(8,128)(2,1)}, u32[]{:S(2)}, u32[]{:S(2)}) %collective-permute-start.6) | collective-permute-done | bytes 786464 | tf_op jit(solution)/shard_map/ppermute | solution.py:40
  77.5 1.8 collective-permute-start.19
  81.4 6.9 %shard_map.318 = (bf16[512,2048]{1,0:T(8,128)(2,1)}, bf16[512,2048]{1,0:T(8,128)(2,1)}, bf16[512,128]{1,0:T(8,128)(2,1)}) custom-call(s32[5]{0:T(128)} %stack.30.index_ref, bf16[128,2048]{1,0:T(8,128)(2,1)} %bitcast.56, bf16[512,128]{1,0:T(8,128)(2,1)} %refs_5_.3, bf16[3344,128]{1,0:T(8,128)(2,1)} %collective-permute-done.2.refs_2_.refs_7_.refs_3_.refs_11_.refs_6_, ...), custom_call_target="tpu_custom_call" | custom-call | flops 268435456 | bytes 3518464 | tf_op jit(solution)/shard_map/pallas_call | solution.py:91
  88.3 1.9 fusion.18
  91.5 5.4 %shard_map.323 = bf16[4,2,128,256]{3,2,1,0:T(8,128)(2,1)} custom-call(s32[5]{0:T(128)} %stack.30.index_ref, bf16[512,2048]{1,0:T(8,128)(2,1)} %get-tuple-element.89.hidden_ref, bf16[512,6144]{1,0:T(8,128)(2,1)} %refs_14_.1, bf16[3,512,512]{2,1,0:T(8,128)(2,1)} %copy-done.1, bf16[1,256,512]{2,1,0:T(8,128)(2,1)} %copy-done.9, bf16[1,256,512]{2,1,0:T(8,128)(2,1)} %copy-done.11, ...), custom_call_target="tpu_custom_call" | custom-call | flops 1073741824 | bytes 4981760 | tf_op jit(solution)/shard_map/pallas_call | solution.py:91
  96.9 4.9 %all-to-all-start = ((bf16[8,128,256]{2,1,0:T(8,128)(2,1)}), bf16[8,128,256]{2,1,0:T(8,128)(2,1)S(1)}, u32[]{:S(2)}, u32[]{:S(2)}) async-start(bf16[8,128,256]{2,1,0:T(8,128)(2,1)} %bitcast.62), calls=%async_computation | async-start | bytes 1048576 | tf_op jit(solution)/shard_map/all_to_all | solution.py:754
  101.8 1.4 collective-permute-start.10
  103.7 6.6 %collective-permute-done.10.refs_4_.refs_12_ = bf16[1,256,512]{2,1,0:T(8,128)(2,1)S(1)} collective-permute-done((bf16[1,256,512]{2,1,0:T(8,128)(2,1)}, bf16[1,256,512]{2,1,0:T(8,128)(2,1)S(1)}, u32[]{:S(2)}, u32[]{:S(2)}) %collective-permute-start.10) | collective-permute-done | bytes 262176 | tf_op jit(solution)/shard_map/ppermute | solution.py:40
  110.4 6.0 %collective-permute-done.9.refs_2_.refs_10_ = bf16[1,256,512]{2,1,0:T(8,128)(2,1)S(1)} collective-permute-done((bf16[1,256,512]{2,1,0:T(8,128)(2,1)S(1)}, bf16[1,256,512]{2,1,0:T(8,128)(2,1)S(1)}, u32[]{:S(2)}, u32[]{:S(2)}) %collective-permute-start.9) | collective-permute-done | bytes 262176 | tf_op jit(solution)/shard_map/ppermute | solution.py:40
  116.3 7.0 %shard_map.322 = (bf16[512,2048]{1,0:T(8,128)(2,1)}, bf16[512,128]{1,0:T(8,128)(2,1)}, bf16[512,128]{1,0:T(8,128)(2,1)}, bf16[4,2,128,256]{3,2,1,0:T(8,128)(2,1)}, bf16[2,128,2048]{2,1,0:T(8,128)(2,1)}) custom-call(s32[5]{0:T(128)} %stack.30.index_ref, bf16[192,2048]{1,0:T(8,128)(2,1)} %pad_maximum_fusion.refs_0_, ...), custom_call_target="tpu_custom_call" | custom-call | flops 1610612736 | bytes 5636096 | tf_op jit(solution)/shard_map/pallas_call | solution.py:91
  123.3 5.9 %all-to-all-start.1 = ((bf16[8,128,256]{2,1,0:T(8,128)(2,1)}), bf16[8,128,256]{2,1,0:T(8,128)(2,1)S(1)}, u32[]{:S(2)}, u32[]{:S(2)}) async-start(bf16[8,128,256]{2,1,0:T(8,128)(2,1)} %bitcast.67), calls=%async_computation.1 | async-start | bytes 1048576 | tf_op jit(solution)/shard_map/all_to_all | solution.py:754
  129.3 2.0 collective-permute-start.14
  131.5 1.3 collective-permute-start.7
  133.9 10.4 %collective-permute-done.14.refs_3_.refs_11_ = bf16[1,256,512]{2,1,0:T(8,128)(2,1)S(1)} collective-permute-done((bf16[1,256,512]{2,1,0:T(8,128)(2,1)S(1)}, bf16[1,256,512]{2,1,0:T(8,128)(2,1)S(1)}, u32[]{:S(2)}, u32[]{:S(2)}) %collective-permute-start.14) | collective-permute-done | bytes 262176 | tf_op jit(solution)/shard_map/ppermute | solution.py:626
  144.3 1.3 collective-permute-done.7.refs_2_.refs_4_
  145.6 3.0 collective-permute-done.15.refs_5_.refs_13_
  149.3 5.4 %shard_map.321 = bf16[4,2,128,256]{3,2,1,0:T(8,128)(2,1)} custom-call(s32[5]{0:T(128)} %stack.30.index_ref, bf16[512,2048]{1,0:T(8,128)(2,1)} %get-tuple-element.89.hidden_ref, bf16[512,6144]{1,0:T(8,128)(2,1)} %refs_14_.1, bf16[3,512,512]{2,1,0:T(8,128)(2,1)} %copy-done.1, bf16[1,256,512]{2,1,0:T(8,128)(2,1)} %copy-done.14, ...), custom_call_target="tpu_custom_call" | custom-call | flops 1073741824 | bytes 4981760 | tf_op jit(solution)/shard_map/pallas_call | solution.py:91
  154.7 4.6 %all-to-all-start.2 = ((bf16[8,128,256]{2,1,0:T(8,128)(2,1)}), bf16[8,128,256]{2,1,0:T(8,128)(2,1)S(1)}, u32[]{:S(2)}, u32[]{:S(2)}) async-start(bf16[8,128,256]{2,1,0:T(8,128)(2,1)} %bitcast.60), calls=%async_computation.2 | async-start | bytes 1048576 | tf_op jit(solution)/shard_map/all_to_all | solution.py:754
  160.0 1.7 collective-permute-start.8
  162.2 6.0 %collective-permute-done.11.refs_2_ = bf16[1,256,2048]{2,1,0:T(8,128)(2,1)} collective-permute-done((bf16[1,256,2048]{2,1,0:T(8,128)(2,1)}, bf16[1,256,2048]{2,1,0:T(8,128)(2,1)}, u32[]{:S(2)}, u32[]{:S(2)}) %collective-permute-start.11) | collective-permute-done | bytes 1048608 | tf_op jit(solution)/shard_map/ppermute | solution.py:40
  169.0 5.0 %collective-permute-done.8.refs_3_.refs_5_ = bf16[1,256,512]{2,1,0:T(8,128)(2,1)S(1)} collective-permute-done((bf16[1,256,512]{2,1,0:T(8,128)(2,1)S(1)}, bf16[1,256,512]{2,1,0:T(8,128)(2,1)S(1)}, u32[]{:S(2)}, u32[]{:S(2)}) %collective-permute-start.8) | collective-permute-done | bytes 262176 | tf_op jit(solution)/shard_map/ppermute | solution.py:626
  174.1 5.5 %collective-permute-done.13.refs_5_.refs_7_ = bf16[1,256,512]{2,1,0:T(8,128)(2,1)S(1)} collective-permute-done((bf16[1,256,512]{2,1,0:T(8,128)(2,1)S(1)}, bf16[1,256,512]{2,1,0:T(8,128)(2,1)S(1)}, u32[]{:S(2)}, u32[]{:S(2)}) %collective-permute-start.13) | collective-permute-done | bytes 262176 | tf_op jit(solution)/shard_map/ppermute | solution.py:626
  180.3 5.4 %shard_map.320 = bf16[4,2,128,256]{3,2,1,0:T(8,128)(2,1)} custom-call(s32[5]{0:T(128)} %stack.30.index_ref, bf16[512,2048]{1,0:T(8,128)(2,1)} %get-tuple-element.89.hidden_ref, bf16[512,6144]{1,0:T(8,128)(2,1)} %refs_14_.1, bf16[3,512,512]{2,1,0:T(8,128)(2,1)} %copy-done.1, bf16[1,256,512]{2,1,0:T(8,128)(2,1)} %copy-done.17, ...), custom_call_target="tpu_custom_call" | custom-call | flops 1073741824 | bytes 4981760 | tf_op jit(solution)/shard_map/pallas_call | solution.py:91
  185.7 4.3 all-to-all-start.3
  191.3 2.0 collective-permute-start.24
  194.2 4.8 %collective-permute-done.22.refs_8_.refs_12_.refs_11_ = bf16[1552,128]{1,0:T(8,128)(2,1)S(1)} collective-permute-done((bf16[1552,128]{1,0:T(8,128)(2,1)}, bf16[1552,128]{1,0:T(8,128)(2,1)S(1)}, u32[]{:S(2)}, u32[]{:S(2)}) %collective-permute-start.22) | collective-permute-done | bytes 397344 | tf_op jit(solution)/shard_map/ppermute | solution.py:40
  199.7 3.1 fusion.5
  202.9 3.5 collective-permute-done.21.refs_3_
  206.4 1.3 all-to-all-done.3
  208.5 9.9 %shard_map.324 = bf16[8,4,128,256]{3,2,1,0:T(8,128)(2,1)} custom-call(bf16[1024,256]{1,0:T(8,128)(2,1)} %bitcast.68, bf16[1024,256]{1,0:T(8,128)(2,1)} %bitcast.66, bf16[1024,256]{1,0:T(8,128)(2,1)} %bitcast.64, bf16[1024,256]{1,0:T(8,128)(2,1)} %bitcast.65, s32[1024,1]{1,0:T(8,128)} %copy.38.begin_ref, s32[1024,1]{1,0:T(8,128)} %fusion.6.place_ref, ...), custom_call_target="tpu_custom_call" | custom-call | flops 3758096384 | bytes 4194304 | tf_op jit(solution)/shard_map/pallas_call | solution.py:550
  218.4 11.5 %collective-permute-done.24.refs_5_ = bf16[1,256,2048]{2,1,0:T(8,128)(2,1)} collective-permute-done((bf16[1,256,2048]{2,1,0:T(8,128)(2,1)}, bf16[1,256,2048]{2,1,0:T(8,128)(2,1)}, u32[]{:S(2)}, u32[]{:S(2)}) %collective-permute-start.24) | collective-permute-done | bytes 1048608 | tf_op jit(solution)/shard_map/ppermute | solution.py:626
  229.9 4.3 all-to-all-start.4
  234.4 1.7 collective-permute-done.26.refs_7_.refs_11_.refs_10_
  236.8 33.6 %shard_map.325 = (f32[512,2048]{1,0:T(8,128)}, f32[512,2048]{1,0:T(8,128)}, f32[512,128]{1,0:T(8,128)}, f32[512,128]{1,0:T(8,128)}, bf16[2048,128]{1,0:T(8,128)(...) custom-call(s32[5]{0:T(128)} %stack.30.index_ref, bf16[512,2048]{1,0:T(8,128)(2,1)} %get-tuple-element.109.hidden_ref, ...), custom_call_target="tpu_custom_call" | custom-call | flops 17179869184 | bytes 24129536 | tf_op jit(solution)/shard_map/pallas_call | solution.py:91
  273.2 1.5 collective-permute-start.32
  276.4 11.6 %all-to-all-done.4 = bf16[8,4,128,256]{3,2,1,0:T(8,128)(2,1)S(1)} async-done(((bf16[8,4,128,256]{3,2,1,0:T(8,128)(2,1)}), bf16[8,4,128,256]{3,2,1,0:T(8,128)(2,1)S(1)}, u32[]{:S(2)}, u32[]{:S(2)}) %all-to-all-start.4) | async-done | bytes 2097184 | tf_op jit(solution)/shard_map/all_to_all | solution.py:754
  287.9 1.3 copy-done
  289.2 7.6 %shard_map.326 = (f32[2,128,2048]{2,1,0:T(8,128)}, bf16[2,128,2048]{2,1,0:T(8,128)(2,1)}, f32[512,128]{1,0:T(8,128)}, bf16[512,128]{1,0:T(8,128)(2,1)}) custom-call(s32[5]{0:T(128)} %stack.30.index_ref, bf16[4,2,4,128,256]{4,3,2,1,0:T(8,128)(2,1)} %bitcast.50, f32[512,2048]{1,0:T(8,128)} %get-tuple-element.113.sum_ref, bf16[512,2048]{1,0:T(8,128)(2,1)} %weight_ref.1, ...), custom_call_target="tpu_custom_call" | custom-call | flops 1073741824 | bytes 8650752 | tf_op jit(solution)/shard_map/pallas_call | solution.py:91
  296.8 4.8 %shard_map.328 = (f32[512,128]{1,0:T(8,128)}, bf16[128,1536]{1,0:T(8,128)(2,1)}) custom-call(s32[5]{0:T(128)} %stack.30.index_ref, bf16[4,2,4,128,256]{4,3,2,1,0:T(8,128)(2,1)} %bitcast.51, bf16[4,2,4,128,256]{4,3,2,1,0:T(8,128)(2,1)} %bitcast.52, bf16[32,6144]{1,0:T(8,128)(2,1)} %refs_10_.3, ...), custom_call_target="tpu_custom_call" | custom-call | flops 402653184 | bytes 4718592 | tf_op jit(solution)/shard_map/pallas_call | solution.py:91
  302.1 11.6 %shard_map.327 = (f32[2,128,2048]{2,1,0:T(8,128)}, bf16[2,128,2048]{2,1,0:T(8,128)(2,1)}) custom-call(s32[5]{0:T(128)} %stack.30.index_ref, bf16[4,2,4,128,256]{4,3,2,1,0:T(8,128)(2,1)} %bitcast.53, bf16[4,2,4,128,256]{4,3,2,1,0:T(8,128)(2,1)} %bitcast.54, bf16[512,6144]{1,0:T(8,128)(2,1)} %refs_14_.1, bf16[3,512,512]{2,1,0:T(8,128)(2,1)} %copy-done.1, ...), custom_call_target="tpu_custom_call" | custom-call | flops 3221225472 | bytes 14688256 | tf_op jit(solution)/shard_map/pallas_call | solution.py:91
  314.0 2.1 collective-permute-start.36
  317.2 3.0 collective-permute-done.30
  320.3 2.7 collective-permute-done.36
  323.2 1.2 convolution_convert_fusion
  324.4 2.2 convolution_convert_fusion.2
  329.1 2.0 convolution_convert_fusion.3
  332.4 10.4 %collective-permute-done.28 = bf16[128,2048]{1,0:T(8,128)(2,1)S(1)} collective-permute-done((bf16[128,2048]{1,0:T(8,128)(2,1)S(1)}, bf16[128,2048]{1,0:T(8,128)(2,1)S(1)}, u32[]{:S(2)}, u32[]{:S(2)}) %collective-permute-start.28) | collective-permute-done | bytes 524320 | tf_op jit(solution)/shard_map/ppermute | solution.py:40
  344.3 7.9 %all-reduce.8.cloned.1.call-done = (bf16[2048,128]{1,0:T(8,128)(2,1)}, bf16[128,2048]{1,0:T(8,128)(2,1)}) async-done(((bf16[2048,128]{1,0:T(8,128)(2,1)}, bf16[128,2048]{1,0:T(8,128)(2,1)}), (bf16[2048,128]{1,0:T(8,128)(2,1)}, bf16[128,2048]{1,0:T(8,128)(2,1)})) %all-reduce.8.cloned.1.call-update) | async-done | bytes 1048592 | tf_op jit(solution)/shard_map/psum | solution.py:894
  353.7 1.3 collective-permute-start.43
  356.5 2.1 convert_element_type.207
  359.4 5.6 %shard_map.329 = f32[128,2048]{1,0:T(8,128)} custom-call(s32[5]{0:T(128)} %stack.30.index_ref, f32[2,128,2048]{2,1,0:T(8,128)} %get-tuple-element.121.refs_0_, bf16[2,128,2048]{2,1,0:T(8,128)(2,1)} %copy-done.6, bf16[128,2048]{1,0:T(8,128)(2,1)} %copy-done.22, bf16[128,128]{1,0:T(8,128)(2,1)} %constant_dynamic-slice_fusion.8.refs_3_, ...), custom_call_target="tpu_custom_call" | custom-call | bytes 5849088 | tf_op jit(solution)/shard_map/pallas_call | solution.py:91
  367.1 72.4 %all-reduce.6.cloned.1.call-done = (bf16[512,128]{1,0:T(8,128)(2,1)}, bf16[32,1536]{1,0:T(8,128)(2,1)}, bf16[32,1536]{1,0:T(8,128)(2,1)}, bf16[32,1536]{1,0:T(8,...) async-done(((bf16[512,128]{1,0:T(8,128)(2,1)}, ...) | async-done | bytes 1048592 | tf_op jit(solution)/shard_map/psum | solution.py:1010
  (239 shorter events, 44.8 us)
Async XLA Ops:
  15.5 23.1 %copy-start.31 = (bf16[32,8192]{1,0:T(8,128)(2,1)S(1)}, bf16[32,8192]{1,0:T(8,128)(2,1)}, u32[]{:S(2)}) copy-start(bf16[32,8192]{1,0:T(8,128)(2,1)} %refs_6_.10) | copy-start | bytes 1572868
  15.5 23.1 %collective-permute-start.3 = (bf16[3344,128]{1,0:T(8,128)(2,1)}, bf16[3344,128]{1,0:T(8,128)(2,1)S(1)}, u32[]{:S(2)}, u32[]{:S(2)}) collective-permute-start(bf16[3344,128]{1,0:T(8,128)(2,1)} %get-tuple-element.88), channel_id=1, source_target_pairs={{0,2},{1,3},{2,0},{3,1},{4,6},{5,7},{6,4},{7,5},{8,10},{9,11},{10,... | collective-permute-start | bytes 2568200 | tf_op jit(solution)/shard_map/ppermute | solution.py:40
  21.0 35.8 %collective-permute-start = (bf16[1,256,512]{2,1,0:T(8,128)(2,1)}, bf16[1,256,512]{2,1,0:T(8,128)(2,1)S(1)}, u32[]{:S(2)}, u32[]{:S(2)}) collective-permute-start(bf16[1,256,512]{2,1,0:T(8,128)(2,1)} %get-tuple-element.75), channel_id=1, source_target_pairs={{0,2},{1,3},{2,0},{3,1},{4,6},{5,7},{6,4},{7,5},{8,10},{9,11},{10,... | collective-permute-start | bytes 786440 | tf_op jit(solution)/shard_map/ppermute | solution.py:40
  21.1 36.2 %collective-permute-start.1 = (bf16[1,256,512]{2,1,0:T(8,128)(2,1)}, bf16[1,256,512]{2,1,0:T(8,128)(2,1)S(1)}, u32[]{:S(2)}, u32[]{:S(2)}) collective-permute-start(bf16[1,256,512]{2,1,0:T(8,128)(2,1)} %get-tuple-element.76), channel_id=1, source_target_pairs={{0,3},{1,2},{2,1},{3,0},{4,7},{5,6},{6,5},{7,4},{8,11},{9,10},{10,... | collective-permute-start | bytes 786440 | tf_op jit(solution)/shard_map/ppermute | solution.py:40
  22.8 67.3 %collective-permute-start.17 = (bf16[192,2048]{1,0:T(8,128)(2,1)}, bf16[192,2048]{1,0:T(8,128)(2,1)}, u32[]{:S(2)}, u32[]{:S(2)}) collective-permute-start(bf16[192,2048]{1,0:T(8,128)(2,1)} %pad_maximum_fusion.refs_0_), channel_id=1, source_target_pairs={{0,1},{1,0},{2,3},{3,2},{4,5},{5,4},{6,7},{7,6},{8,9},{9,8},{10,11... | collective-permute-start | bytes 2359304 | tf_op jit(solution)/shard_map/ppermute | solution.py:40
  24.1 35.4 %collective-permute-start.2 = (bf16[3344,128]{1,0:T(8,128)(2,1)}, bf16[3344,128]{1,0:T(8,128)(2,1)}, u32[]{:S(2)}, u32[]{:S(2)}) collective-permute-start(bf16[3344,128]{1,0:T(8,128)(2,1)} %get-tuple-element.87), channel_id=1, source_target_pairs={{0,1},{1,0},{2,3},{3,2},{4,5},{5,4},{6,7},{7,6},{8,9},{9,8},{10,11... | collective-permute-start | bytes 2568200 | tf_op jit(solution)/shard_map/ppermute | solution.py:40
  38.5 40.7 %copy-start.2 = (bf16[3344,128]{1,0:T(8,128)(2,1)}, bf16[3344,128]{1,0:T(8,128)(2,1)S(1)}, u32[]{:S(2)}) copy-start(bf16[3344,128]{1,0:T(8,128)(2,1)S(1)} %collective-permute-done.3.refs_3_.refs_8_.refs_4_.refs_12_.refs_7_) | copy-start | bytes 2568196
  38.5 40.7 %collective-permute-start.4 = (bf16[3344,128]{1,0:T(8,128)(2,1)S(1)}, bf16[3344,128]{1,0:T(8,128)(2,1)}, u32[]{:S(2)}, u32[]{:S(2)}) collective-permute-start(bf16[3344,128]{1,0:T(8,128)(2,1)S(1)} %collective-permute-done.3.refs_3_.refs_8_.refs_4_.refs_12_.refs_7_), channel_id=1, source_target_pairs={{0,1},{1,0},{2,3},{3,2},{4,5},{5,4},{6,7},{7,6},{8,9},{9,8},{10,11... | collective-permute-start | bytes 2568200 | tf_op jit(solution)/shard_map/ppermute | solution.py:40
  56.8 33.3 %copy-start.9 = (bf16[1,256,512]{2,1,0:T(8,128)(2,1)}, bf16[1,256,512]{2,1,0:T(8,128)(2,1)S(1)}, u32[]{:S(2)}) copy-start(bf16[1,256,512]{2,1,0:T(8,128)(2,1)S(1)} %collective-permute-done.refs_2_.refs_16_) | copy-start | bytes 786436
  56.8 33.4 %collective-permute-start.5 = (bf16[3,512,512]{2,1,0:T(8,128)(2,1)}, bf16[3,512,512]{2,1,0:T(8,128)(2,1)S(1)}, u32[]{:S(2)}, u32[]{:S(2)}) collective-permute-start(bf16[3,512,512]{2,1,0:T(8,128)(2,1)} %shard_map.319), channel_id=1, source_target_pairs={{0,1},{1,0},{2,3},{3,2},{4,5},{5,4},{6,7},{7,6},{8,9},{9,8},{10,11... | collective-permute-start | bytes 4718600 | tf_op jit(solution)/shard_map/ppermute | solution.py:40
  57.3 32.9 %copy-start.10 = (bf16[1,256,512]{2,1,0:T(8,128)(2,1)}, bf16[1,256,512]{2,1,0:T(8,128)(2,1)S(1)}, u32[]{:S(2)}) copy-start(bf16[1,256,512]{2,1,0:T(8,128)(2,1)S(1)} %collective-permute-done.1.refs_4_.refs_18_) | copy-start | bytes 786436
  57.3 20.2 %collective-permute-start.6 = (bf16[192,2048]{1,0:T(8,128)(2,1)}, bf16[192,2048]{1,0:T(8,128)(2,1)}, u32[]{:S(2)}, u32[]{:S(2)}) collective-permute-start(bf16[192,2048]{1,0:T(8,128)(2,1)} %pad_maximum_fusion.refs_0_), channel_id=1, source_target_pairs={{0,2},{1,3},{2,0},{3,1},{4,6},{5,7},{6,4},{7,5},{8,10},{9,11},{10,... | collective-permute-start | bytes 2359304 | tf_op jit(solution)/shard_map/ppermute | solution.py:40
  59.5 30.7 %collective-permute-start.16 = (bf16[1,256,512]{2,1,0:T(8,128)(2,1)S(1)}, bf16[1,256,512]{2,1,0:T(8,128)(2,1)S(1)}, u32[]{:S(2)}, u32[]{:S(2)}) collective-permute-start(bf16[1,256,512]{2,1,0:T(8,128)(2,1)S(1)} %collective-permute-done.refs_2_.refs_16_), channel_id=1, source_target_pairs={{0,4},{4,0},{8,12},{12,8},{16,20},{20,16},{24,28},{28,24},{1,5},{5... | collective-permute-start | bytes 786440 | tf_op jit(solution)/shard_map/ppermute | solution.py:626
  77.5 12.7 %collective-permute-start.19 = (bf16[1,256,512]{2,1,0:T(8,128)(2,1)S(1)}, bf16[1,256,512]{2,1,0:T(8,128)(2,1)S(1)}, u32[]{:S(2)}, u32[]{:S(2)}) collective-permute-start(bf16[1,256,512]{2,1,0:T(8,128)(2,1)S(1)} %collective-permute-done.1.refs_4_.refs_18_), channel_id=1, source_target_pairs={{0,4},{4,0},{8,12},{12,8},{16,20},{20,16},{24,28},{28,24},{1,5},{5... | collective-permute-start | bytes 786440 | tf_op jit(solution)/shard_map/ppermute | solution.py:626
  79.2 10.9 %collective-permute-start.18 = (bf16[192,2048]{1,0:T(8,128)(2,1)}, bf16[192,2048]{1,0:T(8,128)(2,1)}, u32[]{:S(2)}, u32[]{:S(2)}) collective-permute-start(bf16[192,2048]{1,0:T(8,128)(2,1)} %collective-permute-done.6.refs_2_), channel_id=1, source_target_pairs={{0,1},{1,0},{2,3},{3,2},{4,5},{5,4},{6,7},{7,6},{8,9},{9,8},{10,11... | collective-permute-start | bytes 2359304 | tf_op jit(solution)/shard_map/ppermute | solution.py:40
  96.9 26.4 %all-to-all-start = ((bf16[8,128,256]{2,1,0:T(8,128)(2,1)}), bf16[8,128,256]{2,1,0:T(8,128)(2,1)S(1)}, u32[]{:S(2)}, u32[]{:S(2)}) async-start(bf16[8,128,256]{2,1,0:T(8,128)(2,1)} %bitcast.62), calls=%async_computation | async-start | bytes 1048576 | tf_op jit(solution)/shard_map/all_to_all | solution.py:754
  101.8 29.5 %copy-start.50 = (bf16[1,256,512]{2,1,0:T(8,128)(2,1)S(1)}, bf16[1,256,512]{2,1,0:T(8,128)(2,1)}, u32[]{:S(2)}) copy-start(bf16[1,256,512]{2,1,0:T(8,128)(2,1)} %get-tuple-element.96) | copy-start | bytes 786436
  101.8 29.7 %copy-start.49 = (bf16[1,256,512]{2,1,0:T(8,128)(2,1)S(1)}, bf16[1,256,512]{2,1,0:T(8,128)(2,1)}, u32[]{:S(2)}) copy-start(bf16[1,256,512]{2,1,0:T(8,128)(2,1)} %get-tuple-element.91) | copy-start | bytes 786436
  101.8 8.5 %collective-permute-start.10 = (bf16[1,256,512]{2,1,0:T(8,128)(2,1)}, bf16[1,256,512]{2,1,0:T(8,128)(2,1)S(1)}, u32[]{:S(2)}, u32[]{:S(2)}) collective-permute-start(bf16[1,256,512]{2,1,0:T(8,128)(2,1)} %get-tuple-element.93), channel_id=1, source_target_pairs={{0,3},{1,2},{2,1},{3,0},{4,7},{5,6},{6,5},{7,4},{8,11},{9,10},{10,... | collective-permute-start | bytes 786440 | tf_op jit(solution)/shard_map/ppermute | solution.py:40
  103.2 13.1 %collective-permute-start.9 = (bf16[1,256,512]{2,1,0:T(8,128)(2,1)S(1)}, bf16[1,256,512]{2,1,0:T(8,128)(2,1)S(1)}, u32[]{:S(2)}, u32[]{:S(2)}) collective-permute-start(bf16[1,256,512]{2,1,0:T(8,128)(2,1)S(1)} %copy-done.51), channel_id=1, source_target_pairs={{0,2},{1,3},{2,0},{3,1},{4,6},{5,7},{6,4},{7,5},{8,10},{9,11},{10,... | collective-permute-start | bytes 786440 | tf_op jit(solution)/shard_map/ppermute | solution.py:40
  110.4 22.5 %copy-start.13 = (bf16[1,256,512]{2,1,0:T(8,128)(2,1)}, bf16[1,256,512]{2,1,0:T(8,128)(2,1)S(1)}, u32[]{:S(2)}) copy-start(bf16[1,256,512]{2,1,0:T(8,128)(2,1)S(1)} %collective-permute-done.10.refs_4_.refs_12_) | copy-start | bytes 786436
  123.3 31.4 %copy-start.23 = (bf16[8,128,256]{2,1,0:T(8,128)(2,1)}, bf16[8,128,256]{2,1,0:T(8,128)(2,1)S(1)}, u32[]{:S(2)}) copy-start(bf16[8,128,256]{2,1,0:T(8,128)(2,1)S(1)} %all-to-all-done) | copy-start | bytes 1572868
  123.3 31.4 %all-to-all-start.1 = ((bf16[8,128,256]{2,1,0:T(8,128)(2,1)}), bf16[8,128,256]{2,1,0:T(8,128)(2,1)S(1)}, u32[]{:S(2)}, u32[]{:S(2)}) async-start(bf16[8,128,256]{2,1,0:T(8,128)(2,1)} %bitcast.67), calls=%async_computation.1 | async-start | bytes 1048576 | tf_op jit(solution)/shard_map/all_to_all | solution.py:754
  129.3 15.0 %collective-permute-start.14 = (bf16[1,256,512]{2,1,0:T(8,128)(2,1)S(1)}, bf16[1,256,512]{2,1,0:T(8,128)(2,1)S(1)}, u32[]{:S(2)}, u32[]{:S(2)}) collective-permute-start(bf16[1,256,512]{2,1,0:T(8,128)(2,1)S(1)} %collective-permute-done.9.refs_2_.refs_10_), channel_id=1, source_target_pairs={{0,4},{4,0},{8,12},{12,8},{16,20},{20,16},{24,28},{28,24},{1,5},{5... | collective-permute-start | bytes 786440 | tf_op jit(solution)/shard_map/ppermute | solution.py:626
  131.3 13.0 %collective-permute-start.12 = (bf16[1,256,512]{2,1,0:T(8,128)(2,1)S(1)}, bf16[1,256,512]{2,1,0:T(8,128)(2,1)S(1)}, u32[]{:S(2)}, u32[]{:S(2)}) collective-permute-start(bf16[1,256,512]{2,1,0:T(8,128)(2,1)S(1)} %copy-done.50), channel_id=1, source_target_pairs={{0,3},{1,2},{2,1},{3,0},{4,7},{5,6},{6,5},{7,4},{8,11},{9,10},{10,... | collective-permute-start | bytes 786440 | tf_op jit(solution)/shard_map/ppermute | solution.py:40
  131.5 14.0 %collective-permute-start.7 = (bf16[1,256,512]{2,1,0:T(8,128)(2,1)S(1)}, bf16[1,256,512]{2,1,0:T(8,128)(2,1)S(1)}, u32[]{:S(2)}, u32[]{:S(2)}) collective-permute-start(bf16[1,256,512]{2,1,0:T(8,128)(2,1)S(1)} %copy-done.49), channel_id=1, source_target_pairs={{0,2},{1,3},{2,0},{3,1},{4,6},{5,7},{6,4},{7,5},{8,10},{9,11},{10,... | collective-permute-start | bytes 786440 | tf_op jit(solution)/shard_map/ppermute | solution.py:40
  132.9 15.8 %collective-permute-start.15 = (bf16[1,256,512]{2,1,0:T(8,128)(2,1)S(1)}, bf16[1,256,512]{2,1,0:T(8,128)(2,1)S(1)}, u32[]{:S(2)}, u32[]{:S(2)}) collective-permute-start(bf16[1,256,512]{2,1,0:T(8,128)(2,1)S(1)} %collective-permute-done.10.refs_4_.refs_12_), channel_id=1, source_target_pairs={{0,4},{4,0},{8,12},{12,8},{16,20},{20,16},{24,28},{28,24},{1,5},{5... | collective-permute-start | bytes 786440 | tf_op jit(solution)/shard_map/ppermute | solution.py:626
  133.0 35.2 %collective-permute-start.11 = (bf16[1,256,2048]{2,1,0:T(8,128)(2,1)}, bf16[1,256,2048]{2,1,0:T(8,128)(2,1)}, u32[]{:S(2)}, u32[]{:S(2)}) collective-permute-start(bf16[1,256,2048]{2,1,0:T(8,128)(2,1)} %get-tuple-element.94), channel_id=1, source_target_pairs={{0,2},{1,3},{2,0},{3,1},{4,6},{5,7},{6,4},{7,5},{8,10},{9,11},{10,... | collective-permute-start | bytes 3145736 | tf_op jit(solution)/shard_map/ppermute | solution.py:40
  144.3 17.5 %copy-start.16 = (bf16[1,256,512]{2,1,0:T(8,128)(2,1)}, bf16[1,256,512]{2,1,0:T(8,128)(2,1)S(1)}, u32[]{:S(2)}) copy-start(bf16[1,256,512]{2,1,0:T(8,128)(2,1)S(1)} %collective-permute-done.12.refs_4_.refs_6_) | copy-start | bytes 786436
  154.7 31.0 %copy-start.24 = (bf16[8,128,256]{2,1,0:T(8,128)(2,1)}, bf16[8,128,256]{2,1,0:T(8,128)(2,1)S(1)}, u32[]{:S(2)}) copy-start(bf16[8,128,256]{2,1,0:T(8,128)(2,1)S(1)} %all-to-all-done.1) | copy-start | bytes 1572868
  154.7 31.0 %all-to-all-start.2 = ((bf16[8,128,256]{2,1,0:T(8,128)(2,1)}), bf16[8,128,256]{2,1,0:T(8,128)(2,1)S(1)}, u32[]{:S(2)}, u32[]{:S(2)}) async-start(bf16[8,128,256]{2,1,0:T(8,128)(2,1)} %bitcast.60), calls=%async_computation.2 | async-start | bytes 1048576 | tf_op jit(solution)/shard_map/all_to_all | solution.py:754
  159.3 32.0 %collective-permute-start.20 = (bf16[1,256,2048]{2,1,0:T(8,128)(2,1)}, bf16[1,256,2048]{2,1,0:T(8,128)(2,1)}, u32[]{:S(2)}, u32[]{:S(2)}) collective-permute-start(bf16[1,256,2048]{2,1,0:T(8,128)(2,1)} %get-tuple-element.105), channel_id=1, source_target_pairs={{0,3},{1,2},{2,1},{3,0},{4,7},{5,6},{6,5},{7,4},{8,11},{9,10},{10,... | collective-permute-start | bytes 3145736 | tf_op jit(solution)/shard_map/ppermute | solution.py:40
  160.0 14.0 %collective-permute-start.8 = (bf16[1,256,512]{2,1,0:T(8,128)(2,1)S(1)}, bf16[1,256,512]{2,1,0:T(8,128)(2,1)S(1)}, u32[]{:S(2)}, u32[]{:S(2)}) collective-permute-start(bf16[1,256,512]{2,1,0:T(8,128)(2,1)S(1)} %collective-permute-done.7.refs_2_.refs_4_), channel_id=1, source_target_pairs={{0,4},{4,0},{8,12},{12,8},{16,20},{20,16},{24,28},{28,24},{1,5},{5... | collective-permute-start | bytes 786440 | tf_op jit(solution)/shard_map/ppermute | solution.py:626
  161.8 17.8 %collective-permute-start.13 = (bf16[1,256,512]{2,1,0:T(8,128)(2,1)S(1)}, bf16[1,256,512]{2,1,0:T(8,128)(2,1)S(1)}, u32[]{:S(2)}, u32[]{:S(2)}) collective-permute-start(bf16[1,256,512]{2,1,0:T(8,128)(2,1)S(1)} %collective-permute-done.12.refs_4_.refs_6_), channel_id=1, source_target_pairs={{0,4},{4,0},{8,12},{12,8},{16,20},{20,16},{24,28},{28,24},{1,5},{5... | collective-permute-start | bytes 786440 | tf_op jit(solution)/shard_map/ppermute | solution.py:626
  168.1 30.8 %collective-permute-start.22 = (bf16[1552,128]{1,0:T(8,128)(2,1)}, bf16[1552,128]{1,0:T(8,128)(2,1)S(1)}, u32[]{:S(2)}, u32[]{:S(2)}) collective-permute-start(bf16[1552,128]{1,0:T(8,128)(2,1)} %get-tuple-element.106), channel_id=1, source_target_pairs={{0,2},{1,3},{2,0},{3,1},{4,6},{5,7},{6,4},{7,5},{8,10},{9,11},{10,... | collective-permute-start | bytes 1191944 | tf_op jit(solution)/shard_map/ppermute | solution.py:40
  168.3 38.1 %collective-permute-start.21 = (bf16[1,256,2048]{2,1,0:T(8,128)(2,1)}, bf16[1,256,2048]{2,1,0:T(8,128)(2,1)}, u32[]{:S(2)}, u32[]{:S(2)}) collective-permute-start(bf16[1,256,2048]{2,1,0:T(8,128)(2,1)} %collective-permute-done.11.refs_2_), channel_id=1, source_target_pairs={{0,4},{4,0},{8,12},{12,8},{16,20},{20,16},{24,28},{28,24},{1,5},{5... | collective-permute-start | bytes 3145736 | tf_op jit(solution)/shard_map/ppermute | solution.py:626
  174.0 62.1 %collective-permute-start.25 = (bf16[1,512,2048]{2,1,0:T(8,128)(2,1)}, bf16[1,512,2048]{2,1,0:T(8,128)(2,1)}, u32[]{:S(2)}, u32[]{:S(2)}) collective-permute-start(bf16[1,512,2048]{2,1,0:T(8,128)(2,1)} %get-tuple-element.111), channel_id=1, source_target_pairs={{0,1},{1,0},{2,3},{3,2},{4,5},{5,4},{6,7},{7,6},{8,9},{9,8},{10,11... | collective-permute-start | bytes 6291464 | tf_op jit(solution)/shard_map/ppermute | solution.py:40
  185.7 17.1 %copy-start.25 = (bf16[8,128,256]{2,1,0:T(8,128)(2,1)}, bf16[8,128,256]{2,1,0:T(8,128)(2,1)S(1)}, u32[]{:S(2)}) copy-start(bf16[8,128,256]{2,1,0:T(8,128)(2,1)S(1)} %all-to-all-done.2) | copy-start | bytes 1572868
  185.7 22.0 %all-to-all-start.3 = ((bf16[8,128,256]{2,1,0:T(8,128)(2,1)}), bf16[8,128,256]{2,1,0:T(8,128)(2,1)S(1)}, u32[]{:S(2)}, u32[]{:S(2)}) async-start(bf16[8,128,256]{2,1,0:T(8,128)(2,1)} %bitcast.61), calls=%async_computation.3 | async-start | bytes 1048576 | tf_op jit(solution)/shard_map/all_to_all | solution.py:754
  191.3 38.6 %collective-permute-start.24 = (bf16[1,256,2048]{2,1,0:T(8,128)(2,1)}, bf16[1,256,2048]{2,1,0:T(8,128)(2,1)}, u32[]{:S(2)}, u32[]{:S(2)}) collective-permute-start(bf16[1,256,2048]{2,1,0:T(8,128)(2,1)} %collective-permute-done.20.refs_4_), channel_id=1, source_target_pairs={{0,4},{4,0},{8,12},{12,8},{16,20},{20,16},{24,28},{28,24},{1,5},{5... | collective-permute-start | bytes 3145736 | tf_op jit(solution)/shard_map/ppermute | solution.py:626
  199.0 19.4 %copy-start.27 = (bf16[1552,128]{1,0:T(8,128)(2,1)}, bf16[1552,128]{1,0:T(8,128)(2,1)S(1)}, u32[]{:S(2)}) copy-start(bf16[1552,128]{1,0:T(8,128)(2,1)S(1)} %collective-permute-done.22.refs_8_.refs_12_.refs_11_) | copy-start | bytes 1191940
  199.0 3.9 collective-permute-start.23
  229.9 58.1 %all-to-all-start.4 = ((bf16[8,4,128,256]{3,2,1,0:T(8,128)(2,1)}), bf16[8,4,128,256]{3,2,1,0:T(8,128)(2,1)S(1)}, u32[]{:S(2)}, u32[]{:S(2)}) async-start(bf16[8,4,128,256]{3,2,1,0:T(8,128)(2,1)} %shard_map.324), calls=%async_computation.4 | async-start | bytes 4194304 | tf_op jit(solution)/shard_map/all_to_all | solution.py:754
  234.2 118.0 %all-reduce.8.cloned.1.call-start = ((), (), s32[]{:S(2)}) async-start(), calls=%async_computation.6 | async-start | bytes 2097152 | tf_op jit(solution)/shard_map/psum | solution.py:894
  234.3 1.8 collective-permute-start.26
  270.5 1.8 collective-permute-start.31
  270.7 4.1 collective-permute-start.37
  271.1 168.5 %all-reduce.6.cloned.1.call-start = ((), (), s32[]{:S(2)}) async-start(), calls=%async_computation.5 | async-start | bytes 2097152 | tf_op jit(solution)/shard_map/psum | solution.py:1010
  273.2 43.5 %collective-permute-start.32 = (bf16[512,128]{1,0:T(8,128)(2,1)S(1)}, bf16[512,128]{1,0:T(8,128)(2,1)S(1)}, u32[]{:S(2)}, u32[]{:S(2)}) collective-permute-start(bf16[512,128]{1,0:T(8,128)(2,1)S(1)} %add_convert_fusion.4), channel_id=1, source_target_pairs={{0,2},{1,3},{2,0},{3,1},{4,6},{5,7},{6,4},{7,5},{8,10},{9,11},{10,... | collective-permute-start | bytes 393224 | tf_op jit(solution)/shard_map/ppermute | solution.py:40
  275.8 40.9 %collective-permute-start.38 = (bf16[512,128]{1,0:T(8,128)(2,1)S(1)}, bf16[512,128]{1,0:T(8,128)(2,1)S(1)}, u32[]{:S(2)}, u32[]{:S(2)}) collective-permute-start(bf16[512,128]{1,0:T(8,128)(2,1)S(1)} %add_convert_fusion.2), channel_id=1, source_target_pairs={{0,2},{1,3},{2,0},{3,1},{4,6},{5,7},{6,4},{7,5},{8,10},{9,11},{10,... | collective-permute-start | bytes 393224 | tf_op jit(solution)/shard_map/ppermute | solution.py:40
  296.8 16.9 %collective-permute-start.29 = (f32[512,128]{1,0:T(8,128)}, f32[512,128]{1,0:T(8,128)S(1)}, u32[]{:S(2)}, u32[]{:S(2)}) collective-permute-start(f32[512,128]{1,0:T(8,128)} %get-tuple-element.117), channel_id=1, source_target_pairs={{0,1},{1,0},{2,3},{3,2},{4,5},{5,4},{6,7},{7,6},{8,9},{9,8},{10,11... | collective-permute-start | bytes 786440 | tf_op jit(solution)/shard_map/ppermute | solution.py:40
  301.6 12.3 %collective-permute-start.35 = (f32[512,128]{1,0:T(8,128)}, f32[512,128]{1,0:T(8,128)S(1)}, u32[]{:S(2)}, u32[]{:S(2)}) collective-permute-start(f32[512,128]{1,0:T(8,128)} %get-tuple-element.123), channel_id=1, source_target_pairs={{0,1},{1,0},{2,3},{3,2},{4,5},{5,4},{6,7},{7,6},{8,9},{9,8},{10,11... | collective-permute-start | bytes 786440 | tf_op jit(solution)/shard_map/ppermute | solution.py:40
  313.7 17.4 %collective-permute-start.33 = (bf16[2,128,2048]{2,1,0:T(8,128)(2,1)}, bf16[2,128,2048]{2,1,0:T(8,128)(2,1)S(1)}, u32[]{:S(2)}, u32[]{:S(2)}) collective-permute-start(bf16[2,128,2048]{2,1,0:T(8,128)(2,1)} %get-tuple-element.122), channel_id=1, source_target_pairs={{0,1},{1,0},{2,3},{3,2},{4,5},{5,4},{6,7},{7,6},{8,9},{9,8},{10,11... | collective-permute-start | bytes 3145736 | tf_op jit(solution)/shard_map/ppermute | solution.py:40
  313.8 6.4 %collective-permute-start.30 = (bf16[512,128]{1,0:T(8,128)(2,1)S(1)}, bf16[512,128]{1,0:T(8,128)(2,1)S(1)}, u32[]{:S(2)}, u32[]{:S(2)}) collective-permute-start(bf16[512,128]{1,0:T(8,128)(2,1)S(1)} %add_convert_fusion.5), channel_id=1, source_target_pairs={{0,2},{1,3},{2,0},{3,1},{4,6},{5,7},{6,4},{7,5},{8,10},{9,11},{10,... | collective-permute-start | bytes 393224 | tf_op jit(solution)/shard_map/ppermute | solution.py:40
  314.0 9.0 %collective-permute-start.36 = (bf16[512,128]{1,0:T(8,128)(2,1)S(1)}, bf16[512,128]{1,0:T(8,128)(2,1)S(1)}, u32[]{:S(2)}, u32[]{:S(2)}) collective-permute-start(bf16[512,128]{1,0:T(8,128)(2,1)S(1)} %add_convert_fusion.3), channel_id=1, source_target_pairs={{0,2},{1,3},{2,0},{3,1},{4,6},{5,7},{6,4},{7,5},{8,10},{9,11},{10,... | collective-permute-start | bytes 393224 | tf_op jit(solution)/shard_map/ppermute | solution.py:40
  316.7 11.2 %collective-permute-start.27 = (bf16[2,128,2048]{2,1,0:T(8,128)(2,1)S(1)}, bf16[2,128,2048]{2,1,0:T(8,128)(2,1)S(1)}, u32[]{:S(2)}, u32[]{:S(2)}) collective-permute-start(bf16[2,128,2048]{2,1,0:T(8,128)(2,1)S(1)} %copy-done.47), channel_id=1, source_target_pairs={{0,1},{1,0},{2,3},{3,2},{4,5},{5,4},{6,7},{7,6},{8,9},{9,8},{10,11... | collective-permute-start | bytes 3145736 | tf_op jit(solution)/shard_map/ppermute | solution.py:40
  316.7 35.5 %collective-permute-start.39 = (bf16[32,1536]{1,0:T(8,128)(2,1)S(1)}, bf16[32,1536]{1,0:T(8,128)(2,1)S(1)}, u32[]{:S(2)}, u32[]{:S(2)}) collective-permute-start(bf16[32,1536]{1,0:T(8,128)(2,1)S(1)} %get-tuple-element.175), channel_id=1, source_target_pairs={{0,1},{1,0},{2,3},{3,2},{4,5},{5,4},{6,7},{7,6},{8,9},{9,8},{10,11... | collective-permute-start | bytes 294920 | tf_op jit(solution)/shard_map/ppermute | solution.py:40
  320.2 32.0 %collective-permute-start.40 = (bf16[32,1536]{1,0:T(8,128)(2,1)S(1)}, bf16[32,1536]{1,0:T(8,128)(2,1)S(1)}, u32[]{:S(2)}, u32[]{:S(2)}) collective-permute-start(bf16[32,1536]{1,0:T(8,128)(2,1)S(1)} %get-tuple-element.174), channel_id=1, source_target_pairs={{0,2},{1,3},{2,0},{3,1},{4,6},{5,7},{6,4},{7,5},{8,10},{9,11},{10,... | collective-permute-start | bytes 294920 | tf_op jit(solution)/shard_map/ppermute | solution.py:40
  323.0 29.2 %collective-permute-start.41 = (bf16[32,1536]{1,0:T(8,128)(2,1)S(1)}, bf16[32,1536]{1,0:T(8,128)(2,1)S(1)}, u32[]{:S(2)}, u32[]{:S(2)}) collective-permute-start(bf16[32,1536]{1,0:T(8,128)(2,1)S(1)} %get-tuple-element.173), channel_id=1, source_target_pairs={{0,3},{1,2},{2,1},{3,0},{4,7},{5,6},{6,5},{7,4},{8,11},{9,10},{10,... | collective-permute-start | bytes 294920 | tf_op jit(solution)/shard_map/ppermute | solution.py:40
  328.0 14.8 %collective-permute-start.28 = (bf16[128,2048]{1,0:T(8,128)(2,1)S(1)}, bf16[128,2048]{1,0:T(8,128)(2,1)S(1)}, u32[]{:S(2)}, u32[]{:S(2)}) collective-permute-start(bf16[128,2048]{1,0:T(8,128)(2,1)S(1)} %fusion.7), channel_id=1, source_target_pairs={{0,2},{1,3},{2,0},{3,1},{4,6},{5,7},{6,4},{7,5},{8,10},{9,11},{10,... | collective-permute-start | bytes 1572872 | tf_op jit(solution)/shard_map/ppermute | solution.py:40
  331.3 27.3 %collective-permute-start.34 = (bf16[128,2048]{1,0:T(8,128)(2,1)S(1)}, bf16[128,2048]{1,0:T(8,128)(2,1)S(1)}, u32[]{:S(2)}, u32[]{:S(2)}) collective-permute-start(bf16[128,2048]{1,0:T(8,128)(2,1)S(1)} %fusion.8), channel_id=1, source_target_pairs={{0,2},{1,3},{2,0},{3,1},{4,6},{5,7},{6,4},{7,5},{8,10},{9,11},{10,... | collective-permute-start | bytes 1572872 | tf_op jit(solution)/shard_map/ppermute | solution.py:40
  353.4 11.6 %collective-permute-start.42 = (bf16[32,2048]{1,0:T(8,128)(2,1)S(1)}, bf16[32,2048]{1,0:T(8,128)(2,1)S(1)}, u32[]{:S(2)}, u32[]{:S(2)}) collective-permute-start(bf16[32,2048]{1,0:T(8,128)(2,1)S(1)} %get-tuple-element.165), channel_id=1, source_target_pairs={{0,3},{1,2},{2,1},{3,0},{4,7},{5,6},{6,5},{7,4},{8,11},{9,10},{10,... | collective-permute-start | bytes 393224 | tf_op jit(solution)/shard_map/ppermute | solution.py:40
  353.7 11.3 %collective-permute-start.43 = (bf16[32,2048]{1,0:T(8,128)(2,1)S(1)}, bf16[32,2048]{1,0:T(8,128)(2,1)S(1)}, u32[]{:S(2)}, u32[]{:S(2)}) collective-permute-start(bf16[32,2048]{1,0:T(8,128)(2,1)S(1)} %get-tuple-element.164), channel_id=1, source_target_pairs={{0,2},{1,3},{2,0},{3,1},{4,6},{5,7},{6,4},{7,5},{8,10},{9,11},{10,... | collective-permute-start | bytes 393224 | tf_op jit(solution)/shard_map/ppermute | solution.py:40
  355.0 10.0 %collective-permute-start.44 = (bf16[32,2048]{1,0:T(8,128)(2,1)S(1)}, bf16[32,2048]{1,0:T(8,128)(2,1)S(1)}, u32[]{:S(2)}, u32[]{:S(2)}) collective-permute-start(bf16[32,2048]{1,0:T(8,128)(2,1)S(1)} %get-tuple-element.163), channel_id=1, source_target_pairs={{0,1},{1,0},{2,3},{3,2},{4,5},{5,4},{6,7},{7,6},{8,9},{9,8},{10,11... | collective-permute-start | bytes 393224 | tf_op jit(solution)/shard_map/ppermute | solution.py:40
  (40 other events, 288.0 us)
Sparse Core Ops, SparseCore 0:
  271.2 80.9 all-reduce.7
  358.7 80.7 all-reduce.5

commit v3 on v2

--- a/solution.py
+++ b/solution.py
@@ -117,20 +117,20 @@
     rows = weight.shape[0]
     part = size // parts
     inputs, outputs = [], []
-    for r, halved in cuts:
-        height = rows // 2 if halved else rows
-
-        def where(slot, t, ref, r=r, halved=halved):
+    for r, division, number in cuts:
+        height = rows // division
+
+        def where(slot, t, ref, r=r, number=number):
             kind = sum(kind * (slot == i) for i, kind in enumerate(kinds))
-            return (ref[4] if halved else 0, (kind * WA + ref[r]) * parts + t)
+            return (0 if number is None else ref[number], (kind * WA + ref[r]) * parts + t)
 
         inputs.append((weight, (height, part), where))
         outputs.append(
             (
-                (len(kinds), height, size),
+                (height, len(kinds) * size),
                 weight.dtype,
-                (1, height, part),
-                lambda slot, t, ref: (slot, 0, t),
+                (height, part),
+                lambda slot, t, ref: (0, slot * parts + t),
             )
         )
     return call(copy_kernel, index, inputs, outputs, grid=(len(kinds), parts))
@@ -221,20 +221,15 @@
 
 
 def pieces_of(index_ref, refs):
-    wide = refs[0].shape[-2]
-    half = wide // 2
-    y = index_ref[4]
-    firsts = [
-        index_ref[0] * wide,
-        index_ref[1] * wide,
-        index_ref[2] * wide + y * half,
-        index_ref[2] * wide + (1 - y) * half,
-        index_ref[3] * wide + y * half,
-        index_ref[3] * wide + (1 - y) * half,
-    ]
-    return [
-        (pl.ds(pl.multiple_of(first, half), ref.shape[-2]), ref) for first, ref in zip(firsts, refs)
-    ]
+    wide = refs[0].shape[0]
+    pieces = []
+    for r, ref in enumerate(refs):
+        size = ref.shape[0]
+        first = index_ref[r] * wide
+        if len(refs) > WA and r >= 2:
+            first = index_ref[2 + (r - 2) // 2] * wide + (r % 2) * size
+        pieces.append((pl.ds(pl.multiple_of(first, size), size), ref))
+    return pieces
 
 
 def read(ref):
@@ -255,8 +250,8 @@
 
 
 def qkv_kernel(turned, index_ref, hidden_ref, *refs):
-    weights, ups = refs[:6], refs[6:10]
-    inner_ref, bias_ref, cos_ref, sin_ref, out_ref, joined = refs[10:]
+    weights, ups = refs[:4], refs[4:8]
+    inner_ref, bias_ref, cos_ref, sin_ref, out_ref, joined = refs[8:]
     join_ups(index_ref, ups, joined)
     total = product(inner_ref[...], joined[...]) + bias_ref[...]
     for columns, ref in pieces_of(index_ref, weights):
@@ -304,9 +299,13 @@
     return values * below, below + values * bell * (1.0 / math.sqrt(2.0 * math.pi))
 
 
-def feed_kernel(index_ref, hidden_ref, grad_ref, *refs):
-    weights, ups, downs = refs[:6], refs[6:10], refs[10:14]
-    mask_ref, bias_ref, gain_ref, out_w_ref, out_down_ref, out_inner_grad_ref = refs[14:20]
+def feed_kernel(starts, ends, index_ref, hidden_ref, grad_ref, *refs):
+    weights, ups, refs = refs[:6], refs[6:10], refs[10:]
+    if starts:
+        downs, mask_ref, refs = refs[:4], refs[4], refs[5:]
+    else:
+        known_ref, refs = refs[0], refs[1:]
+    bias_ref, gain_ref, out_w_ref, out_down_ref, out_inner_grad_ref = refs[:5]
     (
         out_ref,
         norm_grad_ref,
@@ -316,17 +315,20 @@
         in_up_grad_ref,
         inner_ref,
         joined,
-    ) = refs[20:]
+    ) = refs[5:]
     step = pl.program_id(0)
 
     @pl.when(step == 0)
     def _():
-        wide = downs[0].shape[0]
-        total = 0.0
-        for r in range(WA):
-            columns = pl.ds(pl.multiple_of(index_ref[r] * wide, wide), wide)
-            total += product(hidden_ref[:, columns], downs[r][...])
-        inner_ref[...] = (total * mask_ref[...]).astype(bf16)
+        if starts:
+            wide = downs[0].shape[0]
+            total = 0.0
+            for r in range(WA):
+                columns = pl.ds(pl.multiple_of(index_ref[r] * wide, wide), wide)
+                total += product(hidden_ref[:, columns], downs[r][...])
+            inner_ref[...] = (total * mask_ref[...]).astype(bf16)
+        else:
+            inner_ref[...] = known_ref[...]
         out_ref[...] = jnp.zeros_like(out_ref)
         norm_grad_ref[...] = jnp.zeros_like(norm_grad_ref)
         out_inner_ref[...] = jnp.zeros_like(out_inner_ref)
@@ -426,11 +428,11 @@
 
 
 def norm_grad_kernel(index_ref, *refs):
-    grads, weights = refs[:2], refs[2:20]
-    gain_ref, sum_ref, keep_ref, send_ref, total = refs[20:]
-    sets = [pieces_of(index_ref, weights[6 * kind : 6 * kind + 6]) for kind in range(3)]
+    grads, weights = refs[:2], refs[2:14]
+    gain_ref, sum_ref, keep_ref, send_ref, total = refs[14:]
+    sets = [pieces_of(index_ref, weights[WA * kind : WA * kind + WA]) for kind in range(3)]
     rows = [[mixed_rows(*grads, kind, head) for head in range(2)] for kind in range(3)]
-    for piece in range(6):
+    for piece in range(WA):
         columns = sets[0][piece][0]
         part = 0.0
         for kind in range(3):
@@ -439,6 +441,70 @@
                 part += times_t(rows[kind][head], weight[:, head * HEAD : (head + 1) * HEAD])
         total[:, columns] = part * gain_ref[:, columns] + sum_ref[:, columns]
     scatter_rows(index_ref, total, keep_ref, send_ref)
+
+
+def pack_grads_kernel(index_ref, *refs):
+    first_ref, first_grad_ref, second_ref, second_grad_ref = refs[:4]
+    dense_ref, out_ref, grad_ref, down_ref = refs[4:8]
+    ups, (packed_ref, total) = refs[8:12], refs[12:]
+    size = ADAPT_COLS // WA
+    at = 0
+    for norm, grad in ((first_ref, first_grad_ref), (second_ref, second_grad_ref)):
+        part = t_times(norm[...], grad[...]).astype(bf16)
+        packed_ref[at : at + part.shape[0], :] = part
+        at += part.shape[0]
+    packed_ref[at : at + down_ref.shape[0], :] = down_ref[...]
+    at += down_ref.shape[0]
+    for inner in (dense_ref, out_ref):
+        total[...] = t_times(inner[...], grad_ref[...])
+        own = total[pl.ds(pl.multiple_of(index_ref[0] * size, size), size), :].astype(bf16)
+        at = store_strips(packed_ref, at, own)
+    for ref in ups:
+        at = store_strips(packed_ref, at, ref)
+
+
+def pack_feed_kernel(index_ref, down_ref, *refs):
+    parts, packed_ref = refs[:WA], refs[WA]
+    packed_ref[: down_ref.shape[0], :] = down_ref[...]
+    at = down_ref.shape[0]
+    for ref in parts:
+        at = store_strips(packed_ref, at, ref)
+
+
+def unpack_feed_kernel(index_ref, source_ref, down_ref, up_ref):
+    packed = source_ref[...].reshape(-1, ADAPT_COLS)
+    size = ADAPT_COLS // WA
+    at = down_ref.shape[0]
+    down_ref[...] = packed[:at, :].astype(f32)
+    block = up_ref.shape[1] // WA
+    for r in range(WA):
+        for i in range(block // 128):
+            first = index_ref[r] * block + i * 128
+            up_ref[:, pl.ds(pl.multiple_of(first, 128), 128)] = packed[at : at + size].astype(f32)
+            at += size
+
+
+def unpack_grads_kernel(index_ref, source_ref, *refs):
+    first_ref, second_ref, down_ref, dense_ref, out_ref, up_ref = refs
+    packed_ref = source_ref[...].reshape(-1, ADAPT_COLS)
+    size = ADAPT_COLS // WA
+    at = 0
+    for ref in (first_ref, second_ref, down_ref):
+        ref[...] = packed_ref[at : at + ref.shape[0], :].astype(f32)
+        at += ref.shape[0]
+    for ref in (dense_ref, out_ref):
+        for i in range(ref.shape[1] // 128):
+            ref[:, i * 128 : (i + 1) * 128] = packed_ref[at : at + size, :].astype(f32)
+            at += size
+    width = up_ref.shape[1] // 3
+    block = width // WA
+    for r in range(WA):
+        for kind in range(3):
+            first = kind * width + index_ref[r] * block
+            for i in range(block // 128):
+                columns = pl.ds(pl.multiple_of(first + i * 128, 128), 128)
+                up_ref[:, columns] = packed_ref[at : at + size, :].astype(f32)
+                at += size
 
 
 def finish_kernel(index_ref, *refs):
@@ -494,8 +560,8 @@
         dk_sum[...] = jnp.zeros_like(dk_sum)
         dv_sum[...] = jnp.zeros_like(dv_sum)
 
-    query = query_ref[...]
-    key = key_ref[...]
+    query = query_ref[...].reshape(-1, HEAD)
+    key = key_ref[...].reshape(-1, HEAD)
     value = value_ref[...]
     grad = grad_ref[...]
     key_place = key_place_ref[...]
@@ -531,8 +597,8 @@
 
 
 def attend(query, key, value, grad, begin, place, key_place, q_tables, k_tables, block):
-    rows = query.shape[0]
-    keys = key.shape[0]
+    rows = query.shape[0] * block
+    keys = key.shape[0] * block
     part = min(256, rows)
     joint = rows == keys
     by_rows = lambda i: (i, 0)
@@ -551,8 +617,8 @@
         functools.partial(attention_kernel, joint),
         grid=(rows // part,),
         in_specs=[
-            pl.BlockSpec((part, HEAD), by_rows),
-            pl.BlockSpec((keys, HEAD), all_rows),
+            pl.BlockSpec((part // block, 1, block, HEAD), lambda i: (i, 1, 0, 0)),
+            pl.BlockSpec((keys // block, 1, block, HEAD), fixed),
             pl.BlockSpec((keys, HEAD), all_rows),
             pl.BlockSpec((part, HEAD), by_rows),
             pl.BlockSpec((part, 1), by_rows),
@@ -614,7 +680,7 @@
     groups = contexts // PAIRS
     half = own_width // 2
     relative = [wa, wa ^ 1, wa ^ 2, wa ^ 3]
-    index = jnp.stack(relative + [ctx % 2]).astype(jnp.int32)
+    index = jnp.stack(relative + [ctx % 2, ctx, wa * 0, wa * 0 + 1]).astype(jnp.int32)
 
     def columns(value, which, size):
         return lax.dynamic_slice_in_dim(value, which * size, size, axis=1)
@@ -622,14 +688,22 @@
     def part_rows(value, which, size):
         return lax.dynamic_slice_in_dim(value, which * size, size, axis=0)
 
-    def swap_y(value):
-        return lax.ppermute(value, "ctx", [(i, i ^ 1) for i in range(contexts)])
-
-    def gather(value, peer=None):
-        peer = swap(value, 2) if peer is None else peer
-        return [value, swap(value, 1), peer, swap(peer, 1)]
-
-    value_cuts = cut_columns(index, qkv_weight, own_width, [2], [(2, True), (3, True)])
+    def gather_rows(weight, size, kinds, *earlier):
+        cuts = cut_columns(index, weight, size, kinds, [(2, contexts, 5), (3, contexts, 5)])
+        parts = [swap(after(cuts[0], *earlier), 2), swap(after(cuts[1], *earlier), 3)]
+        part = jnp.concatenate(parts, axis=1)
+        return part, lax.all_gather(part, "ctx", axis=0, tiled=True)
+
+    qkv_others_part, qkv_others = gather_rows(qkv_weight, own_width, [2, 1, 0])
+    in_cuts = cut_columns(
+        index,
+        in_weight,
+        hidden_width,
+        [0],
+        [(2, 2, 6), (2, 2, 7), (3, 2, 6), (3, 2, 7)],
+        4,
+    )
+    in_parts = [swap(after(in_cuts[0], qkv_others_part), 2)]
     limit = 64
     numbers = jnp.concatenate(
         [doc_lengths // limit, doc_lengths % limit, doc_adapter], axis=1
@@ -637,37 +711,18 @@
     numbers = jnp.pad(numbers, ((0, 15), (0, 128 - numbers.shape[1])))
     first_pack = pack_small(index, [tokens[0], qkv_down], qkv_up, [0, 1, 2], numbers)
 
-    def cross(value, *earlier):
-        peer = swap(after(value[0], *earlier), 2)
-        far = swap(after(value[1], *earlier), 3)
-        return [peer, swap_y(peer), far, swap_y(far)]
-
     def hand_on(away, near, *earlier):
         peer = swap(after(away, *earlier), 2)
         return [swap(near, 1), peer, swap(peer, 1)]
 
+    mate_cuts = cut_columns(index, qkv_weight, own_width, [2, 1, 0], [(1, 1, None)])[0]
+    in_mate_cut = cut_columns(index, in_weight, hidden_width, [0], [(1, 1, None)], 2)[0]
     first_packs = hand_on(*first_pack)
-    value_halves = cross(value_cuts)
-    mate_cuts = cut_columns(index, qkv_weight, own_width, [0, 1, 2], [(1, False)])[0]
-    key_cuts = cut_columns(index, qkv_weight, own_width, [1], [(2, True), (3, True)])
-    query_cuts = cut_columns(index, qkv_weight, own_width, [0], [(2, True), (3, True)])
-    in_cuts = cut_columns(
-        index, in_weight, hidden_width, [0], [(2, True), (3, True), (1, False)], 4
-    )
+    grad_pack = jnp.concatenate([cotangent[0], dense_up, out_up], axis=0)
+    grad_packs = hand_on(grad_pack, grad_pack, first_packs[1])
+    mate_weights = swap(after(mate_cuts, first_packs[0]), 1)
     feed_pack = pack_small(index, [in_down], in_up, [0], numbers)
-    value_there = (value_halves[0], value_halves[2])
-    mate_weights = swap(mate_cuts, 1)
-    grad_pack = jnp.concatenate([cotangent[0], dense_up, out_up], axis=0)
-    grad_packs = hand_on(grad_pack, grad_pack, *value_there)
-    key_halves = cross(key_cuts, *value_there)
-    key_there = (key_halves[0], key_halves[2])
-    query_halves = cross(query_cuts, grad_packs[1])
-    query_there = (query_halves[0], query_halves[2])
-    in_mate = swap(after(in_cuts[2], mate_weights), 1)
-    in_peer = swap(after(in_cuts[0], *key_there), 2)
-    in_far = swap(after(in_cuts[1], *query_there), 3)
-    in_halves = [in_peer, swap_y(in_peer), in_far, swap_y(in_far)]
-    feed_packs = hand_on(*feed_pack, in_peer)
+    feed_packs = hand_on(*feed_pack, grad_packs[1])
 
     docs_per_pack = doc_lengths.shape[1]
     tables = [numbers] + [item[-16:] for item in first_packs]
@@ -700,8 +755,7 @@
     first_norm, second_norm, first_inner = call(
         front_kernel,
         index,
-        [whole(after(tokens[0], *value_there, *key_cuts, *query_cuts, *in_cuts, *feed_pack))]
-        + [whole(item) for item in [qkv_down] + first_packs + [mask] + gains],
+        [whole(item) for item in [after(tokens[0], in_parts[0], *feed_pack), qkv_down] + first_packs + [mask] + gains],
         [
             ((total, width), bf16, None, None),
             ((total, width), bf16, None, None),
@@ -714,17 +768,24 @@
     ups_row = (tokens.size + qkv_down.size) // 128
     ups_size = 3 * own_width * part_cols // 128
 
-    def project(kind, halves, turned):
-        own_block = lambda head, ref: (0, (kind * WA + ref[0]) * 2 + head)
+    def project(last, kinds, turned):
+        own_block = lambda i, head, ref: (0, ((last - i) * WA + ref[0]) * 2 + head)
         items = [whole(first_norm), (qkv_weight, (own_width, HEAD), own_block)]
-        items.append((mate_weights, (1, own_width, HEAD), lambda head, ref: (kind, 0, head)))
-        items += [
-            (item, (1, own_width // 2, HEAD), lambda head, ref: (0, 0, head)) for item in halves
-        ]
+        for item, first in ((mate_weights, 0), (qkv_others, 0), (qkv_others, 3)):
+            first = (first + 2 - last) * 2
+            items.append(
+                (
+                    item,
+                    (own_width, HEAD),
+                    lambda i, head, ref, first=first: (0, first + 2 * i + head),
+                )
+            )
         items.append((qkv_up, (part_cols, HEAD), own_block))
         for r, item in zip((1, 2, 3), first_packs):
-            row = (ups_row + (r == 3) * ups_size) // strip + kind * 2
-            items.append((item, (strip, 128), lambda head, ref, row=row: (row + head, 0)))
+            row = (ups_row + (r == 3) * ups_size) // strip + last * 2
+            items.append(
+                (item, (strip, 128), lambda i, head, ref, row=row: (row - 2 * i + head, 0))
+            )
         items += [
             whole(first_inner),
             (qkv_bias[None, :], (1, HEAD), own_block),
@@ -737,17 +798,17 @@
             items,
             [
                 (
-                    (WA, 2, rows, HEAD),
+                    (WA, 2, kinds, rows, HEAD),
                     bf16,
-                    (WA, 1, rows, HEAD),
-                    lambda head, ref: (0, head, 0, 0),
+                    (WA, 1, 1, rows, HEAD),
+                    lambda i, head, ref: (0, head, i, 0, 0),
                 )
             ],
-            grid=(2,),
+            grid=(kinds, 2),
             scratch=[pltpu.VMEM((ADAPT_COLS, HEAD), bf16)],
-            flops=2 * total * width * own_width,
+            flops=2 * total * width * own_width * kinds,
         )[0]
-        return out.reshape(PAIRS, rows, HEAD)
+        return out.reshape(PAIRS, kinds, rows, HEAD)
 
     def to_pairs(item):
         if groups == 1:
@@ -755,16 +816,12 @@
         names = [[g * PAIRS + j for j in range(PAIRS)] for g in range(groups)]
         return lax.all_to_all(item, "ctx", 0, 0, axis_index_groups=names, tiled=True)
 
-    value_halves[1] = after(value_halves[1], *grad_packs)
-    value = to_pairs(project(2, value_halves, False))
-
-    grad_own = after(grad_pack, *key_there, value_halves[1])
     grad, dense_inner_grad, out_inner_grad, attended_grad, all_ups = call(
         grad_kernel,
         index,
         [
             whole(item)
-            for item in [grad_own] + grad_packs + [mask, dense_weight, dense_down]
+            for item in [after(grad_pack, first_inner)] + grad_packs + [mask, dense_weight, dense_down]
         ],
         [
             ((total, width), bf16, None, None),
@@ -776,11 +833,76 @@
         scratch=[pltpu.VMEM((ADAPT_COLS, width), bf16), pltpu.VMEM((ADAPT_COLS, width), bf16)],
         flops=2 * total * width * (own_width + 2 * ADAPT_COLS),
     )
-    attended_grad = to_pairs(after(attended_grad, value).reshape(PAIRS, rows, HEAD))
-    key_halves[1] = after(key_halves[1], *query_there)
-    key = to_pairs(after(project(1, key_halves, True), attended_grad))
-    query_halves[1] = after(query_halves[1], in_peer)
-    query = to_pairs(after(project(0, query_halves, True), key))
+    attended_grad = to_pairs(attended_grad.reshape(PAIRS, rows, HEAD))
+    in_parts.append(swap(after(in_cuts[1], grad_packs[1]), 2))
+    qkv_others = after(qkv_others, first_norm, grad)
+    value = to_pairs(after(project(2, 1, False), attended_grad))
+    in_parts.append(swap(after(in_cuts[2], in_parts[1]), 3))
+    pair_own = after(project(1, 2, True), value, in_parts[2])
+    pair = to_pairs(pair_own)
+    in_parts.append(swap(after(in_cuts[3], in_parts[2]), 3))
+
+    tile = min(512, hidden_width)
+    tiles = hidden_width // tile
+    in_downs = [whole(in_down)] + [
+        (item, (own_width, ADAPT_COLS), lambda *_: (0, 0)) for item in feed_packs
+    ]
+
+    in_mate = swap(after(in_mate_cut, pair_own), 1)
+
+    def feed(part, known, norm, *earlier):
+        count = tiles
+        first = part * count
+        own_tile = lambda t, ref: (0, ref[0] * tiles + first + t)
+        strip = part_cols * tile // 128
+        items = [whole(after(norm, *earlier)), whole(grad)]
+        items += [
+            (in_weight, (own_width, tile), own_tile),
+            (in_mate, (own_width, tile), lambda t, ref: (0, first + t)),
+        ]
+        items += [
+            (item, (own_width // 2, tile), lambda t, ref: (0, first + t)) for item in in_parts
+        ]
+        items.append((in_up, (part_cols, tile), own_tile))
+        for r, item in zip((1, 2, 3), feed_packs):
+            row = (own_width + (r == 3) * part_cols * hidden_width // 128) // strip + first
+            items.append((item, (strip, 128), lambda t, ref, row=row: (row + t, 0)))
+        items += in_downs + [whole(mask)] if known is None else [whole(known)]
+        items += [
+            (in_bias[None, :], (1, tile), own_tile),
+            whole(gains[2]),
+            (out_weight, (tile, width), lambda t, ref: (first + t, 0)),
+            (out_down, (tile, ADAPT_COLS), lambda t, ref: (first + t, 0)),
+            whole(out_inner_grad),
+        ]
+        size = count * tile
+        return call(
+            functools.partial(feed_kernel, known is None, True),
+            index,
+            items,
+            [
+                ((total, width), f32, None, None),
+                ((total, width), f32, None, None),
+                ((total, ADAPT_COLS), f32, None, None),
+                ((total, ADAPT_COLS), f32, None, None),
+                ((size, ADAPT_COLS), bf16, (tile, ADAPT_COLS), lambda t, ref: (t, 0)),
+                ((ADAPT_COLS, size), bf16, (ADAPT_COLS, tile), lambda t, ref: (0, t)),
+                ((total, ADAPT_COLS), bf16, None, None),
+            ],
+            grid=(count,),
+            scratch=[pltpu.VMEM((ADAPT_COLS, tile), bf16)],
+            flops=8 * total * width * size,
+        )
+
+    (
+        branch_sum,
+        norm_grad,
+        out_inner,
+        second_inner_grad,
+        out_down_grad,
+        in_up_grad,
+        second_inner,
+    ) = feed(0, None, second_norm, pair)
 
     pair_rows = PAIRS * rows
     group = ctx // PAIRS
@@ -798,17 +920,16 @@
         q_place = part_rows(all_places, group, pair_rows)
         q_begin = part_rows(all_begins, group, pair_rows)
         q_tables = [part_rows(item, group, pair_rows) for item in k_tables]
-    query, key, value, attended_grad = [
-        item.reshape(pair_rows, HEAD) for item in (query, key, value, attended_grad)
-    ]
+    value, attended_grad = [item.reshape(pair_rows, HEAD) for item in (value, attended_grad)]
+    key = pair
     sets = [[g * PAIRS + j for g in range(groups)] for j in range(PAIRS)]
     if groups > 1:
         key, value = [
             lax.all_gather(item, "ctx", axis=0, axis_index_groups=sets, tiled=True)
-            for item in (key, value)
+            for item in (pair[:, :1], value)
         ]
     both = attend(
-        after(query, in_far, in_halves[1], feed_packs[2]),
+        after(pair, in_parts[3], in_mate, *feed_packs),
         key,
         value,
         attended_grad,
@@ -824,57 +945,9 @@
             both[1], "ctx", scatter_dimension=0, axis_index_groups=sets, tiled=True
         )
         both = [jnp.concatenate([both[0], dkv], axis=1)]
-    both = to_pairs(after(both[0], in_halves[3])).reshape(WA, 2, 4, rows, HEAD)
+    both = to_pairs(both[0]).reshape(WA, 2, 4, rows, HEAD)
+    both = after(both, branch_sum)
     odq, dkv = both, both
-
-    tile = min(512, hidden_width)
-    tiles = hidden_width // tile
-    own_tile = lambda t, ref: (0, ref[0] * tiles + t)
-    items = [whole(second_norm), whole(grad), (in_weight, (own_width, tile), own_tile)]
-    items += [
-        (item, (1, item.shape[1], tile), lambda t, ref: (0, 0, t)) for item in [in_mate] + in_halves
-    ]
-    items += [(in_up, (part_cols, tile), own_tile)]
-    strip = part_cols * tile // 128
-    for r, item in zip((1, 2, 3), feed_packs):
-        row = (own_width + (r == 3) * part_cols * hidden_width // 128) // strip
-        items.append((item, (strip, 128), lambda t, ref, row=row: (row + t, 0)))
-    in_downs = [whole(in_down)] + [
-        (item, (own_width, ADAPT_COLS), lambda *_: (0, 0)) for item in feed_packs
-    ]
-    items += in_downs + [whole(mask)]
-    items += [
-        (in_bias[None, :], (1, tile), own_tile),
-        whole(gains[2]),
-        (out_weight, (tile, width), lambda t, ref: (t, 0)),
-        (out_down, (tile, ADAPT_COLS), lambda t, ref: (t, 0)),
-        whole(out_inner_grad),
-    ]
-    (
-        branch_sum,
-        norm_grad,
-        out_inner,
-        second_inner_grad,
-        out_down_grad,
-        in_up_grad,
-        second_inner,
-    ) = call(
-        feed_kernel,
-        index,
-        items,
-        [
-            ((total, width), f32, None, None),
-            ((total, width), f32, None, None),
-            ((total, ADAPT_COLS), f32, None, None),
-            ((total, ADAPT_COLS), f32, None, None),
-            ((hidden_width, ADAPT_COLS), bf16, (tile, ADAPT_COLS), lambda t, ref: (t, 0)),
-            ((ADAPT_COLS, hidden_width), bf16, (ADAPT_COLS, tile), lambda t, ref: (0, t)),
-            ((total, ADAPT_COLS), bf16, None, None),
-        ],
-        grid=(tiles,),
-        scratch=[pltpu.VMEM((ADAPT_COLS, tile), bf16)],
-        flops=8 * total * width * hidden_width,
-    )
 
     def sum_inner(partial):
         partial = (partial + swap(partial, 1)).astype(bf16)
@@ -886,14 +959,46 @@
             swap(part_rows(value, wa ^ r, part_cols), r) for r in (1, 2, 3)
         ]
 
-    def own_columns(left, right):
-        return t_times(columns(left, wa, left.shape[1] // WA), right).astype(bf16)
-
+    def exchange_sum(value):
+        parts = value.reshape(contexts, -1, ADAPT_COLS)
+        parts = lax.all_to_all(parts, "ctx", 0, 0, tiled=True)
+        return jnp.sum(parts.astype(f32), axis=0).astype(bf16)
+
+    feed_packed = call(
+        pack_feed_kernel,
+        index,
+        [whole(item) for item in [out_down_grad] + spread_rows(in_up_grad)],
+        [((2 * hidden_width, ADAPT_COLS), bf16, None, None)],
+    )[0]
+    feed_sum = exchange_sum(after(feed_packed, both))
     out_inner = sum_inner(out_inner)
     second_inner_grad = sum_inner(second_inner_grad)
-    feed_grads = lax.psum([out_down_grad, in_up_grad], "ctx")
-
-    dense_items = [odq, branch_sum, dense_weight, dense_down, dense_inner_grad]
+
+    mixed_grads = [odq, dkv]
+    up_items = []
+    for kind in range(3):
+        up_items.append(
+            (qkv_up, (part_cols, own_width), lambda _, ref, kind=kind: (0, kind * WA + ref[0]))
+        )
+        for r, item in zip((1, 2, 3), first_packs):
+            row = (ups_row + (r == 3) * ups_size) // (2 * strip_rows) + kind
+            up_items.append(
+                (item, (2 * strip_rows, 128), lambda _, ref, row=row: (row, 0))
+            )
+    mixed_inner, qkv_up_grad = call(
+        mix_kernel,
+        index,
+        [whole(item) for item in mixed_grads] + up_items + [whole(first_inner)],
+        [
+            ((total, ADAPT_COLS), f32, None, None),
+            ((ADAPT_COLS, 3 * own_width), bf16, None, None),
+        ],
+        scratch=[pltpu.VMEM((3, ADAPT_COLS, own_width), bf16)],
+        flops=4 * total * ADAPT_COLS * 3 * own_width,
+    )
+    first_inner_grad = sum_inner(mixed_inner)
+    up_parts = spread_rows(qkv_up_grad)
+    dense_items = [after(odq, mixed_inner), branch_sum, dense_weight, dense_down, dense_inner_grad]
     reduced = [
         ((2, rows, width), f32, None, None),
         ((2, rows, width), bf16, None, None),
@@ -924,31 +1029,8 @@
         + tokens[0].astype(f32)
     ).astype(bf16)[None]
 
-    mixed_grads = [odq, dkv]
-    up_items = []
+    weight_items = []
     for kind in range(3):
-        up_items.append(
-            (qkv_up, (part_cols, own_width), lambda _, ref, kind=kind: (0, kind * WA + ref[0]))
-        )
-        for r, item in zip((1, 2, 3), first_packs):
-            row = (ups_row + (r == 3) * ups_size) // (2 * strip_rows) + kind
-            up_items.append(
-                (item, (2 * strip_rows, 128), lambda _, ref, row=row: (row, 0))
-            )
-    first_inner_grad, qkv_up_grad = call(
-        mix_kernel,
-        index,
-        [whole(item) for item in mixed_grads] + up_items + [whole(first_inner)],
-        [
-            ((total, ADAPT_COLS), f32, None, None),
-            ((ADAPT_COLS, 3 * own_width), bf16, None, None),
-        ],
-        scratch=[pltpu.VMEM((3, ADAPT_COLS, own_width), bf16)],
-        flops=4 * total * ADAPT_COLS * 3 * own_width,
-    )
-    first_inner_grad = sum_inner(first_inner_grad)
-    weight_items = []
-    for kind, halves in ((0, query_halves), (1, key_halves), (2, value_halves)):
         weight_items.append(
             (
                 qkv_weight,
@@ -956,16 +1038,16 @@
                 lambda _, ref, kind=kind: (0, kind * WA + ref[0]),
             )
         )
-        weight_items.append(
-            (mate_weights, (1, own_width, own_width), lambda _, ref, kind=kind: (kind, 0, 0))
-        )
-        weight_items += [whole(item) for item in halves]
+        for item, first in ((mate_weights, 2), (qkv_others, 2), (qkv_others, 5)):
+            weight_items.append(
+                (item, (own_width, own_width), lambda _, ref, at=first - kind: (0, at))
+            )
     keep, send = call(
         norm_grad_kernel,
         index,
         [whole(item) for item in mixed_grads]
         + weight_items
-        + [whole(gains[0]), whole(norm_grad)],
+        + [whole(item) for item in [after(gains[0], keep), norm_grad]],
         reduced,
         scratch=[pltpu.VMEM((total, width), f32)],
         flops=2 * total * width * 3 * own_width,
@@ -996,32 +1078,51 @@
         scratch=[pltpu.VMEM((rows, width), f32)],
     )[0][None]
 
-    attention_grads = [
+    own_norm = lambda _, ref: (0, ref[0])
+    items = [
+        (first_norm, (total, own_width), own_norm),
+        whole(first_inner_grad),
+    ]
+    items += [(second_norm, (total, own_width), own_norm), whole(second_inner_grad)]
+    items += [whole(item) for item in [dense_inner, out_inner, grad, dense_down_grad] + up_parts]
+    packed = call(
+        pack_grads_kernel,
+        index,
+        items,
+        [((8 * own_width, ADAPT_COLS), bf16, None, None)],
+        scratch=[pltpu.VMEM((ADAPT_COLS, width), f32)],
+    )[0]
+    packed = exchange_sum(after(packed, feed_sum))
+    packed = jnp.stack([feed_sum, packed])
+    packed = lax.all_to_all(
+        jnp.broadcast_to(packed[None], (contexts,) + packed.shape), "ctx", 0, 0, tiled=True
+    )
+    packed = after(packed, tokens_grad, output)
+    block = (contexts, 1) + packed.shape[2:]
+    out_down_grad, in_up_grad = call(
+        unpack_feed_kernel,
+        index,
+        [(packed, block, lambda *_: (0, 0, 0, 0))],
+        [
+            ((hidden_width, ADAPT_COLS), f32, None, None),
+            ((part_cols, WA * hidden_width), f32, None, None),
+        ],
+    )
+    down_shape = ((own_width, ADAPT_COLS), f32, None, None)
+    up_shape = ((part_cols, width), f32, None, None)
+    (
+        qkv_down_grad,
+        in_down_grad,
         dense_down_grad,
-        own_columns(dense_inner, grad),
-        own_columns(first_norm, first_inner_grad),
-        own_columns(out_inner, grad),
-        own_columns(second_norm, second_inner_grad),
-    ] + spread_rows(qkv_up_grad)
-    feed_grads = [after(item, *attention_grads, combined, output) for item in feed_grads]
-    out_down_grad, in_up_grad = feed_grads
-    in_up_parts = spread_rows(in_up_grad)
-    attention_grads = [after(item, *feed_grads) for item in attention_grads]
-    attention_grads = lax.psum(attention_grads, "ctx")
-    out_down_grad = out_down_grad.astype(f32)
-    dense_down_grad, dense_up_grad, qkv_down_grad, out_up_grad, in_down_grad = [
-        item.astype(f32) for item in attention_grads[:5]
-    ]
-    in_up_grad = jnp.concatenate(absolute(in_up_parts, wa), axis=1).astype(f32)
-    qkv_parts = absolute(attention_grads[5:], wa)
-    qkv_up_grad = jnp.concatenate(
-        [
-            part[:, kind * own_width : (kind + 1) * own_width]
-            for kind in range(3)
-            for part in qkv_parts
-        ],
-        axis=1,
-    ).astype(f32)
+        dense_up_grad,
+        out_up_grad,
+        qkv_up_grad,
+    ) = call(
+        unpack_grads_kernel,
+        index,
+        [(packed, block, lambda *_: (0, 1, 0, 0))],
+        [down_shape] * 3 + [up_shape] * 2 + [((part_cols, 3 * width), f32, None, None)],
+    )
     return (
         output,
         tokens_grad,

time: 454 us -> 394 us (0.87)
  waiting for transfers between devices: 207 us -> 120 us
  blocking collectives: 0 us -> 32.6 us
  Pallas kernels: 126 us -> 137 us
  other arithmetic: 25.3 us -> 18.4 us
  starting transfers between devices: 57.9 us -> 51.2 us
  matrix products: 8.14 us -> 3.4 us
    psum x2 -> x0, waiting for transfers between devices: 80.3 us -> none  [the longest x1 72.4 us: body(): attention_grads = lax.psum(attention_grads, 'ctx')]
    ppermute x8 -> x0, waiting for transfers between devices: 39 us -> none  [swap_y(): return lax.ppermute(value, 'ctx', [(i, i ^ 1) for i in range(contexts)])]
    all_to_all x0 -> x1, blocking collectives: none -> 32.6 us  [exchange_sum(): parts = lax.all_to_all(parts, 'ctx', 0, 0, tiled=True)]
    ppermute x37 -> x35, waiting for transfers between devices: 74.3 us -> 106 us  [swap(): return lax.ppermute(value, 'wa', [(i, i ^ bits) for i in range(WA)])]
    pallas_call x17 -> x19, Pallas kernels: 116 us -> 127 us  [call(): pl.pallas_call(kernel, grid_spec=pltpu.PrefetchScalarGridSpec(num_scalar_...]
    ppermute x8 -> x0, starting transfers between devices: 10.3 us -> none  [swap_y(): return lax.ppermute(value, 'ctx', [(i, i ^ 1) for i in range(contexts)])]
    all_to_all x0 -> x2, starting transfers between devices: none -> 8.4 us  [the longest x1 4.76 us: exchange_sum(): parts = lax.all_to_all(parts, 'ctx', 0, 0, tiled=True)]
    convert_element_type x8 -> x0, other arithmetic: 7.66 us -> none  [the longest x5 3.61 us: body(): item.astype(f32)]
  transfers between devices with their start and end apart: 52 -> 42, of which waited for: 22 -> 22; matrix products, arithmetic and copies ran while one was open for 7% -> 8% of each run, Pallas kernels for 26% -> 30%
where the time goes in v3:
time: 394 us; the launch traced here: 392 us
  Pallas kernels  137 us (35%)
  waiting for transfers between devices  120 us (30%)
  starting transfers between devices  51.2 us (13%)
  blocking collectives  32.6 us (8%)
  other arithmetic  18.4 us (5%)
  local copies, waits for them, and re-layouts  15 us (4%)
  between operations  14.6 us (4%)
    pallas_call x19, Pallas kernels, call(): pl.pallas_call(kernel, grid_spec=pltpu.PrefetchScalarGridSpec(num_scalar_...  127 us
    ppermute x35, waiting for transfers between devices, swap(): return lax.ppermute(value, 'wa', [(i, i ^ bits) for i in range(WA)])  106 us
    all_to_all x1, blocking collectives, exchange_sum(): parts = lax.all_to_all(parts, 'ctx', 0, 0, tiled=True)  32.6 us
    ppermute x35, starting transfers between devices, swap(): return lax.ppermute(value, 'wa', [(i, i ^ bits) for i in range(WA)])  22.9 us
    all_to_all x4, starting transfers between devices, to_pairs(): return lax.all_to_all(item, 'ctx', 0, 0, tiled=True)  19.9 us
    all_to_all x4, waiting for transfers between devices, to_pairs(): return lax.all_to_all(item, 'ctx', 0, 0, tiled=True)  11.1 us
    pallas_call x1, Pallas kernels, attend(): pl.pallas_call(functools.partial(attention_kernel, joint), grid=(rows //...  9.93 us
  transfers between devices with their start and end apart: 42, of which 22 were waited for; matrix products, arithmetic and copies ran while one was open for 8% of the time, Pallas kernels for 30%

profile of v3, /device:TPU:0, one launch (start us, length us, event | category | flops | bytes accessed | tf_op | source)
XLA Modules:
  0.0 391.9 jit_solution(10532565791479812571)
XLA Ops:
  7.9 3.4 shard_map.313
  11.2 2.9 collective-permute-start
  14.2 5.9 %collective-permute-done = bf16[64,1536]{1,0:T(8,128)(2,1)S(1)} collective-permute-done((bf16[64,1536]{1,0:T(8,128)(2,1)}, bf16[64,1536]{1,0:T(8,128)(2,1)S(1)}, u32[]{:S(2)}, u32[]{:S(2)}) %collective-permute-start) | collective-permute-done | bytes 196640 | tf_op jit(solution)/shard_map/ppermute | solution.py:40
  20.1 2.7 collective-permute-done.1
  25.8 3.3 shard_map.315
  29.1 1.2 collective-permute-start.4
  31.0 5.5 %shard_map.312 = (bf16[256,2048]{1,0:T(8,128)(2,1)}, bf16[256,2048]{1,0:T(8,128)(2,1)}, bf16[256,2048]{1,0:T(8,128)(2,1)}, bf16[256,2048]{1,0:T(8,128)(2,1)}) custom-call(s32[8]{0:T(128)} %stack.43.index_ref, bf16[512,8192]{1,0:T(8,128)(2,1)} %refs_0_.15, bf16[512,8192]{1,0:T(8,128)(2,1)} %refs_0_.15, bf16[512,8192]{1,0:T(8,128)(2,1)} %refs_0_.15, ...), custom_call_target="tpu_custom_call" | custom-call | bytes 4194304 | tf_op jit(solution)/shard_map/pallas_call | solution.py:91
  37.1 14.1 %collective-permute-done.4.refs_3_.refs_6_.refs_4_.refs_8_.refs_12_.refs_7_ = bf16[3344,128]{1,0:T(8,128)(2,1)S(1)} collective-permute-done((bf16[3344,128]{1,0:T(8,128)(2,1)}, bf16[3344,128]{1,0:T(8,128)(2,1)S(1)}, u32[]{:S(2)}, u32[]{:S(2)}) %collective-permute-start.4) | collective-permute-done | bytes 856096 | tf_op jit(solution)/shard_map/ppermute | solution.py:40
  51.2 1.3 collective-permute-start.8
  52.5 1.8 constant_dynamic-slice_fusion.19
  54.3 4.3 %shard_map.317 = bf16[512,1536]{1,0:T(8,128)(2,1)} custom-call(s32[8]{0:T(128)} %stack.43.index_ref, bf16[512,6144]{1,0:T(8,128)(2,1)} %refs_10_.5), custom_call_target="tpu_custom_call" | custom-call | bytes 1572864 | tf_op jit(solution)/shard_map/pallas_call | solution.py:91
  58.5 2.8 shard_map.314
  62.0 11.8 %collective-permute-done.2.refs_2_ = bf16[256,2048]{1,0:T(8,128)(2,1)} collective-permute-done((bf16[256,2048]{1,0:T(8,128)(2,1)}, bf16[256,2048]{1,0:T(8,128)(2,1)}, u32[]{:S(2)}, u32[]{:S(2)}) %collective-permute-start.2) | collective-permute-done | bytes 1048608 | tf_op jit(solution)/shard_map/ppermute | solution.py:40
  73.7 16.4 %collective-permute-done.8.refs_2_ = bf16[192,2048]{1,0:T(8,128)(2,1)} collective-permute-done((bf16[192,2048]{1,0:T(8,128)(2,1)S(1)}, bf16[192,2048]{1,0:T(8,128)(2,1)}, u32[]{:S(2)}, u32[]{:S(2)}) %collective-permute-start.8) | collective-permute-done | bytes 786464 | tf_op jit(solution)/shard_map/ppermute | solution.py:40
  90.2 1.7 collective-permute-start.10
  94.6 6.9 %shard_map.316 = (bf16[512,2048]{1,0:T(8,128)(2,1)}, bf16[512,2048]{1,0:T(8,128)(2,1)}, bf16[512,128]{1,0:T(8,128)(2,1)}) custom-call(s32[8]{0:T(128)} %stack.43.index_ref, bf16[128,2048]{1,0:T(8,128)(2,1)} %bitcast.55, bf16[512,128]{1,0:T(8,128)(2,1)} %refs_5_.3, bf16[3344,128]{1,0:T(8,128)(2,1)} %copy-done.2, bf16[3344,128]{1,0:T(8,128)(2,1)} %copy-done.1, ...), custom_call_target="tpu_custom_call" | custom-call | flops 268435456 | bytes 3518464 | tf_op jit(solution)/shard_map/pallas_call | solution.py:91
  101.5 7.0 %shard_map.318 = (bf16[512,2048]{1,0:T(8,128)(2,1)}, bf16[512,128]{1,0:T(8,128)(2,1)}, bf16[512,128]{1,0:T(8,128)(2,1)}, bf16[4,2,128,256]{3,2,1,0:T(8,128)(2,1)}, bf16[2,128,2048]{2,1,0:T(8,128)(2,1)}) custom-call(s32[8]{0:T(128)} %stack.43.index_ref, bf16[192,2048]{1,0:T(8,128)(2,1)} %copy-done.15, bf16[192,2048]{1,0:T(8,128)(2,1)} %collective-permute-done.7.refs_1_, ...), custom_call_target="tpu_custom_call" | custom-call | flops 1610612736 | bytes 5636096 | tf_op jit(solution)/shard_map/pallas_call | solution.py:91
  108.5 5.8 %all-to-all-start = ((bf16[8,128,256]{2,1,0:T(8,128)(2,1)}), bf16[8,128,256]{2,1,0:T(8,128)(2,1)S(1)}, u32[]{:S(2)}, u32[]{:S(2)}) async-start(bf16[8,128,256]{2,1,0:T(8,128)(2,1)} %bitcast.66), calls=%async_computation | async-start | bytes 1048576 | tf_op jit(solution)/shard_map/all_to_all | solution.py:815
  114.4 1.2 collective-permute-done.10.refs_3_
  116.3 1.8 fusion.16
  118.1 5.2 %shard_map.320 = bf16[4,2,1,128,256]{4,3,2,1,0:T(8,128)(2,1)} custom-call(s32[8]{0:T(128)} %stack.43.index_ref, bf16[512,2048]{1,0:T(8,128)(2,1)} %get-tuple-element.80.hidden_ref.refs_0_, bf16[512,6144]{1,0:T(8,128)(2,1)} %refs_10_.5, bf16[512,1536]{1,0:T(8,128)(2,1)} %collective-permute-done.6.refs_1_.refs_3_.refs_7_.refs_11_, ...), custom_call_target="tpu_custom_call" | custom-call | flops 1073741824 | bytes 4981760 | tf_op jit(solution)/shard_map/pallas_call | solution.py:91
  123.3 6.2 %all-to-all-done = bf16[8,128,256]{2,1,0:T(8,128)(2,1)S(1)} async-done(((bf16[8,128,256]{2,1,0:T(8,128)(2,1)}), bf16[8,128,256]{2,1,0:T(8,128)(2,1)S(1)}, u32[]{:S(2)}, u32[]{:S(2)}) %all-to-all-start) | async-done | bytes 524320 | tf_op jit(solution)/shard_map/all_to_all | solution.py:815
  129.5 3.6 all-to-all-start.1
  133.1 3.3 shard_map.321
  136.5 7.8 %shard_map.319 = bf16[4,2,2,128,256]{4,3,2,1,0:T(8,128)(2,1)} custom-call(s32[8]{0:T(128)} %stack.43.index_ref, bf16[512,2048]{1,0:T(8,128)(2,1)} %get-tuple-element.80.hidden_ref.refs_0_, bf16[512,6144]{1,0:T(8,128)(2,1)} %refs_10_.5, bf16[512,1536]{1,0:T(8,128)(2,1)} %collective-permute-done.6.refs_1_.refs_3_.refs_7_.refs_11_, ...), custom_call_target="tpu_custom_call" | custom-call | flops 2147483648 | bytes 7211008 | tf_op jit(solution)/shard_map/pallas_call | solution.py:91
  144.3 3.5 all-to-all-done.1
  147.8 4.4 %all-to-all-start.2 = ((bf16[8,2,128,256]{3,2,1,0:T(8,128)(2,1)}), bf16[8,2,128,256]{3,2,1,0:T(8,128)(2,1)}, u32[]{:S(2)}, u32[]{:S(2)}) async-start(bf16[8,2,128,256]{3,2,1,0:T(8,128)(2,1)} %bitcast.57), calls=%async_computation.2 | async-start | bytes 2097152 | tf_op jit(solution)/shard_map/all_to_all | solution.py:815
  156.6 8.7 %collective-permute-done.15.refs_8_.refs_12_.refs_11_ = bf16[1552,128]{1,0:T(8,128)(2,1)S(1)} collective-permute-done((bf16[1552,128]{1,0:T(8,128)(2,1)}, bf16[1552,128]{1,0:T(8,128)(2,1)S(1)}, u32[]{:S(2)}, u32[]{:S(2)}) %collective-permute-start.15) | collective-permute-done | bytes 397344 | tf_op jit(solution)/shard_map/ppermute | solution.py:40
  165.9 3.1 fusion.5
  169.8 16.2 %collective-permute-done.12.refs_5_ = bf16[256,2048]{1,0:T(8,128)(2,1)} collective-permute-done((bf16[256,2048]{1,0:T(8,128)(2,1)}, bf16[256,2048]{1,0:T(8,128)(2,1)}, u32[]{:S(2)}, u32[]{:S(2)}) %collective-permute-start.12) | collective-permute-done | bytes 1048608 | tf_op jit(solution)/shard_map/ppermute | solution.py:40
  186.0 9.9 %shard_map.322 = bf16[8,4,128,256]{3,2,1,0:T(8,128)(2,1)} custom-call(bf16[8,2,128,256]{3,2,1,0:T(8,128)(2,1)} %all-to-all-done.2.query_ref.key_ref, bf16[8,2,128,256]{3,2,1,0:T(8,128)(2,1)} %all-to-all-done.2.query_ref.key_ref, bf16[1024,256]{1,0:T(8,128)(2,1)} %bitcast.65, bf16[1024,256]{1,0:T(8,128)(2,1)} %bitcast.64, s32[1024,1]{1,0:T(8,128)} %copy.42.begin_ref, ...), custom_call_target="tpu_custom_call" | custom-call | flops 3758096384 | bytes 4194304 | tf_op jit(solution)/shard_map/pallas_call | solution.py:616
  195.9 6.0 %all-to-all-start.3 = ((bf16[8,4,128,256]{3,2,1,0:T(8,128)(2,1)}), bf16[8,4,128,256]{3,2,1,0:T(8,128)(2,1)S(1)}, u32[]{:S(2)}, u32[]{:S(2)}) async-start(bf16[8,4,128,256]{3,2,1,0:T(8,128)(2,1)} %shard_map.322), calls=%async_computation.3 | async-start | bytes 4194304 | tf_op jit(solution)/shard_map/all_to_all | solution.py:815
  201.9 33.6 %shard_map.323 = (f32[512,2048]{1,0:T(8,128)}, f32[512,2048]{1,0:T(8,128)}, f32[512,128]{1,0:T(8,128)}, f32[512,128]{1,0:T(8,128)}, bf16[2048,128]{1,0:T(8,128)(...) custom-call(s32[8]{0:T(128)} %stack.43.index_ref, bf16[512,2048]{1,0:T(8,128)(2,1)} %get-tuple-element.100.hidden_ref.refs_2_, ...), custom_call_target="tpu_custom_call" | custom-call | flops 17179869184 | bytes 24129536 | tf_op jit(solution)/shard_map/pallas_call | solution.py:91
  235.5 1.8 constant_dynamic-slice_fusion.4
  239.7 4.2 %collective-permute-done.30.refs_2_ = bf16[32,2048]{1,0:T(8,128)(2,1)S(1)} collective-permute-done((bf16[32,2048]{1,0:T(8,128)(2,1)S(1)}, bf16[32,2048]{1,0:T(8,128)(2,1)S(1)}, u32[]{:S(2)}, u32[]{:S(2)}) %collective-permute-start.30) | collective-permute-done | bytes 131104 | tf_op jit(solution)/shard_map/ppermute | solution.py:40
  243.8 1.7 collective-permute-done.31.refs_3_
  246.1 3.2 shard_map.328
  249.3 1.4 all-to-all-done.3
  250.8 4.8 %all-to-all-start.4 = ((bf16[8,512,128]{2,1,0:T(8,128)(2,1)}), bf16[8,512,128]{2,1,0:T(8,128)(2,1)S(1)}, u32[]{:S(2)}, u32[]{:S(2)}) async-start(bf16[8,512,128]{2,1,0:T(8,128)(2,1)} %bitcast.59), calls=%async_computation.4 | async-start | bytes 2097152 | tf_op jit(solution)/shard_map/all_to_all | solution.py:964
  257.5 4.7 %shard_map.324 = (f32[512,128]{1,0:T(8,128)}, bf16[128,1536]{1,0:T(8,128)(2,1)}) custom-call(s32[8]{0:T(128)} %stack.43.index_ref, bf16[4,2,4,128,256]{4,3,2,1,0:T(8,128)(2,1)} %bitcast.49, bf16[4,2,4,128,256]{4,3,2,1,0:T(8,128)(2,1)} %bitcast.50, bf16[32,6144]{1,0:T(8,128)(2,1)} %refs_10_.4, bf16[3344,128]{1,0:T(8,128)(2,1)} %copy-done.2, ...), custom_call_target="tpu_custom_call" | custom-call | flops 402653184 | bytes 4718592 | tf_op jit(solution)/shard_map/pallas_call | solution.py:91
  262.2 7.6 %shard_map.325 = (f32[2,128,2048]{2,1,0:T(8,128)}, bf16[2,128,2048]{2,1,0:T(8,128)(2,1)}, f32[512,128]{1,0:T(8,128)}, bf16[512,128]{1,0:T(8,128)(2,1)}) custom-call(s32[8]{0:T(128)} %stack.43.index_ref, bf16[4,2,4,128,256]{4,3,2,1,0:T(8,128)(2,1)} %bitcast.51, f32[512,2048]{1,0:T(8,128)} %get-tuple-element.102.sum_ref, bf16[512,2048]{1,0:T(8,128)(2,1)} %weight_ref.1, ...), custom_call_target="tpu_custom_call" | custom-call | flops 1073741824 | bytes 8650752 | tf_op jit(solution)/shard_map/pallas_call | solution.py:91
  270.4 1.6 collective-permute-start.22
  273.6 1.6 collective-permute-start.20
  277.7 1.9 collective-permute-done.26
  279.7 2.8 collective-permute-done.20
  285.4 5.0 %shard_map.329 = bf16[4096,128]{1,0:T(8,128)(2,1)} custom-call(s32[8]{0:T(128)} %stack.43.index_ref, bf16[512,2048]{1,0:T(8,128)(2,1)} %get-tuple-element.80.hidden_ref.refs_0_, bf16[512,128]{1,0:T(8,128)(2,1)} %get-tuple-element.165.refs_1_, bf16[512,2048]{1,0:T(8,128)(2,1)} %get-tuple-element.100.hidden_ref.refs_2_, ...), custom_call_target="tpu_custom_call" | custom-call | bytes 4194304 | tf_op jit(solution)/shard_map/pallas_call | solution.py:91
  290.6 32.6 %all_to_all.35 = bf16[8,512,128]{2,1,0:T(8,128)(2,1)S(1)} all-to-all(bf16[8,512,128]{2,1,0:T(8,128)(2,1)} %bitcast.58), channel_id=1, replica_groups=mesh['ctx'=8,'wa'=4] {'ctx'}, dimensions={0} | all-to-all | bytes 2097152 | tf_op jit(solution)/shard_map/all_to_all | solution.py:964
  323.3 1.7 broadcast_in_dim.153
  325.0 3.6 all-to-all-start.6
  328.7 11.4 %shard_map.326 = (f32[2,128,2048]{2,1,0:T(8,128)}, bf16[2,128,2048]{2,1,0:T(8,128)(2,1)}) custom-call(s32[8]{0:T(128)} %stack.43.index_ref, bf16[4,2,4,128,256]{4,3,2,1,0:T(8,128)(2,1)} %bitcast.52, bf16[4,2,4,128,256]{4,3,2,1,0:T(8,128)(2,1)} %bitcast.53, bf16[512,6144]{1,0:T(8,128)(2,1)} %refs_10_.5, ...), custom_call_target="tpu_custom_call" | custom-call | flops 3221225472 | bytes 14688256 | tf_op jit(solution)/shard_map/pallas_call | solution.py:91
  340.6 3.0 collective-permute-done.23.refs_1_
  343.6 2.5 fusion.8
  346.1 1.5 collective-permute-start.24
  349.3 1.4 constant_dynamic-slice_fusion.9.refs_3_
  350.7 1.4 constant_dynamic-slice_fusion.8.refs_4_
  352.0 9.2 %collective-permute-done.24.refs_2_ = bf16[128,2048]{1,0:T(8,128)(2,1)} collective-permute-done((bf16[128,2048]{1,0:T(8,128)(2,1)}, bf16[128,2048]{1,0:T(8,128)(2,1)}, u32[]{:S(2)}, u32[]{:S(2)}) %collective-permute-start.24) | collective-permute-done | bytes 524320 | tf_op jit(solution)/shard_map/ppermute | solution.py:40
  361.2 5.6 %shard_map.327 = f32[128,2048]{1,0:T(8,128)} custom-call(s32[8]{0:T(128)} %stack.43.index_ref, f32[2,128,2048]{2,1,0:T(8,128)} %get-tuple-element.114.refs_0_, bf16[2,128,2048]{2,1,0:T(8,128)(2,1)} %copy-done.7, bf16[128,2048]{1,0:T(8,128)(2,1)} %collective-permute-done.24.refs_2_, bf16[128,128]{1,0:T(8,128)(2,1)} %constant_dynamic-slice_fusion.9.refs_3_, ...), custom_call_target="tpu_custom_call" | custom-call | bytes 5849088 | tf_op jit(solution)/shard_map/pallas_call | solution.py:91
  366.8 4.8 %collective-permute-done.18 = bf16[128,2048]{1,0:T(8,128)(2,1)} collective-permute-done((bf16[128,2048]{1,0:T(8,128)(2,1)}, bf16[128,2048]{1,0:T(8,128)(2,1)}, u32[]{:S(2)}, u32[]{:S(2)}) %collective-permute-start.18) | collective-permute-done | bytes 524320 | tf_op jit(solution)/shard_map/ppermute | solution.py:40
  371.6 1.5 convolution_add_fusion.1
  373.2 1.9 fusion.4
  375.1 2.1 all-to-all-done.6.source_ref
  377.1 1.3 copy-done.4
  378.4 3.3 shard_map.330
  381.7 3.4 shard_map.331
  (181 shorter events, 29.7 us)
Async XLA Ops:
  7.2 110.9 %all-gather.2.cloned.1.call-start = ((), (), s32[]{:S(2)}) async-start(), calls=%async_computation.7 | async-start | bytes 3538944 | tf_op jit(solution)/shard_map/all_gather | solution.py:695
  7.9 15.8 %copy-start.40 = (s32[1,16]{1,0:T(1,128)S(1)}, s32[1,16]{1,0:T(1,128)}, u32[]{:S(2)}) copy-start(s32[1,16]{1,0:T(1,128)} %param.29) | copy-start | bytes 196
  7.9 15.9 %copy-start.41 = (s32[1,16]{1,0:T(1,128)S(1)}, s32[1,16]{1,0:T(1,128)}, u32[]{:S(2)}) copy-start(s32[1,16]{1,0:T(1,128)} %param.28) | copy-start | bytes 196
  7.9 16.6 %copy-start.5 = (bf16[32,6144]{1,0:T(8,128)(2,1)S(1)}, bf16[32,6144]{1,0:T(8,128)(2,1)}, u32[]{:S(2)}) copy-start(bf16[32,6144]{1,0:T(8,128)(2,1)} %refs_10_.4) | copy-start | bytes 1179652
  11.2 8.9 %collective-permute-start = (bf16[64,1536]{1,0:T(8,128)(2,1)}, bf16[64,1536]{1,0:T(8,128)(2,1)S(1)}, u32[]{:S(2)}, u32[]{:S(2)}) collective-permute-start(bf16[64,1536]{1,0:T(8,128)(2,1)} %get-tuple-element.72), channel_id=1, source_target_pairs={{0,2},{1,3},{2,0},{3,1},{4,6},{5,7},{6,4},{7,5},{8,10},{9,11},{10,... | collective-permute-start | bytes 589832 | tf_op jit(solution)/shard_map/ppermute | solution.py:40
  14.2 8.7 %collective-permute-start.1 = (bf16[64,1536]{1,0:T(8,128)(2,1)}, bf16[64,1536]{1,0:T(8,128)(2,1)S(1)}, u32[]{:S(2)}, u32[]{:S(2)}) collective-permute-start(bf16[64,1536]{1,0:T(8,128)(2,1)} %get-tuple-element.73), channel_id=1, source_target_pairs={{0,3},{1,2},{2,1},{3,0},{4,7},{5,6},{6,5},{7,4},{8,11},{9,10},{10,... | collective-permute-start | bytes 589832 | tf_op jit(solution)/shard_map/ppermute | solution.py:40
  29.1 22.0 %collective-permute-start.4 = (bf16[3344,128]{1,0:T(8,128)(2,1)}, bf16[3344,128]{1,0:T(8,128)(2,1)S(1)}, u32[]{:S(2)}, u32[]{:S(2)}) collective-permute-start(bf16[3344,128]{1,0:T(8,128)(2,1)} %get-tuple-element.79), channel_id=1, source_target_pairs={{0,2},{1,3},{2,0},{3,1},{4,6},{5,7},{6,4},{7,5},{8,10},{9,11},{10,... | collective-permute-start | bytes 2568200 | tf_op jit(solution)/shard_map/ppermute | solution.py:40
  30.4 31.1 %collective-permute-start.3 = (bf16[3344,128]{1,0:T(8,128)(2,1)}, bf16[3344,128]{1,0:T(8,128)(2,1)S(1)}, u32[]{:S(2)}, u32[]{:S(2)}) collective-permute-start(bf16[3344,128]{1,0:T(8,128)(2,1)} %get-tuple-element.78), channel_id=1, source_target_pairs={{0,1},{1,0},{2,3},{3,2},{4,5},{5,4},{6,7},{7,6},{8,9},{9,8},{10,11... | collective-permute-start | bytes 2568200 | tf_op jit(solution)/shard_map/ppermute | solution.py:40
  36.5 37.2 %collective-permute-start.2 = (bf16[256,2048]{1,0:T(8,128)(2,1)}, bf16[256,2048]{1,0:T(8,128)(2,1)}, u32[]{:S(2)}, u32[]{:S(2)}) collective-permute-start(bf16[256,2048]{1,0:T(8,128)(2,1)} %get-tuple-element.74), channel_id=1, source_target_pairs={{0,2},{1,3},{2,0},{3,1},{4,6},{5,7},{6,4},{7,5},{8,10},{9,11},{10,... | collective-permute-start | bytes 3145736 | tf_op jit(solution)/shard_map/ppermute | solution.py:40
  37.0 21.5 %copy-start.15 = (bf16[192,2048]{1,0:T(8,128)(2,1)}, bf16[192,2048]{1,0:T(8,128)(2,1)S(1)}, u32[]{:S(2)}) copy-start(bf16[192,2048]{1,0:T(8,128)(2,1)S(1)} %pad_maximum_fusion.refs_0_) | copy-start | bytes 2359300
  37.0 64.5 %collective-permute-start.7 = (bf16[192,2048]{1,0:T(8,128)(2,1)S(1)}, bf16[192,2048]{1,0:T(8,128)(2,1)}, u32[]{:S(2)}, u32[]{:S(2)}) collective-permute-start(bf16[192,2048]{1,0:T(8,128)(2,1)S(1)} %pad_maximum_fusion.refs_0_), channel_id=1, source_target_pairs={{0,1},{1,0},{2,3},{3,2},{4,5},{5,4},{6,7},{7,6},{8,9},{9,8},{10,11... | collective-permute-start | bytes 2359304 | tf_op jit(solution)/shard_map/ppermute | solution.py:40
  51.2 40.7 %copy-start.1 = (bf16[3344,128]{1,0:T(8,128)(2,1)}, bf16[3344,128]{1,0:T(8,128)(2,1)S(1)}, u32[]{:S(2)}) copy-start(bf16[3344,128]{1,0:T(8,128)(2,1)S(1)} %collective-permute-done.4.refs_3_.refs_6_.refs_4_.refs_8_.refs_12_.refs_7_) | copy-start | bytes 2568196
  51.2 39.0 %collective-permute-start.8 = (bf16[192,2048]{1,0:T(8,128)(2,1)S(1)}, bf16[192,2048]{1,0:T(8,128)(2,1)}, u32[]{:S(2)}, u32[]{:S(2)}) collective-permute-start(bf16[192,2048]{1,0:T(8,128)(2,1)S(1)} %pad_maximum_fusion.refs_0_), channel_id=1, source_target_pairs={{0,2},{1,3},{2,0},{3,1},{4,6},{5,7},{6,4},{7,5},{8,10},{9,11},{10,... | collective-permute-start | bytes 2359304 | tf_op jit(solution)/shard_map/ppermute | solution.py:40
  52.5 39.4 %collective-permute-start.5 = (bf16[3344,128]{1,0:T(8,128)(2,1)S(1)}, bf16[3344,128]{1,0:T(8,128)(2,1)S(1)}, u32[]{:S(2)}, u32[]{:S(2)}) collective-permute-start(bf16[3344,128]{1,0:T(8,128)(2,1)S(1)} %collective-permute-done.4.refs_3_.refs_6_.refs_4_.refs_8_.refs_12_.refs_7_), channel_id=1, source_target_pairs={{0,1},{1,0},{2,3},{3,2},{4,5},{5,4},{6,7},{7,6},{8,9},{9,8},{10,11... | collective-permute-start | bytes 2568200 | tf_op jit(solution)/shard_map/ppermute | solution.py:40
  54.3 7.1 %copy-start.37 = (s32[16]{0:T(128)S(1)}, s32[16]{0:T(128)}, u32[]{:S(2)}) copy-start(s32[16]{0:T(128)} %param.27) | copy-start | bytes 196
  61.3 47.2 %copy-start.34 = (s32[128]{0:T(128)}, s32[128]{0:T(128)S(1)}, u32[]{:S(2)}) copy-start(s32[128]{0:T(128)S(1)} %and_select_fusion.4) | copy-start | bytes 1540
  61.4 33.2 %copy-start.2 = (bf16[3344,128]{1,0:T(8,128)(2,1)}, bf16[3344,128]{1,0:T(8,128)(2,1)S(1)}, u32[]{:S(2)}) copy-start(bf16[3344,128]{1,0:T(8,128)(2,1)S(1)} %collective-permute-done.3.refs_2_.refs_5_.refs_3_.refs_7_.refs_11_.refs_6_) | copy-start | bytes 2568196
  61.4 56.6 %collective-permute-start.6 = (bf16[512,1536]{1,0:T(8,128)(2,1)}, bf16[512,1536]{1,0:T(8,128)(2,1)}, u32[]{:S(2)}, u32[]{:S(2)}) collective-permute-start(bf16[512,1536]{1,0:T(8,128)(2,1)} %shard_map.317), channel_id=1, source_target_pairs={{0,1},{1,0},{2,3},{3,2},{4,5},{5,4},{6,7},{7,6},{8,9},{9,8},{10,11... | collective-permute-start | bytes 4718600 | tf_op jit(solution)/shard_map/ppermute | solution.py:40
  90.2 25.5 %collective-permute-start.10 = (bf16[256,2048]{1,0:T(8,128)(2,1)}, bf16[256,2048]{1,0:T(8,128)(2,1)}, u32[]{:S(2)}, u32[]{:S(2)}) collective-permute-start(bf16[256,2048]{1,0:T(8,128)(2,1)} %get-tuple-element.91), channel_id=1, source_target_pairs={{0,2},{1,3},{2,0},{3,1},{4,6},{5,7},{6,4},{7,5},{8,10},{9,11},{10,... | collective-permute-start | bytes 3145736 | tf_op jit(solution)/shard_map/ppermute | solution.py:40
  91.9 9.6 %collective-permute-start.9 = (bf16[192,2048]{1,0:T(8,128)(2,1)}, bf16[192,2048]{1,0:T(8,128)(2,1)}, u32[]{:S(2)}, u32[]{:S(2)}) collective-permute-start(bf16[192,2048]{1,0:T(8,128)(2,1)} %collective-permute-done.8.refs_2_), channel_id=1, source_target_pairs={{0,1},{1,0},{2,3},{3,2},{4,5},{5,4},{6,7},{7,6},{8,9},{9,8},{10,11... | collective-permute-start | bytes 2359304 | tf_op jit(solution)/shard_map/ppermute | solution.py:40
  108.5 21.0 %all-to-all-start = ((bf16[8,128,256]{2,1,0:T(8,128)(2,1)}), bf16[8,128,256]{2,1,0:T(8,128)(2,1)S(1)}, u32[]{:S(2)}, u32[]{:S(2)}) async-start(bf16[8,128,256]{2,1,0:T(8,128)(2,1)} %bitcast.66), calls=%async_computation | async-start | bytes 1048576 | tf_op jit(solution)/shard_map/all_to_all | solution.py:815
  115.6 28.7 %collective-permute-start.11 = (bf16[256,2048]{1,0:T(8,128)(2,1)}, bf16[256,2048]{1,0:T(8,128)(2,1)}, u32[]{:S(2)}, u32[]{:S(2)}) collective-permute-start(bf16[256,2048]{1,0:T(8,128)(2,1)} %get-tuple-element.92), channel_id=1, source_target_pairs={{0,3},{1,2},{2,1},{3,0},{4,7},{5,6},{6,5},{7,4},{8,11},{9,10},{10,... | collective-permute-start | bytes 3145736 | tf_op jit(solution)/shard_map/ppermute | solution.py:40
  129.5 7.0 %copy-start.16 = (bf16[8,128,256]{2,1,0:T(8,128)(2,1)}, bf16[8,128,256]{2,1,0:T(8,128)(2,1)S(1)}, u32[]{:S(2)}) copy-start(bf16[8,128,256]{2,1,0:T(8,128)(2,1)S(1)} %all-to-all-done) | copy-start | bytes 1572868
  129.5 18.3 %all-to-all-start.1 = ((bf16[8,1,128,256]{3,2,1,0:T(8,128)(2,1)}), bf16[8,1,128,256]{3,2,1,0:T(8,128)(2,1)S(1)}, u32[]{:S(2)}, u32[]{:S(2)}) async-start(bf16[8,1,128,256]{3,2,1,0:T(8,128)(2,1)} %bitcast.62), calls=%async_computation.1 | async-start | bytes 1048576 | tf_op jit(solution)/shard_map/all_to_all | solution.py:815
  136.5 11.4 %copy-start.11 = (bf16[512,2048]{1,0:T(8,128)(2,1)S(1)}, bf16[512,2048]{1,0:T(8,128)(2,1)}, u32[]{:S(2)}) copy-start(bf16[512,2048]{1,0:T(8,128)(2,1)} %shard_map.321) | copy-start | bytes 6291460
  144.3 8.5 %copy-start.38 = (s32[16]{0:T(128)S(1)}, s32[16]{0:T(128)}, u32[]{:S(2)}) copy-start(s32[16]{0:T(128)} %param.27) | copy-start | bytes 196
  144.3 10.1 %copy-start.36 = (s32[16]{0:T(128)S(1)}, s32[16]{0:T(128)}, u32[]{:S(2)}) copy-start(s32[16]{0:T(128)} %get-tuple-element.134) | copy-start | bytes 196
  147.8 7.7 %copy-start.17 = (bf16[8,1,128,256]{3,2,1,0:T(8,128)(2,1)}, bf16[8,1,128,256]{3,2,1,0:T(8,128)(2,1)S(1)}, u32[]{:S(2)}) copy-start(bf16[8,1,128,256]{3,2,1,0:T(8,128)(2,1)S(1)} %all-to-all-done.1) | copy-start | bytes 1572868
  147.8 38.2 %collective-permute-start.13 = (bf16[512,2048]{1,0:T(8,128)(2,1)S(1)}, bf16[512,2048]{1,0:T(8,128)(2,1)}, u32[]{:S(2)}, u32[]{:S(2)}) collective-permute-start(bf16[512,2048]{1,0:T(8,128)(2,1)S(1)} %copy-done.11), channel_id=1, source_target_pairs={{0,1},{1,0},{2,3},{3,2},{4,5},{5,4},{6,7},{7,6},{8,9},{9,8},{10,11... | collective-permute-start | bytes 6291464 | tf_op jit(solution)/shard_map/ppermute | solution.py:40
  147.8 38.2 %all-to-all-start.2 = ((bf16[8,2,128,256]{3,2,1,0:T(8,128)(2,1)}), bf16[8,2,128,256]{3,2,1,0:T(8,128)(2,1)}, u32[]{:S(2)}, u32[]{:S(2)}) async-start(bf16[8,2,128,256]{3,2,1,0:T(8,128)(2,1)} %bitcast.57), calls=%async_computation.2 | async-start | bytes 2097152 | tf_op jit(solution)/shard_map/all_to_all | solution.py:815
  152.3 16.7 %collective-permute-start.14 = (bf16[1552,128]{1,0:T(8,128)(2,1)}, bf16[1552,128]{1,0:T(8,128)(2,1)S(1)}, u32[]{:S(2)}, u32[]{:S(2)}) collective-permute-start(bf16[1552,128]{1,0:T(8,128)(2,1)} %get-tuple-element.76), channel_id=1, source_target_pairs={{0,1},{1,0},{2,3},{3,2},{4,5},{5,4},{6,7},{7,6},{8,9},{9,8},{10,11... | collective-permute-start | bytes 1191944 | tf_op jit(solution)/shard_map/ppermute | solution.py:40
  152.9 12.3 %collective-permute-start.15 = (bf16[1552,128]{1,0:T(8,128)(2,1)}, bf16[1552,128]{1,0:T(8,128)(2,1)S(1)}, u32[]{:S(2)}, u32[]{:S(2)}) collective-permute-start(bf16[1552,128]{1,0:T(8,128)(2,1)} %get-tuple-element.97), channel_id=1, source_target_pairs={{0,2},{1,3},{2,0},{3,1},{4,6},{5,7},{6,4},{7,5},{8,10},{9,11},{10,... | collective-permute-start | bytes 1191944 | tf_op jit(solution)/shard_map/ppermute | solution.py:40
  153.6 32.4 %collective-permute-start.12 = (bf16[256,2048]{1,0:T(8,128)(2,1)}, bf16[256,2048]{1,0:T(8,128)(2,1)}, u32[]{:S(2)}, u32[]{:S(2)}) collective-permute-start(bf16[256,2048]{1,0:T(8,128)(2,1)} %get-tuple-element.95), channel_id=1, source_target_pairs={{0,3},{1,2},{2,1},{3,0},{4,7},{5,6},{6,5},{7,4},{8,11},{9,10},{10,... | collective-permute-start | bytes 3145736 | tf_op jit(solution)/shard_map/ppermute | solution.py:40
  165.3 30.7 %copy-start.19 = (bf16[1552,128]{1,0:T(8,128)(2,1)}, bf16[1552,128]{1,0:T(8,128)(2,1)S(1)}, u32[]{:S(2)}) copy-start(bf16[1552,128]{1,0:T(8,128)(2,1)S(1)} %collective-permute-done.15.refs_8_.refs_12_.refs_11_) | copy-start | bytes 1191940
  165.3 3.7 collective-permute-start.16
  169.0 26.9 %copy-start.18 = (bf16[1552,128]{1,0:T(8,128)(2,1)}, bf16[1552,128]{1,0:T(8,128)(2,1)S(1)}, u32[]{:S(2)}) copy-start(bf16[1552,128]{1,0:T(8,128)(2,1)S(1)} %collective-permute-done.14.refs_7_.refs_11_.refs_10_) | copy-start | bytes 1191940
  195.9 54.8 %all-to-all-start.3 = ((bf16[8,4,128,256]{3,2,1,0:T(8,128)(2,1)}), bf16[8,4,128,256]{3,2,1,0:T(8,128)(2,1)S(1)}, u32[]{:S(2)}, u32[]{:S(2)}) async-start(bf16[8,4,128,256]{3,2,1,0:T(8,128)(2,1)} %shard_map.322), calls=%async_computation.3 | async-start | bytes 4194304 | tf_op jit(solution)/shard_map/all_to_all | solution.py:815
  237.3 2.3 collective-permute-start.29
  237.5 6.3 %collective-permute-start.30 = (bf16[32,2048]{1,0:T(8,128)(2,1)S(1)}, bf16[32,2048]{1,0:T(8,128)(2,1)S(1)}, u32[]{:S(2)}, u32[]{:S(2)}) collective-permute-start(bf16[32,2048]{1,0:T(8,128)(2,1)S(1)} %get-tuple-element.141), channel_id=1, source_target_pairs={{0,2},{1,3},{2,0},{3,1},{4,6},{5,7},{6,4},{7,5},{8,10},{9,11},{10,... | collective-permute-start | bytes 393224 | tf_op jit(solution)/shard_map/ppermute | solution.py:40
  238.1 7.4 %collective-permute-start.31 = (bf16[32,2048]{1,0:T(8,128)(2,1)S(1)}, bf16[32,2048]{1,0:T(8,128)(2,1)S(1)}, u32[]{:S(2)}, u32[]{:S(2)}) collective-permute-start(bf16[32,2048]{1,0:T(8,128)(2,1)S(1)} %get-tuple-element.140), channel_id=1, source_target_pairs={{0,3},{1,2},{2,1},{3,0},{4,7},{5,6},{6,5},{7,4},{8,11},{9,10},{10,... | collective-permute-start | bytes 393224 | tf_op jit(solution)/shard_map/ppermute | solution.py:40
  239.2 16.6 %collective-permute-start.27 = (f32[512,128]{1,0:T(8,128)}, f32[512,128]{1,0:T(8,128)}, u32[]{:S(2)}, u32[]{:S(2)}) collective-permute-start(f32[512,128]{1,0:T(8,128)} %get-tuple-element.116), channel_id=1, source_target_pairs={{0,1},{1,0},{2,3},{3,2},{4,5},{5,4},{6,7},{7,6},{8,9},{9,8},{10,11... | collective-permute-start | bytes 786440 | tf_op jit(solution)/shard_map/ppermute | solution.py:40
  246.1 9.4 %copy-start.22 = (f32[512,128]{1,0:T(8,128)S(1)}, f32[512,128]{1,0:T(8,128)}, u32[]{:S(2)}) copy-start(f32[512,128]{1,0:T(8,128)} %get-tuple-element.111) | copy-start | bytes 786436
  250.8 39.6 %all-to-all-start.4 = ((bf16[8,512,128]{2,1,0:T(8,128)(2,1)}), bf16[8,512,128]{2,1,0:T(8,128)(2,1)S(1)}, u32[]{:S(2)}, u32[]{:S(2)}) async-start(bf16[8,512,128]{2,1,0:T(8,128)(2,1)} %bitcast.59), calls=%async_computation.4 | async-start | bytes 2097152 | tf_op jit(solution)/shard_map/all_to_all | solution.py:964
  255.5 14.8 %collective-permute-start.21 = (f32[512,128]{1,0:T(8,128)S(1)}, f32[512,128]{1,0:T(8,128)S(1)}, u32[]{:S(2)}, u32[]{:S(2)}) collective-permute-start(f32[512,128]{1,0:T(8,128)S(1)} %copy-done.22), channel_id=1, source_target_pairs={{0,1},{1,0},{2,3},{3,2},{4,5},{5,4},{6,7},{7,6},{8,9},{9,8},{10,11... | collective-permute-start | bytes 786440 | tf_op jit(solution)/shard_map/ppermute | solution.py:40
  256.9 19.0 %collective-permute-start.28 = (bf16[512,128]{1,0:T(8,128)(2,1)S(1)}, bf16[512,128]{1,0:T(8,128)(2,1)S(1)}, u32[]{:S(2)}, u32[]{:S(2)}) collective-permute-start(bf16[512,128]{1,0:T(8,128)(2,1)S(1)} %add_convert_fusion.2), channel_id=1, source_target_pairs={{0,2},{1,3},{2,0},{3,1},{4,6},{5,7},{6,4},{7,5},{8,10},{9,11},{10,... | collective-permute-start | bytes 393224 | tf_op jit(solution)/shard_map/ppermute | solution.py:40
  262.2 9.8 %collective-permute-start.25 = (f32[512,128]{1,0:T(8,128)}, f32[512,128]{1,0:T(8,128)S(1)}, u32[]{:S(2)}, u32[]{:S(2)}) collective-permute-start(f32[512,128]{1,0:T(8,128)} %get-tuple-element.104), channel_id=1, source_target_pairs={{0,1},{1,0},{2,3},{3,2},{4,5},{5,4},{6,7},{7,6},{8,9},{9,8},{10,11... | collective-permute-start | bytes 786440 | tf_op jit(solution)/shard_map/ppermute | solution.py:40
  262.2 9.8 %copy-start.23 = (f32[512,128]{1,0:T(8,128)S(1)}, f32[512,128]{1,0:T(8,128)}, u32[]{:S(2)}) copy-start(f32[512,128]{1,0:T(8,128)} %get-tuple-element.104) | copy-start | bytes 786436
  269.8 12.7 %copy-start.35 = (s32[128]{0:T(128)S(1)}, s32[128]{0:T(128)}, u32[]{:S(2)}) copy-start(s32[128]{0:T(128)} %copy-done.34) | copy-start | bytes 1540
  269.8 2.8 collective-permute-start.19
  270.4 6.4 %collective-permute-start.22 = (bf16[512,128]{1,0:T(8,128)(2,1)S(1)}, bf16[512,128]{1,0:T(8,128)(2,1)S(1)}, u32[]{:S(2)}, u32[]{:S(2)}) collective-permute-start(bf16[512,128]{1,0:T(8,128)(2,1)S(1)} %add_convert_fusion.4), channel_id=1, source_target_pairs={{0,2},{1,3},{2,0},{3,1},{4,6},{5,7},{6,4},{7,5},{8,10},{9,11},{10,... | collective-permute-start | bytes 393224 | tf_op jit(solution)/shard_map/ppermute | solution.py:40
  272.0 7.6 %collective-permute-start.26 = (bf16[512,128]{1,0:T(8,128)(2,1)S(1)}, bf16[512,128]{1,0:T(8,128)(2,1)S(1)}, u32[]{:S(2)}, u32[]{:S(2)}) collective-permute-start(bf16[512,128]{1,0:T(8,128)(2,1)S(1)} %add_convert_fusion.3), channel_id=1, source_target_pairs={{0,2},{1,3},{2,0},{3,1},{4,6},{5,7},{6,4},{7,5},{8,10},{9,11},{10,... | collective-permute-start | bytes 393224 | tf_op jit(solution)/shard_map/ppermute | solution.py:40
  273.6 8.9 %collective-permute-start.20 = (bf16[512,128]{1,0:T(8,128)(2,1)S(1)}, bf16[512,128]{1,0:T(8,128)(2,1)S(1)}, u32[]{:S(2)}, u32[]{:S(2)}) collective-permute-start(bf16[512,128]{1,0:T(8,128)(2,1)S(1)} %add_convert_fusion.5), channel_id=1, source_target_pairs={{0,2},{1,3},{2,0},{3,1},{4,6},{5,7},{6,4},{7,5},{8,10},{9,11},{10,... | collective-permute-start | bytes 393224 | tf_op jit(solution)/shard_map/ppermute | solution.py:40
  275.9 7.6 %collective-permute-start.32 = (bf16[32,1536]{1,0:T(8,128)(2,1)S(1)}, bf16[32,1536]{1,0:T(8,128)(2,1)S(1)}, u32[]{:S(2)}, u32[]{:S(2)}) collective-permute-start(bf16[32,1536]{1,0:T(8,128)(2,1)S(1)} %get-tuple-element.149), channel_id=1, source_target_pairs={{0,1},{1,0},{2,3},{3,2},{4,5},{5,4},{6,7},{7,6},{8,9},{9,8},{10,11... | collective-permute-start | bytes 294920 | tf_op jit(solution)/shard_map/ppermute | solution.py:40
  275.9 8.7 %collective-permute-start.33 = (bf16[32,1536]{1,0:T(8,128)(2,1)S(1)}, bf16[32,1536]{1,0:T(8,128)(2,1)S(1)}, u32[]{:S(2)}, u32[]{:S(2)}) collective-permute-start(bf16[32,1536]{1,0:T(8,128)(2,1)S(1)} %get-tuple-element.148), channel_id=1, source_target_pairs={{0,2},{1,3},{2,0},{3,1},{4,6},{5,7},{6,4},{7,5},{8,10},{9,11},{10,... | collective-permute-start | bytes 294920 | tf_op jit(solution)/shard_map/ppermute | solution.py:40
  276.8 8.0 %collective-permute-start.34 = (bf16[32,1536]{1,0:T(8,128)(2,1)S(1)}, bf16[32,1536]{1,0:T(8,128)(2,1)S(1)}, u32[]{:S(2)}, u32[]{:S(2)}) collective-permute-start(bf16[32,1536]{1,0:T(8,128)(2,1)S(1)} %get-tuple-element.147), channel_id=1, source_target_pairs={{0,3},{1,2},{2,1},{3,0},{4,7},{5,6},{6,5},{7,4},{8,11},{9,10},{10,... | collective-permute-start | bytes 294920 | tf_op jit(solution)/shard_map/ppermute | solution.py:40
  325.0 52.1 %all-to-all-start.6 = ((bf16[8,2,512,128]{3,2,1,0:T(8,128)(2,1)}), bf16[8,2,512,128]{3,2,1,0:T(8,128)(2,1)S(1)}, u32[]{:S(2)}, u32[]{:S(2)}) async-start(bf16[8,2,512,128]{3,2,1,0:T(8,128)(2,1)} %broadcast_in_dim.153), calls=%async_computation.6 | async-start | bytes 4194304 | tf_op jit(solution)/shard_map/all_to_all | solution.py:1097
  328.7 11.4 %copy-start.39 = (bf16[2,128,2048]{2,1,0:T(8,128)(2,1)S(1)}, bf16[2,128,2048]{2,1,0:T(8,128)(2,1)}, u32[]{:S(2)}) copy-start(bf16[2,128,2048]{2,1,0:T(8,128)(2,1)} %get-tuple-element.108) | copy-start | bytes 3145732
  340.1 7.5 %copy-start.9 = (f32[2,128,2048]{2,1,0:T(8,128)S(1)}, f32[2,128,2048]{2,1,0:T(8,128)}, u32[]{:S(2)}) copy-start(f32[2,128,2048]{2,1,0:T(8,128)} %get-tuple-element.107) | copy-start | bytes 6291460
  340.1 3.5 collective-permute-start.23
  340.1 7.5 %collective-permute-start.17 = (bf16[2,128,2048]{2,1,0:T(8,128)(2,1)S(1)}, bf16[2,128,2048]{2,1,0:T(8,128)(2,1)S(1)}, u32[]{:S(2)}, u32[]{:S(2)}) collective-permute-start(bf16[2,128,2048]{2,1,0:T(8,128)(2,1)S(1)} %copy-done.39), channel_id=1, source_target_pairs={{0,1},{1,0},{2,3},{3,2},{4,5},{5,4},{6,7},{7,6},{8,9},{9,8},{10,11... | collective-permute-start | bytes 3145736 | tf_op jit(solution)/shard_map/ppermute | solution.py:40
  346.1 15.1 %collective-permute-start.24 = (bf16[128,2048]{1,0:T(8,128)(2,1)}, bf16[128,2048]{1,0:T(8,128)(2,1)}, u32[]{:S(2)}, u32[]{:S(2)}) collective-permute-start(bf16[128,2048]{1,0:T(8,128)(2,1)} %fusion.8), channel_id=1, source_target_pairs={{0,2},{1,3},{2,0},{3,1},{4,6},{5,7},{6,4},{7,5},{8,10},{9,11},{10,... | collective-permute-start | bytes 1572872 | tf_op jit(solution)/shard_map/ppermute | solution.py:40
  348.7 22.9 %collective-permute-start.18 = (bf16[128,2048]{1,0:T(8,128)(2,1)}, bf16[128,2048]{1,0:T(8,128)(2,1)}, u32[]{:S(2)}, u32[]{:S(2)}) collective-permute-start(bf16[128,2048]{1,0:T(8,128)(2,1)} %fusion.7), channel_id=1, source_target_pairs={{0,2},{1,3},{2,0},{3,1},{4,6},{5,7},{6,4},{7,5},{8,10},{9,11},{10,... | collective-permute-start | bytes 1572872 | tf_op jit(solution)/shard_map/ppermute | solution.py:40
  352.0 19.6 %copy-start.10 = (f32[2,128,2048]{2,1,0:T(8,128)S(1)}, f32[2,128,2048]{2,1,0:T(8,128)}, u32[]{:S(2)}) copy-start(f32[2,128,2048]{2,1,0:T(8,128)} %get-tuple-element.107) | copy-start | bytes 6291460
  352.0 19.6 %copy-start.12 = (bf16[2,128,2048]{2,1,0:T(8,128)(2,1)S(1)}, bf16[2,128,2048]{2,1,0:T(8,128)(2,1)}, u32[]{:S(2)}) copy-start(bf16[2,128,2048]{2,1,0:T(8,128)(2,1)} %get-tuple-element.110) | copy-start | bytes 3145732
  (20 other events, 73.4 us)
Sparse Core Ops, SparseCore 0:
  23.8 62.0 all-gather.1

commit v4 on v3

--- a/solution.py
+++ b/solution.py
@@ -688,13 +688,20 @@
     def part_rows(value, which, size):
         return lax.dynamic_slice_in_dim(value, which * size, size, axis=0)
 
+    limit = 64
+    numbers = jnp.concatenate(
+        [doc_lengths // limit, doc_lengths % limit, doc_adapter], axis=1
+    ).astype(bf16)
+    numbers = jnp.pad(numbers, ((0, 15), (0, 128 - numbers.shape[1])))
+    first_pack = pack_small(index, [tokens[0], qkv_down], qkv_up, [0, 1, 2], numbers)
+
     def gather_rows(weight, size, kinds, *earlier):
         cuts = cut_columns(index, weight, size, kinds, [(2, contexts, 5), (3, contexts, 5)])
-        parts = [swap(after(cuts[0], *earlier), 2), swap(after(cuts[1], *earlier), 3)]
-        part = jnp.concatenate(parts, axis=1)
+        parts = [swap(cuts[0], 2), swap(cuts[1], 3)]
+        part = after(jnp.concatenate(parts, axis=1), *earlier)
         return part, lax.all_gather(part, "ctx", axis=0, tiled=True)
 
-    qkv_others_part, qkv_others = gather_rows(qkv_weight, own_width, [2, 1, 0])
+    qkv_others_part, qkv_others = gather_rows(qkv_weight, own_width, [2, 1, 0], *first_pack)
     in_cuts = cut_columns(
         index,
         in_weight,
@@ -704,13 +711,6 @@
         4,
     )
     in_parts = [swap(after(in_cuts[0], qkv_others_part), 2)]
-    limit = 64
-    numbers = jnp.concatenate(
-        [doc_lengths // limit, doc_lengths % limit, doc_adapter], axis=1
-    ).astype(bf16)
-    numbers = jnp.pad(numbers, ((0, 15), (0, 128 - numbers.shape[1])))
-    first_pack = pack_small(index, [tokens[0], qkv_down], qkv_up, [0, 1, 2], numbers)
-
     def hand_on(away, near, *earlier):
         peer = swap(after(away, *earlier), 2)
         return [swap(near, 1), peer, swap(peer, 1)]
@@ -1094,9 +1094,7 @@
     )[0]
     packed = exchange_sum(after(packed, feed_sum))
     packed = jnp.stack([feed_sum, packed])
-    packed = lax.all_to_all(
-        jnp.broadcast_to(packed[None], (contexts,) + packed.shape), "ctx", 0, 0, tiled=True
-    )
+    packed = lax.all_gather(packed, "ctx", axis=0)
     packed = after(packed, tokens_grad, output)
     block = (contexts, 1) + packed.shape[2:]
     out_down_grad, in_up_grad = call(

time: 394 us -> 383 us (0.972)
  waiting for transfers between devices: 120 us -> 115 us
    ppermute x35, waiting for transfers between devices: 106 us -> 100 us  [swap(): return lax.ppermute(value, 'wa', [(i, i ^ bits) for i in range(WA)])]
  transfers between devices with their start and end apart: 42 -> 42, of which waited for: 22 -> 21; matrix products, arithmetic and copies ran while one was open for 8% -> 8% of each run, Pallas kernels for 30% -> 31%
where the time goes in v4:
time: 383 us; the launch traced here: 382 us
  Pallas kernels  137 us (36%)
  waiting for transfers between devices  115 us (30%)
  starting transfers between devices  48.6 us (13%)
  blocking collectives  32.4 us (8%)
  other arithmetic  19.6 us (5%)
  between operations  14.5 us (4%)
  local copies, waits for them, and re-layouts  11.1 us (3%)
    pallas_call x19, Pallas kernels, call(): pl.pallas_call(kernel, grid_spec=pltpu.PrefetchScalarGridSpec(num_scalar_...  127 us
    ppermute x35, waiting for transfers between devices, swap(): return lax.ppermute(value, 'wa', [(i, i ^ bits) for i in range(WA)])  100 us
    all_to_all x1, blocking collectives, exchange_sum(): parts = lax.all_to_all(parts, 'ctx', 0, 0, tiled=True)  32.4 us
    ppermute x35, starting transfers between devices, swap(): return lax.ppermute(value, 'wa', [(i, i ^ bits) for i in range(WA)])  23.7 us
    all_to_all x4, starting transfers between devices, to_pairs(): return lax.all_to_all(item, 'ctx', 0, 0, tiled=True)  19.9 us
    all_to_all x4, waiting for transfers between devices, to_pairs(): return lax.all_to_all(item, 'ctx', 0, 0, tiled=True)  12.2 us
    pallas_call x1, Pallas kernels, attend(): pl.pallas_call(functools.partial(attention_kernel, joint), grid=(rows //...  9.96 us
  transfers between devices with their start and end apart: 42, of which 21 were waited for; matrix products, arithmetic and copies ran while one was open for 8% of the time, Pallas kernels for 31%

profile of v4, /device:TPU:0, one launch (start us, length us, event | category | flops | bytes accessed | tf_op | source)
XLA Modules:
  0.0 381.6 jit_solution(8577237031024440841)
XLA Ops:
  7.9 3.4 shard_map.313
  11.3 2.4 collective-permute-start.1
  16.4 3.3 shard_map.314
  19.7 3.9 %collective-permute-done = bf16[64,1536]{1,0:T(8,128)(2,1)S(1)} collective-permute-done((bf16[64,1536]{1,0:T(8,128)(2,1)}, bf16[64,1536]{1,0:T(8,128)(2,1)S(1)}, u32[]{:S(2)}, u32[]{:S(2)}) %collective-permute-start) | collective-permute-done | bytes 196640 | tf_op jit(solution)/shard_map/ppermute | solution.py:40
  24.4 2.4 collective-permute-start.4
  26.7 5.3 %shard_map.312 = (bf16[256,2048]{1,0:T(8,128)(2,1)}, bf16[256,2048]{1,0:T(8,128)(2,1)}, bf16[256,2048]{1,0:T(8,128)(2,1)}, bf16[256,2048]{1,0:T(8,128)(2,1)}) custom-call(s32[8]{0:T(128)} %stack.43.index_ref, bf16[512,8192]{1,0:T(8,128)(2,1)} %refs_0_.15, bf16[512,8192]{1,0:T(8,128)(2,1)} %refs_0_.15, bf16[512,8192]{1,0:T(8,128)(2,1)} %refs_0_.15, ...), custom_call_target="tpu_custom_call" | custom-call | bytes 4194304 | tf_op jit(solution)/shard_map/pallas_call | solution.py:91
  32.8 14.0 %collective-permute-done.4.refs_3_.refs_6_.refs_4_.refs_8_.refs_12_.refs_7_ = bf16[3344,128]{1,0:T(8,128)(2,1)S(1)} collective-permute-done((bf16[3344,128]{1,0:T(8,128)(2,1)}, bf16[3344,128]{1,0:T(8,128)(2,1)S(1)}, u32[]{:S(2)}, u32[]{:S(2)}) %collective-permute-start.4) | collective-permute-done | bytes 856096 | tf_op jit(solution)/shard_map/ppermute | solution.py:40
  46.8 2.1 collective-permute-start.8
  48.8 1.8 constant_dynamic-slice_fusion.10
  50.6 4.2 %shard_map.317 = bf16[512,1536]{1,0:T(8,128)(2,1)} custom-call(s32[8]{0:T(128)} %stack.43.index_ref, bf16[512,6144]{1,0:T(8,128)(2,1)} %refs_10_.5), custom_call_target="tpu_custom_call" | custom-call | bytes 1572864 | tf_op jit(solution)/shard_map/pallas_call | solution.py:91
  54.8 3.0 shard_map.315
  58.5 10.9 %collective-permute-done.2.refs_2_ = bf16[256,2048]{1,0:T(8,128)(2,1)} collective-permute-done((bf16[256,2048]{1,0:T(8,128)(2,1)}, bf16[256,2048]{1,0:T(8,128)(2,1)}, u32[]{:S(2)}, u32[]{:S(2)}) %collective-permute-start.2) | collective-permute-done | bytes 1048608 | tf_op jit(solution)/shard_map/ppermute | solution.py:40
  69.3 16.3 %collective-permute-done.8.refs_2_ = bf16[192,2048]{1,0:T(8,128)(2,1)} collective-permute-done((bf16[192,2048]{1,0:T(8,128)(2,1)S(1)}, bf16[192,2048]{1,0:T(8,128)(2,1)}, u32[]{:S(2)}, u32[]{:S(2)}) %collective-permute-start.8) | collective-permute-done | bytes 786464 | tf_op jit(solution)/shard_map/ppermute | solution.py:40
  85.7 1.7 collective-permute-start.10
  90.0 6.9 %shard_map.316 = (bf16[512,2048]{1,0:T(8,128)(2,1)}, bf16[512,2048]{1,0:T(8,128)(2,1)}, bf16[512,128]{1,0:T(8,128)(2,1)}) custom-call(s32[8]{0:T(128)} %stack.43.index_ref, bf16[128,2048]{1,0:T(8,128)(2,1)} %bitcast.58, bf16[512,128]{1,0:T(8,128)(2,1)} %refs_5_.3, bf16[3344,128]{1,0:T(8,128)(2,1)} %copy-done.2, bf16[3344,128]{1,0:T(8,128)(2,1)} %copy-done.1, ...), custom_call_target="tpu_custom_call" | custom-call | flops 268435456 | bytes 3518464 | tf_op jit(solution)/shard_map/pallas_call | solution.py:91
  97.0 7.0 %shard_map.318 = (bf16[512,2048]{1,0:T(8,128)(2,1)}, bf16[512,128]{1,0:T(8,128)(2,1)}, bf16[512,128]{1,0:T(8,128)(2,1)}, bf16[4,2,128,256]{3,2,1,0:T(8,128)(2,1)}, bf16[2,128,2048]{2,1,0:T(8,128)(2,1)}) custom-call(s32[8]{0:T(128)} %stack.43.index_ref, bf16[192,2048]{1,0:T(8,128)(2,1)} %copy-done.11, bf16[192,2048]{1,0:T(8,128)(2,1)} %collective-permute-done.7.refs_1_, ...), custom_call_target="tpu_custom_call" | custom-call | flops 1610612736 | bytes 5636096 | tf_op jit(solution)/shard_map/pallas_call | solution.py:91
  104.0 5.8 %all-to-all-start = ((bf16[8,128,256]{2,1,0:T(8,128)(2,1)}), bf16[8,128,256]{2,1,0:T(8,128)(2,1)S(1)}, u32[]{:S(2)}, u32[]{:S(2)}) async-start(bf16[8,128,256]{2,1,0:T(8,128)(2,1)} %bitcast.69), calls=%async_computation | async-start | bytes 1048576 | tf_op jit(solution)/shard_map/all_to_all | solution.py:815
  110.6 1.8 fusion.16
  112.4 5.2 %shard_map.320 = bf16[4,2,1,128,256]{4,3,2,1,0:T(8,128)(2,1)} custom-call(s32[8]{0:T(128)} %stack.43.index_ref, bf16[512,2048]{1,0:T(8,128)(2,1)} %get-tuple-element.82.hidden_ref.refs_0_, bf16[512,6144]{1,0:T(8,128)(2,1)} %refs_10_.5, bf16[512,1536]{1,0:T(8,128)(2,1)} %collective-permute-done.6.refs_1_.refs_3_.refs_7_.refs_11_, ...), custom_call_target="tpu_custom_call" | custom-call | flops 1073741824 | bytes 4981760 | tf_op jit(solution)/shard_map/pallas_call | solution.py:91
  117.7 7.3 %all-to-all-done = bf16[8,128,256]{2,1,0:T(8,128)(2,1)S(1)} async-done(((bf16[8,128,256]{2,1,0:T(8,128)(2,1)}), bf16[8,128,256]{2,1,0:T(8,128)(2,1)S(1)}, u32[]{:S(2)}, u32[]{:S(2)}) %all-to-all-start) | async-done | bytes 524320 | tf_op jit(solution)/shard_map/all_to_all | solution.py:815
  125.0 3.6 all-to-all-start.1
  128.6 3.3 shard_map.321
  131.9 7.8 %shard_map.319 = bf16[4,2,2,128,256]{4,3,2,1,0:T(8,128)(2,1)} custom-call(s32[8]{0:T(128)} %stack.43.index_ref, bf16[512,2048]{1,0:T(8,128)(2,1)} %get-tuple-element.82.hidden_ref.refs_0_, bf16[512,6144]{1,0:T(8,128)(2,1)} %refs_10_.5, bf16[512,1536]{1,0:T(8,128)(2,1)} %collective-permute-done.6.refs_1_.refs_3_.refs_7_.refs_11_, ...), custom_call_target="tpu_custom_call" | custom-call | flops 2147483648 | bytes 7211008 | tf_op jit(solution)/shard_map/pallas_call | solution.py:91
  139.8 3.5 all-to-all-done.1
  143.3 4.4 %all-to-all-start.2 = ((bf16[8,2,128,256]{3,2,1,0:T(8,128)(2,1)}), bf16[8,2,128,256]{3,2,1,0:T(8,128)(2,1)}, u32[]{:S(2)}, u32[]{:S(2)}) async-start(bf16[8,2,128,256]{3,2,1,0:T(8,128)(2,1)} %bitcast.60), calls=%async_computation.2 | async-start | bytes 2097152 | tf_op jit(solution)/shard_map/all_to_all | solution.py:815
  150.0 1.0 copy.42.begin_ref
  152.1 8.7 %collective-permute-done.15.refs_8_.refs_12_.refs_11_ = bf16[1552,128]{1,0:T(8,128)(2,1)S(1)} collective-permute-done((bf16[1552,128]{1,0:T(8,128)(2,1)}, bf16[1552,128]{1,0:T(8,128)(2,1)S(1)}, u32[]{:S(2)}, u32[]{:S(2)}) %collective-permute-start.15) | collective-permute-done | bytes 397344 | tf_op jit(solution)/shard_map/ppermute | solution.py:40
  161.4 3.1 fusion.5
  165.3 16.2 %collective-permute-done.12.refs_5_ = bf16[256,2048]{1,0:T(8,128)(2,1)} collective-permute-done((bf16[256,2048]{1,0:T(8,128)(2,1)}, bf16[256,2048]{1,0:T(8,128)(2,1)}, u32[]{:S(2)}, u32[]{:S(2)}) %collective-permute-start.12) | collective-permute-done | bytes 1048608 | tf_op jit(solution)/shard_map/ppermute | solution.py:40
  181.5 10.0 %shard_map.322 = bf16[8,4,128,256]{3,2,1,0:T(8,128)(2,1)} custom-call(bf16[8,2,128,256]{3,2,1,0:T(8,128)(2,1)} %all-to-all-done.2.query_ref.key_ref, bf16[8,2,128,256]{3,2,1,0:T(8,128)(2,1)} %all-to-all-done.2.query_ref.key_ref, bf16[1024,256]{1,0:T(8,128)(2,1)} %bitcast.68, bf16[1024,256]{1,0:T(8,128)(2,1)} %bitcast.67, s32[1024,1]{1,0:T(8,128)} %copy.42.begin_ref, ...), custom_call_target="tpu_custom_call" | custom-call | flops 3758096384 | bytes 4194304 | tf_op jit(solution)/shard_map/pallas_call | solution.py:616
  191.5 6.0 %all-to-all-start.3 = ((bf16[8,4,128,256]{3,2,1,0:T(8,128)(2,1)}), bf16[8,4,128,256]{3,2,1,0:T(8,128)(2,1)S(1)}, u32[]{:S(2)}, u32[]{:S(2)}) async-start(bf16[8,4,128,256]{3,2,1,0:T(8,128)(2,1)} %shard_map.322), calls=%async_computation.3 | async-start | bytes 4194304 | tf_op jit(solution)/shard_map/all_to_all | solution.py:815
  197.4 33.6 %shard_map.323 = (f32[512,2048]{1,0:T(8,128)}, f32[512,2048]{1,0:T(8,128)}, f32[512,128]{1,0:T(8,128)}, f32[512,128]{1,0:T(8,128)}, bf16[2048,128]{1,0:T(8,128)(...) custom-call(s32[8]{0:T(128)} %stack.43.index_ref, bf16[512,2048]{1,0:T(8,128)(2,1)} %get-tuple-element.102.hidden_ref.refs_2_, ...), custom_call_target="tpu_custom_call" | custom-call | flops 17179869184 | bytes 24129536 | tf_op jit(solution)/shard_map/pallas_call | solution.py:91
  231.1 1.8 constant_dynamic-slice_fusion.4
  233.5 1.2 collective-permute-start.31
  235.2 4.2 %collective-permute-done.30.refs_2_ = bf16[32,2048]{1,0:T(8,128)(2,1)S(1)} collective-permute-done((bf16[32,2048]{1,0:T(8,128)(2,1)S(1)}, bf16[32,2048]{1,0:T(8,128)(2,1)S(1)}, u32[]{:S(2)}, u32[]{:S(2)}) %collective-permute-start.30) | collective-permute-done | bytes 131104 | tf_op jit(solution)/shard_map/ppermute | solution.py:40
  239.3 1.7 collective-permute-done.31.refs_3_
  241.7 3.2 shard_map.328
  244.9 1.4 all-to-all-done.3
  246.3 4.8 %all-to-all-start.4 = ((bf16[8,512,128]{2,1,0:T(8,128)(2,1)}), bf16[8,512,128]{2,1,0:T(8,128)(2,1)S(1)}, u32[]{:S(2)}, u32[]{:S(2)}) async-start(bf16[8,512,128]{2,1,0:T(8,128)(2,1)} %bitcast.62), calls=%async_computation.4 | async-start | bytes 2097152 | tf_op jit(solution)/shard_map/all_to_all | solution.py:964
  251.6 1.1 add_convert_fusion.2
  253.3 4.7 %shard_map.324 = (f32[512,128]{1,0:T(8,128)}, bf16[128,1536]{1,0:T(8,128)(2,1)}) custom-call(s32[8]{0:T(128)} %stack.43.index_ref, bf16[4,2,4,128,256]{4,3,2,1,0:T(8,128)(2,1)} %bitcast.50, bf16[4,2,4,128,256]{4,3,2,1,0:T(8,128)(2,1)} %bitcast.51, bf16[32,6144]{1,0:T(8,128)(2,1)} %refs_10_.4, bf16[3344,128]{1,0:T(8,128)(2,1)} %copy-done.2, ...), custom_call_target="tpu_custom_call" | custom-call | flops 402653184 | bytes 4718592 | tf_op jit(solution)/shard_map/pallas_call | solution.py:91
  258.0 7.7 %shard_map.325 = (f32[2,128,2048]{2,1,0:T(8,128)}, bf16[2,128,2048]{2,1,0:T(8,128)(2,1)}, f32[512,128]{1,0:T(8,128)}, bf16[512,128]{1,0:T(8,128)(2,1)}) custom-call(s32[8]{0:T(128)} %stack.43.index_ref, bf16[4,2,4,128,256]{4,3,2,1,0:T(8,128)(2,1)} %bitcast.52, f32[512,2048]{1,0:T(8,128)} %get-tuple-element.104.sum_ref, bf16[512,2048]{1,0:T(8,128)(2,1)} %weight_ref.1, ...), custom_call_target="tpu_custom_call" | custom-call | flops 1073741824 | bytes 8650752 | tf_op jit(solution)/shard_map/pallas_call | solution.py:91
  266.2 1.6 collective-permute-start.22
  268.4 1.0 add_convert_fusion.5
  269.4 1.6 collective-permute-start.20
  273.5 1.9 collective-permute-done.26
  275.5 2.8 collective-permute-done.20
  279.2 1.1 collective-permute-done.33.refs_10_
  281.2 5.0 %shard_map.329 = bf16[4096,128]{1,0:T(8,128)(2,1)} custom-call(s32[8]{0:T(128)} %stack.43.index_ref, bf16[512,2048]{1,0:T(8,128)(2,1)} %get-tuple-element.82.hidden_ref.refs_0_, bf16[512,128]{1,0:T(8,128)(2,1)} %get-tuple-element.167.refs_1_, bf16[512,2048]{1,0:T(8,128)(2,1)} %get-tuple-element.102.hidden_ref.refs_2_, ...), custom_call_target="tpu_custom_call" | custom-call | bytes 4194304 | tf_op jit(solution)/shard_map/pallas_call | solution.py:91
  286.4 32.4 %all_to_all.30 = bf16[8,512,128]{2,1,0:T(8,128)(2,1)S(1)} all-to-all(bf16[8,512,128]{2,1,0:T(8,128)(2,1)} %bitcast.61), channel_id=1, replica_groups=mesh['ctx'=8,'wa'=4] {'ctx'}, dimensions={0} | all-to-all | bytes 2097152 | tf_op jit(solution)/shard_map/all_to_all | solution.py:964
  319.6 11.4 %shard_map.326 = (f32[2,128,2048]{2,1,0:T(8,128)}, bf16[2,128,2048]{2,1,0:T(8,128)(2,1)}) custom-call(s32[8]{0:T(128)} %stack.43.index_ref, bf16[4,2,4,128,256]{4,3,2,1,0:T(8,128)(2,1)} %bitcast.53, bf16[4,2,4,128,256]{4,3,2,1,0:T(8,128)(2,1)} %bitcast.54, bf16[512,6144]{1,0:T(8,128)(2,1)} %refs_10_.5, ...), custom_call_target="tpu_custom_call" | custom-call | flops 3221225472 | bytes 14688256 | tf_op jit(solution)/shard_map/pallas_call | solution.py:91
  331.6 3.0 collective-permute-done.23.refs_1_
  334.6 2.5 fusion.8
  337.1 1.5 collective-permute-start.24
  340.0 1.4 constant_dynamic-slice_fusion.9.refs_3_
  341.4 1.4 constant_dynamic-slice_fusion.8.refs_4_
  342.8 9.4 %collective-permute-done.24.refs_2_ = bf16[128,2048]{1,0:T(8,128)(2,1)} collective-permute-done((bf16[128,2048]{1,0:T(8,128)(2,1)}, bf16[128,2048]{1,0:T(8,128)(2,1)}, u32[]{:S(2)}, u32[]{:S(2)}) %collective-permute-start.24) | collective-permute-done | bytes 524320 | tf_op jit(solution)/shard_map/ppermute | solution.py:40
  352.2 5.6 %shard_map.327 = f32[128,2048]{1,0:T(8,128)} custom-call(s32[8]{0:T(128)} %stack.43.index_ref, f32[2,128,2048]{2,1,0:T(8,128)} %get-tuple-element.116.refs_0_, bf16[2,128,2048]{2,1,0:T(8,128)(2,1)} %copy-done.6, bf16[128,2048]{1,0:T(8,128)(2,1)} %collective-permute-done.24.refs_2_, bf16[128,128]{1,0:T(8,128)(2,1)} %constant_dynamic-slice_fusion.9.refs_3_, ...), custom_call_target="tpu_custom_call" | custom-call | bytes 5849088 | tf_op jit(solution)/shard_map/pallas_call | solution.py:91
  357.8 4.8 %collective-permute-done.18 = bf16[128,2048]{1,0:T(8,128)(2,1)} collective-permute-done((bf16[128,2048]{1,0:T(8,128)(2,1)}, bf16[128,2048]{1,0:T(8,128)(2,1)}, u32[]{:S(2)}, u32[]{:S(2)}) %collective-permute-start.18) | collective-permute-done | bytes 524320 | tf_op jit(solution)/shard_map/ppermute | solution.py:40
  362.6 1.3 convolution_add_fusion.1
  364.0 1.9 fusion.4
  365.9 2.2 all-gather.6.cloned.1.call-done
  368.1 3.3 shard_map.330
  371.4 3.4 shard_map.331
  (172 shorter events, 25.2 us)
Async XLA Ops:
  7.2 105.3 %all-gather.4.cloned.1.call-start = ((), (), s32[]{:S(2)}) async-start(), calls=%async_computation.6 | async-start | bytes 3538944 | tf_op jit(solution)/shard_map/all_gather | solution.py:702
  7.9 7.1 %copy-start.4 = (bf16[32,6144]{1,0:T(8,128)(2,1)S(1)}, bf16[32,6144]{1,0:T(8,128)(2,1)}, u32[]{:S(2)}) copy-start(bf16[32,6144]{1,0:T(8,128)(2,1)} %refs_10_.4) | copy-start | bytes 1179652
  11.3 8.4 %collective-permute-start.1 = (bf16[64,1536]{1,0:T(8,128)(2,1)}, bf16[64,1536]{1,0:T(8,128)(2,1)S(1)}, u32[]{:S(2)}, u32[]{:S(2)}) collective-permute-start(bf16[64,1536]{1,0:T(8,128)(2,1)} %get-tuple-element.74), channel_id=1, source_target_pairs={{0,3},{1,2},{2,1},{3,0},{4,7},{5,6},{6,5},{7,4},{8,11},{9,10},{10,... | collective-permute-start | bytes 589832 | tf_op jit(solution)/shard_map/ppermute | solution.py:40
  13.6 9.9 %collective-permute-start = (bf16[64,1536]{1,0:T(8,128)(2,1)}, bf16[64,1536]{1,0:T(8,128)(2,1)S(1)}, u32[]{:S(2)}, u32[]{:S(2)}) collective-permute-start(bf16[64,1536]{1,0:T(8,128)(2,1)} %get-tuple-element.73), channel_id=1, source_target_pairs={{0,2},{1,3},{2,0},{3,1},{4,6},{5,7},{6,4},{7,5},{8,10},{9,11},{10,... | collective-permute-start | bytes 589832 | tf_op jit(solution)/shard_map/ppermute | solution.py:40
  24.3 7.9 %copy-start.7 = (bf16[1,128,2048]{2,1,0:T(8,128)(2,1)S(1)}, bf16[1,128,2048]{2,1,0:T(8,128)(2,1)}, u32[]{:S(2)}) copy-start(bf16[1,128,2048]{2,1,0:T(8,128)(2,1)} %param.26) | copy-start | bytes 1572868
  24.3 7.9 %copy-start.20 = (bf16[32,2048]{1,0:T(8,128)(2,1)S(1)}, bf16[32,2048]{1,0:T(8,128)(2,1)}, u32[]{:S(2)}) copy-start(bf16[32,2048]{1,0:T(8,128)(2,1)} %param.49) | copy-start | bytes 393220
  24.3 7.9 %copy-start.21 = (bf16[32,2048]{1,0:T(8,128)(2,1)S(1)}, bf16[32,2048]{1,0:T(8,128)(2,1)}, u32[]{:S(2)}) copy-start(bf16[32,2048]{1,0:T(8,128)(2,1)} %param.45) | copy-start | bytes 393220
  24.4 22.4 %collective-permute-start.4 = (bf16[3344,128]{1,0:T(8,128)(2,1)}, bf16[3344,128]{1,0:T(8,128)(2,1)S(1)}, u32[]{:S(2)}, u32[]{:S(2)}) collective-permute-start(bf16[3344,128]{1,0:T(8,128)(2,1)} %get-tuple-element.75), channel_id=1, source_target_pairs={{0,2},{1,3},{2,0},{3,1},{4,6},{5,7},{6,4},{7,5},{8,10},{9,11},{10,... | collective-permute-start | bytes 2568200 | tf_op jit(solution)/shard_map/ppermute | solution.py:40
  26.7 31.2 %collective-permute-start.3 = (bf16[3344,128]{1,0:T(8,128)(2,1)}, bf16[3344,128]{1,0:T(8,128)(2,1)S(1)}, u32[]{:S(2)}, u32[]{:S(2)}) collective-permute-start(bf16[3344,128]{1,0:T(8,128)(2,1)} %get-tuple-element.76), channel_id=1, source_target_pairs={{0,1},{1,0},{2,3},{3,2},{4,5},{5,4},{6,7},{7,6},{8,9},{9,8},{10,11... | collective-permute-start | bytes 2568200 | tf_op jit(solution)/shard_map/ppermute | solution.py:40
  32.1 37.3 %collective-permute-start.2 = (bf16[256,2048]{1,0:T(8,128)(2,1)}, bf16[256,2048]{1,0:T(8,128)(2,1)}, u32[]{:S(2)}, u32[]{:S(2)}) collective-permute-start(bf16[256,2048]{1,0:T(8,128)(2,1)} %get-tuple-element.78), channel_id=1, source_target_pairs={{0,2},{1,3},{2,0},{3,1},{4,6},{5,7},{6,4},{7,5},{8,10},{9,11},{10,... | collective-permute-start | bytes 3145736 | tf_op jit(solution)/shard_map/ppermute | solution.py:40
  32.3 22.5 %copy-start.11 = (bf16[192,2048]{1,0:T(8,128)(2,1)}, bf16[192,2048]{1,0:T(8,128)(2,1)S(1)}, u32[]{:S(2)}) copy-start(bf16[192,2048]{1,0:T(8,128)(2,1)S(1)} %pad_maximum_fusion.refs_0_) | copy-start | bytes 2359300
  32.3 64.6 %collective-permute-start.7 = (bf16[192,2048]{1,0:T(8,128)(2,1)S(1)}, bf16[192,2048]{1,0:T(8,128)(2,1)}, u32[]{:S(2)}, u32[]{:S(2)}) collective-permute-start(bf16[192,2048]{1,0:T(8,128)(2,1)S(1)} %pad_maximum_fusion.refs_0_), channel_id=1, source_target_pairs={{0,1},{1,0},{2,3},{3,2},{4,5},{5,4},{6,7},{7,6},{8,9},{9,8},{10,11... | collective-permute-start | bytes 2359304 | tf_op jit(solution)/shard_map/ppermute | solution.py:40
  46.8 40.7 %copy-start.1 = (bf16[3344,128]{1,0:T(8,128)(2,1)}, bf16[3344,128]{1,0:T(8,128)(2,1)S(1)}, u32[]{:S(2)}) copy-start(bf16[3344,128]{1,0:T(8,128)(2,1)S(1)} %collective-permute-done.4.refs_3_.refs_6_.refs_4_.refs_8_.refs_12_.refs_7_) | copy-start | bytes 2568196
  46.8 38.9 %collective-permute-start.8 = (bf16[192,2048]{1,0:T(8,128)(2,1)S(1)}, bf16[192,2048]{1,0:T(8,128)(2,1)}, u32[]{:S(2)}, u32[]{:S(2)}) collective-permute-start(bf16[192,2048]{1,0:T(8,128)(2,1)S(1)} %pad_maximum_fusion.refs_0_), channel_id=1, source_target_pairs={{0,2},{1,3},{2,0},{3,1},{4,6},{5,7},{6,4},{7,5},{8,10},{9,11},{10,... | collective-permute-start | bytes 2359304 | tf_op jit(solution)/shard_map/ppermute | solution.py:40
  48.8 38.6 %collective-permute-start.5 = (bf16[3344,128]{1,0:T(8,128)(2,1)S(1)}, bf16[3344,128]{1,0:T(8,128)(2,1)S(1)}, u32[]{:S(2)}, u32[]{:S(2)}) collective-permute-start(bf16[3344,128]{1,0:T(8,128)(2,1)S(1)} %collective-permute-done.4.refs_3_.refs_6_.refs_4_.refs_8_.refs_12_.refs_7_), channel_id=1, source_target_pairs={{0,1},{1,0},{2,3},{3,2},{4,5},{5,4},{6,7},{7,6},{8,9},{9,8},{10,11... | collective-permute-start | bytes 2568200 | tf_op jit(solution)/shard_map/ppermute | solution.py:40
  50.6 7.2 %copy-start.33 = (s32[16]{0:T(128)S(1)}, s32[16]{0:T(128)}, u32[]{:S(2)}) copy-start(s32[16]{0:T(128)} %param.27) | copy-start | bytes 196
  57.8 46.2 %copy-start.30 = (s32[128]{0:T(128)}, s32[128]{0:T(128)S(1)}, u32[]{:S(2)}) copy-start(s32[128]{0:T(128)S(1)} %and_select_fusion.4) | copy-start | bytes 1540
  58.0 32.1 %copy-start.2 = (bf16[3344,128]{1,0:T(8,128)(2,1)}, bf16[3344,128]{1,0:T(8,128)(2,1)S(1)}, u32[]{:S(2)}) copy-start(bf16[3344,128]{1,0:T(8,128)(2,1)S(1)} %collective-permute-done.3.refs_2_.refs_5_.refs_3_.refs_7_.refs_11_.refs_6_) | copy-start | bytes 2568196
  58.0 54.5 %collective-permute-start.6 = (bf16[512,1536]{1,0:T(8,128)(2,1)}, bf16[512,1536]{1,0:T(8,128)(2,1)}, u32[]{:S(2)}, u32[]{:S(2)}) collective-permute-start(bf16[512,1536]{1,0:T(8,128)(2,1)} %shard_map.317), channel_id=1, source_target_pairs={{0,1},{1,0},{2,3},{3,2},{4,5},{5,4},{6,7},{7,6},{8,9},{9,8},{10,11... | collective-permute-start | bytes 4718600 | tf_op jit(solution)/shard_map/ppermute | solution.py:40
  85.7 25.0 %collective-permute-start.10 = (bf16[256,2048]{1,0:T(8,128)(2,1)}, bf16[256,2048]{1,0:T(8,128)(2,1)}, u32[]{:S(2)}, u32[]{:S(2)}) collective-permute-start(bf16[256,2048]{1,0:T(8,128)(2,1)} %get-tuple-element.93), channel_id=1, source_target_pairs={{0,2},{1,3},{2,0},{3,1},{4,6},{5,7},{6,4},{7,5},{8,10},{9,11},{10,... | collective-permute-start | bytes 3145736 | tf_op jit(solution)/shard_map/ppermute | solution.py:40
  87.4 9.6 %collective-permute-start.9 = (bf16[192,2048]{1,0:T(8,128)(2,1)}, bf16[192,2048]{1,0:T(8,128)(2,1)}, u32[]{:S(2)}, u32[]{:S(2)}) collective-permute-start(bf16[192,2048]{1,0:T(8,128)(2,1)} %collective-permute-done.8.refs_2_), channel_id=1, source_target_pairs={{0,1},{1,0},{2,3},{3,2},{4,5},{5,4},{6,7},{7,6},{8,9},{9,8},{10,11... | collective-permute-start | bytes 2359304 | tf_op jit(solution)/shard_map/ppermute | solution.py:40
  104.0 21.0 %all-to-all-start = ((bf16[8,128,256]{2,1,0:T(8,128)(2,1)}), bf16[8,128,256]{2,1,0:T(8,128)(2,1)S(1)}, u32[]{:S(2)}, u32[]{:S(2)}) async-start(bf16[8,128,256]{2,1,0:T(8,128)(2,1)} %bitcast.69), calls=%async_computation | async-start | bytes 1048576 | tf_op jit(solution)/shard_map/all_to_all | solution.py:815
  110.6 29.1 %collective-permute-start.11 = (bf16[256,2048]{1,0:T(8,128)(2,1)}, bf16[256,2048]{1,0:T(8,128)(2,1)}, u32[]{:S(2)}, u32[]{:S(2)}) collective-permute-start(bf16[256,2048]{1,0:T(8,128)(2,1)} %get-tuple-element.94), channel_id=1, source_target_pairs={{0,3},{1,2},{2,1},{3,0},{4,7},{5,6},{6,5},{7,4},{8,11},{9,10},{10,... | collective-permute-start | bytes 3145736 | tf_op jit(solution)/shard_map/ppermute | solution.py:40
  125.0 18.3 %all-to-all-start.1 = ((bf16[8,1,128,256]{3,2,1,0:T(8,128)(2,1)}), bf16[8,1,128,256]{3,2,1,0:T(8,128)(2,1)S(1)}, u32[]{:S(2)}, u32[]{:S(2)}) async-start(bf16[8,1,128,256]{3,2,1,0:T(8,128)(2,1)} %bitcast.65), calls=%async_computation.1 | async-start | bytes 1048576 | tf_op jit(solution)/shard_map/all_to_all | solution.py:815
  131.9 11.4 %copy-start.9 = (bf16[512,2048]{1,0:T(8,128)(2,1)S(1)}, bf16[512,2048]{1,0:T(8,128)(2,1)}, u32[]{:S(2)}) copy-start(bf16[512,2048]{1,0:T(8,128)(2,1)} %shard_map.321) | copy-start | bytes 6291460
  139.7 8.6 %copy-start.34 = (s32[16]{0:T(128)S(1)}, s32[16]{0:T(128)}, u32[]{:S(2)}) copy-start(s32[16]{0:T(128)} %param.27) | copy-start | bytes 196
  139.8 10.1 %copy-start.32 = (s32[16]{0:T(128)S(1)}, s32[16]{0:T(128)}, u32[]{:S(2)}) copy-start(s32[16]{0:T(128)} %get-tuple-element.136) | copy-start | bytes 196
  143.3 7.7 %copy-start.13 = (bf16[8,1,128,256]{3,2,1,0:T(8,128)(2,1)}, bf16[8,1,128,256]{3,2,1,0:T(8,128)(2,1)S(1)}, u32[]{:S(2)}) copy-start(bf16[8,1,128,256]{3,2,1,0:T(8,128)(2,1)S(1)} %all-to-all-done.1) | copy-start | bytes 1572868
  143.3 38.2 %collective-permute-start.13 = (bf16[512,2048]{1,0:T(8,128)(2,1)S(1)}, bf16[512,2048]{1,0:T(8,128)(2,1)}, u32[]{:S(2)}, u32[]{:S(2)}) collective-permute-start(bf16[512,2048]{1,0:T(8,128)(2,1)S(1)} %copy-done.9), channel_id=1, source_target_pairs={{0,1},{1,0},{2,3},{3,2},{4,5},{5,4},{6,7},{7,6},{8,9},{9,8},{10,11... | collective-permute-start | bytes 6291464 | tf_op jit(solution)/shard_map/ppermute | solution.py:40
  143.3 38.2 %all-to-all-start.2 = ((bf16[8,2,128,256]{3,2,1,0:T(8,128)(2,1)}), bf16[8,2,128,256]{3,2,1,0:T(8,128)(2,1)}, u32[]{:S(2)}, u32[]{:S(2)}) async-start(bf16[8,2,128,256]{3,2,1,0:T(8,128)(2,1)} %bitcast.60), calls=%async_computation.2 | async-start | bytes 2097152 | tf_op jit(solution)/shard_map/all_to_all | solution.py:815
  147.8 16.7 %collective-permute-start.14 = (bf16[1552,128]{1,0:T(8,128)(2,1)}, bf16[1552,128]{1,0:T(8,128)(2,1)S(1)}, u32[]{:S(2)}, u32[]{:S(2)}) collective-permute-start(bf16[1552,128]{1,0:T(8,128)(2,1)} %get-tuple-element.80), channel_id=1, source_target_pairs={{0,1},{1,0},{2,3},{3,2},{4,5},{5,4},{6,7},{7,6},{8,9},{9,8},{10,11... | collective-permute-start | bytes 1191944 | tf_op jit(solution)/shard_map/ppermute | solution.py:40
  148.4 12.3 %collective-permute-start.15 = (bf16[1552,128]{1,0:T(8,128)(2,1)}, bf16[1552,128]{1,0:T(8,128)(2,1)S(1)}, u32[]{:S(2)}, u32[]{:S(2)}) collective-permute-start(bf16[1552,128]{1,0:T(8,128)(2,1)} %get-tuple-element.99), channel_id=1, source_target_pairs={{0,2},{1,3},{2,0},{3,1},{4,6},{5,7},{6,4},{7,5},{8,10},{9,11},{10,... | collective-permute-start | bytes 1191944 | tf_op jit(solution)/shard_map/ppermute | solution.py:40
  149.0 32.5 %collective-permute-start.12 = (bf16[256,2048]{1,0:T(8,128)(2,1)}, bf16[256,2048]{1,0:T(8,128)(2,1)}, u32[]{:S(2)}, u32[]{:S(2)}) collective-permute-start(bf16[256,2048]{1,0:T(8,128)(2,1)} %get-tuple-element.97), channel_id=1, source_target_pairs={{0,3},{1,2},{2,1},{3,0},{4,7},{5,6},{6,5},{7,4},{8,11},{9,10},{10,... | collective-permute-start | bytes 3145736 | tf_op jit(solution)/shard_map/ppermute | solution.py:40
  160.8 30.7 %copy-start.15 = (bf16[1552,128]{1,0:T(8,128)(2,1)}, bf16[1552,128]{1,0:T(8,128)(2,1)S(1)}, u32[]{:S(2)}) copy-start(bf16[1552,128]{1,0:T(8,128)(2,1)S(1)} %collective-permute-done.15.refs_8_.refs_12_.refs_11_) | copy-start | bytes 1191940
  160.8 3.7 collective-permute-start.16
  164.5 27.0 %copy-start.14 = (bf16[1552,128]{1,0:T(8,128)(2,1)}, bf16[1552,128]{1,0:T(8,128)(2,1)S(1)}, u32[]{:S(2)}) copy-start(bf16[1552,128]{1,0:T(8,128)(2,1)S(1)} %collective-permute-done.14.refs_7_.refs_11_.refs_10_) | copy-start | bytes 1191940
  191.5 54.8 %all-to-all-start.3 = ((bf16[8,4,128,256]{3,2,1,0:T(8,128)(2,1)}), bf16[8,4,128,256]{3,2,1,0:T(8,128)(2,1)S(1)}, u32[]{:S(2)}, u32[]{:S(2)}) async-start(bf16[8,4,128,256]{3,2,1,0:T(8,128)(2,1)} %shard_map.322), calls=%async_computation.3 | async-start | bytes 4194304 | tf_op jit(solution)/shard_map/all_to_all | solution.py:815
  232.9 2.3 collective-permute-start.29
  233.0 6.3 %collective-permute-start.30 = (bf16[32,2048]{1,0:T(8,128)(2,1)S(1)}, bf16[32,2048]{1,0:T(8,128)(2,1)S(1)}, u32[]{:S(2)}, u32[]{:S(2)}) collective-permute-start(bf16[32,2048]{1,0:T(8,128)(2,1)S(1)} %get-tuple-element.143), channel_id=1, source_target_pairs={{0,2},{1,3},{2,0},{3,1},{4,6},{5,7},{6,4},{7,5},{8,10},{9,11},{10,... | collective-permute-start | bytes 393224 | tf_op jit(solution)/shard_map/ppermute | solution.py:40
  233.5 7.5 %collective-permute-start.31 = (bf16[32,2048]{1,0:T(8,128)(2,1)S(1)}, bf16[32,2048]{1,0:T(8,128)(2,1)S(1)}, u32[]{:S(2)}, u32[]{:S(2)}) collective-permute-start(bf16[32,2048]{1,0:T(8,128)(2,1)S(1)} %get-tuple-element.142), channel_id=1, source_target_pairs={{0,3},{1,2},{2,1},{3,0},{4,7},{5,6},{6,5},{7,4},{8,11},{9,10},{10,... | collective-permute-start | bytes 393224 | tf_op jit(solution)/shard_map/ppermute | solution.py:40
  234.7 16.9 %collective-permute-start.27 = (f32[512,128]{1,0:T(8,128)}, f32[512,128]{1,0:T(8,128)}, u32[]{:S(2)}, u32[]{:S(2)}) collective-permute-start(f32[512,128]{1,0:T(8,128)} %get-tuple-element.118), channel_id=1, source_target_pairs={{0,1},{1,0},{2,3},{3,2},{4,5},{5,4},{6,7},{7,6},{8,9},{9,8},{10,11... | collective-permute-start | bytes 786440 | tf_op jit(solution)/shard_map/ppermute | solution.py:40
  241.7 9.6 %copy-start.18 = (f32[512,128]{1,0:T(8,128)S(1)}, f32[512,128]{1,0:T(8,128)}, u32[]{:S(2)}) copy-start(f32[512,128]{1,0:T(8,128)} %get-tuple-element.113) | copy-start | bytes 786436
  246.3 7.0 %copy-start = (bf16[8,4,128,256]{3,2,1,0:T(8,128)(2,1)}, bf16[8,4,128,256]{3,2,1,0:T(8,128)(2,1)S(1)}, u32[]{:S(2)}) copy-start(bf16[8,4,128,256]{3,2,1,0:T(8,128)(2,1)S(1)} %all-to-all-done.3) | copy-start | bytes 6291460
  246.3 39.9 %all-to-all-start.4 = ((bf16[8,512,128]{2,1,0:T(8,128)(2,1)}), bf16[8,512,128]{2,1,0:T(8,128)(2,1)S(1)}, u32[]{:S(2)}, u32[]{:S(2)}) async-start(bf16[8,512,128]{2,1,0:T(8,128)(2,1)} %bitcast.62), calls=%async_computation.4 | async-start | bytes 2097152 | tf_op jit(solution)/shard_map/all_to_all | solution.py:964
  251.0 117.1 %all-gather.6.cloned.1.call-start = ((), (), s32[]{:S(2)}) async-start(), calls=%async_computation.7 | async-start | bytes 2359296 | tf_op jit(solution)/shard_map/all_gather | solution.py:1097
  251.3 14.9 %collective-permute-start.21 = (f32[512,128]{1,0:T(8,128)S(1)}, f32[512,128]{1,0:T(8,128)S(1)}, u32[]{:S(2)}, u32[]{:S(2)}) collective-permute-start(f32[512,128]{1,0:T(8,128)S(1)} %copy-done.18), channel_id=1, source_target_pairs={{0,1},{1,0},{2,3},{3,2},{4,5},{5,4},{6,7},{7,6},{8,9},{9,8},{10,11... | collective-permute-start | bytes 786440 | tf_op jit(solution)/shard_map/ppermute | solution.py:40
  252.7 19.0 %collective-permute-start.28 = (bf16[512,128]{1,0:T(8,128)(2,1)S(1)}, bf16[512,128]{1,0:T(8,128)(2,1)S(1)}, u32[]{:S(2)}, u32[]{:S(2)}) collective-permute-start(bf16[512,128]{1,0:T(8,128)(2,1)S(1)} %add_convert_fusion.2), channel_id=1, source_target_pairs={{0,2},{1,3},{2,0},{3,1},{4,6},{5,7},{6,4},{7,5},{8,10},{9,11},{10,... | collective-permute-start | bytes 393224 | tf_op jit(solution)/shard_map/ppermute | solution.py:40
  257.9 9.9 %collective-permute-start.25 = (f32[512,128]{1,0:T(8,128)}, f32[512,128]{1,0:T(8,128)S(1)}, u32[]{:S(2)}, u32[]{:S(2)}) collective-permute-start(f32[512,128]{1,0:T(8,128)} %get-tuple-element.106), channel_id=1, source_target_pairs={{0,1},{1,0},{2,3},{3,2},{4,5},{5,4},{6,7},{7,6},{8,9},{9,8},{10,11... | collective-permute-start | bytes 786440 | tf_op jit(solution)/shard_map/ppermute | solution.py:40
  258.0 9.8 %copy-start.19 = (f32[512,128]{1,0:T(8,128)S(1)}, f32[512,128]{1,0:T(8,128)}, u32[]{:S(2)}) copy-start(f32[512,128]{1,0:T(8,128)} %get-tuple-element.106) | copy-start | bytes 786436
  265.6 12.7 %copy-start.31 = (s32[128]{0:T(128)S(1)}, s32[128]{0:T(128)}, u32[]{:S(2)}) copy-start(s32[128]{0:T(128)} %copy-done.30) | copy-start | bytes 1540
  265.6 2.8 collective-permute-start.19
  266.2 6.4 %collective-permute-start.22 = (bf16[512,128]{1,0:T(8,128)(2,1)S(1)}, bf16[512,128]{1,0:T(8,128)(2,1)S(1)}, u32[]{:S(2)}, u32[]{:S(2)}) collective-permute-start(bf16[512,128]{1,0:T(8,128)(2,1)S(1)} %add_convert_fusion.4), channel_id=1, source_target_pairs={{0,2},{1,3},{2,0},{3,1},{4,6},{5,7},{6,4},{7,5},{8,10},{9,11},{10,... | collective-permute-start | bytes 393224 | tf_op jit(solution)/shard_map/ppermute | solution.py:40
  267.8 7.6 %collective-permute-start.26 = (bf16[512,128]{1,0:T(8,128)(2,1)S(1)}, bf16[512,128]{1,0:T(8,128)(2,1)S(1)}, u32[]{:S(2)}, u32[]{:S(2)}) collective-permute-start(bf16[512,128]{1,0:T(8,128)(2,1)S(1)} %add_convert_fusion.3), channel_id=1, source_target_pairs={{0,2},{1,3},{2,0},{3,1},{4,6},{5,7},{6,4},{7,5},{8,10},{9,11},{10,... | collective-permute-start | bytes 393224 | tf_op jit(solution)/shard_map/ppermute | solution.py:40
  269.4 8.9 %collective-permute-start.20 = (bf16[512,128]{1,0:T(8,128)(2,1)S(1)}, bf16[512,128]{1,0:T(8,128)(2,1)S(1)}, u32[]{:S(2)}, u32[]{:S(2)}) collective-permute-start(bf16[512,128]{1,0:T(8,128)(2,1)S(1)} %add_convert_fusion.5), channel_id=1, source_target_pairs={{0,2},{1,3},{2,0},{3,1},{4,6},{5,7},{6,4},{7,5},{8,10},{9,11},{10,... | collective-permute-start | bytes 393224 | tf_op jit(solution)/shard_map/ppermute | solution.py:40
  271.7 7.6 %collective-permute-start.32 = (bf16[32,1536]{1,0:T(8,128)(2,1)S(1)}, bf16[32,1536]{1,0:T(8,128)(2,1)S(1)}, u32[]{:S(2)}, u32[]{:S(2)}) collective-permute-start(bf16[32,1536]{1,0:T(8,128)(2,1)S(1)} %get-tuple-element.151), channel_id=1, source_target_pairs={{0,1},{1,0},{2,3},{3,2},{4,5},{5,4},{6,7},{7,6},{8,9},{9,8},{10,11... | collective-permute-start | bytes 294920 | tf_op jit(solution)/shard_map/ppermute | solution.py:40
  271.7 8.7 %collective-permute-start.33 = (bf16[32,1536]{1,0:T(8,128)(2,1)S(1)}, bf16[32,1536]{1,0:T(8,128)(2,1)S(1)}, u32[]{:S(2)}, u32[]{:S(2)}) collective-permute-start(bf16[32,1536]{1,0:T(8,128)(2,1)S(1)} %get-tuple-element.150), channel_id=1, source_target_pairs={{0,2},{1,3},{2,0},{3,1},{4,6},{5,7},{6,4},{7,5},{8,10},{9,11},{10,... | collective-permute-start | bytes 294920 | tf_op jit(solution)/shard_map/ppermute | solution.py:40
  272.6 8.0 %collective-permute-start.34 = (bf16[32,1536]{1,0:T(8,128)(2,1)S(1)}, bf16[32,1536]{1,0:T(8,128)(2,1)S(1)}, u32[]{:S(2)}, u32[]{:S(2)}) collective-permute-start(bf16[32,1536]{1,0:T(8,128)(2,1)S(1)} %get-tuple-element.149), channel_id=1, source_target_pairs={{0,3},{1,2},{2,1},{3,0},{4,7},{5,6},{6,5},{7,4},{8,11},{9,10},{10,... | collective-permute-start | bytes 294920 | tf_op jit(solution)/shard_map/ppermute | solution.py:40
  319.6 11.5 %copy-start.35 = (bf16[2,128,2048]{2,1,0:T(8,128)(2,1)S(1)}, bf16[2,128,2048]{2,1,0:T(8,128)(2,1)}, u32[]{:S(2)}) copy-start(bf16[2,128,2048]{2,1,0:T(8,128)(2,1)} %get-tuple-element.110) | copy-start | bytes 3145732
  331.1 7.5 %copy-start.8 = (f32[2,128,2048]{2,1,0:T(8,128)S(1)}, f32[2,128,2048]{2,1,0:T(8,128)}, u32[]{:S(2)}) copy-start(f32[2,128,2048]{2,1,0:T(8,128)} %get-tuple-element.109) | copy-start | bytes 6291460
  331.1 3.5 collective-permute-start.23
  331.1 7.5 %collective-permute-start.17 = (bf16[2,128,2048]{2,1,0:T(8,128)(2,1)S(1)}, bf16[2,128,2048]{2,1,0:T(8,128)(2,1)S(1)}, u32[]{:S(2)}, u32[]{:S(2)}) collective-permute-start(bf16[2,128,2048]{2,1,0:T(8,128)(2,1)S(1)} %copy-done.35), channel_id=1, source_target_pairs={{0,1},{1,0},{2,3},{3,2},{4,5},{5,4},{6,7},{7,6},{8,9},{9,8},{10,11... | collective-permute-start | bytes 3145736 | tf_op jit(solution)/shard_map/ppermute | solution.py:40
  337.1 15.1 %collective-permute-start.24 = (bf16[128,2048]{1,0:T(8,128)(2,1)}, bf16[128,2048]{1,0:T(8,128)(2,1)}, u32[]{:S(2)}, u32[]{:S(2)}) collective-permute-start(bf16[128,2048]{1,0:T(8,128)(2,1)} %fusion.8), channel_id=1, source_target_pairs={{0,2},{1,3},{2,0},{3,1},{4,6},{5,7},{6,4},{7,5},{8,10},{9,11},{10,... | collective-permute-start | bytes 1572872 | tf_op jit(solution)/shard_map/ppermute | solution.py:40
  339.5 23.1 %collective-permute-start.18 = (bf16[128,2048]{1,0:T(8,128)(2,1)}, bf16[128,2048]{1,0:T(8,128)(2,1)}, u32[]{:S(2)}, u32[]{:S(2)}) collective-permute-start(bf16[128,2048]{1,0:T(8,128)(2,1)} %fusion.7), channel_id=1, source_target_pairs={{0,2},{1,3},{2,0},{3,1},{4,6},{5,7},{6,4},{7,5},{8,10},{9,11},{10,... | collective-permute-start | bytes 1572872 | tf_op jit(solution)/shard_map/ppermute | solution.py:40
  342.8 19.8 %copy-start.10 = (bf16[2,128,2048]{2,1,0:T(8,128)(2,1)S(1)}, bf16[2,128,2048]{2,1,0:T(8,128)(2,1)}, u32[]{:S(2)}) copy-start(bf16[2,128,2048]{2,1,0:T(8,128)(2,1)} %get-tuple-element.112) | copy-start | bytes 3145732
  (16 other events, 62.7 us)
Sparse Core Ops, SparseCore 0:
  24.4 62.5 all-gather.3
  319.7 48.3 all-gather.5

commit v5 on v4

--- a/solution.py
+++ b/solution.py
@@ -443,68 +443,48 @@
     scatter_rows(index_ref, total, keep_ref, send_ref)
 
 
+def own_rows_of(inner, grad, index_ref, total):
+    size = ADAPT_COLS // WA
+    total[...] = t_times(inner, grad)
+    return total[pl.ds(pl.multiple_of(index_ref[0] * size, size), size), :].astype(bf16)
+
+
 def pack_grads_kernel(index_ref, *refs):
-    first_ref, first_grad_ref, second_ref, second_grad_ref = refs[:4]
-    dense_ref, out_ref, grad_ref, down_ref = refs[4:8]
-    ups, (packed_ref, total) = refs[8:12], refs[12:]
-    size = ADAPT_COLS // WA
-    at = 0
-    for norm, grad in ((first_ref, first_grad_ref), (second_ref, second_grad_ref)):
-        part = t_times(norm[...], grad[...]).astype(bf16)
-        packed_ref[at : at + part.shape[0], :] = part
-        at += part.shape[0]
-    packed_ref[at : at + down_ref.shape[0], :] = down_ref[...]
-    at += down_ref.shape[0]
-    for inner in (dense_ref, out_ref):
-        total[...] = t_times(inner[...], grad_ref[...])
-        own = total[pl.ds(pl.multiple_of(index_ref[0] * size, size), size), :].astype(bf16)
-        at = store_strips(packed_ref, at, own)
+    down_ref, norm_ref, norm_grad_ref, inner_ref, grad_ref = refs[:5]
+    ups, (packed_ref, total) = refs[5:9], refs[9:]
+    at = down_ref.shape[0]
+    packed_ref[:at, :] = down_ref[...]
+    part = t_times(norm_ref[...], norm_grad_ref[...]).astype(bf16)
+    packed_ref[at : at + part.shape[0], :] = part
+    at += part.shape[0]
+    at = store_strips(packed_ref, at, own_rows_of(inner_ref[...], grad_ref[...], index_ref, total))
     for ref in ups:
         at = store_strips(packed_ref, at, ref)
 
 
-def pack_feed_kernel(index_ref, down_ref, *refs):
-    parts, packed_ref = refs[:WA], refs[WA]
-    packed_ref[: down_ref.shape[0], :] = down_ref[...]
-    at = down_ref.shape[0]
-    for ref in parts:
-        at = store_strips(packed_ref, at, ref)
-
-
-def unpack_feed_kernel(index_ref, source_ref, down_ref, up_ref):
-    packed = source_ref[...].reshape(-1, ADAPT_COLS)
+def unpack_grads_kernel(feed_size, index_ref, source_ref, *refs):
+    packed = source_ref[...]
     size = ADAPT_COLS // WA
-    at = down_ref.shape[0]
-    down_ref[...] = packed[:at, :].astype(f32)
-    block = up_ref.shape[1] // WA
-    for r in range(WA):
-        for i in range(block // 128):
-            first = index_ref[r] * block + i * 128
-            up_ref[:, pl.ds(pl.multiple_of(first, 128), 128)] = packed[at : at + size].astype(f32)
+    for outs, start, end in ((refs[:4], 0, feed_size), (refs[4:], feed_size, packed.shape[1])):
+        part = packed[:, start:end].reshape(-1, ADAPT_COLS)
+        down_ref, norm_ref, inner_ref, up_ref = outs
+        at = 0
+        for ref in (down_ref, norm_ref):
+            ref[...] = part[at : at + ref.shape[0], :].astype(f32)
+            at += ref.shape[0]
+        for i in range(inner_ref.shape[1] // 128):
+            inner_ref[:, i * 128 : (i + 1) * 128] = part[at : at + size, :].astype(f32)
             at += size
-
-
-def unpack_grads_kernel(index_ref, source_ref, *refs):
-    first_ref, second_ref, down_ref, dense_ref, out_ref, up_ref = refs
-    packed_ref = source_ref[...].reshape(-1, ADAPT_COLS)
-    size = ADAPT_COLS // WA
-    at = 0
-    for ref in (first_ref, second_ref, down_ref):
-        ref[...] = packed_ref[at : at + ref.shape[0], :].astype(f32)
-        at += ref.shape[0]
-    for ref in (dense_ref, out_ref):
-        for i in range(ref.shape[1] // 128):
-            ref[:, i * 128 : (i + 1) * 128] = packed_ref[at : at + size, :].astype(f32)
-            at += size
-    width = up_ref.shape[1] // 3
-    block = width // WA
-    for r in range(WA):
-        for kind in range(3):
-            first = kind * width + index_ref[r] * block
-            for i in range(block // 128):
-                columns = pl.ds(pl.multiple_of(first + i * 128, 128), 128)
-                up_ref[:, columns] = packed_ref[at : at + size, :].astype(f32)
-                at += size
+        kinds = 3 if start else 1
+        width = up_ref.shape[1] // kinds
+        block = width // WA
+        for r in range(WA):
+            for kind in range(kinds):
+                for i in range(block // 128):
+                    first = kind * width + index_ref[r] * block + i * 128
+                    columns = pl.ds(pl.multiple_of(first, 128), 128)
+                    up_ref[:, columns] = part[at : at + size, :].astype(f32)
+                    at += size
 
 
 def finish_kernel(index_ref, *refs):
@@ -964,15 +944,27 @@
         parts = lax.all_to_all(parts, "ctx", 0, 0, tiled=True)
         return jnp.sum(parts.astype(f32), axis=0).astype(bf16)
 
-    feed_packed = call(
-        pack_feed_kernel,
-        index,
-        [whole(item) for item in [out_down_grad] + spread_rows(in_up_grad)],
-        [((2 * hidden_width, ADAPT_COLS), bf16, None, None)],
-    )[0]
-    feed_sum = exchange_sum(after(feed_packed, both))
+    def pack_grads(down_grad, norm, norm_grad, inner, ups):
+        items = [whole(down_grad), (norm, (total, own_width), lambda _, ref: (0, ref[0]))]
+        items += [whole(item) for item in [norm_grad, inner, grad] + ups]
+        size = down_grad.size + own_width * ADAPT_COLS + part_cols * width
+        size += sum(item.size for item in ups)
+        return call(
+            pack_grads_kernel,
+            index,
+            items,
+            [((size // ADAPT_COLS, ADAPT_COLS), bf16, None, None)],
+            scratch=[pltpu.VMEM((ADAPT_COLS, width), f32)],
+        )[0]
+
+    in_up_parts = spread_rows(in_up_grad)
     out_inner = sum_inner(out_inner)
     second_inner_grad = sum_inner(second_inner_grad)
+    feed_packed = pack_grads(
+        out_down_grad, second_norm, second_inner_grad, out_inner, in_up_parts
+    )
+    feed_sum = exchange_sum(after(feed_packed, both))
+    odq = dkv = after(both, feed_packed)
 
     mixed_grads = [odq, dkv]
     up_items = []
@@ -1078,48 +1070,36 @@
         scratch=[pltpu.VMEM((rows, width), f32)],
     )[0][None]
 
-    own_norm = lambda _, ref: (0, ref[0])
-    items = [
-        (first_norm, (total, own_width), own_norm),
-        whole(first_inner_grad),
-    ]
-    items += [(second_norm, (total, own_width), own_norm), whole(second_inner_grad)]
-    items += [whole(item) for item in [dense_inner, out_inner, grad, dense_down_grad] + up_parts]
-    packed = call(
-        pack_grads_kernel,
-        index,
-        items,
-        [((8 * own_width, ADAPT_COLS), bf16, None, None)],
-        scratch=[pltpu.VMEM((ADAPT_COLS, width), f32)],
-    )[0]
+    packed = pack_grads(dense_down_grad, first_norm, first_inner_grad, dense_inner, up_parts)
     packed = exchange_sum(after(packed, feed_sum))
-    packed = jnp.stack([feed_sum, packed])
+    packed = jnp.concatenate([feed_sum, packed], axis=0)
     packed = lax.all_gather(packed, "ctx", axis=0)
     packed = after(packed, tokens_grad, output)
-    block = (contexts, 1) + packed.shape[2:]
-    out_down_grad, in_up_grad = call(
-        unpack_feed_kernel,
-        index,
-        [(packed, block, lambda *_: (0, 0, 0, 0))],
-        [
-            ((hidden_width, ADAPT_COLS), f32, None, None),
-            ((part_cols, WA * hidden_width), f32, None, None),
-        ],
-    )
     down_shape = ((own_width, ADAPT_COLS), f32, None, None)
     up_shape = ((part_cols, width), f32, None, None)
     (
+        out_down_grad,
+        in_down_grad,
+        out_up_grad,
+        in_up_grad,
+        dense_down_grad,
         qkv_down_grad,
-        in_down_grad,
-        dense_down_grad,
         dense_up_grad,
-        out_up_grad,
         qkv_up_grad,
     ) = call(
-        unpack_grads_kernel,
+        functools.partial(unpack_grads_kernel, feed_sum.shape[0]),
         index,
-        [(packed, block, lambda *_: (0, 1, 0, 0))],
-        [down_shape] * 3 + [up_shape] * 2 + [((part_cols, 3 * width), f32, None, None)],
+        [whole(packed)],
+        [
+            ((hidden_width, ADAPT_COLS), f32, None, None),
+            down_shape,
+            up_shape,
+            ((part_cols, WA * hidden_width), f32, None, None),
+            down_shape,
+            down_shape,
+            up_shape,
+            ((part_cols, 3 * width), f32, None, None),
+        ],
     )
     return (
         output,

time: 383 us -> 377 us (0.984)
  blocking collectives: 32.4 us -> 24.9 us
    all_to_all x1, blocking collectives: 32.4 us -> 24.9 us  [exchange_sum(): parts = lax.all_to_all(parts, 'ctx', 0, 0, tiled=True)]
    pallas_call x19 -> x18, Pallas kernels: 127 us -> 126 us  [call(): pl.pallas_call(kernel, grid_spec=pltpu.PrefetchScalarGridSpec(num_scalar_...]
  transfers between devices with their start and end apart: 42 -> 42, of which waited for: 21 -> 22; matrix products, arithmetic and copies ran while one was open for 8% -> 8% of each run, Pallas kernels for 31% -> 32%
where the time goes in v5:
time: 377 us; the launch traced here: 375 us
  Pallas kernels  136 us (36%)
  waiting for transfers between devices  115 us (31%)
  starting transfers between devices  49.1 us (13%)
  blocking collectives  24.9 us (7%)
  other arithmetic  20.8 us (6%)
  between operations  14.5 us (4%)
  local copies, waits for them, and re-layouts  11.1 us (3%)
    pallas_call x18, Pallas kernels, call(): pl.pallas_call(kernel, grid_spec=pltpu.PrefetchScalarGridSpec(num_scalar_...  126 us
    ppermute x35, waiting for transfers between devices, swap(): return lax.ppermute(value, 'wa', [(i, i ^ bits) for i in range(WA)])  102 us
    all_to_all x1, blocking collectives, exchange_sum(): parts = lax.all_to_all(parts, 'ctx', 0, 0, tiled=True)  24.9 us
    ppermute x35, starting transfers between devices, swap(): return lax.ppermute(value, 'wa', [(i, i ^ bits) for i in range(WA)])  23.1 us
    all_to_all x4, starting transfers between devices, to_pairs(): return lax.all_to_all(item, 'ctx', 0, 0, tiled=True)  19.9 us
    all_to_all x4, waiting for transfers between devices, to_pairs(): return lax.all_to_all(item, 'ctx', 0, 0, tiled=True)  10.3 us
    pallas_call x1, Pallas kernels, attend(): pl.pallas_call(functools.partial(attention_kernel, joint), grid=(rows //...  9.93 us
  transfers between devices with their start and end apart: 42, of which 22 were waited for; matrix products, arithmetic and copies ran while one was open for 8% of the time, Pallas kernels for 32%

profile of v5, /device:TPU:0, one launch (start us, length us, event | category | flops | bytes accessed | tf_op | source)
XLA Modules:
  0.0 374.9 jit_solution(7620456109492676861)
XLA Ops:
  7.9 3.4 shard_map.313
  11.3 2.4 collective-permute-start.1
  16.4 3.3 shard_map.314
  19.7 3.8 %collective-permute-done = bf16[64,1536]{1,0:T(8,128)(2,1)S(1)} collective-permute-done((bf16[64,1536]{1,0:T(8,128)(2,1)}, bf16[64,1536]{1,0:T(8,128)(2,1)S(1)}, u32[]{:S(2)}, u32[]{:S(2)}) %collective-permute-start) | collective-permute-done | bytes 196640 | tf_op jit(solution)/shard_map/ppermute | solution.py:40
  24.4 2.4 collective-permute-start.4
  26.7 5.4 %shard_map.312 = (bf16[256,2048]{1,0:T(8,128)(2,1)}, bf16[256,2048]{1,0:T(8,128)(2,1)}, bf16[256,2048]{1,0:T(8,128)(2,1)}, bf16[256,2048]{1,0:T(8,128)(2,1)}) custom-call(s32[8]{0:T(128)} %stack.34.index_ref, bf16[512,8192]{1,0:T(8,128)(2,1)} %refs_0_.15, bf16[512,8192]{1,0:T(8,128)(2,1)} %refs_0_.15, bf16[512,8192]{1,0:T(8,128)(2,1)} %refs_0_.15, ...), custom_call_target="tpu_custom_call" | custom-call | bytes 4194304 | tf_op jit(solution)/shard_map/pallas_call | solution.py:91
  32.8 13.9 %collective-permute-done.4.refs_3_.refs_6_.refs_4_.refs_8_.refs_12_.refs_7_ = bf16[3344,128]{1,0:T(8,128)(2,1)S(1)} collective-permute-done((bf16[3344,128]{1,0:T(8,128)(2,1)}, bf16[3344,128]{1,0:T(8,128)(2,1)S(1)}, u32[]{:S(2)}, u32[]{:S(2)}) %collective-permute-start.4) | collective-permute-done | bytes 856096 | tf_op jit(solution)/shard_map/ppermute | solution.py:40
  46.8 2.1 collective-permute-start.8
  48.8 1.8 constant_dynamic-slice_fusion.10
  50.6 4.2 %shard_map.317 = bf16[512,1536]{1,0:T(8,128)(2,1)} custom-call(s32[8]{0:T(128)} %stack.34.index_ref, bf16[512,6144]{1,0:T(8,128)(2,1)} %refs_10_.5), custom_call_target="tpu_custom_call" | custom-call | bytes 1572864 | tf_op jit(solution)/shard_map/pallas_call | solution.py:91
  54.8 3.0 shard_map.315
  58.5 10.9 %collective-permute-done.2.refs_2_ = bf16[256,2048]{1,0:T(8,128)(2,1)} collective-permute-done((bf16[256,2048]{1,0:T(8,128)(2,1)}, bf16[256,2048]{1,0:T(8,128)(2,1)}, u32[]{:S(2)}, u32[]{:S(2)}) %collective-permute-start.2) | collective-permute-done | bytes 1048608 | tf_op jit(solution)/shard_map/ppermute | solution.py:40
  69.3 16.3 %collective-permute-done.8.refs_2_ = bf16[192,2048]{1,0:T(8,128)(2,1)} collective-permute-done((bf16[192,2048]{1,0:T(8,128)(2,1)S(1)}, bf16[192,2048]{1,0:T(8,128)(2,1)}, u32[]{:S(2)}, u32[]{:S(2)}) %collective-permute-start.8) | collective-permute-done | bytes 786464 | tf_op jit(solution)/shard_map/ppermute | solution.py:40
  85.7 1.7 collective-permute-start.10
  89.5 7.0 %shard_map.316 = (bf16[512,2048]{1,0:T(8,128)(2,1)}, bf16[512,2048]{1,0:T(8,128)(2,1)}, bf16[512,128]{1,0:T(8,128)(2,1)}) custom-call(s32[8]{0:T(128)} %stack.34.index_ref, bf16[128,2048]{1,0:T(8,128)(2,1)} %bitcast.54, bf16[512,128]{1,0:T(8,128)(2,1)} %refs_5_.3, bf16[3344,128]{1,0:T(8,128)(2,1)} %copy-done.2, bf16[3344,128]{1,0:T(8,128)(2,1)} %copy-done.1, ...), custom_call_target="tpu_custom_call" | custom-call | flops 268435456 | bytes 3518464 | tf_op jit(solution)/shard_map/pallas_call | solution.py:91
  96.5 7.0 %shard_map.318 = (bf16[512,2048]{1,0:T(8,128)(2,1)}, bf16[512,128]{1,0:T(8,128)(2,1)}, bf16[512,128]{1,0:T(8,128)(2,1)}, bf16[4,2,128,256]{3,2,1,0:T(8,128)(2,1)}, bf16[2,128,2048]{2,1,0:T(8,128)(2,1)}) custom-call(s32[8]{0:T(128)} %stack.34.index_ref, bf16[192,2048]{1,0:T(8,128)(2,1)} %copy-done.11, bf16[192,2048]{1,0:T(8,128)(2,1)} %collective-permute-done.7.refs_1_, ...), custom_call_target="tpu_custom_call" | custom-call | flops 1610612736 | bytes 5636096 | tf_op jit(solution)/shard_map/pallas_call | solution.py:91
  103.5 5.8 %all-to-all-start = ((bf16[8,128,256]{2,1,0:T(8,128)(2,1)}), bf16[8,128,256]{2,1,0:T(8,128)(2,1)S(1)}, u32[]{:S(2)}, u32[]{:S(2)}) async-start(bf16[8,128,256]{2,1,0:T(8,128)(2,1)} %bitcast.66), calls=%async_computation | async-start | bytes 1048576 | tf_op jit(solution)/shard_map/all_to_all | solution.py:795
  109.4 1.3 collective-permute-done.10.refs_3_
  110.6 1.8 fusion.16
  112.5 5.2 %shard_map.320 = bf16[4,2,1,128,256]{4,3,2,1,0:T(8,128)(2,1)} custom-call(s32[8]{0:T(128)} %stack.34.index_ref, bf16[512,2048]{1,0:T(8,128)(2,1)} %get-tuple-element.83.hidden_ref.refs_1_, bf16[512,6144]{1,0:T(8,128)(2,1)} %refs_10_.5, bf16[512,1536]{1,0:T(8,128)(2,1)} %collective-permute-done.6.refs_1_.refs_3_.refs_7_.refs_11_, ...), custom_call_target="tpu_custom_call" | custom-call | flops 1073741824 | bytes 4981760 | tf_op jit(solution)/shard_map/pallas_call | solution.py:91
  117.7 6.8 %all-to-all-done = bf16[8,128,256]{2,1,0:T(8,128)(2,1)S(1)} async-done(((bf16[8,128,256]{2,1,0:T(8,128)(2,1)}), bf16[8,128,256]{2,1,0:T(8,128)(2,1)S(1)}, u32[]{:S(2)}, u32[]{:S(2)}) %all-to-all-start) | async-done | bytes 524320 | tf_op jit(solution)/shard_map/all_to_all | solution.py:795
  124.5 3.6 all-to-all-start.1
  128.1 3.3 shard_map.321
  131.5 7.8 %shard_map.319 = bf16[4,2,2,128,256]{4,3,2,1,0:T(8,128)(2,1)} custom-call(s32[8]{0:T(128)} %stack.34.index_ref, bf16[512,2048]{1,0:T(8,128)(2,1)} %get-tuple-element.83.hidden_ref.refs_1_, bf16[512,6144]{1,0:T(8,128)(2,1)} %refs_10_.5, bf16[512,1536]{1,0:T(8,128)(2,1)} %collective-permute-done.6.refs_1_.refs_3_.refs_7_.refs_11_, ...), custom_call_target="tpu_custom_call" | custom-call | flops 2147483648 | bytes 7211008 | tf_op jit(solution)/shard_map/pallas_call | solution.py:91
  139.3 3.5 all-to-all-done.1
  142.8 4.4 %all-to-all-start.2 = ((bf16[8,2,128,256]{3,2,1,0:T(8,128)(2,1)}), bf16[8,2,128,256]{3,2,1,0:T(8,128)(2,1)}, u32[]{:S(2)}, u32[]{:S(2)}) async-start(bf16[8,2,128,256]{3,2,1,0:T(8,128)(2,1)} %bitcast.57), calls=%async_computation.2 | async-start | bytes 2097152 | tf_op jit(solution)/shard_map/all_to_all | solution.py:795
  149.5 1.0 copy.42.begin_ref
  151.6 8.7 %collective-permute-done.15.refs_8_.refs_12_.refs_11_ = bf16[1552,128]{1,0:T(8,128)(2,1)S(1)} collective-permute-done((bf16[1552,128]{1,0:T(8,128)(2,1)}, bf16[1552,128]{1,0:T(8,128)(2,1)S(1)}, u32[]{:S(2)}, u32[]{:S(2)}) %collective-permute-start.15) | collective-permute-done | bytes 397344 | tf_op jit(solution)/shard_map/ppermute | solution.py:40
  160.9 3.1 fusion.5
  164.8 16.1 %collective-permute-done.12.refs_5_ = bf16[256,2048]{1,0:T(8,128)(2,1)} collective-permute-done((bf16[256,2048]{1,0:T(8,128)(2,1)}, bf16[256,2048]{1,0:T(8,128)(2,1)}, u32[]{:S(2)}, u32[]{:S(2)}) %collective-permute-start.12) | collective-permute-done | bytes 1048608 | tf_op jit(solution)/shard_map/ppermute | solution.py:40
  181.0 9.9 %shard_map.322 = bf16[8,4,128,256]{3,2,1,0:T(8,128)(2,1)} custom-call(bf16[8,2,128,256]{3,2,1,0:T(8,128)(2,1)} %all-to-all-done.2.query_ref.key_ref, bf16[8,2,128,256]{3,2,1,0:T(8,128)(2,1)} %all-to-all-done.2.query_ref.key_ref, bf16[1024,256]{1,0:T(8,128)(2,1)} %bitcast.65, bf16[1024,256]{1,0:T(8,128)(2,1)} %bitcast.64, s32[1024,1]{1,0:T(8,128)} %copy.42.begin_ref, ...), custom_call_target="tpu_custom_call" | custom-call | flops 3758096384 | bytes 4194304 | tf_op jit(solution)/shard_map/pallas_call | solution.py:596
  190.9 6.0 %all-to-all-start.3 = ((bf16[8,4,128,256]{3,2,1,0:T(8,128)(2,1)}), bf16[8,4,128,256]{3,2,1,0:T(8,128)(2,1)S(1)}, u32[]{:S(2)}, u32[]{:S(2)}) async-start(bf16[8,4,128,256]{3,2,1,0:T(8,128)(2,1)} %shard_map.322), calls=%async_computation.3 | async-start | bytes 4194304 | tf_op jit(solution)/shard_map/all_to_all | solution.py:795
  196.9 33.6 %shard_map.323 = (f32[512,2048]{1,0:T(8,128)}, f32[512,2048]{1,0:T(8,128)}, f32[512,128]{1,0:T(8,128)}, f32[512,128]{1,0:T(8,128)}, bf16[2048,128]{1,0:T(8,128)(...) custom-call(s32[8]{0:T(128)} %stack.34.index_ref, bf16[512,2048]{1,0:T(8,128)(2,1)} %get-tuple-element.103.hidden_ref.refs_1_, ...), custom_call_target="tpu_custom_call" | custom-call | flops 17179869184 | bytes 24129536 | tf_op jit(solution)/shard_map/pallas_call | solution.py:91
  231.1 1.2 collective-permute-done.19
  234.9 1.6 collective-permute-start.18
  236.5 1.8 constant_dynamic-slice_fusion.6
  238.8 1.3 collective-permute-start.23
  240.2 1.9 collective-permute-done.18
  242.9 2.0 collective-permute-done.22.refs_7_
  244.9 2.2 collective-permute-done.23.refs_8_
  247.7 4.6 %shard_map.324 = bf16[5120,128]{1,0:T(8,128)(2,1)} custom-call(s32[8]{0:T(128)} %stack.34.index_ref, bf16[2048,128]{1,0:T(8,128)(2,1)} %get-tuple-element.107.refs_0_, bf16[512,2048]{1,0:T(8,128)(2,1)} %get-tuple-element.103.hidden_ref.refs_1_, bf16[512,128]{1,0:T(8,128)(2,1)} %get-tuple-element.171.refs_2_, bf16[512,128]{1,0:T(8,128)(2,1)} %get-tuple-element.170.refs_3_, ...), custom_call_target="tpu_custom_call" | custom-call | bytes 3932160 | tf_op jit(solution)/shard_map/pallas_call | solution.py:91
  252.3 6.0 %all-to-all-start.4 = ((bf16[8,640,128]{2,1,0:T(8,128)(2,1)}), bf16[8,640,128]{2,1,0:T(8,128)(2,1)S(1)}, u32[]{:S(2)}, u32[]{:S(2)}) async-start(bf16[8,640,128]{2,1,0:T(8,128)(2,1)} %bitcast.56), calls=%async_computation.4 | async-start | bytes 2621440 | tf_op jit(solution)/shard_map/all_to_all | solution.py:944
  258.4 4.7 %shard_map.325 = (f32[512,128]{1,0:T(8,128)}, bf16[128,1536]{1,0:T(8,128)(2,1)}) custom-call(s32[8]{0:T(128)} %stack.34.index_ref, bf16[4,2,4,128,256]{4,3,2,1,0:T(8,128)(2,1)} %bitcast.48, bf16[4,2,4,128,256]{4,3,2,1,0:T(8,128)(2,1)} %bitcast.49, bf16[32,6144]{1,0:T(8,128)(2,1)} %refs_10_.4, bf16[3344,128]{1,0:T(8,128)(2,1)} %copy-done.2, ...), custom_call_target="tpu_custom_call" | custom-call | flops 402653184 | bytes 4718592 | tf_op jit(solution)/shard_map/pallas_call | solution.py:91
  263.1 7.7 %shard_map.326 = (f32[2,128,2048]{2,1,0:T(8,128)}, bf16[2,128,2048]{2,1,0:T(8,128)(2,1)}, f32[512,128]{1,0:T(8,128)}, bf16[512,128]{1,0:T(8,128)(2,1)}) custom-call(s32[8]{0:T(128)} %stack.34.index_ref, bf16[4,2,4,128,256]{4,3,2,1,0:T(8,128)(2,1)} %bitcast.50, f32[512,2048]{1,0:T(8,128)} %get-tuple-element.105.sum_ref, bf16[512,2048]{1,0:T(8,128)(2,1)} %weight_ref.1, ...), custom_call_target="tpu_custom_call" | custom-call | flops 1073741824 | bytes 8650752 | tf_op jit(solution)/shard_map/pallas_call | solution.py:91
  275.1 1.4 collective-permute-start.33
  277.0 3.0 collective-permute-done.27
  280.9 1.3 collective-permute-done.33.refs_7_
  282.1 1.2 collective-permute-done.34.refs_8_
  284.0 4.1 %shard_map.329 = bf16[3072,128]{1,0:T(8,128)(2,1)} custom-call(s32[8]{0:T(128)} %stack.34.index_ref, bf16[512,128]{1,0:T(8,128)(2,1)} %get-tuple-element.124.refs_0_, bf16[512,2048]{1,0:T(8,128)(2,1)} %get-tuple-element.83.hidden_ref.refs_1_, bf16[512,128]{1,0:T(8,128)(2,1)} %get-tuple-element.168.refs_2_, bf16[512,128]{1,0:T(8,128)(2,1)} %get-tuple-element.169.refs_3_, ...), custom_call_target="tpu_custom_call" | custom-call | bytes 3407872 | tf_op jit(solution)/shard_map/pallas_call | solution.py:91
  288.1 1.9 all-to-all-done.4
  290.2 24.9 %all_to_all.30 = bf16[8,384,128]{2,1,0:T(8,128)(2,1)S(1)} all-to-all(bf16[8,384,128]{2,1,0:T(8,128)(2,1)} %bitcast.58), channel_id=1, replica_groups=mesh['ctx'=8,'wa'=4] {'ctx'}, dimensions={0} | all-to-all | bytes 1572864 | tf_op jit(solution)/shard_map/all_to_all | solution.py:944
  316.0 11.5 %shard_map.327 = (f32[2,128,2048]{2,1,0:T(8,128)}, bf16[2,128,2048]{2,1,0:T(8,128)(2,1)}) custom-call(s32[8]{0:T(128)} %stack.34.index_ref, bf16[4,2,4,128,256]{4,3,2,1,0:T(8,128)(2,1)} %bitcast.51, bf16[4,2,4,128,256]{4,3,2,1,0:T(8,128)(2,1)} %bitcast.52, bf16[512,6144]{1,0:T(8,128)(2,1)} %refs_10_.5, ...), custom_call_target="tpu_custom_call" | custom-call | flops 3221225472 | bytes 14688256 | tf_op jit(solution)/shard_map/pallas_call | solution.py:91
  328.0 3.0 collective-permute-done.28.refs_1_
  331.1 2.5 fusion.8
  334.9 1.6 collective-permute-start.25
  336.5 1.4 constant_dynamic-slice_fusion.4.refs_4_
  337.9 1.4 constant_dynamic-slice_fusion.5.refs_3_
  339.3 9.4 %collective-permute-done.29.refs_2_ = bf16[128,2048]{1,0:T(8,128)(2,1)} collective-permute-done((bf16[128,2048]{1,0:T(8,128)(2,1)}, bf16[128,2048]{1,0:T(8,128)(2,1)}, u32[]{:S(2)}, u32[]{:S(2)}) %collective-permute-start.29) | collective-permute-done | bytes 524320 | tf_op jit(solution)/shard_map/ppermute | solution.py:40
  348.7 5.6 %shard_map.328 = f32[128,2048]{1,0:T(8,128)} custom-call(s32[8]{0:T(128)} %stack.34.index_ref, f32[2,128,2048]{2,1,0:T(8,128)} %get-tuple-element.121.refs_0_, bf16[2,128,2048]{2,1,0:T(8,128)(2,1)} %copy-done.6, bf16[128,2048]{1,0:T(8,128)(2,1)} %collective-permute-done.29.refs_2_, bf16[128,128]{1,0:T(8,128)(2,1)} %constant_dynamic-slice_fusion.5.refs_3_, ...), custom_call_target="tpu_custom_call" | custom-call | bytes 5849088 | tf_op jit(solution)/shard_map/pallas_call | solution.py:91
  354.3 4.8 %collective-permute-done.25 = bf16[128,2048]{1,0:T(8,128)(2,1)} collective-permute-done((bf16[128,2048]{1,0:T(8,128)(2,1)}, bf16[128,2048]{1,0:T(8,128)(2,1)}, u32[]{:S(2)}, u32[]{:S(2)}) %collective-permute-start.25) | collective-permute-done | bytes 524320 | tf_op jit(solution)/shard_map/ppermute | solution.py:40
  359.1 1.3 convolution_add_fusion.1
  360.5 1.9 fusion.4
  362.4 1.2 all-gather.6.cloned.1.call-done
  363.6 4.5 %shard_map.330 = (f32[2048,128]{1,0:T(8,128)}, f32[512,128]{1,0:T(8,128)}, f32[32,2048]{1,0:T(8,128)}, f32[32,8192]{1,0:T(8,128)}, f32[512,128]{1,0:T(8,128)}, /...) custom-call(s32[8]{0:T(128)} %stack.34.index_ref, bf16[8,1024,128]{2,1,0:T(8,128)(2,1)} %bitcast.62), custom_call_target="tpu_custom_call" | custom-call | bytes 2097152 | tf_op jit(solution)/shard_map/pallas_call | solution.py:91
  (162 shorter events, 26.8 us)
Async XLA Ops:
  7.2 105.3 %all-gather.4.cloned.1.call-start = ((), (), s32[]{:S(2)}) async-start(), calls=%async_computation.6 | async-start | bytes 3538944 | tf_op jit(solution)/shard_map/all_gather | solution.py:682
  7.9 6.4 %copy-start.31 = (s32[1,16]{1,0:T(1,128)S(1)}, s32[1,16]{1,0:T(1,128)}, u32[]{:S(2)}) copy-start(s32[1,16]{1,0:T(1,128)} %param.29) | copy-start | bytes 196
  7.9 6.4 %copy-start.32 = (s32[1,16]{1,0:T(1,128)S(1)}, s32[1,16]{1,0:T(1,128)}, u32[]{:S(2)}) copy-start(s32[1,16]{1,0:T(1,128)} %param.28) | copy-start | bytes 196
  7.9 7.1 %copy-start.4 = (bf16[32,6144]{1,0:T(8,128)(2,1)S(1)}, bf16[32,6144]{1,0:T(8,128)(2,1)}, u32[]{:S(2)}) copy-start(bf16[32,6144]{1,0:T(8,128)(2,1)} %refs_10_.4) | copy-start | bytes 1179652
  11.3 8.4 %collective-permute-start.1 = (bf16[64,1536]{1,0:T(8,128)(2,1)}, bf16[64,1536]{1,0:T(8,128)(2,1)S(1)}, u32[]{:S(2)}, u32[]{:S(2)}) collective-permute-start(bf16[64,1536]{1,0:T(8,128)(2,1)} %get-tuple-element.75), channel_id=1, source_target_pairs={{0,3},{1,2},{2,1},{3,0},{4,7},{5,6},{6,5},{7,4},{8,11},{9,10},{10,... | collective-permute-start | bytes 589832 | tf_op jit(solution)/shard_map/ppermute | solution.py:40
  13.7 9.9 %collective-permute-start = (bf16[64,1536]{1,0:T(8,128)(2,1)}, bf16[64,1536]{1,0:T(8,128)(2,1)S(1)}, u32[]{:S(2)}, u32[]{:S(2)}) collective-permute-start(bf16[64,1536]{1,0:T(8,128)(2,1)} %get-tuple-element.74), channel_id=1, source_target_pairs={{0,2},{1,3},{2,0},{3,1},{4,6},{5,7},{6,4},{7,5},{8,10},{9,11},{10,... | collective-permute-start | bytes 589832 | tf_op jit(solution)/shard_map/ppermute | solution.py:40
  24.3 8.0 %copy-start.7 = (bf16[1,128,2048]{2,1,0:T(8,128)(2,1)S(1)}, bf16[1,128,2048]{2,1,0:T(8,128)(2,1)}, u32[]{:S(2)}) copy-start(bf16[1,128,2048]{2,1,0:T(8,128)(2,1)} %param.26) | copy-start | bytes 1572868
  24.3 8.0 %copy-start.19 = (bf16[32,2048]{1,0:T(8,128)(2,1)S(1)}, bf16[32,2048]{1,0:T(8,128)(2,1)}, u32[]{:S(2)}) copy-start(bf16[32,2048]{1,0:T(8,128)(2,1)} %param.49) | copy-start | bytes 393220
  24.4 8.0 %copy-start.20 = (bf16[32,2048]{1,0:T(8,128)(2,1)S(1)}, bf16[32,2048]{1,0:T(8,128)(2,1)}, u32[]{:S(2)}) copy-start(bf16[32,2048]{1,0:T(8,128)(2,1)} %param.45) | copy-start | bytes 393220
  24.4 22.4 %collective-permute-start.4 = (bf16[3344,128]{1,0:T(8,128)(2,1)}, bf16[3344,128]{1,0:T(8,128)(2,1)S(1)}, u32[]{:S(2)}, u32[]{:S(2)}) collective-permute-start(bf16[3344,128]{1,0:T(8,128)(2,1)} %get-tuple-element.76), channel_id=1, source_target_pairs={{0,2},{1,3},{2,0},{3,1},{4,6},{5,7},{6,4},{7,5},{8,10},{9,11},{10,... | collective-permute-start | bytes 2568200 | tf_op jit(solution)/shard_map/ppermute | solution.py:40
  26.7 31.2 %collective-permute-start.3 = (bf16[3344,128]{1,0:T(8,128)(2,1)}, bf16[3344,128]{1,0:T(8,128)(2,1)S(1)}, u32[]{:S(2)}, u32[]{:S(2)}) collective-permute-start(bf16[3344,128]{1,0:T(8,128)(2,1)} %get-tuple-element.77), channel_id=1, source_target_pairs={{0,1},{1,0},{2,3},{3,2},{4,5},{5,4},{6,7},{7,6},{8,9},{9,8},{10,11... | collective-permute-start | bytes 2568200 | tf_op jit(solution)/shard_map/ppermute | solution.py:40
  32.1 37.2 %collective-permute-start.2 = (bf16[256,2048]{1,0:T(8,128)(2,1)}, bf16[256,2048]{1,0:T(8,128)(2,1)}, u32[]{:S(2)}, u32[]{:S(2)}) collective-permute-start(bf16[256,2048]{1,0:T(8,128)(2,1)} %get-tuple-element.79), channel_id=1, source_target_pairs={{0,2},{1,3},{2,0},{3,1},{4,6},{5,7},{6,4},{7,5},{8,10},{9,11},{10,... | collective-permute-start | bytes 3145736 | tf_op jit(solution)/shard_map/ppermute | solution.py:40
  32.4 22.4 %copy-start.11 = (bf16[192,2048]{1,0:T(8,128)(2,1)}, bf16[192,2048]{1,0:T(8,128)(2,1)S(1)}, u32[]{:S(2)}) copy-start(bf16[192,2048]{1,0:T(8,128)(2,1)S(1)} %pad_maximum_fusion.refs_0_) | copy-start | bytes 2359300
  32.4 64.1 %collective-permute-start.7 = (bf16[192,2048]{1,0:T(8,128)(2,1)S(1)}, bf16[192,2048]{1,0:T(8,128)(2,1)}, u32[]{:S(2)}, u32[]{:S(2)}) collective-permute-start(bf16[192,2048]{1,0:T(8,128)(2,1)S(1)} %pad_maximum_fusion.refs_0_), channel_id=1, source_target_pairs={{0,1},{1,0},{2,3},{3,2},{4,5},{5,4},{6,7},{7,6},{8,9},{9,8},{10,11... | collective-permute-start | bytes 2359304 | tf_op jit(solution)/shard_map/ppermute | solution.py:40
  46.8 40.7 %copy-start.1 = (bf16[3344,128]{1,0:T(8,128)(2,1)}, bf16[3344,128]{1,0:T(8,128)(2,1)S(1)}, u32[]{:S(2)}) copy-start(bf16[3344,128]{1,0:T(8,128)(2,1)S(1)} %collective-permute-done.4.refs_3_.refs_6_.refs_4_.refs_8_.refs_12_.refs_7_) | copy-start | bytes 2568196
  46.8 38.9 %collective-permute-start.8 = (bf16[192,2048]{1,0:T(8,128)(2,1)S(1)}, bf16[192,2048]{1,0:T(8,128)(2,1)}, u32[]{:S(2)}, u32[]{:S(2)}) collective-permute-start(bf16[192,2048]{1,0:T(8,128)(2,1)S(1)} %pad_maximum_fusion.refs_0_), channel_id=1, source_target_pairs={{0,2},{1,3},{2,0},{3,1},{4,6},{5,7},{6,4},{7,5},{8,10},{9,11},{10,... | collective-permute-start | bytes 2359304 | tf_op jit(solution)/shard_map/ppermute | solution.py:40
  48.8 38.6 %collective-permute-start.5 = (bf16[3344,128]{1,0:T(8,128)(2,1)S(1)}, bf16[3344,128]{1,0:T(8,128)(2,1)S(1)}, u32[]{:S(2)}, u32[]{:S(2)}) collective-permute-start(bf16[3344,128]{1,0:T(8,128)(2,1)S(1)} %collective-permute-done.4.refs_3_.refs_6_.refs_4_.refs_8_.refs_12_.refs_7_), channel_id=1, source_target_pairs={{0,1},{1,0},{2,3},{3,2},{4,5},{5,4},{6,7},{7,6},{8,9},{9,8},{10,11... | collective-permute-start | bytes 2568200 | tf_op jit(solution)/shard_map/ppermute | solution.py:40
  50.6 7.2 %copy-start.29 = (s32[16]{0:T(128)S(1)}, s32[16]{0:T(128)}, u32[]{:S(2)}) copy-start(s32[16]{0:T(128)} %param.27) | copy-start | bytes 196
  58.0 31.6 %copy-start.2 = (bf16[3344,128]{1,0:T(8,128)(2,1)}, bf16[3344,128]{1,0:T(8,128)(2,1)S(1)}, u32[]{:S(2)}) copy-start(bf16[3344,128]{1,0:T(8,128)(2,1)S(1)} %collective-permute-done.3.refs_2_.refs_5_.refs_3_.refs_7_.refs_11_.refs_6_) | copy-start | bytes 2568196
  58.0 54.5 %collective-permute-start.6 = (bf16[512,1536]{1,0:T(8,128)(2,1)}, bf16[512,1536]{1,0:T(8,128)(2,1)}, u32[]{:S(2)}, u32[]{:S(2)}) collective-permute-start(bf16[512,1536]{1,0:T(8,128)(2,1)} %shard_map.317), channel_id=1, source_target_pairs={{0,1},{1,0},{2,3},{3,2},{4,5},{5,4},{6,7},{7,6},{8,9},{9,8},{10,11... | collective-permute-start | bytes 4718600 | tf_op jit(solution)/shard_map/ppermute | solution.py:40
  85.7 25.0 %collective-permute-start.10 = (bf16[256,2048]{1,0:T(8,128)(2,1)}, bf16[256,2048]{1,0:T(8,128)(2,1)}, u32[]{:S(2)}, u32[]{:S(2)}) collective-permute-start(bf16[256,2048]{1,0:T(8,128)(2,1)} %get-tuple-element.94), channel_id=1, source_target_pairs={{0,2},{1,3},{2,0},{3,1},{4,6},{5,7},{6,4},{7,5},{8,10},{9,11},{10,... | collective-permute-start | bytes 3145736 | tf_op jit(solution)/shard_map/ppermute | solution.py:40
  87.4 9.1 %collective-permute-start.9 = (bf16[192,2048]{1,0:T(8,128)(2,1)}, bf16[192,2048]{1,0:T(8,128)(2,1)}, u32[]{:S(2)}, u32[]{:S(2)}) collective-permute-start(bf16[192,2048]{1,0:T(8,128)(2,1)} %collective-permute-done.8.refs_2_), channel_id=1, source_target_pairs={{0,1},{1,0},{2,3},{3,2},{4,5},{5,4},{6,7},{7,6},{8,9},{9,8},{10,11... | collective-permute-start | bytes 2359304 | tf_op jit(solution)/shard_map/ppermute | solution.py:40
  103.5 21.0 %all-to-all-start = ((bf16[8,128,256]{2,1,0:T(8,128)(2,1)}), bf16[8,128,256]{2,1,0:T(8,128)(2,1)S(1)}, u32[]{:S(2)}, u32[]{:S(2)}) async-start(bf16[8,128,256]{2,1,0:T(8,128)(2,1)} %bitcast.66), calls=%async_computation | async-start | bytes 1048576 | tf_op jit(solution)/shard_map/all_to_all | solution.py:795
  110.6 28.7 %collective-permute-start.11 = (bf16[256,2048]{1,0:T(8,128)(2,1)}, bf16[256,2048]{1,0:T(8,128)(2,1)}, u32[]{:S(2)}, u32[]{:S(2)}) collective-permute-start(bf16[256,2048]{1,0:T(8,128)(2,1)} %get-tuple-element.95), channel_id=1, source_target_pairs={{0,3},{1,2},{2,1},{3,0},{4,7},{5,6},{6,5},{7,4},{8,11},{9,10},{10,... | collective-permute-start | bytes 3145736 | tf_op jit(solution)/shard_map/ppermute | solution.py:40
  124.5 7.0 %copy-start.12 = (bf16[8,128,256]{2,1,0:T(8,128)(2,1)}, bf16[8,128,256]{2,1,0:T(8,128)(2,1)S(1)}, u32[]{:S(2)}) copy-start(bf16[8,128,256]{2,1,0:T(8,128)(2,1)S(1)} %all-to-all-done) | copy-start | bytes 1572868
  124.5 18.3 %all-to-all-start.1 = ((bf16[8,1,128,256]{3,2,1,0:T(8,128)(2,1)}), bf16[8,1,128,256]{3,2,1,0:T(8,128)(2,1)S(1)}, u32[]{:S(2)}, u32[]{:S(2)}) async-start(bf16[8,1,128,256]{3,2,1,0:T(8,128)(2,1)} %bitcast.61), calls=%async_computation.1 | async-start | bytes 1048576 | tf_op jit(solution)/shard_map/all_to_all | solution.py:795
  131.5 11.4 %copy-start.9 = (bf16[512,2048]{1,0:T(8,128)(2,1)S(1)}, bf16[512,2048]{1,0:T(8,128)(2,1)}, u32[]{:S(2)}) copy-start(bf16[512,2048]{1,0:T(8,128)(2,1)} %shard_map.321) | copy-start | bytes 6291460
  142.8 7.7 %copy-start.13 = (bf16[8,1,128,256]{3,2,1,0:T(8,128)(2,1)}, bf16[8,1,128,256]{3,2,1,0:T(8,128)(2,1)S(1)}, u32[]{:S(2)}) copy-start(bf16[8,1,128,256]{3,2,1,0:T(8,128)(2,1)S(1)} %all-to-all-done.1) | copy-start | bytes 1572868
  142.8 38.2 %collective-permute-start.13 = (bf16[512,2048]{1,0:T(8,128)(2,1)S(1)}, bf16[512,2048]{1,0:T(8,128)(2,1)}, u32[]{:S(2)}, u32[]{:S(2)}) collective-permute-start(bf16[512,2048]{1,0:T(8,128)(2,1)S(1)} %copy-done.9), channel_id=1, source_target_pairs={{0,1},{1,0},{2,3},{3,2},{4,5},{5,4},{6,7},{7,6},{8,9},{9,8},{10,11... | collective-permute-start | bytes 6291464 | tf_op jit(solution)/shard_map/ppermute | solution.py:40
  142.8 38.1 %all-to-all-start.2 = ((bf16[8,2,128,256]{3,2,1,0:T(8,128)(2,1)}), bf16[8,2,128,256]{3,2,1,0:T(8,128)(2,1)}, u32[]{:S(2)}, u32[]{:S(2)}) async-start(bf16[8,2,128,256]{3,2,1,0:T(8,128)(2,1)} %bitcast.57), calls=%async_computation.2 | async-start | bytes 2097152 | tf_op jit(solution)/shard_map/all_to_all | solution.py:795
  147.3 16.7 %collective-permute-start.14 = (bf16[1552,128]{1,0:T(8,128)(2,1)}, bf16[1552,128]{1,0:T(8,128)(2,1)S(1)}, u32[]{:S(2)}, u32[]{:S(2)}) collective-permute-start(bf16[1552,128]{1,0:T(8,128)(2,1)} %get-tuple-element.81), channel_id=1, source_target_pairs={{0,1},{1,0},{2,3},{3,2},{4,5},{5,4},{6,7},{7,6},{8,9},{9,8},{10,11... | collective-permute-start | bytes 1191944 | tf_op jit(solution)/shard_map/ppermute | solution.py:40
  148.0 12.3 %collective-permute-start.15 = (bf16[1552,128]{1,0:T(8,128)(2,1)}, bf16[1552,128]{1,0:T(8,128)(2,1)S(1)}, u32[]{:S(2)}, u32[]{:S(2)}) collective-permute-start(bf16[1552,128]{1,0:T(8,128)(2,1)} %get-tuple-element.100), channel_id=1, source_target_pairs={{0,2},{1,3},{2,0},{3,1},{4,6},{5,7},{6,4},{7,5},{8,10},{9,11},{10,... | collective-permute-start | bytes 1191944 | tf_op jit(solution)/shard_map/ppermute | solution.py:40
  148.5 32.5 %collective-permute-start.12 = (bf16[256,2048]{1,0:T(8,128)(2,1)}, bf16[256,2048]{1,0:T(8,128)(2,1)}, u32[]{:S(2)}, u32[]{:S(2)}) collective-permute-start(bf16[256,2048]{1,0:T(8,128)(2,1)} %get-tuple-element.98), channel_id=1, source_target_pairs={{0,3},{1,2},{2,1},{3,0},{4,7},{5,6},{6,5},{7,4},{8,11},{9,10},{10,... | collective-permute-start | bytes 3145736 | tf_op jit(solution)/shard_map/ppermute | solution.py:40
  160.3 30.6 %copy-start.15 = (bf16[1552,128]{1,0:T(8,128)(2,1)}, bf16[1552,128]{1,0:T(8,128)(2,1)S(1)}, u32[]{:S(2)}) copy-start(bf16[1552,128]{1,0:T(8,128)(2,1)S(1)} %collective-permute-done.15.refs_8_.refs_12_.refs_11_) | copy-start | bytes 1191940
  160.3 3.7 collective-permute-start.16
  164.0 26.9 %copy-start.14 = (bf16[1552,128]{1,0:T(8,128)(2,1)}, bf16[1552,128]{1,0:T(8,128)(2,1)S(1)}, u32[]{:S(2)}) copy-start(bf16[1552,128]{1,0:T(8,128)(2,1)S(1)} %collective-permute-done.14.refs_7_.refs_11_.refs_10_) | copy-start | bytes 1191940
  190.9 61.4 %all-to-all-start.3 = ((bf16[8,4,128,256]{3,2,1,0:T(8,128)(2,1)}), bf16[8,4,128,256]{3,2,1,0:T(8,128)(2,1)S(1)}, u32[]{:S(2)}, u32[]{:S(2)}) async-start(bf16[8,4,128,256]{3,2,1,0:T(8,128)(2,1)} %shard_map.322), calls=%async_computation.3 | async-start | bytes 4194304 | tf_op jit(solution)/shard_map/all_to_all | solution.py:795
  230.6 1.8 collective-permute-start.19
  230.8 3.2 collective-permute-start.17
  233.4 6.8 %collective-permute-start.20 = (bf16[512,128]{1,0:T(8,128)(2,1)S(1)}, bf16[512,128]{1,0:T(8,128)(2,1)S(1)}, u32[]{:S(2)}, u32[]{:S(2)}) collective-permute-start(bf16[512,128]{1,0:T(8,128)(2,1)S(1)} %add_convert_fusion.4), channel_id=1, source_target_pairs={{0,2},{1,3},{2,0},{3,1},{4,6},{5,7},{6,4},{7,5},{8,10},{9,11},{10,... | collective-permute-start | bytes 393224 | tf_op jit(solution)/shard_map/ppermute | solution.py:40
  234.9 7.2 %collective-permute-start.18 = (bf16[512,128]{1,0:T(8,128)(2,1)S(1)}, bf16[512,128]{1,0:T(8,128)(2,1)S(1)}, u32[]{:S(2)}, u32[]{:S(2)}) collective-permute-start(bf16[512,128]{1,0:T(8,128)(2,1)S(1)} %add_convert_fusion.5), channel_id=1, source_target_pairs={{0,2},{1,3},{2,0},{3,1},{4,6},{5,7},{6,4},{7,5},{8,10},{9,11},{10,... | collective-permute-start | bytes 393224 | tf_op jit(solution)/shard_map/ppermute | solution.py:40
  238.3 4.6 %collective-permute-start.21 = (bf16[32,2048]{1,0:T(8,128)(2,1)S(1)}, bf16[32,2048]{1,0:T(8,128)(2,1)S(1)}, u32[]{:S(2)}, u32[]{:S(2)}) collective-permute-start(bf16[32,2048]{1,0:T(8,128)(2,1)S(1)} %get-tuple-element.146), channel_id=1, source_target_pairs={{0,1},{1,0},{2,3},{3,2},{4,5},{5,4},{6,7},{7,6},{8,9},{9,8},{10,11... | collective-permute-start | bytes 393224 | tf_op jit(solution)/shard_map/ppermute | solution.py:40
  238.3 6.6 %collective-permute-start.22 = (bf16[32,2048]{1,0:T(8,128)(2,1)S(1)}, bf16[32,2048]{1,0:T(8,128)(2,1)S(1)}, u32[]{:S(2)}, u32[]{:S(2)}) collective-permute-start(bf16[32,2048]{1,0:T(8,128)(2,1)S(1)} %get-tuple-element.145), channel_id=1, source_target_pairs={{0,2},{1,3},{2,0},{3,1},{4,6},{5,7},{6,4},{7,5},{8,10},{9,11},{10,... | collective-permute-start | bytes 393224 | tf_op jit(solution)/shard_map/ppermute | solution.py:40
  238.8 8.3 %collective-permute-start.23 = (bf16[32,2048]{1,0:T(8,128)(2,1)S(1)}, bf16[32,2048]{1,0:T(8,128)(2,1)S(1)}, u32[]{:S(2)}, u32[]{:S(2)}) collective-permute-start(bf16[32,2048]{1,0:T(8,128)(2,1)S(1)} %get-tuple-element.144), channel_id=1, source_target_pairs={{0,3},{1,2},{2,1},{3,0},{4,7},{5,6},{6,5},{7,4},{8,11},{9,10},{10,... | collective-permute-start | bytes 393224 | tf_op jit(solution)/shard_map/ppermute | solution.py:40
  252.3 37.7 %all-to-all-start.4 = ((bf16[8,640,128]{2,1,0:T(8,128)(2,1)}), bf16[8,640,128]{2,1,0:T(8,128)(2,1)S(1)}, u32[]{:S(2)}, u32[]{:S(2)}) async-start(bf16[8,640,128]{2,1,0:T(8,128)(2,1)} %bitcast.56), calls=%async_computation.4 | async-start | bytes 2621440 | tf_op jit(solution)/shard_map/all_to_all | solution.py:944
  258.3 105.2 %all-gather.6.cloned.1.call-start = ((), (), s32[]{:S(2)}) async-start(), calls=%async_computation.7 | async-start | bytes 2359296 | tf_op jit(solution)/shard_map/all_gather | solution.py:1076
  263.1 8.2 %collective-permute-start.30 = (f32[512,128]{1,0:T(8,128)}, f32[512,128]{1,0:T(8,128)S(1)}, u32[]{:S(2)}, u32[]{:S(2)}) collective-permute-start(f32[512,128]{1,0:T(8,128)} %get-tuple-element.112), channel_id=1, source_target_pairs={{0,1},{1,0},{2,3},{3,2},{4,5},{5,4},{6,7},{7,6},{8,9},{9,8},{10,11... | collective-permute-start | bytes 786440 | tf_op jit(solution)/shard_map/ppermute | solution.py:40
  263.1 8.2 %copy-start.18 = (f32[512,128]{1,0:T(8,128)S(1)}, f32[512,128]{1,0:T(8,128)}, u32[]{:S(2)}) copy-start(f32[512,128]{1,0:T(8,128)} %get-tuple-element.112) | copy-start | bytes 786436
  263.1 11.4 %copy-start.17 = (bf16[128,1536]{1,0:T(8,128)(2,1)S(1)}, bf16[128,1536]{1,0:T(8,128)(2,1)}, u32[]{:S(2)}) copy-start(bf16[128,1536]{1,0:T(8,128)(2,1)} %get-tuple-element.125) | copy-start | bytes 1179652
  270.8 1.9 collective-permute-start.26
  271.3 5.7 %collective-permute-start.31 = (bf16[512,128]{1,0:T(8,128)(2,1)S(1)}, bf16[512,128]{1,0:T(8,128)(2,1)S(1)}, u32[]{:S(2)}, u32[]{:S(2)}) collective-permute-start(bf16[512,128]{1,0:T(8,128)(2,1)S(1)} %add_convert_fusion.2), channel_id=1, source_target_pairs={{0,2},{1,3},{2,0},{3,1},{4,6},{5,7},{6,4},{7,5},{8,10},{9,11},{10,... | collective-permute-start | bytes 393224 | tf_op jit(solution)/shard_map/ppermute | solution.py:40
  273.6 6.4 %collective-permute-start.27 = (bf16[512,128]{1,0:T(8,128)(2,1)S(1)}, bf16[512,128]{1,0:T(8,128)(2,1)S(1)}, u32[]{:S(2)}, u32[]{:S(2)}) collective-permute-start(bf16[512,128]{1,0:T(8,128)(2,1)S(1)} %add_convert_fusion.3), channel_id=1, source_target_pairs={{0,2},{1,3},{2,0},{3,1},{4,6},{5,7},{6,4},{7,5},{8,10},{9,11},{10,... | collective-permute-start | bytes 393224 | tf_op jit(solution)/shard_map/ppermute | solution.py:40
  275.1 5.7 %collective-permute-start.32 = (bf16[32,1536]{1,0:T(8,128)(2,1)S(1)}, bf16[32,1536]{1,0:T(8,128)(2,1)S(1)}, u32[]{:S(2)}, u32[]{:S(2)}) collective-permute-start(bf16[32,1536]{1,0:T(8,128)(2,1)S(1)} %get-tuple-element.153), channel_id=1, source_target_pairs={{0,1},{1,0},{2,3},{3,2},{4,5},{5,4},{6,7},{7,6},{8,9},{9,8},{10,11... | collective-permute-start | bytes 294920 | tf_op jit(solution)/shard_map/ppermute | solution.py:40
  275.1 7.0 %collective-permute-start.33 = (bf16[32,1536]{1,0:T(8,128)(2,1)S(1)}, bf16[32,1536]{1,0:T(8,128)(2,1)S(1)}, u32[]{:S(2)}, u32[]{:S(2)}) collective-permute-start(bf16[32,1536]{1,0:T(8,128)(2,1)S(1)} %get-tuple-element.152), channel_id=1, source_target_pairs={{0,2},{1,3},{2,0},{3,1},{4,6},{5,7},{6,4},{7,5},{8,10},{9,11},{10,... | collective-permute-start | bytes 294920 | tf_op jit(solution)/shard_map/ppermute | solution.py:40
  276.5 6.9 %collective-permute-start.34 = (bf16[32,1536]{1,0:T(8,128)(2,1)S(1)}, bf16[32,1536]{1,0:T(8,128)(2,1)S(1)}, u32[]{:S(2)}, u32[]{:S(2)}) collective-permute-start(bf16[32,1536]{1,0:T(8,128)(2,1)S(1)} %get-tuple-element.151), channel_id=1, source_target_pairs={{0,3},{1,2},{2,1},{3,0},{4,7},{5,6},{6,5},{7,4},{8,11},{9,10},{10,... | collective-permute-start | bytes 294920 | tf_op jit(solution)/shard_map/ppermute | solution.py:40
  316.0 11.6 %copy-start.30 = (bf16[2,128,2048]{2,1,0:T(8,128)(2,1)S(1)}, bf16[2,128,2048]{2,1,0:T(8,128)(2,1)}, u32[]{:S(2)}) copy-start(bf16[2,128,2048]{2,1,0:T(8,128)(2,1)} %get-tuple-element.116) | copy-start | bytes 3145732
  327.5 6.5 %copy-start.8 = (f32[2,128,2048]{2,1,0:T(8,128)S(1)}, f32[2,128,2048]{2,1,0:T(8,128)}, u32[]{:S(2)}) copy-start(f32[2,128,2048]{2,1,0:T(8,128)} %get-tuple-element.115) | copy-start | bytes 6291460
  327.5 3.5 collective-permute-start.28
  327.5 6.4 %collective-permute-start.24 = (bf16[2,128,2048]{2,1,0:T(8,128)(2,1)S(1)}, bf16[2,128,2048]{2,1,0:T(8,128)(2,1)S(1)}, u32[]{:S(2)}, u32[]{:S(2)}) collective-permute-start(bf16[2,128,2048]{2,1,0:T(8,128)(2,1)S(1)} %copy-done.30), channel_id=1, source_target_pairs={{0,1},{1,0},{2,3},{3,2},{4,5},{5,4},{6,7},{7,6},{8,9},{9,8},{10,11... | collective-permute-start | bytes 3145736 | tf_op jit(solution)/shard_map/ppermute | solution.py:40
  333.6 15.1 %collective-permute-start.29 = (bf16[128,2048]{1,0:T(8,128)(2,1)}, bf16[128,2048]{1,0:T(8,128)(2,1)}, u32[]{:S(2)}, u32[]{:S(2)}) collective-permute-start(bf16[128,2048]{1,0:T(8,128)(2,1)} %fusion.8), channel_id=1, source_target_pairs={{0,2},{1,3},{2,0},{3,1},{4,6},{5,7},{6,4},{7,5},{8,10},{9,11},{10,... | collective-permute-start | bytes 1572872 | tf_op jit(solution)/shard_map/ppermute | solution.py:40
  334.9 24.2 %collective-permute-start.25 = (bf16[128,2048]{1,0:T(8,128)(2,1)}, bf16[128,2048]{1,0:T(8,128)(2,1)}, u32[]{:S(2)}, u32[]{:S(2)}) collective-permute-start(bf16[128,2048]{1,0:T(8,128)(2,1)} %fusion.7), channel_id=1, source_target_pairs={{0,2},{1,3},{2,0},{3,1},{4,6},{5,7},{6,4},{7,5},{8,10},{9,11},{10,... | collective-permute-start | bytes 1572872 | tf_op jit(solution)/shard_map/ppermute | solution.py:40
  339.3 19.8 %copy-start.10 = (bf16[2,128,2048]{2,1,0:T(8,128)(2,1)S(1)}, bf16[2,128,2048]{2,1,0:T(8,128)(2,1)}, u32[]{:S(2)}) copy-start(bf16[2,128,2048]{2,1,0:T(8,128)(2,1)} %get-tuple-element.118) | copy-start | bytes 3145732
  354.2 6.2 %copy-start.27 = (f32[2048]{0:T(1024)S(1)}, f32[2048]{0:T(1024)}, u32[]{:S(2)}) copy-start(f32[2048]{0:T(1024)} %param.41) | copy-start | bytes 24580
  354.3 6.2 %copy-start.28 = (f32[2048]{0:T(1024)S(1)}, f32[2048]{0:T(1024)}, u32[]{:S(2)}) copy-start(f32[2048]{0:T(1024)} %param.37) | copy-start | bytes 24580
  (11 other events, 30.4 us)
Sparse Core Ops, SparseCore 0:
  24.5 62.5 all-gather.3
  316.1 47.4 all-gather.5

commit v6 on v5

--- a/solution.py
+++ b/solution.py
@@ -909,7 +909,7 @@
             for item in (pair[:, :1], value)
         ]
     both = attend(
-        after(pair, in_parts[3], in_mate, *feed_packs),
+        after(pair, in_mate, *feed_packs),
         key,
         value,
         attended_grad,
@@ -925,7 +925,7 @@
             both[1], "ctx", scatter_dimension=0, axis_index_groups=sets, tiled=True
         )
         both = [jnp.concatenate([both[0], dkv], axis=1)]
-    both = to_pairs(both[0]).reshape(WA, 2, 4, rows, HEAD)
+    both = to_pairs(after(both[0], in_parts[3])).reshape(WA, 2, 4, rows, HEAD)
     both = after(both, branch_sum)
     odq, dkv = both, both
 

time: 377 us -> 367 us (0.973)
  waiting for transfers between devices: 115 us -> 109 us
    ppermute x35, waiting for transfers between devices: 102 us -> 85.8 us  [swap(): return lax.ppermute(value, 'wa', [(i, i ^ bits) for i in range(WA)])]
    all_to_all x4, waiting for transfers between devices: 10.3 us -> 20.1 us  [to_pairs(): return lax.all_to_all(item, 'ctx', 0, 0, tiled=True)]
  transfers between devices with their start and end apart: 42 -> 42, of which waited for: 22 -> 22; matrix products, arithmetic and copies ran while one was open for 8% -> 8% of each run, Pallas kernels for 32% -> 35%
where the time goes in v6:
time: 367 us; the launch traced here: 365 us
  Pallas kernels  136 us (37%)
  waiting for transfers between devices  109 us (30%)
  starting transfers between devices  46.7 us (13%)
  blocking collectives  24.9 us (7%)
  other arithmetic  20.8 us (6%)
  between operations  14.5 us (4%)
  local copies, waits for them, and re-layouts  10.3 us (3%)
    pallas_call x18, Pallas kernels, call(): pl.pallas_call(kernel, grid_spec=pltpu.PrefetchScalarGridSpec(num_scalar_...  126 us
    ppermute x35, waiting for transfers between devices, swap(): return lax.ppermute(value, 'wa', [(i, i ^ bits) for i in range(WA)])  85.8 us
    all_to_all x1, blocking collectives, exchange_sum(): parts = lax.all_to_all(parts, 'ctx', 0, 0, tiled=True)  24.9 us
    ppermute x35, starting transfers between devices, swap(): return lax.ppermute(value, 'wa', [(i, i ^ bits) for i in range(WA)])  23.2 us
    all_to_all x4, waiting for transfers between devices, to_pairs(): return lax.all_to_all(item, 'ctx', 0, 0, tiled=True)  20.1 us
    all_to_all x4, starting transfers between devices, to_pairs(): return lax.all_to_all(item, 'ctx', 0, 0, tiled=True)  17.5 us
    pallas_call x1, Pallas kernels, attend(): pl.pallas_call(functools.partial(attention_kernel, joint), grid=(rows //...  10 us
  transfers between devices with their start and end apart: 42, of which 22 were waited for; matrix products, arithmetic and copies ran while one was open for 8% of the time, Pallas kernels for 35%

profile of v6, /device:TPU:0, one launch (start us, length us, event | category | flops | bytes accessed | tf_op | source)
XLA Modules:
  0.0 365.4 jit_solution(1165393212816295433)
XLA Ops:
  7.9 3.4 shard_map.313
  11.2 2.4 collective-permute-start.1
  16.3 3.3 shard_map.314
  19.6 3.8 %collective-permute-done = bf16[64,1536]{1,0:T(8,128)(2,1)S(1)} collective-permute-done((bf16[64,1536]{1,0:T(8,128)(2,1)}, bf16[64,1536]{1,0:T(8,128)(2,1)S(1)}, u32[]{:S(2)}, u32[]{:S(2)}) %collective-permute-start) | collective-permute-done | bytes 196640 | tf_op jit(solution)/shard_map/ppermute | solution.py:40
  24.3 2.4 collective-permute-start.4
  26.7 5.4 %shard_map.312 = (bf16[256,2048]{1,0:T(8,128)(2,1)}, bf16[256,2048]{1,0:T(8,128)(2,1)}, bf16[256,2048]{1,0:T(8,128)(2,1)}, bf16[256,2048]{1,0:T(8,128)(2,1)}) custom-call(s32[8]{0:T(128)} %stack.34.index_ref, bf16[512,8192]{1,0:T(8,128)(2,1)} %refs_0_.15, bf16[512,8192]{1,0:T(8,128)(2,1)} %refs_0_.15, bf16[512,8192]{1,0:T(8,128)(2,1)} %refs_0_.15, ...), custom_call_target="tpu_custom_call" | custom-call | bytes 4194304 | tf_op jit(solution)/shard_map/pallas_call | solution.py:91
  32.8 13.9 %collective-permute-done.4.refs_3_.refs_6_.refs_4_.refs_8_.refs_12_.refs_7_ = bf16[3344,128]{1,0:T(8,128)(2,1)S(1)} collective-permute-done((bf16[3344,128]{1,0:T(8,128)(2,1)}, bf16[3344,128]{1,0:T(8,128)(2,1)S(1)}, u32[]{:S(2)}, u32[]{:S(2)}) %collective-permute-start.4) | collective-permute-done | bytes 856096 | tf_op jit(solution)/shard_map/ppermute | solution.py:40
  46.7 2.1 collective-permute-start.8
  48.8 1.8 constant_dynamic-slice_fusion.10
  50.6 4.2 %shard_map.317 = bf16[512,1536]{1,0:T(8,128)(2,1)} custom-call(s32[8]{0:T(128)} %stack.34.index_ref, bf16[512,6144]{1,0:T(8,128)(2,1)} %refs_10_.5), custom_call_target="tpu_custom_call" | custom-call | bytes 1572864 | tf_op jit(solution)/shard_map/pallas_call | solution.py:91
  54.8 3.0 shard_map.315
  58.4 10.9 %collective-permute-done.2.refs_2_ = bf16[256,2048]{1,0:T(8,128)(2,1)} collective-permute-done((bf16[256,2048]{1,0:T(8,128)(2,1)}, bf16[256,2048]{1,0:T(8,128)(2,1)}, u32[]{:S(2)}, u32[]{:S(2)}) %collective-permute-start.2) | collective-permute-done | bytes 1048608 | tf_op jit(solution)/shard_map/ppermute | solution.py:40
  69.3 16.3 %collective-permute-done.8.refs_2_ = bf16[192,2048]{1,0:T(8,128)(2,1)} collective-permute-done((bf16[192,2048]{1,0:T(8,128)(2,1)S(1)}, bf16[192,2048]{1,0:T(8,128)(2,1)}, u32[]{:S(2)}, u32[]{:S(2)}) %collective-permute-start.8) | collective-permute-done | bytes 786464 | tf_op jit(solution)/shard_map/ppermute | solution.py:40
  85.6 1.7 collective-permute-start.10
  89.5 6.9 %shard_map.316 = (bf16[512,2048]{1,0:T(8,128)(2,1)}, bf16[512,2048]{1,0:T(8,128)(2,1)}, bf16[512,128]{1,0:T(8,128)(2,1)}) custom-call(s32[8]{0:T(128)} %stack.34.index_ref, bf16[128,2048]{1,0:T(8,128)(2,1)} %bitcast.54, bf16[512,128]{1,0:T(8,128)(2,1)} %refs_5_.3, bf16[3344,128]{1,0:T(8,128)(2,1)} %copy-done.2, bf16[3344,128]{1,0:T(8,128)(2,1)} %copy-done.1, ...), custom_call_target="tpu_custom_call" | custom-call | flops 268435456 | bytes 3518464 | tf_op jit(solution)/shard_map/pallas_call | solution.py:91
  96.4 7.0 %shard_map.318 = (bf16[512,2048]{1,0:T(8,128)(2,1)}, bf16[512,128]{1,0:T(8,128)(2,1)}, bf16[512,128]{1,0:T(8,128)(2,1)}, bf16[4,2,128,256]{3,2,1,0:T(8,128)(2,1)}, bf16[2,128,2048]{2,1,0:T(8,128)(2,1)}) custom-call(s32[8]{0:T(128)} %stack.34.index_ref, bf16[192,2048]{1,0:T(8,128)(2,1)} %copy-done.11, bf16[192,2048]{1,0:T(8,128)(2,1)} %collective-permute-done.7.refs_1_, ...), custom_call_target="tpu_custom_call" | custom-call | flops 1610612736 | bytes 5636096 | tf_op jit(solution)/shard_map/pallas_call | solution.py:91
  103.4 5.8 %all-to-all-start = ((bf16[8,128,256]{2,1,0:T(8,128)(2,1)}), bf16[8,128,256]{2,1,0:T(8,128)(2,1)S(1)}, u32[]{:S(2)}, u32[]{:S(2)}) async-start(bf16[8,128,256]{2,1,0:T(8,128)(2,1)} %bitcast.66), calls=%async_computation | async-start | bytes 1048576 | tf_op jit(solution)/shard_map/all_to_all | solution.py:795
  109.3 1.3 collective-permute-done.10.refs_3_
  110.6 1.8 fusion.16
  112.4 5.2 %shard_map.320 = bf16[4,2,1,128,256]{4,3,2,1,0:T(8,128)(2,1)} custom-call(s32[8]{0:T(128)} %stack.34.index_ref, bf16[512,2048]{1,0:T(8,128)(2,1)} %get-tuple-element.84.hidden_ref.refs_1_, bf16[512,6144]{1,0:T(8,128)(2,1)} %refs_10_.5, bf16[512,1536]{1,0:T(8,128)(2,1)} %collective-permute-done.6.refs_1_.refs_3_.refs_7_.refs_11_, ...), custom_call_target="tpu_custom_call" | custom-call | flops 1073741824 | bytes 4981760 | tf_op jit(solution)/shard_map/pallas_call | solution.py:91
  117.6 6.8 %all-to-all-done = bf16[8,128,256]{2,1,0:T(8,128)(2,1)S(1)} async-done(((bf16[8,128,256]{2,1,0:T(8,128)(2,1)}), bf16[8,128,256]{2,1,0:T(8,128)(2,1)S(1)}, u32[]{:S(2)}, u32[]{:S(2)}) %all-to-all-start) | async-done | bytes 524320 | tf_op jit(solution)/shard_map/all_to_all | solution.py:795
  124.4 3.6 all-to-all-start.1
  128.1 3.3 shard_map.321
  131.4 7.8 %shard_map.319 = bf16[4,2,2,128,256]{4,3,2,1,0:T(8,128)(2,1)} custom-call(s32[8]{0:T(128)} %stack.34.index_ref, bf16[512,2048]{1,0:T(8,128)(2,1)} %get-tuple-element.84.hidden_ref.refs_1_, bf16[512,6144]{1,0:T(8,128)(2,1)} %refs_10_.5, bf16[512,1536]{1,0:T(8,128)(2,1)} %collective-permute-done.6.refs_1_.refs_3_.refs_7_.refs_11_, ...), custom_call_target="tpu_custom_call" | custom-call | flops 2147483648 | bytes 7211008 | tf_op jit(solution)/shard_map/pallas_call | solution.py:91
  139.2 3.5 all-to-all-done.1
  142.8 4.4 %all-to-all-start.2 = ((bf16[8,2,128,256]{3,2,1,0:T(8,128)(2,1)}), bf16[8,2,128,256]{3,2,1,0:T(8,128)(2,1)}, u32[]{:S(2)}, u32[]{:S(2)}) async-start(bf16[8,2,128,256]{3,2,1,0:T(8,128)(2,1)} %bitcast.57), calls=%async_computation.2 | async-start | bytes 2097152 | tf_op jit(solution)/shard_map/all_to_all | solution.py:795
  148.6 1.0 copy.42.begin_ref
  151.6 8.6 %collective-permute-done.14.refs_8_.refs_12_.refs_11_ = bf16[1552,128]{1,0:T(8,128)(2,1)S(1)} collective-permute-done((bf16[1552,128]{1,0:T(8,128)(2,1)}, bf16[1552,128]{1,0:T(8,128)(2,1)S(1)}, u32[]{:S(2)}, u32[]{:S(2)}) %collective-permute-start.14) | collective-permute-done | bytes 397344 | tf_op jit(solution)/shard_map/ppermute | solution.py:40
  160.9 3.1 fusion.5
  163.9 9.8 %all-to-all-done.2.query_ref.key_ref = bf16[8,2,128,256]{3,2,1,0:T(8,128)(2,1)} async-done(((bf16[8,2,128,256]{3,2,1,0:T(8,128)(2,1)}), bf16[8,2,128,256]{3,2,1,0:T(8,128)(2,1)}, u32[]{:S(2)}, u32[]{:S(2)}) %all-to-all-start.2) | async-done | bytes 1048608 | tf_op jit(solution)/shard_map/all_to_all | solution.py:795
  173.7 10.0 %shard_map.322 = bf16[8,4,128,256]{3,2,1,0:T(8,128)(2,1)} custom-call(bf16[8,2,128,256]{3,2,1,0:T(8,128)(2,1)} %all-to-all-done.2.query_ref.key_ref, bf16[8,2,128,256]{3,2,1,0:T(8,128)(2,1)} %all-to-all-done.2.query_ref.key_ref, bf16[1024,256]{1,0:T(8,128)(2,1)} %bitcast.65, bf16[1024,256]{1,0:T(8,128)(2,1)} %bitcast.64, s32[1024,1]{1,0:T(8,128)} %copy.42.begin_ref, ...), custom_call_target="tpu_custom_call" | custom-call | flops 3758096384 | bytes 4194304 | tf_op jit(solution)/shard_map/pallas_call | solution.py:596
  183.8 3.6 all-to-all-start.3
  187.4 33.7 %shard_map.323 = (f32[512,2048]{1,0:T(8,128)}, f32[512,2048]{1,0:T(8,128)}, f32[512,128]{1,0:T(8,128)}, f32[512,128]{1,0:T(8,128)}, bf16[2048,128]{1,0:T(8,128)(...) custom-call(s32[8]{0:T(128)} %stack.34.index_ref, bf16[512,2048]{1,0:T(8,128)(2,1)} %get-tuple-element.105.hidden_ref.refs_1_, ...), custom_call_target="tpu_custom_call" | custom-call | flops 17179869184 | bytes 24129536 | tf_op jit(solution)/shard_map/pallas_call | solution.py:91
  221.7 1.2 collective-permute-done.19
  225.5 1.6 collective-permute-start.18
  227.0 1.8 constant_dynamic-slice_fusion.6
  229.4 1.4 collective-permute-start.23
  230.7 1.9 collective-permute-done.18
  233.5 1.9 collective-permute-done.22.refs_7_
  235.4 2.2 collective-permute-done.23.refs_8_
  238.3 4.6 %shard_map.324 = bf16[5120,128]{1,0:T(8,128)(2,1)} custom-call(s32[8]{0:T(128)} %stack.34.index_ref, bf16[2048,128]{1,0:T(8,128)(2,1)} %get-tuple-element.109.refs_0_, bf16[512,2048]{1,0:T(8,128)(2,1)} %get-tuple-element.105.hidden_ref.refs_1_, bf16[512,128]{1,0:T(8,128)(2,1)} %get-tuple-element.173.refs_2_, bf16[512,128]{1,0:T(8,128)(2,1)} %get-tuple-element.172.refs_3_, ...), custom_call_target="tpu_custom_call" | custom-call | bytes 3932160 | tf_op jit(solution)/shard_map/pallas_call | solution.py:91
  242.9 5.9 %all-to-all-start.4 = ((bf16[8,640,128]{2,1,0:T(8,128)(2,1)}), bf16[8,640,128]{2,1,0:T(8,128)(2,1)S(1)}, u32[]{:S(2)}, u32[]{:S(2)}) async-start(bf16[8,640,128]{2,1,0:T(8,128)(2,1)} %bitcast.56), calls=%async_computation.4 | async-start | bytes 2621440 | tf_op jit(solution)/shard_map/all_to_all | solution.py:944
  248.9 4.7 %shard_map.325 = (f32[512,128]{1,0:T(8,128)}, bf16[128,1536]{1,0:T(8,128)(2,1)}) custom-call(s32[8]{0:T(128)} %stack.34.index_ref, bf16[4,2,4,128,256]{4,3,2,1,0:T(8,128)(2,1)} %bitcast.48, bf16[4,2,4,128,256]{4,3,2,1,0:T(8,128)(2,1)} %bitcast.49, bf16[32,6144]{1,0:T(8,128)(2,1)} %refs_10_.4, bf16[3344,128]{1,0:T(8,128)(2,1)} %copy-done.2, ...), custom_call_target="tpu_custom_call" | custom-call | flops 402653184 | bytes 4718592 | tf_op jit(solution)/shard_map/pallas_call | solution.py:91
  253.6 7.6 %shard_map.326 = (f32[2,128,2048]{2,1,0:T(8,128)}, bf16[2,128,2048]{2,1,0:T(8,128)(2,1)}, f32[512,128]{1,0:T(8,128)}, bf16[512,128]{1,0:T(8,128)(2,1)}) custom-call(s32[8]{0:T(128)} %stack.34.index_ref, bf16[4,2,4,128,256]{4,3,2,1,0:T(8,128)(2,1)} %bitcast.50, f32[512,2048]{1,0:T(8,128)} %get-tuple-element.107.sum_ref, bf16[512,2048]{1,0:T(8,128)(2,1)} %weight_ref.1, ...), custom_call_target="tpu_custom_call" | custom-call | flops 1073741824 | bytes 8650752 | tf_op jit(solution)/shard_map/pallas_call | solution.py:91
  265.6 1.4 collective-permute-start.33
  267.4 3.0 collective-permute-done.27
  271.3 1.3 collective-permute-done.33.refs_7_
  272.6 1.2 collective-permute-done.34.refs_8_
  274.5 4.1 %shard_map.329 = bf16[3072,128]{1,0:T(8,128)(2,1)} custom-call(s32[8]{0:T(128)} %stack.34.index_ref, bf16[512,128]{1,0:T(8,128)(2,1)} %get-tuple-element.126.refs_0_, bf16[512,2048]{1,0:T(8,128)(2,1)} %get-tuple-element.84.hidden_ref.refs_1_, bf16[512,128]{1,0:T(8,128)(2,1)} %get-tuple-element.170.refs_2_, bf16[512,128]{1,0:T(8,128)(2,1)} %get-tuple-element.171.refs_3_, ...), custom_call_target="tpu_custom_call" | custom-call | bytes 3407872 | tf_op jit(solution)/shard_map/pallas_call | solution.py:91
  278.6 1.9 all-to-all-done.4
  280.7 24.9 %all_to_all.30 = bf16[8,384,128]{2,1,0:T(8,128)(2,1)S(1)} all-to-all(bf16[8,384,128]{2,1,0:T(8,128)(2,1)} %bitcast.58), channel_id=1, replica_groups=mesh['ctx'=8,'wa'=4] {'ctx'}, dimensions={0} | all-to-all | bytes 1572864 | tf_op jit(solution)/shard_map/all_to_all | solution.py:944
  306.5 11.5 %shard_map.327 = (f32[2,128,2048]{2,1,0:T(8,128)}, bf16[2,128,2048]{2,1,0:T(8,128)(2,1)}) custom-call(s32[8]{0:T(128)} %stack.34.index_ref, bf16[4,2,4,128,256]{4,3,2,1,0:T(8,128)(2,1)} %bitcast.51, bf16[4,2,4,128,256]{4,3,2,1,0:T(8,128)(2,1)} %bitcast.52, bf16[512,6144]{1,0:T(8,128)(2,1)} %refs_10_.5, ...), custom_call_target="tpu_custom_call" | custom-call | flops 3221225472 | bytes 14688256 | tf_op jit(solution)/shard_map/pallas_call | solution.py:91
  318.5 3.0 collective-permute-done.28.refs_1_
  321.5 2.5 fusion.8
  325.3 1.6 collective-permute-start.25
  327.0 1.4 constant_dynamic-slice_fusion.4.refs_4_
  328.4 1.4 constant_dynamic-slice_fusion.5.refs_3_
  329.7 9.4 %collective-permute-done.29.refs_2_ = bf16[128,2048]{1,0:T(8,128)(2,1)} collective-permute-done((bf16[128,2048]{1,0:T(8,128)(2,1)}, bf16[128,2048]{1,0:T(8,128)(2,1)}, u32[]{:S(2)}, u32[]{:S(2)}) %collective-permute-start.29) | collective-permute-done | bytes 524320 | tf_op jit(solution)/shard_map/ppermute | solution.py:40
  339.1 5.6 %shard_map.328 = f32[128,2048]{1,0:T(8,128)} custom-call(s32[8]{0:T(128)} %stack.34.index_ref, f32[2,128,2048]{2,1,0:T(8,128)} %get-tuple-element.123.refs_0_, bf16[2,128,2048]{2,1,0:T(8,128)(2,1)} %copy-done.6, bf16[128,2048]{1,0:T(8,128)(2,1)} %collective-permute-done.29.refs_2_, bf16[128,128]{1,0:T(8,128)(2,1)} %constant_dynamic-slice_fusion.5.refs_3_, ...), custom_call_target="tpu_custom_call" | custom-call | bytes 5849088 | tf_op jit(solution)/shard_map/pallas_call | solution.py:91
  344.7 4.8 %collective-permute-done.25 = bf16[128,2048]{1,0:T(8,128)(2,1)} collective-permute-done((bf16[128,2048]{1,0:T(8,128)(2,1)}, bf16[128,2048]{1,0:T(8,128)(2,1)}, u32[]{:S(2)}, u32[]{:S(2)}) %collective-permute-start.25) | collective-permute-done | bytes 524320 | tf_op jit(solution)/shard_map/ppermute | solution.py:40
  349.6 1.3 convolution_add_fusion.1
  350.9 1.9 fusion.4
  352.9 1.2 all-gather.6.cloned.1.call-done
  354.0 4.5 %shard_map.330 = (f32[2048,128]{1,0:T(8,128)}, f32[512,128]{1,0:T(8,128)}, f32[32,2048]{1,0:T(8,128)}, f32[32,8192]{1,0:T(8,128)}, f32[512,128]{1,0:T(8,128)}, /...) custom-call(s32[8]{0:T(128)} %stack.34.index_ref, bf16[8,1024,128]{2,1,0:T(8,128)(2,1)} %bitcast.62), custom_call_target="tpu_custom_call" | custom-call | bytes 2097152 | tf_op jit(solution)/shard_map/pallas_call | solution.py:91
  (160 shorter events, 26.0 us)
Async XLA Ops:
  7.2 105.2 %all-gather.4.cloned.1.call-start = ((), (), s32[]{:S(2)}) async-start(), calls=%async_computation.6 | async-start | bytes 3538944 | tf_op jit(solution)/shard_map/all_gather | solution.py:682
  7.8 6.4 %copy-start.30 = (s32[1,16]{1,0:T(1,128)S(1)}, s32[1,16]{1,0:T(1,128)}, u32[]{:S(2)}) copy-start(s32[1,16]{1,0:T(1,128)} %param.29) | copy-start | bytes 196
  7.9 6.4 %copy-start.31 = (s32[1,16]{1,0:T(1,128)S(1)}, s32[1,16]{1,0:T(1,128)}, u32[]{:S(2)}) copy-start(s32[1,16]{1,0:T(1,128)} %param.28) | copy-start | bytes 196
  7.9 7.1 %copy-start.4 = (bf16[32,6144]{1,0:T(8,128)(2,1)S(1)}, bf16[32,6144]{1,0:T(8,128)(2,1)}, u32[]{:S(2)}) copy-start(bf16[32,6144]{1,0:T(8,128)(2,1)} %refs_10_.4) | copy-start | bytes 1179652
  11.2 8.4 %collective-permute-start.1 = (bf16[64,1536]{1,0:T(8,128)(2,1)}, bf16[64,1536]{1,0:T(8,128)(2,1)S(1)}, u32[]{:S(2)}, u32[]{:S(2)}) collective-permute-start(bf16[64,1536]{1,0:T(8,128)(2,1)} %get-tuple-element.76), channel_id=1, source_target_pairs={{0,3},{1,2},{2,1},{3,0},{4,7},{5,6},{6,5},{7,4},{8,11},{9,10},{10,... | collective-permute-start | bytes 589832 | tf_op jit(solution)/shard_map/ppermute | solution.py:40
  13.6 9.9 %collective-permute-start = (bf16[64,1536]{1,0:T(8,128)(2,1)}, bf16[64,1536]{1,0:T(8,128)(2,1)S(1)}, u32[]{:S(2)}, u32[]{:S(2)}) collective-permute-start(bf16[64,1536]{1,0:T(8,128)(2,1)} %get-tuple-element.75), channel_id=1, source_target_pairs={{0,2},{1,3},{2,0},{3,1},{4,6},{5,7},{6,4},{7,5},{8,10},{9,11},{10,... | collective-permute-start | bytes 589832 | tf_op jit(solution)/shard_map/ppermute | solution.py:40
  24.3 8.0 %copy-start.7 = (bf16[1,128,2048]{2,1,0:T(8,128)(2,1)S(1)}, bf16[1,128,2048]{2,1,0:T(8,128)(2,1)}, u32[]{:S(2)}) copy-start(bf16[1,128,2048]{2,1,0:T(8,128)(2,1)} %param.26) | copy-start | bytes 1572868
  24.3 8.0 %copy-start.18 = (bf16[32,2048]{1,0:T(8,128)(2,1)S(1)}, bf16[32,2048]{1,0:T(8,128)(2,1)}, u32[]{:S(2)}) copy-start(bf16[32,2048]{1,0:T(8,128)(2,1)} %param.49) | copy-start | bytes 393220
  24.3 8.0 %copy-start.19 = (bf16[32,2048]{1,0:T(8,128)(2,1)S(1)}, bf16[32,2048]{1,0:T(8,128)(2,1)}, u32[]{:S(2)}) copy-start(bf16[32,2048]{1,0:T(8,128)(2,1)} %param.45) | copy-start | bytes 393220
  24.3 22.4 %collective-permute-start.4 = (bf16[3344,128]{1,0:T(8,128)(2,1)}, bf16[3344,128]{1,0:T(8,128)(2,1)S(1)}, u32[]{:S(2)}, u32[]{:S(2)}) collective-permute-start(bf16[3344,128]{1,0:T(8,128)(2,1)} %get-tuple-element.77), channel_id=1, source_target_pairs={{0,2},{1,3},{2,0},{3,1},{4,6},{5,7},{6,4},{7,5},{8,10},{9,11},{10,... | collective-permute-start | bytes 2568200 | tf_op jit(solution)/shard_map/ppermute | solution.py:40
  26.7 31.2 %collective-permute-start.3 = (bf16[3344,128]{1,0:T(8,128)(2,1)}, bf16[3344,128]{1,0:T(8,128)(2,1)S(1)}, u32[]{:S(2)}, u32[]{:S(2)}) collective-permute-start(bf16[3344,128]{1,0:T(8,128)(2,1)} %get-tuple-element.78), channel_id=1, source_target_pairs={{0,1},{1,0},{2,3},{3,2},{4,5},{5,4},{6,7},{7,6},{8,9},{9,8},{10,11... | collective-permute-start | bytes 2568200 | tf_op jit(solution)/shard_map/ppermute | solution.py:40
  32.1 37.2 %collective-permute-start.2 = (bf16[256,2048]{1,0:T(8,128)(2,1)}, bf16[256,2048]{1,0:T(8,128)(2,1)}, u32[]{:S(2)}, u32[]{:S(2)}) collective-permute-start(bf16[256,2048]{1,0:T(8,128)(2,1)} %get-tuple-element.80), channel_id=1, source_target_pairs={{0,2},{1,3},{2,0},{3,1},{4,6},{5,7},{6,4},{7,5},{8,10},{9,11},{10,... | collective-permute-start | bytes 3145736 | tf_op jit(solution)/shard_map/ppermute | solution.py:40
  32.3 22.4 %copy-start.11 = (bf16[192,2048]{1,0:T(8,128)(2,1)}, bf16[192,2048]{1,0:T(8,128)(2,1)S(1)}, u32[]{:S(2)}) copy-start(bf16[192,2048]{1,0:T(8,128)(2,1)S(1)} %pad_maximum_fusion.refs_0_) | copy-start | bytes 2359300
  32.4 64.1 %collective-permute-start.7 = (bf16[192,2048]{1,0:T(8,128)(2,1)S(1)}, bf16[192,2048]{1,0:T(8,128)(2,1)}, u32[]{:S(2)}, u32[]{:S(2)}) collective-permute-start(bf16[192,2048]{1,0:T(8,128)(2,1)S(1)} %pad_maximum_fusion.refs_0_), channel_id=1, source_target_pairs={{0,1},{1,0},{2,3},{3,2},{4,5},{5,4},{6,7},{7,6},{8,9},{9,8},{10,11... | collective-permute-start | bytes 2359304 | tf_op jit(solution)/shard_map/ppermute | solution.py:40
  46.7 40.7 %copy-start.1 = (bf16[3344,128]{1,0:T(8,128)(2,1)}, bf16[3344,128]{1,0:T(8,128)(2,1)S(1)}, u32[]{:S(2)}) copy-start(bf16[3344,128]{1,0:T(8,128)(2,1)S(1)} %collective-permute-done.4.refs_3_.refs_6_.refs_4_.refs_8_.refs_12_.refs_7_) | copy-start | bytes 2568196
  46.7 38.9 %collective-permute-start.8 = (bf16[192,2048]{1,0:T(8,128)(2,1)S(1)}, bf16[192,2048]{1,0:T(8,128)(2,1)}, u32[]{:S(2)}, u32[]{:S(2)}) collective-permute-start(bf16[192,2048]{1,0:T(8,128)(2,1)S(1)} %pad_maximum_fusion.refs_0_), channel_id=1, source_target_pairs={{0,2},{1,3},{2,0},{3,1},{4,6},{5,7},{6,4},{7,5},{8,10},{9,11},{10,... | collective-permute-start | bytes 2359304 | tf_op jit(solution)/shard_map/ppermute | solution.py:40
  48.8 38.6 %collective-permute-start.5 = (bf16[3344,128]{1,0:T(8,128)(2,1)S(1)}, bf16[3344,128]{1,0:T(8,128)(2,1)S(1)}, u32[]{:S(2)}, u32[]{:S(2)}) collective-permute-start(bf16[3344,128]{1,0:T(8,128)(2,1)S(1)} %collective-permute-done.4.refs_3_.refs_6_.refs_4_.refs_8_.refs_12_.refs_7_), channel_id=1, source_target_pairs={{0,1},{1,0},{2,3},{3,2},{4,5},{5,4},{6,7},{7,6},{8,9},{9,8},{10,11... | collective-permute-start | bytes 2568200 | tf_op jit(solution)/shard_map/ppermute | solution.py:40
  50.6 7.2 %copy-start.28 = (s32[16]{0:T(128)S(1)}, s32[16]{0:T(128)}, u32[]{:S(2)}) copy-start(s32[16]{0:T(128)} %param.27) | copy-start | bytes 196
  57.9 31.6 %copy-start.2 = (bf16[3344,128]{1,0:T(8,128)(2,1)}, bf16[3344,128]{1,0:T(8,128)(2,1)S(1)}, u32[]{:S(2)}) copy-start(bf16[3344,128]{1,0:T(8,128)(2,1)S(1)} %collective-permute-done.3.refs_2_.refs_5_.refs_3_.refs_7_.refs_11_.refs_6_) | copy-start | bytes 2568196
  57.9 54.5 %collective-permute-start.6 = (bf16[512,1536]{1,0:T(8,128)(2,1)}, bf16[512,1536]{1,0:T(8,128)(2,1)}, u32[]{:S(2)}, u32[]{:S(2)}) collective-permute-start(bf16[512,1536]{1,0:T(8,128)(2,1)} %shard_map.317), channel_id=1, source_target_pairs={{0,1},{1,0},{2,3},{3,2},{4,5},{5,4},{6,7},{7,6},{8,9},{9,8},{10,11... | collective-permute-start | bytes 4718600 | tf_op jit(solution)/shard_map/ppermute | solution.py:40
  85.6 25.0 %collective-permute-start.10 = (bf16[256,2048]{1,0:T(8,128)(2,1)}, bf16[256,2048]{1,0:T(8,128)(2,1)}, u32[]{:S(2)}, u32[]{:S(2)}) collective-permute-start(bf16[256,2048]{1,0:T(8,128)(2,1)} %get-tuple-element.95), channel_id=1, source_target_pairs={{0,2},{1,3},{2,0},{3,1},{4,6},{5,7},{6,4},{7,5},{8,10},{9,11},{10,... | collective-permute-start | bytes 3145736 | tf_op jit(solution)/shard_map/ppermute | solution.py:40
  87.4 9.1 %collective-permute-start.9 = (bf16[192,2048]{1,0:T(8,128)(2,1)}, bf16[192,2048]{1,0:T(8,128)(2,1)}, u32[]{:S(2)}, u32[]{:S(2)}) collective-permute-start(bf16[192,2048]{1,0:T(8,128)(2,1)} %collective-permute-done.8.refs_2_), channel_id=1, source_target_pairs={{0,1},{1,0},{2,3},{3,2},{4,5},{5,4},{6,7},{7,6},{8,9},{9,8},{10,11... | collective-permute-start | bytes 2359304 | tf_op jit(solution)/shard_map/ppermute | solution.py:40
  103.4 21.0 %all-to-all-start = ((bf16[8,128,256]{2,1,0:T(8,128)(2,1)}), bf16[8,128,256]{2,1,0:T(8,128)(2,1)S(1)}, u32[]{:S(2)}, u32[]{:S(2)}) async-start(bf16[8,128,256]{2,1,0:T(8,128)(2,1)} %bitcast.66), calls=%async_computation | async-start | bytes 1048576 | tf_op jit(solution)/shard_map/all_to_all | solution.py:795
  110.6 28.6 %collective-permute-start.11 = (bf16[256,2048]{1,0:T(8,128)(2,1)}, bf16[256,2048]{1,0:T(8,128)(2,1)}, u32[]{:S(2)}, u32[]{:S(2)}) collective-permute-start(bf16[256,2048]{1,0:T(8,128)(2,1)} %get-tuple-element.96), channel_id=1, source_target_pairs={{0,3},{1,2},{2,1},{3,0},{4,7},{5,6},{6,5},{7,4},{8,11},{9,10},{10,... | collective-permute-start | bytes 3145736 | tf_op jit(solution)/shard_map/ppermute | solution.py:40
  124.4 6.9 %copy-start.12 = (bf16[8,128,256]{2,1,0:T(8,128)(2,1)}, bf16[8,128,256]{2,1,0:T(8,128)(2,1)S(1)}, u32[]{:S(2)}) copy-start(bf16[8,128,256]{2,1,0:T(8,128)(2,1)S(1)} %all-to-all-done) | copy-start | bytes 1572868
  124.4 18.3 %all-to-all-start.1 = ((bf16[8,1,128,256]{3,2,1,0:T(8,128)(2,1)}), bf16[8,1,128,256]{3,2,1,0:T(8,128)(2,1)S(1)}, u32[]{:S(2)}, u32[]{:S(2)}) async-start(bf16[8,1,128,256]{3,2,1,0:T(8,128)(2,1)} %bitcast.61), calls=%async_computation.1 | async-start | bytes 1048576 | tf_op jit(solution)/shard_map/all_to_all | solution.py:795
  131.4 11.4 %copy-start.9 = (bf16[512,2048]{1,0:T(8,128)(2,1)S(1)}, bf16[512,2048]{1,0:T(8,128)(2,1)}, u32[]{:S(2)}) copy-start(bf16[512,2048]{1,0:T(8,128)(2,1)} %shard_map.321) | copy-start | bytes 6291460
  142.8 6.8 %copy-start.13 = (bf16[8,1,128,256]{3,2,1,0:T(8,128)(2,1)}, bf16[8,1,128,256]{3,2,1,0:T(8,128)(2,1)S(1)}, u32[]{:S(2)}) copy-start(bf16[8,1,128,256]{3,2,1,0:T(8,128)(2,1)S(1)} %all-to-all-done.1) | copy-start | bytes 1572868
  142.8 31.0 %collective-permute-start.12 = (bf16[512,2048]{1,0:T(8,128)(2,1)S(1)}, bf16[512,2048]{1,0:T(8,128)(2,1)}, u32[]{:S(2)}, u32[]{:S(2)}) collective-permute-start(bf16[512,2048]{1,0:T(8,128)(2,1)S(1)} %copy-done.9), channel_id=1, source_target_pairs={{0,1},{1,0},{2,3},{3,2},{4,5},{5,4},{6,7},{7,6},{8,9},{9,8},{10,11... | collective-permute-start | bytes 6291464 | tf_op jit(solution)/shard_map/ppermute | solution.py:40
  142.8 31.0 %all-to-all-start.2 = ((bf16[8,2,128,256]{3,2,1,0:T(8,128)(2,1)}), bf16[8,2,128,256]{3,2,1,0:T(8,128)(2,1)}, u32[]{:S(2)}, u32[]{:S(2)}) async-start(bf16[8,2,128,256]{3,2,1,0:T(8,128)(2,1)} %bitcast.57), calls=%async_computation.2 | async-start | bytes 2097152 | tf_op jit(solution)/shard_map/all_to_all | solution.py:795
  147.2 16.7 %collective-permute-start.13 = (bf16[1552,128]{1,0:T(8,128)(2,1)}, bf16[1552,128]{1,0:T(8,128)(2,1)S(1)}, u32[]{:S(2)}, u32[]{:S(2)}) collective-permute-start(bf16[1552,128]{1,0:T(8,128)(2,1)} %get-tuple-element.82), channel_id=1, source_target_pairs={{0,1},{1,0},{2,3},{3,2},{4,5},{5,4},{6,7},{7,6},{8,9},{9,8},{10,11... | collective-permute-start | bytes 1191944 | tf_op jit(solution)/shard_map/ppermute | solution.py:40
  147.9 12.3 %collective-permute-start.14 = (bf16[1552,128]{1,0:T(8,128)(2,1)}, bf16[1552,128]{1,0:T(8,128)(2,1)S(1)}, u32[]{:S(2)}, u32[]{:S(2)}) collective-permute-start(bf16[1552,128]{1,0:T(8,128)(2,1)} %get-tuple-element.99), channel_id=1, source_target_pairs={{0,2},{1,3},{2,0},{3,1},{4,6},{5,7},{6,4},{7,5},{8,10},{9,11},{10,... | collective-permute-start | bytes 1191944 | tf_op jit(solution)/shard_map/ppermute | solution.py:40
  149.8 34.0 %collective-permute-start.16 = (bf16[256,2048]{1,0:T(8,128)(2,1)}, bf16[256,2048]{1,0:T(8,128)(2,1)}, u32[]{:S(2)}, u32[]{:S(2)}) collective-permute-start(bf16[256,2048]{1,0:T(8,128)(2,1)} %get-tuple-element.102), channel_id=1, source_target_pairs={{0,3},{1,2},{2,1},{3,0},{4,7},{5,6},{6,5},{7,4},{8,11},{9,10},{10,... | collective-permute-start | bytes 3145736 | tf_op jit(solution)/shard_map/ppermute | solution.py:40
  160.2 23.5 %copy-start.15 = (bf16[1552,128]{1,0:T(8,128)(2,1)}, bf16[1552,128]{1,0:T(8,128)(2,1)S(1)}, u32[]{:S(2)}) copy-start(bf16[1552,128]{1,0:T(8,128)(2,1)S(1)} %collective-permute-done.14.refs_8_.refs_12_.refs_11_) | copy-start | bytes 1191940
  160.2 3.7 %collective-permute-start.15 = (bf16[1552,128]{1,0:T(8,128)(2,1)S(1)}, bf16[1552,128]{1,0:T(8,128)(2,1)}, u32[]{:S(2)}, u32[]{:S(2)}) collective-permute-start(bf16[1552,128]{1,0:T(8,128)(2,1)S(1)} %collective-permute-done.14.refs_8_.refs_12_.refs_11_), channel_id=1, source_target_pairs={{0,1},{1,0},{2,3},{3,2},{4,5},{5,4},{6,7},{7,6},{8,9},{9,8},{10,11... | collective-permute-start | bytes 1191944 | tf_op jit(solution)/shard_map/ppermute | solution.py:40
  163.9 19.8 %copy-start.14 = (bf16[1552,128]{1,0:T(8,128)(2,1)}, bf16[1552,128]{1,0:T(8,128)(2,1)S(1)}, u32[]{:S(2)}) copy-start(bf16[1552,128]{1,0:T(8,128)(2,1)S(1)} %collective-permute-done.13.refs_7_.refs_11_.refs_10_) | copy-start | bytes 1191940
  183.8 59.1 %all-to-all-start.3 = ((bf16[8,4,128,256]{3,2,1,0:T(8,128)(2,1)}), bf16[8,4,128,256]{3,2,1,0:T(8,128)(2,1)S(1)}, u32[]{:S(2)}, u32[]{:S(2)}) async-start(bf16[8,4,128,256]{3,2,1,0:T(8,128)(2,1)} %shard_map.322), calls=%async_computation.3 | async-start | bytes 4194304 | tf_op jit(solution)/shard_map/all_to_all | solution.py:795
  221.1 1.8 collective-permute-start.19
  221.2 3.3 collective-permute-start.17
  223.9 6.8 %collective-permute-start.20 = (bf16[512,128]{1,0:T(8,128)(2,1)S(1)}, bf16[512,128]{1,0:T(8,128)(2,1)S(1)}, u32[]{:S(2)}, u32[]{:S(2)}) collective-permute-start(bf16[512,128]{1,0:T(8,128)(2,1)S(1)} %add_convert_fusion.4), channel_id=1, source_target_pairs={{0,2},{1,3},{2,0},{3,1},{4,6},{5,7},{6,4},{7,5},{8,10},{9,11},{10,... | collective-permute-start | bytes 393224 | tf_op jit(solution)/shard_map/ppermute | solution.py:40
  225.5 7.2 %collective-permute-start.18 = (bf16[512,128]{1,0:T(8,128)(2,1)S(1)}, bf16[512,128]{1,0:T(8,128)(2,1)S(1)}, u32[]{:S(2)}, u32[]{:S(2)}) collective-permute-start(bf16[512,128]{1,0:T(8,128)(2,1)S(1)} %add_convert_fusion.5), channel_id=1, source_target_pairs={{0,2},{1,3},{2,0},{3,1},{4,6},{5,7},{6,4},{7,5},{8,10},{9,11},{10,... | collective-permute-start | bytes 393224 | tf_op jit(solution)/shard_map/ppermute | solution.py:40
  228.8 4.6 %collective-permute-start.21 = (bf16[32,2048]{1,0:T(8,128)(2,1)S(1)}, bf16[32,2048]{1,0:T(8,128)(2,1)S(1)}, u32[]{:S(2)}, u32[]{:S(2)}) collective-permute-start(bf16[32,2048]{1,0:T(8,128)(2,1)S(1)} %get-tuple-element.148), channel_id=1, source_target_pairs={{0,1},{1,0},{2,3},{3,2},{4,5},{5,4},{6,7},{7,6},{8,9},{9,8},{10,11... | collective-permute-start | bytes 393224 | tf_op jit(solution)/shard_map/ppermute | solution.py:40
  228.8 6.6 %collective-permute-start.22 = (bf16[32,2048]{1,0:T(8,128)(2,1)S(1)}, bf16[32,2048]{1,0:T(8,128)(2,1)S(1)}, u32[]{:S(2)}, u32[]{:S(2)}) collective-permute-start(bf16[32,2048]{1,0:T(8,128)(2,1)S(1)} %get-tuple-element.147), channel_id=1, source_target_pairs={{0,2},{1,3},{2,0},{3,1},{4,6},{5,7},{6,4},{7,5},{8,10},{9,11},{10,... | collective-permute-start | bytes 393224 | tf_op jit(solution)/shard_map/ppermute | solution.py:40
  229.4 8.3 %collective-permute-start.23 = (bf16[32,2048]{1,0:T(8,128)(2,1)S(1)}, bf16[32,2048]{1,0:T(8,128)(2,1)S(1)}, u32[]{:S(2)}, u32[]{:S(2)}) collective-permute-start(bf16[32,2048]{1,0:T(8,128)(2,1)S(1)} %get-tuple-element.146), channel_id=1, source_target_pairs={{0,3},{1,2},{2,1},{3,0},{4,7},{5,6},{6,5},{7,4},{8,11},{9,10},{10,... | collective-permute-start | bytes 393224 | tf_op jit(solution)/shard_map/ppermute | solution.py:40
  242.9 37.6 %all-to-all-start.4 = ((bf16[8,640,128]{2,1,0:T(8,128)(2,1)}), bf16[8,640,128]{2,1,0:T(8,128)(2,1)S(1)}, u32[]{:S(2)}, u32[]{:S(2)}) async-start(bf16[8,640,128]{2,1,0:T(8,128)(2,1)} %bitcast.56), calls=%async_computation.4 | async-start | bytes 2621440 | tf_op jit(solution)/shard_map/all_to_all | solution.py:944
  248.8 105.2 %all-gather.6.cloned.1.call-start = ((), (), s32[]{:S(2)}) async-start(), calls=%async_computation.7 | async-start | bytes 2359296 | tf_op jit(solution)/shard_map/all_gather | solution.py:1076
  253.6 8.2 %collective-permute-start.30 = (f32[512,128]{1,0:T(8,128)}, f32[512,128]{1,0:T(8,128)S(1)}, u32[]{:S(2)}, u32[]{:S(2)}) collective-permute-start(f32[512,128]{1,0:T(8,128)} %get-tuple-element.114), channel_id=1, source_target_pairs={{0,1},{1,0},{2,3},{3,2},{4,5},{5,4},{6,7},{7,6},{8,9},{9,8},{10,11... | collective-permute-start | bytes 786440 | tf_op jit(solution)/shard_map/ppermute | solution.py:40
  253.6 8.1 %copy-start.17 = (f32[512,128]{1,0:T(8,128)S(1)}, f32[512,128]{1,0:T(8,128)}, u32[]{:S(2)}) copy-start(f32[512,128]{1,0:T(8,128)} %get-tuple-element.114) | copy-start | bytes 786436
  253.6 11.3 %copy-start.16 = (bf16[128,1536]{1,0:T(8,128)(2,1)S(1)}, bf16[128,1536]{1,0:T(8,128)(2,1)}, u32[]{:S(2)}) copy-start(bf16[128,1536]{1,0:T(8,128)(2,1)} %get-tuple-element.127) | copy-start | bytes 1179652
  261.2 1.9 collective-permute-start.26
  261.8 5.7 %collective-permute-start.31 = (bf16[512,128]{1,0:T(8,128)(2,1)S(1)}, bf16[512,128]{1,0:T(8,128)(2,1)S(1)}, u32[]{:S(2)}, u32[]{:S(2)}) collective-permute-start(bf16[512,128]{1,0:T(8,128)(2,1)S(1)} %add_convert_fusion.2), channel_id=1, source_target_pairs={{0,2},{1,3},{2,0},{3,1},{4,6},{5,7},{6,4},{7,5},{8,10},{9,11},{10,... | collective-permute-start | bytes 393224 | tf_op jit(solution)/shard_map/ppermute | solution.py:40
  264.1 6.4 %collective-permute-start.27 = (bf16[512,128]{1,0:T(8,128)(2,1)S(1)}, bf16[512,128]{1,0:T(8,128)(2,1)S(1)}, u32[]{:S(2)}, u32[]{:S(2)}) collective-permute-start(bf16[512,128]{1,0:T(8,128)(2,1)S(1)} %add_convert_fusion.3), channel_id=1, source_target_pairs={{0,2},{1,3},{2,0},{3,1},{4,6},{5,7},{6,4},{7,5},{8,10},{9,11},{10,... | collective-permute-start | bytes 393224 | tf_op jit(solution)/shard_map/ppermute | solution.py:40
  265.6 5.7 %collective-permute-start.32 = (bf16[32,1536]{1,0:T(8,128)(2,1)S(1)}, bf16[32,1536]{1,0:T(8,128)(2,1)S(1)}, u32[]{:S(2)}, u32[]{:S(2)}) collective-permute-start(bf16[32,1536]{1,0:T(8,128)(2,1)S(1)} %get-tuple-element.155), channel_id=1, source_target_pairs={{0,1},{1,0},{2,3},{3,2},{4,5},{5,4},{6,7},{7,6},{8,9},{9,8},{10,11... | collective-permute-start | bytes 294920 | tf_op jit(solution)/shard_map/ppermute | solution.py:40
  265.6 7.0 %collective-permute-start.33 = (bf16[32,1536]{1,0:T(8,128)(2,1)S(1)}, bf16[32,1536]{1,0:T(8,128)(2,1)S(1)}, u32[]{:S(2)}, u32[]{:S(2)}) collective-permute-start(bf16[32,1536]{1,0:T(8,128)(2,1)S(1)} %get-tuple-element.154), channel_id=1, source_target_pairs={{0,2},{1,3},{2,0},{3,1},{4,6},{5,7},{6,4},{7,5},{8,10},{9,11},{10,... | collective-permute-start | bytes 294920 | tf_op jit(solution)/shard_map/ppermute | solution.py:40
  266.9 6.9 %collective-permute-start.34 = (bf16[32,1536]{1,0:T(8,128)(2,1)S(1)}, bf16[32,1536]{1,0:T(8,128)(2,1)S(1)}, u32[]{:S(2)}, u32[]{:S(2)}) collective-permute-start(bf16[32,1536]{1,0:T(8,128)(2,1)S(1)} %get-tuple-element.153), channel_id=1, source_target_pairs={{0,3},{1,2},{2,1},{3,0},{4,7},{5,6},{6,5},{7,4},{8,11},{9,10},{10,... | collective-permute-start | bytes 294920 | tf_op jit(solution)/shard_map/ppermute | solution.py:40
  306.5 11.6 %copy-start.29 = (bf16[2,128,2048]{2,1,0:T(8,128)(2,1)S(1)}, bf16[2,128,2048]{2,1,0:T(8,128)(2,1)}, u32[]{:S(2)}) copy-start(bf16[2,128,2048]{2,1,0:T(8,128)(2,1)} %get-tuple-element.118) | copy-start | bytes 3145732
  318.0 6.4 %copy-start.8 = (f32[2,128,2048]{2,1,0:T(8,128)S(1)}, f32[2,128,2048]{2,1,0:T(8,128)}, u32[]{:S(2)}) copy-start(f32[2,128,2048]{2,1,0:T(8,128)} %get-tuple-element.117) | copy-start | bytes 6291460
  318.0 3.5 collective-permute-start.28
  318.0 6.4 %collective-permute-start.24 = (bf16[2,128,2048]{2,1,0:T(8,128)(2,1)S(1)}, bf16[2,128,2048]{2,1,0:T(8,128)(2,1)S(1)}, u32[]{:S(2)}, u32[]{:S(2)}) collective-permute-start(bf16[2,128,2048]{2,1,0:T(8,128)(2,1)S(1)} %copy-done.29), channel_id=1, source_target_pairs={{0,1},{1,0},{2,3},{3,2},{4,5},{5,4},{6,7},{7,6},{8,9},{9,8},{10,11... | collective-permute-start | bytes 3145736 | tf_op jit(solution)/shard_map/ppermute | solution.py:40
  324.0 15.1 %collective-permute-start.29 = (bf16[128,2048]{1,0:T(8,128)(2,1)}, bf16[128,2048]{1,0:T(8,128)(2,1)}, u32[]{:S(2)}, u32[]{:S(2)}) collective-permute-start(bf16[128,2048]{1,0:T(8,128)(2,1)} %fusion.8), channel_id=1, source_target_pairs={{0,2},{1,3},{2,0},{3,1},{4,6},{5,7},{6,4},{7,5},{8,10},{9,11},{10,... | collective-permute-start | bytes 1572872 | tf_op jit(solution)/shard_map/ppermute | solution.py:40
  325.3 24.2 %collective-permute-start.25 = (bf16[128,2048]{1,0:T(8,128)(2,1)}, bf16[128,2048]{1,0:T(8,128)(2,1)}, u32[]{:S(2)}, u32[]{:S(2)}) collective-permute-start(bf16[128,2048]{1,0:T(8,128)(2,1)} %fusion.7), channel_id=1, source_target_pairs={{0,2},{1,3},{2,0},{3,1},{4,6},{5,7},{6,4},{7,5},{8,10},{9,11},{10,... | collective-permute-start | bytes 1572872 | tf_op jit(solution)/shard_map/ppermute | solution.py:40
  329.7 19.8 %copy-start.10 = (bf16[2,128,2048]{2,1,0:T(8,128)(2,1)S(1)}, bf16[2,128,2048]{2,1,0:T(8,128)(2,1)}, u32[]{:S(2)}) copy-start(bf16[2,128,2048]{2,1,0:T(8,128)(2,1)} %get-tuple-element.120) | copy-start | bytes 3145732
  344.7 6.2 %copy-start.26 = (f32[2048]{0:T(1024)S(1)}, f32[2048]{0:T(1024)}, u32[]{:S(2)}) copy-start(f32[2048]{0:T(1024)} %param.41) | copy-start | bytes 24580
  344.7 6.2 %copy-start.27 = (f32[2048]{0:T(1024)S(1)}, f32[2048]{0:T(1024)}, u32[]{:S(2)}) copy-start(f32[2048]{0:T(1024)} %param.37) | copy-start | bytes 24580
  (10 other events, 29.5 us)
Sparse Core Ops, SparseCore 0:
  24.4 62.5 all-gather.3
  306.6 47.4 all-gather.5

commit v7 on v6

--- a/solution.py
+++ b/solution.py
@@ -312,9 +312,10 @@
         out_inner_ref,
         inner_grad_ref,
         out_down_grad_ref,
-        in_up_grad_ref,
+        *in_up_grad_refs,
         inner_ref,
         joined,
+        up_grad,
     ) = refs[5:]
     step = pl.program_id(0)
 
@@ -350,7 +351,11 @@
     out_inner_ref[...] += product(units, out_down_ref[...])
     inner_grad_ref[...] += times_t(pre_grad, joined[...])
     out_down_grad_ref[...] = t_times(units, out_inner_grad_ref[...]).astype(bf16)
-    in_up_grad_ref[...] = t_times(inner_ref[...], pre_grad).astype(bf16)
+    up_grad[...] = t_times(inner_ref[...], pre_grad)
+    size = ADAPT_COLS // WA
+    for r, ref in enumerate(in_up_grad_refs):
+        first = pl.multiple_of(index_ref[r] * size, size)
+        ref[...] = up_grad[pl.ds(first, size), :].astype(bf16)
 
     @pl.when(step == pl.num_programs(0) - 1)
     def _():
@@ -866,11 +871,11 @@
                 ((total, ADAPT_COLS), f32, None, None),
                 ((total, ADAPT_COLS), f32, None, None),
                 ((size, ADAPT_COLS), bf16, (tile, ADAPT_COLS), lambda t, ref: (t, 0)),
-                ((ADAPT_COLS, size), bf16, (ADAPT_COLS, tile), lambda t, ref: (0, t)),
-                ((total, ADAPT_COLS), bf16, None, None),
-            ],
+            ]
+            + [((part_cols, size), bf16, (part_cols, tile), lambda t, ref: (0, t))] * WA
+            + [((total, ADAPT_COLS), bf16, None, None)],
             grid=(count,),
-            scratch=[pltpu.VMEM((ADAPT_COLS, tile), bf16)],
+            scratch=[pltpu.VMEM((ADAPT_COLS, tile), bf16), pltpu.VMEM((ADAPT_COLS, tile), f32)],
             flops=8 * total * width * size,
         )
 
@@ -880,7 +885,7 @@
         out_inner,
         second_inner_grad,
         out_down_grad,
-        in_up_grad,
+        *in_up_grads,
         second_inner,
     ) = feed(0, None, second_norm, pair)
 
@@ -957,7 +962,7 @@
             scratch=[pltpu.VMEM((ADAPT_COLS, width), f32)],
         )[0]
 
-    in_up_parts = spread_rows(in_up_grad)
+    in_up_parts = in_up_grads[:1] + [swap(in_up_grads[r], r) for r in (1, 2, 3)]
     out_inner = sum_inner(out_inner)
     second_inner_grad = sum_inner(second_inner_grad)
     feed_packed = pack_grads(

time: 367 us -> 367 us (level)
  transfers between devices with their start and end apart: 42 -> 42, of which waited for: 22 -> 24; matrix products, arithmetic and copies ran while one was open for 8% -> 8% of each run, Pallas kernels for 35% -> 35%
where the time goes in v7:
time: 367 us; the launch traced here: 365 us
  Pallas kernels  136 us (37%)
  waiting for transfers between devices  111 us (30%)
  starting transfers between devices  46.8 us (13%)
  blocking collectives  24.4 us (7%)
  other arithmetic  20.8 us (6%)
  between operations  14.5 us (4%)
  local copies, waits for them, and re-layouts  8.54 us (2%)
    pallas_call x18, Pallas kernels, call(): pl.pallas_call(kernel, grid_spec=pltpu.PrefetchScalarGridSpec(num_scalar_...  126 us
    ppermute x35, waiting for transfers between devices, swap(): return lax.ppermute(value, 'wa', [(i, i ^ bits) for i in range(WA)])  87.4 us
    all_to_all x1, blocking collectives, exchange_sum(): parts = lax.all_to_all(parts, 'ctx', 0, 0, tiled=True)  24.4 us
    ppermute x35, starting transfers between devices, swap(): return lax.ppermute(value, 'wa', [(i, i ^ bits) for i in range(WA)])  23.2 us
    all_to_all x4, waiting for transfers between devices, to_pairs(): return lax.all_to_all(item, 'ctx', 0, 0, tiled=True)  20.1 us
    all_to_all x4, starting transfers between devices, to_pairs(): return lax.all_to_all(item, 'ctx', 0, 0, tiled=True)  17.5 us
    pallas_call x1, Pallas kernels, attend(): pl.pallas_call(functools.partial(attention_kernel, joint), grid=(rows //...  10 us
  transfers between devices with their start and end apart: 42, of which 24 were waited for; matrix products, arithmetic and copies ran while one was open for 8% of the time, Pallas kernels for 35%

profile of v7, /device:TPU:0, one launch (start us, length us, event | category | flops | bytes accessed | tf_op | source)
XLA Modules:
  0.0 365.1 jit_solution(18155980611106961734)
XLA Ops:
  7.9 3.4 shard_map.313
  11.3 2.4 collective-permute-start.1
  16.4 3.3 shard_map.314
  19.7 3.8 %collective-permute-done = bf16[64,1536]{1,0:T(8,128)(2,1)S(1)} collective-permute-done((bf16[64,1536]{1,0:T(8,128)(2,1)}, bf16[64,1536]{1,0:T(8,128)(2,1)S(1)}, u32[]{:S(2)}, u32[]{:S(2)}) %collective-permute-start) | collective-permute-done | bytes 196640 | tf_op jit(solution)/shard_map/ppermute | solution.py:40
  24.4 2.4 collective-permute-start.4
  26.7 5.4 %shard_map.312 = (bf16[256,2048]{1,0:T(8,128)(2,1)}, bf16[256,2048]{1,0:T(8,128)(2,1)}, bf16[256,2048]{1,0:T(8,128)(2,1)}, bf16[256,2048]{1,0:T(8,128)(2,1)}) custom-call(s32[8]{0:T(128)} %stack.34.index_ref, bf16[512,8192]{1,0:T(8,128)(2,1)} %refs_0_.15, bf16[512,8192]{1,0:T(8,128)(2,1)} %refs_0_.15, bf16[512,8192]{1,0:T(8,128)(2,1)} %refs_0_.15, ...), custom_call_target="tpu_custom_call" | custom-call | bytes 4194304 | tf_op jit(solution)/shard_map/pallas_call | solution.py:91
  32.8 13.9 %collective-permute-done.4.refs_3_.refs_6_.refs_4_.refs_8_.refs_12_.refs_7_ = bf16[3344,128]{1,0:T(8,128)(2,1)S(1)} collective-permute-done((bf16[3344,128]{1,0:T(8,128)(2,1)}, bf16[3344,128]{1,0:T(8,128)(2,1)S(1)}, u32[]{:S(2)}, u32[]{:S(2)}) %collective-permute-start.4) | collective-permute-done | bytes 856096 | tf_op jit(solution)/shard_map/ppermute | solution.py:40
  46.8 2.1 collective-permute-start.8
  48.8 1.8 constant_dynamic-slice_fusion.6
  50.6 4.2 %shard_map.317 = bf16[512,1536]{1,0:T(8,128)(2,1)} custom-call(s32[8]{0:T(128)} %stack.34.index_ref, bf16[512,6144]{1,0:T(8,128)(2,1)} %refs_10_.5), custom_call_target="tpu_custom_call" | custom-call | bytes 1572864 | tf_op jit(solution)/shard_map/pallas_call | solution.py:91
  54.8 3.0 shard_map.315
  58.4 10.9 %collective-permute-done.2.refs_2_ = bf16[256,2048]{1,0:T(8,128)(2,1)} collective-permute-done((bf16[256,2048]{1,0:T(8,128)(2,1)}, bf16[256,2048]{1,0:T(8,128)(2,1)}, u32[]{:S(2)}, u32[]{:S(2)}) %collective-permute-start.2) | collective-permute-done | bytes 1048608 | tf_op jit(solution)/shard_map/ppermute | solution.py:40
  69.3 16.3 %collective-permute-done.8.refs_2_ = bf16[192,2048]{1,0:T(8,128)(2,1)} collective-permute-done((bf16[192,2048]{1,0:T(8,128)(2,1)S(1)}, bf16[192,2048]{1,0:T(8,128)(2,1)}, u32[]{:S(2)}, u32[]{:S(2)}) %collective-permute-start.8) | collective-permute-done | bytes 786464 | tf_op jit(solution)/shard_map/ppermute | solution.py:40
  85.7 1.7 collective-permute-start.10
  89.5 6.9 %shard_map.316 = (bf16[512,2048]{1,0:T(8,128)(2,1)}, bf16[512,2048]{1,0:T(8,128)(2,1)}, bf16[512,128]{1,0:T(8,128)(2,1)}) custom-call(s32[8]{0:T(128)} %stack.34.index_ref, bf16[128,2048]{1,0:T(8,128)(2,1)} %bitcast.54, bf16[512,128]{1,0:T(8,128)(2,1)} %refs_5_.3, bf16[3344,128]{1,0:T(8,128)(2,1)} %copy-done.2, bf16[3344,128]{1,0:T(8,128)(2,1)} %copy-done.1, ...), custom_call_target="tpu_custom_call" | custom-call | flops 268435456 | bytes 3518464 | tf_op jit(solution)/shard_map/pallas_call | solution.py:91
  96.5 7.0 %shard_map.318 = (bf16[512,2048]{1,0:T(8,128)(2,1)}, bf16[512,128]{1,0:T(8,128)(2,1)}, bf16[512,128]{1,0:T(8,128)(2,1)}, bf16[4,2,128,256]{3,2,1,0:T(8,128)(2,1)}, bf16[2,128,2048]{2,1,0:T(8,128)(2,1)}) custom-call(s32[8]{0:T(128)} %stack.34.index_ref, bf16[192,2048]{1,0:T(8,128)(2,1)} %copy-done.11, bf16[192,2048]{1,0:T(8,128)(2,1)} %collective-permute-done.7.refs_1_, ...), custom_call_target="tpu_custom_call" | custom-call | flops 1610612736 | bytes 5636096 | tf_op jit(solution)/shard_map/pallas_call | solution.py:91
  103.5 5.8 %all-to-all-start = ((bf16[8,128,256]{2,1,0:T(8,128)(2,1)}), bf16[8,128,256]{2,1,0:T(8,128)(2,1)S(1)}, u32[]{:S(2)}, u32[]{:S(2)}) async-start(bf16[8,128,256]{2,1,0:T(8,128)(2,1)} %bitcast.66), calls=%async_computation | async-start | bytes 1048576 | tf_op jit(solution)/shard_map/all_to_all | solution.py:800
  109.3 1.3 collective-permute-done.10.refs_3_
  110.6 1.8 fusion.16
  112.4 5.2 %shard_map.320 = bf16[4,2,1,128,256]{4,3,2,1,0:T(8,128)(2,1)} custom-call(s32[8]{0:T(128)} %stack.34.index_ref, bf16[512,2048]{1,0:T(8,128)(2,1)} %get-tuple-element.87.hidden_ref.refs_1_, bf16[512,6144]{1,0:T(8,128)(2,1)} %refs_10_.5, bf16[512,1536]{1,0:T(8,128)(2,1)} %collective-permute-done.6.refs_1_.refs_3_.refs_7_.refs_11_, ...), custom_call_target="tpu_custom_call" | custom-call | flops 1073741824 | bytes 4981760 | tf_op jit(solution)/shard_map/pallas_call | solution.py:91
  117.7 6.8 %all-to-all-done = bf16[8,128,256]{2,1,0:T(8,128)(2,1)S(1)} async-done(((bf16[8,128,256]{2,1,0:T(8,128)(2,1)}), bf16[8,128,256]{2,1,0:T(8,128)(2,1)S(1)}, u32[]{:S(2)}, u32[]{:S(2)}) %all-to-all-start) | async-done | bytes 524320 | tf_op jit(solution)/shard_map/all_to_all | solution.py:800
  124.5 3.6 all-to-all-start.1
  128.1 3.3 shard_map.321
  131.4 7.8 %shard_map.319 = bf16[4,2,2,128,256]{4,3,2,1,0:T(8,128)(2,1)} custom-call(s32[8]{0:T(128)} %stack.34.index_ref, bf16[512,2048]{1,0:T(8,128)(2,1)} %get-tuple-element.87.hidden_ref.refs_1_, bf16[512,6144]{1,0:T(8,128)(2,1)} %refs_10_.5, bf16[512,1536]{1,0:T(8,128)(2,1)} %collective-permute-done.6.refs_1_.refs_3_.refs_7_.refs_11_, ...), custom_call_target="tpu_custom_call" | custom-call | flops 2147483648 | bytes 7211008 | tf_op jit(solution)/shard_map/pallas_call | solution.py:91
  139.3 3.6 all-to-all-done.1
  142.8 4.4 %all-to-all-start.2 = ((bf16[8,2,128,256]{3,2,1,0:T(8,128)(2,1)}), bf16[8,2,128,256]{3,2,1,0:T(8,128)(2,1)}, u32[]{:S(2)}, u32[]{:S(2)}) async-start(bf16[8,2,128,256]{3,2,1,0:T(8,128)(2,1)} %bitcast.57), calls=%async_computation.2 | async-start | bytes 2097152 | tf_op jit(solution)/shard_map/all_to_all | solution.py:800
  148.6 1.0 copy.42.begin_ref
  151.7 8.6 %collective-permute-done.14.refs_8_.refs_12_.refs_11_ = bf16[1552,128]{1,0:T(8,128)(2,1)S(1)} collective-permute-done((bf16[1552,128]{1,0:T(8,128)(2,1)}, bf16[1552,128]{1,0:T(8,128)(2,1)S(1)}, u32[]{:S(2)}, u32[]{:S(2)}) %collective-permute-start.14) | collective-permute-done | bytes 397344 | tf_op jit(solution)/shard_map/ppermute | solution.py:40
  160.9 3.1 fusion.5
  164.0 9.8 %all-to-all-done.2.query_ref.key_ref = bf16[8,2,128,256]{3,2,1,0:T(8,128)(2,1)} async-done(((bf16[8,2,128,256]{3,2,1,0:T(8,128)(2,1)}), bf16[8,2,128,256]{3,2,1,0:T(8,128)(2,1)}, u32[]{:S(2)}, u32[]{:S(2)}) %all-to-all-start.2) | async-done | bytes 1048608 | tf_op jit(solution)/shard_map/all_to_all | solution.py:800
  173.8 10.0 %shard_map.322 = bf16[8,4,128,256]{3,2,1,0:T(8,128)(2,1)} custom-call(bf16[8,2,128,256]{3,2,1,0:T(8,128)(2,1)} %all-to-all-done.2.query_ref.key_ref, bf16[8,2,128,256]{3,2,1,0:T(8,128)(2,1)} %all-to-all-done.2.query_ref.key_ref, bf16[1024,256]{1,0:T(8,128)(2,1)} %bitcast.65, bf16[1024,256]{1,0:T(8,128)(2,1)} %bitcast.64, s32[1024,1]{1,0:T(8,128)} %copy.42.begin_ref, ...), custom_call_target="tpu_custom_call" | custom-call | flops 3758096384 | bytes 4194304 | tf_op jit(solution)/shard_map/pallas_call | solution.py:601
  183.8 3.6 all-to-all-start.3
  187.5 33.8 %shard_map.323 = (f32[512,2048]{1,0:T(8,128)}, f32[512,2048]{1,0:T(8,128)}, f32[512,128]{1,0:T(8,128)}, f32[512,128]{1,0:T(8,128)}, bf16[2048,128]{1,0:T(8,128)(...) custom-call(s32[8]{0:T(128)} %stack.34.index_ref, ...), custom_call_target="tpu_custom_call" | custom-call | flops 17179869184 | bytes 24129536 | tf_op jit(solution)/shard_map/pallas_call | solution.py:91
  221.8 1.2 collective-permute-done.19
  225.6 1.6 collective-permute-start.18
  227.7 1.3 collective-permute-start.23
  229.1 1.4 collective-permute-done.20
  230.5 2.8 collective-permute-done.18
  234.1 1.9 collective-permute-done.22.refs_7_
  236.1 1.2 collective-permute-done.23.refs_8_
  237.9 4.6 %shard_map.324 = bf16[5120,128]{1,0:T(8,128)(2,1)} custom-call(s32[8]{0:T(128)} %stack.34.index_ref, bf16[2048,128]{1,0:T(8,128)(2,1)} %get-tuple-element.112.refs_0_, bf16[512,2048]{1,0:T(8,128)(2,1)} %get-tuple-element.108.hidden_ref.refs_1_, bf16[512,128]{1,0:T(8,128)(2,1)} %get-tuple-element.175.refs_2_, bf16[512,128]{1,0:T(8,128)(2,1)} %get-tuple-element.174.refs_3_, ...), custom_call_target="tpu_custom_call" | custom-call | bytes 3932160 | tf_op jit(solution)/shard_map/pallas_call | solution.py:91
  242.5 5.9 %all-to-all-start.4 = ((bf16[8,640,128]{2,1,0:T(8,128)(2,1)}), bf16[8,640,128]{2,1,0:T(8,128)(2,1)S(1)}, u32[]{:S(2)}, u32[]{:S(2)}) async-start(bf16[8,640,128]{2,1,0:T(8,128)(2,1)} %bitcast.56), calls=%async_computation.4 | async-start | bytes 2621440 | tf_op jit(solution)/shard_map/all_to_all | solution.py:949
  248.5 4.7 %shard_map.325 = (f32[512,128]{1,0:T(8,128)}, bf16[128,1536]{1,0:T(8,128)(2,1)}) custom-call(s32[8]{0:T(128)} %stack.34.index_ref, bf16[4,2,4,128,256]{4,3,2,1,0:T(8,128)(2,1)} %bitcast.48, bf16[4,2,4,128,256]{4,3,2,1,0:T(8,128)(2,1)} %bitcast.49, bf16[32,6144]{1,0:T(8,128)(2,1)} %refs_10_.4, bf16[3344,128]{1,0:T(8,128)(2,1)} %copy-done.2, ...), custom_call_target="tpu_custom_call" | custom-call | flops 402653184 | bytes 4718592 | tf_op jit(solution)/shard_map/pallas_call | solution.py:91
  253.5 7.6 %shard_map.326 = (f32[2,128,2048]{2,1,0:T(8,128)}, bf16[2,128,2048]{2,1,0:T(8,128)(2,1)}, f32[512,128]{1,0:T(8,128)}, bf16[512,128]{1,0:T(8,128)(2,1)}) custom-call(s32[8]{0:T(128)} %stack.34.index_ref, bf16[4,2,4,128,256]{4,3,2,1,0:T(8,128)(2,1)} %bitcast.50, f32[512,2048]{1,0:T(8,128)} %get-tuple-element.110.sum_ref, bf16[512,2048]{1,0:T(8,128)(2,1)} %weight_ref.1, ...), custom_call_target="tpu_custom_call" | custom-call | flops 1073741824 | bytes 8650752 | tf_op jit(solution)/shard_map/pallas_call | solution.py:91
  265.2 1.4 collective-permute-start.33
  267.6 2.8 collective-permute-done.27
  271.2 1.3 collective-permute-done.33.refs_7_
  272.5 1.3 collective-permute-done.34.refs_8_
  274.5 4.1 %shard_map.329 = bf16[3072,128]{1,0:T(8,128)(2,1)} custom-call(s32[8]{0:T(128)} %stack.34.index_ref, bf16[512,128]{1,0:T(8,128)(2,1)} %get-tuple-element.132.refs_0_, bf16[512,2048]{1,0:T(8,128)(2,1)} %get-tuple-element.87.hidden_ref.refs_1_, bf16[512,128]{1,0:T(8,128)(2,1)} %get-tuple-element.172.refs_2_, bf16[512,128]{1,0:T(8,128)(2,1)} %get-tuple-element.173.refs_3_, ...), custom_call_target="tpu_custom_call" | custom-call | bytes 3407872 | tf_op jit(solution)/shard_map/pallas_call | solution.py:91
  278.6 2.0 all-to-all-done.4
  280.8 24.4 %all_to_all.30 = bf16[8,384,128]{2,1,0:T(8,128)(2,1)S(1)} all-to-all(bf16[8,384,128]{2,1,0:T(8,128)(2,1)} %bitcast.58), channel_id=1, replica_groups=mesh['ctx'=8,'wa'=4] {'ctx'}, dimensions={0} | all-to-all | bytes 1572864 | tf_op jit(solution)/shard_map/all_to_all | solution.py:949
  306.1 11.5 %shard_map.327 = (f32[2,128,2048]{2,1,0:T(8,128)}, bf16[2,128,2048]{2,1,0:T(8,128)(2,1)}) custom-call(s32[8]{0:T(128)} %stack.34.index_ref, bf16[4,2,4,128,256]{4,3,2,1,0:T(8,128)(2,1)} %bitcast.51, bf16[4,2,4,128,256]{4,3,2,1,0:T(8,128)(2,1)} %bitcast.52, bf16[512,6144]{1,0:T(8,128)(2,1)} %refs_10_.5, ...), custom_call_target="tpu_custom_call" | custom-call | flops 3221225472 | bytes 14688256 | tf_op jit(solution)/shard_map/pallas_call | solution.py:91
  318.2 3.0 collective-permute-done.28.refs_1_
  321.2 2.5 fusion.8
  325.2 1.5 collective-permute-start.25
  326.6 1.4 constant_dynamic-slice_fusion.4.refs_4_
  328.0 1.4 constant_dynamic-slice_fusion.5.refs_3_
  329.4 9.4 %collective-permute-done.29.refs_2_ = bf16[128,2048]{1,0:T(8,128)(2,1)} collective-permute-done((bf16[128,2048]{1,0:T(8,128)(2,1)}, bf16[128,2048]{1,0:T(8,128)(2,1)}, u32[]{:S(2)}, u32[]{:S(2)}) %collective-permute-start.29) | collective-permute-done | bytes 524320 | tf_op jit(solution)/shard_map/ppermute | solution.py:40
  338.8 5.6 %shard_map.328 = f32[128,2048]{1,0:T(8,128)} custom-call(s32[8]{0:T(128)} %stack.34.index_ref, f32[2,128,2048]{2,1,0:T(8,128)} %get-tuple-element.129.refs_0_, bf16[2,128,2048]{2,1,0:T(8,128)(2,1)} %copy-done.6, bf16[128,2048]{1,0:T(8,128)(2,1)} %collective-permute-done.29.refs_2_, bf16[128,128]{1,0:T(8,128)(2,1)} %constant_dynamic-slice_fusion.5.refs_3_, ...), custom_call_target="tpu_custom_call" | custom-call | bytes 5849088 | tf_op jit(solution)/shard_map/pallas_call | solution.py:91
  344.4 4.8 %collective-permute-done.25 = bf16[128,2048]{1,0:T(8,128)(2,1)} collective-permute-done((bf16[128,2048]{1,0:T(8,128)(2,1)}, bf16[128,2048]{1,0:T(8,128)(2,1)}, u32[]{:S(2)}, u32[]{:S(2)}) %collective-permute-start.25) | collective-permute-done | bytes 524320 | tf_op jit(solution)/shard_map/ppermute | solution.py:40
  349.2 1.3 convolution_add_fusion.1
  350.6 1.9 fusion.4
  352.5 1.3 all-gather.6.cloned.1.call-done
  353.8 4.5 %shard_map.330 = (f32[2048,128]{1,0:T(8,128)}, f32[512,128]{1,0:T(8,128)}, f32[32,2048]{1,0:T(8,128)}, f32[32,8192]{1,0:T(8,128)}, f32[512,128]{1,0:T(8,128)}, /...) custom-call(s32[8]{0:T(128)} %stack.34.index_ref, bf16[8,1024,128]{2,1,0:T(8,128)(2,1)} %bitcast.62), custom_call_target="tpu_custom_call" | custom-call | bytes 2097152 | tf_op jit(solution)/shard_map/pallas_call | solution.py:91
  (161 shorter events, 26.7 us)
Async XLA Ops:
  7.2 105.3 %all-gather.4.cloned.1.call-start = ((), (), s32[]{:S(2)}) async-start(), calls=%async_computation.6 | async-start | bytes 3538944 | tf_op jit(solution)/shard_map/all_gather | solution.py:687
  7.9 6.4 %copy-start.31 = (s32[1,16]{1,0:T(1,128)S(1)}, s32[1,16]{1,0:T(1,128)}, u32[]{:S(2)}) copy-start(s32[1,16]{1,0:T(1,128)} %param.29) | copy-start | bytes 196
  7.9 6.4 %copy-start.32 = (s32[1,16]{1,0:T(1,128)S(1)}, s32[1,16]{1,0:T(1,128)}, u32[]{:S(2)}) copy-start(s32[1,16]{1,0:T(1,128)} %param.28) | copy-start | bytes 196
  7.9 7.1 %copy-start.4 = (bf16[32,6144]{1,0:T(8,128)(2,1)S(1)}, bf16[32,6144]{1,0:T(8,128)(2,1)}, u32[]{:S(2)}) copy-start(bf16[32,6144]{1,0:T(8,128)(2,1)} %refs_10_.4) | copy-start | bytes 1179652
  11.3 8.4 %collective-permute-start.1 = (bf16[64,1536]{1,0:T(8,128)(2,1)}, bf16[64,1536]{1,0:T(8,128)(2,1)S(1)}, u32[]{:S(2)}, u32[]{:S(2)}) collective-permute-start(bf16[64,1536]{1,0:T(8,128)(2,1)} %get-tuple-element.79), channel_id=1, source_target_pairs={{0,3},{1,2},{2,1},{3,0},{4,7},{5,6},{6,5},{7,4},{8,11},{9,10},{10,... | collective-permute-start | bytes 589832 | tf_op jit(solution)/shard_map/ppermute | solution.py:40
  13.6 9.9 %collective-permute-start = (bf16[64,1536]{1,0:T(8,128)(2,1)}, bf16[64,1536]{1,0:T(8,128)(2,1)S(1)}, u32[]{:S(2)}, u32[]{:S(2)}) collective-permute-start(bf16[64,1536]{1,0:T(8,128)(2,1)} %get-tuple-element.78), channel_id=1, source_target_pairs={{0,2},{1,3},{2,0},{3,1},{4,6},{5,7},{6,4},{7,5},{8,10},{9,11},{10,... | collective-permute-start | bytes 589832 | tf_op jit(solution)/shard_map/ppermute | solution.py:40
  24.3 8.0 %copy-start.7 = (bf16[1,128,2048]{2,1,0:T(8,128)(2,1)S(1)}, bf16[1,128,2048]{2,1,0:T(8,128)(2,1)}, u32[]{:S(2)}) copy-start(bf16[1,128,2048]{2,1,0:T(8,128)(2,1)} %param.26) | copy-start | bytes 1572868
  24.3 8.0 %copy-start.19 = (bf16[32,2048]{1,0:T(8,128)(2,1)S(1)}, bf16[32,2048]{1,0:T(8,128)(2,1)}, u32[]{:S(2)}) copy-start(bf16[32,2048]{1,0:T(8,128)(2,1)} %param.49) | copy-start | bytes 393220
  24.3 8.0 %copy-start.20 = (bf16[32,2048]{1,0:T(8,128)(2,1)S(1)}, bf16[32,2048]{1,0:T(8,128)(2,1)}, u32[]{:S(2)}) copy-start(bf16[32,2048]{1,0:T(8,128)(2,1)} %param.45) | copy-start | bytes 393220
  24.4 22.4 %collective-permute-start.4 = (bf16[3344,128]{1,0:T(8,128)(2,1)}, bf16[3344,128]{1,0:T(8,128)(2,1)S(1)}, u32[]{:S(2)}, u32[]{:S(2)}) collective-permute-start(bf16[3344,128]{1,0:T(8,128)(2,1)} %get-tuple-element.80), channel_id=1, source_target_pairs={{0,2},{1,3},{2,0},{3,1},{4,6},{5,7},{6,4},{7,5},{8,10},{9,11},{10,... | collective-permute-start | bytes 2568200 | tf_op jit(solution)/shard_map/ppermute | solution.py:40
  26.7 31.2 %collective-permute-start.3 = (bf16[3344,128]{1,0:T(8,128)(2,1)}, bf16[3344,128]{1,0:T(8,128)(2,1)S(1)}, u32[]{:S(2)}, u32[]{:S(2)}) collective-permute-start(bf16[3344,128]{1,0:T(8,128)(2,1)} %get-tuple-element.81), channel_id=1, source_target_pairs={{0,1},{1,0},{2,3},{3,2},{4,5},{5,4},{6,7},{7,6},{8,9},{9,8},{10,11... | collective-permute-start | bytes 2568200 | tf_op jit(solution)/shard_map/ppermute | solution.py:40
  32.1 37.2 %collective-permute-start.2 = (bf16[256,2048]{1,0:T(8,128)(2,1)}, bf16[256,2048]{1,0:T(8,128)(2,1)}, u32[]{:S(2)}, u32[]{:S(2)}) collective-permute-start(bf16[256,2048]{1,0:T(8,128)(2,1)} %get-tuple-element.83), channel_id=1, source_target_pairs={{0,2},{1,3},{2,0},{3,1},{4,6},{5,7},{6,4},{7,5},{8,10},{9,11},{10,... | collective-permute-start | bytes 3145736 | tf_op jit(solution)/shard_map/ppermute | solution.py:40
  32.4 22.4 %copy-start.11 = (bf16[192,2048]{1,0:T(8,128)(2,1)}, bf16[192,2048]{1,0:T(8,128)(2,1)S(1)}, u32[]{:S(2)}) copy-start(bf16[192,2048]{1,0:T(8,128)(2,1)S(1)} %pad_maximum_fusion.refs_0_) | copy-start | bytes 2359300
  32.4 64.1 %collective-permute-start.7 = (bf16[192,2048]{1,0:T(8,128)(2,1)S(1)}, bf16[192,2048]{1,0:T(8,128)(2,1)}, u32[]{:S(2)}, u32[]{:S(2)}) collective-permute-start(bf16[192,2048]{1,0:T(8,128)(2,1)S(1)} %pad_maximum_fusion.refs_0_), channel_id=1, source_target_pairs={{0,1},{1,0},{2,3},{3,2},{4,5},{5,4},{6,7},{7,6},{8,9},{9,8},{10,11... | collective-permute-start | bytes 2359304 | tf_op jit(solution)/shard_map/ppermute | solution.py:40
  46.8 40.7 %copy-start.1 = (bf16[3344,128]{1,0:T(8,128)(2,1)}, bf16[3344,128]{1,0:T(8,128)(2,1)S(1)}, u32[]{:S(2)}) copy-start(bf16[3344,128]{1,0:T(8,128)(2,1)S(1)} %collective-permute-done.4.refs_3_.refs_6_.refs_4_.refs_8_.refs_12_.refs_7_) | copy-start | bytes 2568196
  46.8 38.9 %collective-permute-start.8 = (bf16[192,2048]{1,0:T(8,128)(2,1)S(1)}, bf16[192,2048]{1,0:T(8,128)(2,1)}, u32[]{:S(2)}, u32[]{:S(2)}) collective-permute-start(bf16[192,2048]{1,0:T(8,128)(2,1)S(1)} %pad_maximum_fusion.refs_0_), channel_id=1, source_target_pairs={{0,2},{1,3},{2,0},{3,1},{4,6},{5,7},{6,4},{7,5},{8,10},{9,11},{10,... | collective-permute-start | bytes 2359304 | tf_op jit(solution)/shard_map/ppermute | solution.py:40
  48.8 38.6 %collective-permute-start.5 = (bf16[3344,128]{1,0:T(8,128)(2,1)S(1)}, bf16[3344,128]{1,0:T(8,128)(2,1)S(1)}, u32[]{:S(2)}, u32[]{:S(2)}) collective-permute-start(bf16[3344,128]{1,0:T(8,128)(2,1)S(1)} %collective-permute-done.4.refs_3_.refs_6_.refs_4_.refs_8_.refs_12_.refs_7_), channel_id=1, source_target_pairs={{0,1},{1,0},{2,3},{3,2},{4,5},{5,4},{6,7},{7,6},{8,9},{9,8},{10,11... | collective-permute-start | bytes 2568200 | tf_op jit(solution)/shard_map/ppermute | solution.py:40
  50.6 7.2 %copy-start.29 = (s32[16]{0:T(128)S(1)}, s32[16]{0:T(128)}, u32[]{:S(2)}) copy-start(s32[16]{0:T(128)} %param.27) | copy-start | bytes 196
  57.9 31.6 %copy-start.2 = (bf16[3344,128]{1,0:T(8,128)(2,1)}, bf16[3344,128]{1,0:T(8,128)(2,1)S(1)}, u32[]{:S(2)}) copy-start(bf16[3344,128]{1,0:T(8,128)(2,1)S(1)} %collective-permute-done.3.refs_2_.refs_5_.refs_3_.refs_7_.refs_11_.refs_6_) | copy-start | bytes 2568196
  57.9 54.5 %collective-permute-start.6 = (bf16[512,1536]{1,0:T(8,128)(2,1)}, bf16[512,1536]{1,0:T(8,128)(2,1)}, u32[]{:S(2)}, u32[]{:S(2)}) collective-permute-start(bf16[512,1536]{1,0:T(8,128)(2,1)} %shard_map.317), channel_id=1, source_target_pairs={{0,1},{1,0},{2,3},{3,2},{4,5},{5,4},{6,7},{7,6},{8,9},{9,8},{10,11... | collective-permute-start | bytes 4718600 | tf_op jit(solution)/shard_map/ppermute | solution.py:40
  85.7 25.0 %collective-permute-start.10 = (bf16[256,2048]{1,0:T(8,128)(2,1)}, bf16[256,2048]{1,0:T(8,128)(2,1)}, u32[]{:S(2)}, u32[]{:S(2)}) collective-permute-start(bf16[256,2048]{1,0:T(8,128)(2,1)} %get-tuple-element.98), channel_id=1, source_target_pairs={{0,2},{1,3},{2,0},{3,1},{4,6},{5,7},{6,4},{7,5},{8,10},{9,11},{10,... | collective-permute-start | bytes 3145736 | tf_op jit(solution)/shard_map/ppermute | solution.py:40
  87.4 9.1 %collective-permute-start.9 = (bf16[192,2048]{1,0:T(8,128)(2,1)}, bf16[192,2048]{1,0:T(8,128)(2,1)}, u32[]{:S(2)}, u32[]{:S(2)}) collective-permute-start(bf16[192,2048]{1,0:T(8,128)(2,1)} %collective-permute-done.8.refs_2_), channel_id=1, source_target_pairs={{0,1},{1,0},{2,3},{3,2},{4,5},{5,4},{6,7},{7,6},{8,9},{9,8},{10,11... | collective-permute-start | bytes 2359304 | tf_op jit(solution)/shard_map/ppermute | solution.py:40
  103.5 21.0 %all-to-all-start = ((bf16[8,128,256]{2,1,0:T(8,128)(2,1)}), bf16[8,128,256]{2,1,0:T(8,128)(2,1)S(1)}, u32[]{:S(2)}, u32[]{:S(2)}) async-start(bf16[8,128,256]{2,1,0:T(8,128)(2,1)} %bitcast.66), calls=%async_computation | async-start | bytes 1048576 | tf_op jit(solution)/shard_map/all_to_all | solution.py:800
  110.6 28.6 %collective-permute-start.11 = (bf16[256,2048]{1,0:T(8,128)(2,1)}, bf16[256,2048]{1,0:T(8,128)(2,1)}, u32[]{:S(2)}, u32[]{:S(2)}) collective-permute-start(bf16[256,2048]{1,0:T(8,128)(2,1)} %get-tuple-element.99), channel_id=1, source_target_pairs={{0,3},{1,2},{2,1},{3,0},{4,7},{5,6},{6,5},{7,4},{8,11},{9,10},{10,... | collective-permute-start | bytes 3145736 | tf_op jit(solution)/shard_map/ppermute | solution.py:40
  124.5 6.9 %copy-start.12 = (bf16[8,128,256]{2,1,0:T(8,128)(2,1)}, bf16[8,128,256]{2,1,0:T(8,128)(2,1)S(1)}, u32[]{:S(2)}) copy-start(bf16[8,128,256]{2,1,0:T(8,128)(2,1)S(1)} %all-to-all-done) | copy-start | bytes 1572868
  124.5 18.3 %all-to-all-start.1 = ((bf16[8,1,128,256]{3,2,1,0:T(8,128)(2,1)}), bf16[8,1,128,256]{3,2,1,0:T(8,128)(2,1)S(1)}, u32[]{:S(2)}, u32[]{:S(2)}) async-start(bf16[8,1,128,256]{3,2,1,0:T(8,128)(2,1)} %bitcast.61), calls=%async_computation.1 | async-start | bytes 1048576 | tf_op jit(solution)/shard_map/all_to_all | solution.py:800
  131.4 11.4 %copy-start.9 = (bf16[512,2048]{1,0:T(8,128)(2,1)S(1)}, bf16[512,2048]{1,0:T(8,128)(2,1)}, u32[]{:S(2)}) copy-start(bf16[512,2048]{1,0:T(8,128)(2,1)} %shard_map.321) | copy-start | bytes 6291460
  142.8 6.8 %copy-start.13 = (bf16[8,1,128,256]{3,2,1,0:T(8,128)(2,1)}, bf16[8,1,128,256]{3,2,1,0:T(8,128)(2,1)S(1)}, u32[]{:S(2)}) copy-start(bf16[8,1,128,256]{3,2,1,0:T(8,128)(2,1)S(1)} %all-to-all-done.1) | copy-start | bytes 1572868
  142.8 31.0 %collective-permute-start.12 = (bf16[512,2048]{1,0:T(8,128)(2,1)S(1)}, bf16[512,2048]{1,0:T(8,128)(2,1)}, u32[]{:S(2)}, u32[]{:S(2)}) collective-permute-start(bf16[512,2048]{1,0:T(8,128)(2,1)S(1)} %copy-done.9), channel_id=1, source_target_pairs={{0,1},{1,0},{2,3},{3,2},{4,5},{5,4},{6,7},{7,6},{8,9},{9,8},{10,11... | collective-permute-start | bytes 6291464 | tf_op jit(solution)/shard_map/ppermute | solution.py:40
  142.8 31.0 %all-to-all-start.2 = ((bf16[8,2,128,256]{3,2,1,0:T(8,128)(2,1)}), bf16[8,2,128,256]{3,2,1,0:T(8,128)(2,1)}, u32[]{:S(2)}, u32[]{:S(2)}) async-start(bf16[8,2,128,256]{3,2,1,0:T(8,128)(2,1)} %bitcast.57), calls=%async_computation.2 | async-start | bytes 2097152 | tf_op jit(solution)/shard_map/all_to_all | solution.py:800
  147.3 16.7 %collective-permute-start.13 = (bf16[1552,128]{1,0:T(8,128)(2,1)}, bf16[1552,128]{1,0:T(8,128)(2,1)S(1)}, u32[]{:S(2)}, u32[]{:S(2)}) collective-permute-start(bf16[1552,128]{1,0:T(8,128)(2,1)} %get-tuple-element.85), channel_id=1, source_target_pairs={{0,1},{1,0},{2,3},{3,2},{4,5},{5,4},{6,7},{7,6},{8,9},{9,8},{10,11... | collective-permute-start | bytes 1191944 | tf_op jit(solution)/shard_map/ppermute | solution.py:40
  147.9 12.3 %collective-permute-start.14 = (bf16[1552,128]{1,0:T(8,128)(2,1)}, bf16[1552,128]{1,0:T(8,128)(2,1)S(1)}, u32[]{:S(2)}, u32[]{:S(2)}) collective-permute-start(bf16[1552,128]{1,0:T(8,128)(2,1)} %get-tuple-element.102), channel_id=1, source_target_pairs={{0,2},{1,3},{2,0},{3,1},{4,6},{5,7},{6,4},{7,5},{8,10},{9,11},{10,... | collective-permute-start | bytes 1191944 | tf_op jit(solution)/shard_map/ppermute | solution.py:40
  149.9 34.0 %collective-permute-start.16 = (bf16[256,2048]{1,0:T(8,128)(2,1)}, bf16[256,2048]{1,0:T(8,128)(2,1)}, u32[]{:S(2)}, u32[]{:S(2)}) collective-permute-start(bf16[256,2048]{1,0:T(8,128)(2,1)} %get-tuple-element.105), channel_id=1, source_target_pairs={{0,3},{1,2},{2,1},{3,0},{4,7},{5,6},{6,5},{7,4},{8,11},{9,10},{10,... | collective-permute-start | bytes 3145736 | tf_op jit(solution)/shard_map/ppermute | solution.py:40
  160.3 23.5 %copy-start.15 = (bf16[1552,128]{1,0:T(8,128)(2,1)}, bf16[1552,128]{1,0:T(8,128)(2,1)S(1)}, u32[]{:S(2)}) copy-start(bf16[1552,128]{1,0:T(8,128)(2,1)S(1)} %collective-permute-done.14.refs_8_.refs_12_.refs_11_) | copy-start | bytes 1191940
  160.3 3.7 %collective-permute-start.15 = (bf16[1552,128]{1,0:T(8,128)(2,1)S(1)}, bf16[1552,128]{1,0:T(8,128)(2,1)S(1)}, u32[]{:S(2)}, u32[]{:S(2)}) collective-permute-start(bf16[1552,128]{1,0:T(8,128)(2,1)S(1)} %collective-permute-done.14.refs_8_.refs_12_.refs_11_), channel_id=1, source_target_pairs={{0,1},{1,0},{2,3},{3,2},{4,5},{5,4},{6,7},{7,6},{8,9},{9,8},{10,11... | collective-permute-start | bytes 1191944 | tf_op jit(solution)/shard_map/ppermute | solution.py:40
  164.0 19.8 %copy-start.14 = (bf16[1552,128]{1,0:T(8,128)(2,1)}, bf16[1552,128]{1,0:T(8,128)(2,1)S(1)}, u32[]{:S(2)}) copy-start(bf16[1552,128]{1,0:T(8,128)(2,1)S(1)} %collective-permute-done.13.refs_7_.refs_11_.refs_10_) | copy-start | bytes 1191940
  164.0 19.8 %copy-start.16 = (bf16[1552,128]{1,0:T(8,128)(2,1)}, bf16[1552,128]{1,0:T(8,128)(2,1)S(1)}, u32[]{:S(2)}) copy-start(bf16[1552,128]{1,0:T(8,128)(2,1)S(1)} %collective-permute-done.15.refs_9_.refs_13_.refs_12_) | copy-start | bytes 1191940
  183.8 58.7 %all-to-all-start.3 = ((bf16[8,4,128,256]{3,2,1,0:T(8,128)(2,1)}), bf16[8,4,128,256]{3,2,1,0:T(8,128)(2,1)S(1)}, u32[]{:S(2)}, u32[]{:S(2)}) async-start(bf16[8,4,128,256]{3,2,1,0:T(8,128)(2,1)} %shard_map.322), calls=%async_computation.3 | async-start | bytes 4194304 | tf_op jit(solution)/shard_map/all_to_all | solution.py:800
  221.2 1.8 collective-permute-start.19
  221.3 3.3 collective-permute-start.17
  224.0 6.4 %collective-permute-start.20 = (bf16[512,128]{1,0:T(8,128)(2,1)S(1)}, bf16[512,128]{1,0:T(8,128)(2,1)S(1)}, u32[]{:S(2)}, u32[]{:S(2)}) collective-permute-start(bf16[512,128]{1,0:T(8,128)(2,1)S(1)} %add_convert_fusion.4), channel_id=1, source_target_pairs={{0,2},{1,3},{2,0},{3,1},{4,6},{5,7},{6,4},{7,5},{8,10},{9,11},{10,... | collective-permute-start | bytes 393224 | tf_op jit(solution)/shard_map/ppermute | solution.py:40
  225.6 7.6 %collective-permute-start.18 = (bf16[512,128]{1,0:T(8,128)(2,1)S(1)}, bf16[512,128]{1,0:T(8,128)(2,1)S(1)}, u32[]{:S(2)}, u32[]{:S(2)}) collective-permute-start(bf16[512,128]{1,0:T(8,128)(2,1)S(1)} %add_convert_fusion.5), channel_id=1, source_target_pairs={{0,2},{1,3},{2,0},{3,1},{4,6},{5,7},{6,4},{7,5},{8,10},{9,11},{10,... | collective-permute-start | bytes 393224 | tf_op jit(solution)/shard_map/ppermute | solution.py:40
  227.2 6.9 %collective-permute-start.21 = (bf16[32,2048]{1,0:T(8,128)(2,1)}, bf16[32,2048]{1,0:T(8,128)(2,1)S(1)}, u32[]{:S(2)}, u32[]{:S(2)}) collective-permute-start(bf16[32,2048]{1,0:T(8,128)(2,1)} %get-tuple-element.116), channel_id=1, source_target_pairs={{0,1},{1,0},{2,3},{3,2},{4,5},{5,4},{6,7},{7,6},{8,9},{9,8},{10,11... | collective-permute-start | bytes 393224 | tf_op jit(solution)/shard_map/ppermute | solution.py:40
  227.2 8.9 %collective-permute-start.22 = (bf16[32,2048]{1,0:T(8,128)(2,1)}, bf16[32,2048]{1,0:T(8,128)(2,1)S(1)}, u32[]{:S(2)}, u32[]{:S(2)}) collective-permute-start(bf16[32,2048]{1,0:T(8,128)(2,1)} %get-tuple-element.117), channel_id=1, source_target_pairs={{0,2},{1,3},{2,0},{3,1},{4,6},{5,7},{6,4},{7,5},{8,10},{9,11},{10,... | collective-permute-start | bytes 393224 | tf_op jit(solution)/shard_map/ppermute | solution.py:40
  227.7 9.5 %collective-permute-start.23 = (bf16[32,2048]{1,0:T(8,128)(2,1)}, bf16[32,2048]{1,0:T(8,128)(2,1)S(1)}, u32[]{:S(2)}, u32[]{:S(2)}) collective-permute-start(bf16[32,2048]{1,0:T(8,128)(2,1)} %get-tuple-element.118), channel_id=1, source_target_pairs={{0,3},{1,2},{2,1},{3,0},{4,7},{5,6},{6,5},{7,4},{8,11},{9,10},{10,... | collective-permute-start | bytes 393224 | tf_op jit(solution)/shard_map/ppermute | solution.py:40
  242.5 38.1 %all-to-all-start.4 = ((bf16[8,640,128]{2,1,0:T(8,128)(2,1)}), bf16[8,640,128]{2,1,0:T(8,128)(2,1)S(1)}, u32[]{:S(2)}, u32[]{:S(2)}) async-start(bf16[8,640,128]{2,1,0:T(8,128)(2,1)} %bitcast.56), calls=%async_computation.4 | async-start | bytes 2621440 | tf_op jit(solution)/shard_map/all_to_all | solution.py:949
  248.4 105.3 %all-gather.6.cloned.1.call-start = ((), (), s32[]{:S(2)}) async-start(), calls=%async_computation.7 | async-start | bytes 2359296 | tf_op jit(solution)/shard_map/all_gather | solution.py:1081
  253.2 8.2 %collective-permute-start.30 = (f32[512,128]{1,0:T(8,128)}, f32[512,128]{1,0:T(8,128)S(1)}, u32[]{:S(2)}, u32[]{:S(2)}) collective-permute-start(f32[512,128]{1,0:T(8,128)} %get-tuple-element.120), channel_id=1, source_target_pairs={{0,1},{1,0},{2,3},{3,2},{4,5},{5,4},{6,7},{7,6},{8,9},{9,8},{10,11... | collective-permute-start | bytes 786440 | tf_op jit(solution)/shard_map/ppermute | solution.py:40
  253.5 7.8 %copy-start.18 = (f32[512,128]{1,0:T(8,128)S(1)}, f32[512,128]{1,0:T(8,128)}, u32[]{:S(2)}) copy-start(f32[512,128]{1,0:T(8,128)} %get-tuple-element.120) | copy-start | bytes 786436
  253.5 11.0 %copy-start.17 = (bf16[128,1536]{1,0:T(8,128)(2,1)S(1)}, bf16[128,1536]{1,0:T(8,128)(2,1)}, u32[]{:S(2)}) copy-start(bf16[128,1536]{1,0:T(8,128)(2,1)} %get-tuple-element.133) | copy-start | bytes 1179652
  261.2 1.7 collective-permute-start.26
  261.4 6.2 %collective-permute-start.31 = (bf16[512,128]{1,0:T(8,128)(2,1)S(1)}, bf16[512,128]{1,0:T(8,128)(2,1)S(1)}, u32[]{:S(2)}, u32[]{:S(2)}) collective-permute-start(bf16[512,128]{1,0:T(8,128)(2,1)S(1)} %add_convert_fusion.2), channel_id=1, source_target_pairs={{0,2},{1,3},{2,0},{3,1},{4,6},{5,7},{6,4},{7,5},{8,10},{9,11},{10,... | collective-permute-start | bytes 393224 | tf_op jit(solution)/shard_map/ppermute | solution.py:40
  263.9 6.5 %collective-permute-start.27 = (bf16[512,128]{1,0:T(8,128)(2,1)S(1)}, bf16[512,128]{1,0:T(8,128)(2,1)S(1)}, u32[]{:S(2)}, u32[]{:S(2)}) collective-permute-start(bf16[512,128]{1,0:T(8,128)(2,1)S(1)} %add_convert_fusion.3), channel_id=1, source_target_pairs={{0,2},{1,3},{2,0},{3,1},{4,6},{5,7},{6,4},{7,5},{8,10},{9,11},{10,... | collective-permute-start | bytes 393224 | tf_op jit(solution)/shard_map/ppermute | solution.py:40
  265.2 6.0 %collective-permute-start.32 = (bf16[32,1536]{1,0:T(8,128)(2,1)S(1)}, bf16[32,1536]{1,0:T(8,128)(2,1)S(1)}, u32[]{:S(2)}, u32[]{:S(2)}) collective-permute-start(bf16[32,1536]{1,0:T(8,128)(2,1)S(1)} %get-tuple-element.157), channel_id=1, source_target_pairs={{0,1},{1,0},{2,3},{3,2},{4,5},{5,4},{6,7},{7,6},{8,9},{9,8},{10,11... | collective-permute-start | bytes 294920 | tf_op jit(solution)/shard_map/ppermute | solution.py:40
  265.2 7.3 %collective-permute-start.33 = (bf16[32,1536]{1,0:T(8,128)(2,1)S(1)}, bf16[32,1536]{1,0:T(8,128)(2,1)S(1)}, u32[]{:S(2)}, u32[]{:S(2)}) collective-permute-start(bf16[32,1536]{1,0:T(8,128)(2,1)S(1)} %get-tuple-element.156), channel_id=1, source_target_pairs={{0,2},{1,3},{2,0},{3,1},{4,6},{5,7},{6,4},{7,5},{8,10},{9,11},{10,... | collective-permute-start | bytes 294920 | tf_op jit(solution)/shard_map/ppermute | solution.py:40
  266.7 7.2 %collective-permute-start.34 = (bf16[32,1536]{1,0:T(8,128)(2,1)S(1)}, bf16[32,1536]{1,0:T(8,128)(2,1)S(1)}, u32[]{:S(2)}, u32[]{:S(2)}) collective-permute-start(bf16[32,1536]{1,0:T(8,128)(2,1)S(1)} %get-tuple-element.155), channel_id=1, source_target_pairs={{0,3},{1,2},{2,1},{3,0},{4,7},{5,6},{6,5},{7,4},{8,11},{9,10},{10,... | collective-permute-start | bytes 294920 | tf_op jit(solution)/shard_map/ppermute | solution.py:40
  306.1 11.5 %copy-start.30 = (bf16[2,128,2048]{2,1,0:T(8,128)(2,1)S(1)}, bf16[2,128,2048]{2,1,0:T(8,128)(2,1)}, u32[]{:S(2)}) copy-start(bf16[2,128,2048]{2,1,0:T(8,128)(2,1)} %get-tuple-element.124) | copy-start | bytes 3145732
  317.6 6.6 %copy-start.8 = (f32[2,128,2048]{2,1,0:T(8,128)S(1)}, f32[2,128,2048]{2,1,0:T(8,128)}, u32[]{:S(2)}) copy-start(f32[2,128,2048]{2,1,0:T(8,128)} %get-tuple-element.123) | copy-start | bytes 6291460
  317.6 3.5 collective-permute-start.28
  317.7 6.6 %collective-permute-start.24 = (bf16[2,128,2048]{2,1,0:T(8,128)(2,1)S(1)}, bf16[2,128,2048]{2,1,0:T(8,128)(2,1)S(1)}, u32[]{:S(2)}, u32[]{:S(2)}) collective-permute-start(bf16[2,128,2048]{2,1,0:T(8,128)(2,1)S(1)} %copy-done.30), channel_id=1, source_target_pairs={{0,1},{1,0},{2,3},{3,2},{4,5},{5,4},{6,7},{7,6},{8,9},{9,8},{10,11... | collective-permute-start | bytes 3145736 | tf_op jit(solution)/shard_map/ppermute | solution.py:40
  323.7 15.1 %collective-permute-start.29 = (bf16[128,2048]{1,0:T(8,128)(2,1)}, bf16[128,2048]{1,0:T(8,128)(2,1)}, u32[]{:S(2)}, u32[]{:S(2)}) collective-permute-start(bf16[128,2048]{1,0:T(8,128)(2,1)} %fusion.8), channel_id=1, source_target_pairs={{0,2},{1,3},{2,0},{3,1},{4,6},{5,7},{6,4},{7,5},{8,10},{9,11},{10,... | collective-permute-start | bytes 1572872 | tf_op jit(solution)/shard_map/ppermute | solution.py:40
  325.2 24.0 %collective-permute-start.25 = (bf16[128,2048]{1,0:T(8,128)(2,1)}, bf16[128,2048]{1,0:T(8,128)(2,1)}, u32[]{:S(2)}, u32[]{:S(2)}) collective-permute-start(bf16[128,2048]{1,0:T(8,128)(2,1)} %fusion.7), channel_id=1, source_target_pairs={{0,2},{1,3},{2,0},{3,1},{4,6},{5,7},{6,4},{7,5},{8,10},{9,11},{10,... | collective-permute-start | bytes 1572872 | tf_op jit(solution)/shard_map/ppermute | solution.py:40
  329.4 19.8 %copy-start.10 = (bf16[2,128,2048]{2,1,0:T(8,128)(2,1)S(1)}, bf16[2,128,2048]{2,1,0:T(8,128)(2,1)}, u32[]{:S(2)}) copy-start(bf16[2,128,2048]{2,1,0:T(8,128)(2,1)} %get-tuple-element.126) | copy-start | bytes 3145732
  344.4 6.2 %copy-start.28 = (f32[2048]{0:T(1024)S(1)}, f32[2048]{0:T(1024)}, u32[]{:S(2)}) copy-start(f32[2048]{0:T(1024)} %param.37) | copy-start | bytes 24580
  (11 other events, 34.1 us)
Sparse Core Ops, SparseCore 0:
  24.4 62.5 all-gather.3
  306.2 47.5 all-gather.5
